TPU v7x, 32 devices: a whole 2x2x4 slice. The times are simulated.
32 devices in a mesh: ctx: 8 (over z, y), tp: 4 (over x, core).
Axes of the slice: x: 2, y: 2, z: 4, core: 2. Of those that a mesh axis runs over, the one named last changes fastest.
Arguments:
- gate_in: bfloat16 [1024, 4096], P('ctx', 'tp'), may hold values from -250 to 250, as said below
- conv_in: bfloat16 [1024, 4096], P('ctx', 'tp'), may hold values from -6 to 6
- value_in: bfloat16 [1024, 4096], P('ctx', 'tp'), may hold values from -6 to 6
- filter_taps: float32 [128, 4096], P(None, 'tp'), may hold values from -0.5 to 0.5
- norm_gain: float32 [4096], P('tp'), may hold values from 0.1 to 1.9
- qkv_weight: bfloat16 [4096, 3, 2048], P(None, None, 'tp'), may hold values from -0.5 to 0.5
Outputs:
- attended: bfloat16 [1024, 2048], P('ctx', 'tp')
Inputs may be any that keep to these rules, and one draw needn't show every extreme that they name: `gate_in`: gate values; channels and bases carry different scales.
All inputs are finite; a program needn't handle non-finite values.
Results may differ from a plain program's by a relative error of at most 0.027.
Values may be sent and summed in bfloat16 or wider, within the bound.
No kernel may reach another device: no remote copies, remote signals or barrier semaphores. Data moves between devices by JAX's collectives and lax.ppermute only.
A program may use at most 192 MiB of HBM per device.

v0:
```python
import math

import jax
import jax.numpy as jnp
from jax import lax
from jax.sharding import PartitionSpec as P

D = 4096
HEAD_DIM = 128


def passed_along(value, axis, by):
    devices = lax.axis_size(axis)
    pairs = [(i, i + by) for i in range(devices) if 0 <= i + by < devices]
    return lax.ppermute(value, axis, pairs)


def causal_filter(full, taps):
    span = taps.shape[0]
    channels = full.shape[1]
    stride = math.gcd(span, 32)
    reach_count = span // stride
    out_blocks = (full.shape[0] - span) // stride
    blocks = full.reshape(full.shape[0] // stride, stride, channels)
    windows = jnp.stack(
        [blocks[offset : offset + out_blocks] for offset in range(reach_count + 1)], axis=0
    )
    within = jnp.arange(stride, dtype=jnp.int32)
    block_start = jnp.arange(reach_count + 1, dtype=jnp.int32) * stride
    tap_index = span + within[None, :, None] - block_start[:, None, None] - within[None, None, :]
    valid = (tap_index >= 0) & (tap_index < span)
    weights_table = jnp.where(valid[:, :, :, None], taps[jnp.clip(tap_index, 0, span - 1)], 0.0)
    result = jnp.einsum("mksc,misc->kic", windows, weights_table, precision=lax.Precision.HIGHEST)
    return result.reshape(out_blocks * stride, channels)


def body(gate_in, conv_in, value_in, filter_taps, norm_gain, qkv_weight):
    rows = gate_in.shape[0]
    taps = filter_taps.shape[0]
    channels = gate_in.shape[1]
    mixed = (conv_in.astype(jnp.float32) * value_in.astype(jnp.float32)).astype(jnp.bfloat16)
    rim = passed_along(mixed[rows - (taps - 1) :], "ctx", 1)
    full = jnp.concatenate([jnp.zeros((1, channels), jnp.bfloat16), rim, mixed], axis=0).astype(
        jnp.float32
    )
    filtered = causal_filter(full, filter_taps)
    hyena = (gate_in.astype(jnp.float32) * filtered).astype(jnp.bfloat16).astype(jnp.float32)
    squares = jnp.sum(hyena * hyena, axis=1)
    summed = lax.psum(squares, "tp")
    normed = (hyena * lax.rsqrt(summed / D + 1e-06)[:, None] * norm_gain[None, :]).astype(
        jnp.bfloat16
    )
    width = qkv_weight.shape[2]
    heads_here = width // HEAD_DIM
    flat = qkv_weight.reshape(qkv_weight.shape[0], 3 * width)
    proj = jnp.dot(
        lax.all_gather(normed, "tp", axis=1, tiled=True), flat, preferred_element_type=jnp.float32
    )
    proj = proj.astype(jnp.bfloat16).reshape(rows, 3, heads_here, HEAD_DIM)
    query = proj[:, 0]
    keys = proj[:, 1]
    values = proj[:, 2]
    index = lax.axis_index("ctx")
    half = rows // 2
    local = jnp.arange(rows, dtype=jnp.int32)
    positions = index * rows + local
    scale = 1.0 / math.sqrt(HEAD_DIM)
    start = jnp.int32(0)
    key_piece = lax.all_gather(keys, "ctx", axis=0, tiled=True)
    value_piece = lax.all_gather(values, "ctx", axis=0, tiled=True)
    key_pos = jnp.arange(key_piece.shape[0], dtype=jnp.int32)
    running_max = jnp.full((rows, heads_here), -1e30, jnp.float32)
    running_total = jnp.zeros((rows, heads_here), jnp.float32)
    running_acc = jnp.zeros((rows, heads_here, HEAD_DIM), jnp.float32)
    outputs = []
    for which in range(2):
        lower = which * half
        qpart = query[lower : lower + half]
        qpos = positions[lower : lower + half]
        state = (
            running_max[lower : lower + half],
            running_total[lower : lower + half],
            running_acc[lower : lower + half],
        )

        def compute(state):
            old_max, old_total, old_acc = state
            scores = (
                jnp.einsum("qhd,khd->hqk", qpart, key_piece, preferred_element_type=jnp.float32)
                * scale
            )
            allowed = (qpos[:, None] >= key_pos[None, :])[None]
            scores = jnp.where(allowed, scores, -1e30)
            new_max = jnp.maximum(old_max, jnp.max(scores, axis=2).T)
            expo = jnp.where(allowed, jnp.exp(scores - new_max.T[:, :, None]), 0.0)
            new_total = jnp.sum(expo, axis=2).T
            weights = expo.astype(jnp.bfloat16)
            added = jnp.einsum(
                "hqk,khd->qhd", weights, value_piece, preferred_element_type=jnp.float32
            )
            return (new_max, new_total, added)

        def keep(state):
            return state

        outputs.append(lax.cond(start <= jnp.max(qpos), compute, keep, state))
    final_max, final_total, final_acc = tuple(
        (jnp.concatenate([outputs[0][slot], outputs[1][slot]], axis=0) for slot in range(3))
    )
    attended = (final_acc / final_total[:, :, None]).astype(jnp.bfloat16).reshape(rows, width)
    return attended


def solution(mesh):
    placed = (
        P("ctx", "tp"),
        P("ctx", "tp"),
        P("ctx", "tp"),
        P(None, "tp"),
        P("tp"),
        P(None, None, "tp"),
    )
    return jax.shard_map(
        body, mesh=mesh, in_specs=placed, out_specs=P("ctx", "tp"), check_vma=False
    )
```

profile of v0, /device:TPU:1, one launch (start us, length us, event | category | flops | bytes accessed | tf_op | source)
XLA Modules:
  0.0 329.0 jit_solution(9267805371440373997)
XLA Ops:
  6.5 0.0 copy-start
  6.5 0.0 all-gather.6.cloned.1.call-start
  6.5 1.2 multiply_convert_fusion
  7.7 0.1 slice.66
  7.8 4.0 %collective-permute-start = (bf16[127,1024]{1,0:T(8,128)(2,1)S(1)}, bf16[127,1024]{1,0:T(8,128)(2,1)S(1)}, u32[]{:S(2)}, u32[]{:S(2)}) collective-permute-start(bf16[127,1024]{1,0:T(8,128)(2,1)S(1)} %slice.66), channel_id=1, source_target_pairs={{0,4},{4,8},{8,12},{12,16},{16,20},{20,24},{24,28},{1,5},{5,9},{9,... | collective-permute-start | bytes 780296 | tf_op jit(solution)/shard_map/ppermute | solution.py:15
  11.8 0.1 broadcast_subtract_fusion
  11.9 0.1 compare_select_fusion
  12.0 0.1 reshape.159
  12.1 0.0 copy-done
  12.1 23.0 %gather_fusion = f32[5120,1024]{1,0:T(8,128)} fusion(f32[128,1024]{1,0:T(8,128)S(1)} %copy-done, s32[5120]{0:T(1024)S(1)} %broadcast_clamp_fusion), kind=kCustom, calls=%fused_computation | custom fusion | bytes 41963520 | tf_op jit(solution)/shard_map/gather | solution.py:32
  35.1 62.4 %copy.36 = f32[5,32,32,1024]{2,1,0,3:T(8,128)} copy(f32[5,32,32,1024]{3,2,1,0:T(8,128)} %bitcast.65) | data formatting | bytes 41943040 | tf_op jit(solution)/shard_map/gather | solution.py:32
  97.5 0.1 fusion.30
  97.6 0.0 collective-permute-done
  97.6 0.1 maximum_convert_fusion
  97.7 0.3 fusion.34
  98.3 6.6 %copy.37 = f32[5,4,32,1024]{2,1,0,3:T(4,128)} copy(f32[5,4,32,1024]{3,2,1,0:T(8,128)S(1)} %constant_dynamic-update-slice_fusion) | data formatting | bytes 5242880 | tf_op jit(solution)/shard_map/stack | solution.py:25
  104.9 0.0 copy-start.2
  104.9 0.0 copy-start.3
  104.9 92.6 %fusion.20 = f32[4,32,1024]{1,0,2:T(4,128)S(1)} fusion(f32[5,4,32,1024]{2,1,0,3:T(4,128)} %copy.37, f32[5,32,32,1024]{2,1,0,3:T(8,128)} %copy.36, pred[5,32,32]{2,1,0:T(8,128)(4,1)S(1)} %fusion.30), kind=kOutput, calls=%fused_computation.34 | convolution fusion | flops 256901120 | bytes 24122368 | tf_op jit(solution)/shard_map/mksc,misc->kic/dot_general | solution.py:33
  197.5 0.8 copy.38
  198.2 0.0 copy-done.2
  198.3 0.2 fusion.23
  198.4 6.0 %psum.7 = f32[128]{0:T(128)S(1)} all-reduce(f32[128]{0:T(128)S(1)} %fusion.23), channel_id=1, replica_groups=mesh['ctx'=8,'tp'=4] {'tp'}, use_global_device_ids=true, to_apply=%region_2.3 | all-reduce | flops 128 | bytes 1024 | tf_op jit(solution)/shard_map/psum | solution.py:49
  204.4 0.0 copy-done.3
  204.4 0.8 fusion.25
  205.2 0.0 all-gather.6.cloned.1.call-update
  205.2 0.0 all-gather.8.cloned.1.call-start
  205.3 17.0 %copy.39 = bf16[4096,3,512]{0,2,1:T(8,128)(2,1)} copy(bf16[4096,3,512]{2,0,1:T(8,128)(2,1)} %param.15) | data formatting | bytes 25165824 | tf_op args[5]
  222.2 0.8 all-gather.6.cloned.1.call-done
  223.0 0.0 copy-start.1
  223.0 9.2 %convolution_convert_fusion = bf16[128,1536]{1,0:T(8,128)(2,1)S(1)} fusion(bf16[128,4096]{1,0:T(8,128)(2,1)} %all-gather.6.cloned.1.call-done, bf16[4096,1536]{0,1:T(8,128)(2,1)} %bitcast.66), kind=kOutput, calls=%fused_computation.33 | convolution fusion | flops 1610809344 | bytes 14024704 | tf_op jit(solution)/shard_map/dot_general | solution.py:56
  232.2 0.1 reshape.156
  232.3 0.1 fusion.35
  232.4 0.7 copy.46
  233.1 0.0 all-gather.8.cloned.1.call-update
  233.1 0.2 all-gather.10.cloned.1.call-start
  233.4 0.7 copy.47
  234.0 0.0 all-gather.10.cloned.1.call-update
  234.1 0.8 slice_reduce_fusion.1
  236.2 36.1 %all-gather.8.cloned.1.call-done = bf16[1024,1,4,128]{3,0,2,1:T(8,128)(2,1)} async-done(((bf16[128,1,4,128]{3,0,2,1:T(8,128)(2,1)}), bf16[1024,1,4,128]{3,0,2,1:T(8,128)(2,1)}) %all-gather.8.cloned.1.call-update) | async-done | bytes 1048592 | tf_op jit(solution)/shard_map/all_gather | solution.py:69
  272.2 41.2 %all-gather.10.cloned.1.call-done = bf16[1024,1,4,128]{3,0,2,1:T(8,128)(2,1)} async-done(((bf16[128,1,4,128]{3,0,2,1:T(8,128)(2,1)}), bf16[1024,1,4,128]{3,0,2,1:T(8,128)(2,1)}) %all-gather.10.cloned.1.call-update) | async-done | bytes 1048592 | tf_op jit(solution)/shard_map/all_gather | solution.py:70
  313.4 4.0 %conditional.2 = (f32[64,4]{0,1:T(4,128)S(1)}, f32[64,512]{1,0:T(8,128)S(1)}) conditional(s32[]{:T(128)} %convert_element_type.43, () %tuple.25, (s32[64]{0:T(128)S(1)}, s32[1024]{0:T(1024)S(1)}, bf16[128,3,4,128]{3,2,1,0:T(4,128)(2,1)S(1)}, bf16[1024,4,128]{2,0,1:T(8,128)(2,1)}, bf16[1024,4,128]{2,0,1:T(8,128)(2,1)}) %tuple.57), branch_computations={%region_3.4_spmd, %region_4.7_spmd} | conditional | flops 136642304 | bytes 6760720 | solution.py:106
  313.4 0.1 broadcast_compare_fusion
  313.5 0.1 copy.42
  313.6 1.8 fusion.32
  315.4 1.6 convolution_bitcast_fusion
  317.0 0.4 fusion.2
  317.4 4.0 %conditional.3 = (f32[64,4]{0,1:T(4,128)S(1)}, f32[64,512]{1,0:T(8,128)S(1)}) conditional(s32[]{:T(128)} %convert_element_type.53, () %tuple.27, (s32[64]{0:T(128)S(1)}, s32[1024]{0:T(1024)S(1)}, bf16[128,3,4,128]{3,2,1,0:T(4,128)(2,1)S(1)}, bf16[1024,4,128]{2,0,1:T(8,128)(2,1)}, bf16[1024,4,128]{2,0,1:T(8,128)(2,1)}) %tuple.58), branch_computations={%region_8.9_spmd, %region_9.12_spmd} | conditional | flops 136642304 | bytes 6760720 | solution.py:106
  317.4 0.1 broadcast_compare_fusion.1
  317.5 0.1 copy.43
  317.6 1.8 fusion.33
  319.4 1.6 convolution_bitcast_fusion.1
  321.0 0.4 fusion.10
  321.4 0.1 pad_maximum_fusion
  321.5 0.1 copy.44
  321.6 0.2 div.19
  321.8 0.7 fusion.27
  322.5 0.0 copy-done.1
  (17 shorter events, 0.3 us)
Async XLA Ops:
  6.5 5.5 %copy-start = (f32[128,1024]{1,0:T(8,128)S(1)}, f32[128,1024]{1,0:T(8,128)}, u32[]{:S(2)}) copy-start(f32[128,1024]{1,0:T(8,128)} %param.13) | copy-start | bytes 1572868
  6.5 216.5 %all-gather.6.cloned.1.call-start = ((), (), s32[]{:S(2)}) async-start(), calls=%async_computation | async-start | bytes 1310720 | tf_op jit(solution)/shard_map/all_gather | solution.py:57
  7.8 89.8 %collective-permute-start = (bf16[127,1024]{1,0:T(8,128)(2,1)S(1)}, bf16[127,1024]{1,0:T(8,128)(2,1)S(1)}, u32[]{:S(2)}, u32[]{:S(2)}) collective-permute-start(bf16[127,1024]{1,0:T(8,128)(2,1)S(1)} %slice.66), channel_id=1, source_target_pairs={{0,4},{4,8},{8,12},{12,16},{16,20},{20,24},{24,28},{1,5},{5,9},{9,... | collective-permute-start | bytes 780296 | tf_op jit(solution)/shard_map/ppermute | solution.py:15
  104.9 93.3 %copy-start.2 = (bf16[128,1024]{1,0:T(8,128)(2,1)S(1)}, bf16[128,1024]{1,0:T(8,128)(2,1)}, u32[]{:S(2)}) copy-start(bf16[128,1024]{1,0:T(8,128)(2,1)} %param.10) | copy-start | bytes 786436
  104.9 99.5 %copy-start.3 = (f32[1024]{0:T(1024)S(1)}, f32[1024]{0:T(1024)}, u32[]{:S(2)}) copy-start(f32[1024]{0:T(1024)} %param.14) | copy-start | bytes 12292
  205.2 67.0 %all-gather.8.cloned.1.call-start = ((), (), s32[]{:S(2)}) async-start(), calls=%async_computation.1 | async-start | bytes 1179648 | tf_op jit(solution)/shard_map/all_gather | solution.py:69
  223.0 99.5 %copy-start.1 = (f32[128,1024]{1,0:T(8,128)S(1)}, f32[128,1024]{1,0:T(8,128)}, u32[]{:S(2)}) copy-start(f32[128,1024]{1,0:T(8,128)} %param.13) | copy-start | bytes 1572868
  233.1 80.3 %all-gather.10.cloned.1.call-start = ((), (), s32[]{:S(2)}) async-start(), calls=%async_computation.2 | async-start | bytes 1179648 | tf_op jit(solution)/shard_map/all_gather | solution.py:70
Sparse Core Ops, SparseCore 0:
  205.3 17.6 all-gather.5
  233.3 38.9 all-gather.7
  274.4 38.9 all-gather.9
where the time goes:
time: 332 us; the launch traced here: 329 us
  local copies, waits for them, and re-layouts  112 us (34%)
  matrix products  109 us (33%)
  waiting for transfers between devices  78 us (23%)
  between operations  14.6 us (4%)
  blocking collectives  5.97 us (2%)
  other arithmetic  5.01 us (2%)
  starting transfers between devices  4.26 us (1%)
    dot_general x1, matrix products, causal_filter(): jnp.einsum('mksc,misc->kic', windows, weights_table, precision=lax.Precis...  92.6 us
    gather x2, local copies, waits for them, and re-layouts, causal_filter(): taps[jnp.clip(tap_index, 0, span - 1)]  85.4 us
    all_gather x1, waiting for transfers between devices, body(): value_piece = lax.all_gather(values, 'ctx', axis=0, tiled=True)  41.2 us
    all_gather x1, waiting for transfers between devices, body(): key_piece = lax.all_gather(keys, 'ctx', axis=0, tiled=True)  36.1 us
    unnamed x15, local copies, waits for them, and re-layouts  18.5 us
    dot_general x1, matrix products, body(): jnp.dot(lax.all_gather(normed, 'tp', axis=1, tiled=True), flat, preferred...  9.23 us
    another operation x2, local copies, waits for them, and re-layouts, causal_filter(): jnp.stack([blocks[offset:offset + out_blocks] for offset in range(reach_c...  6.68 us
  transfers between devices with their start and end apart: 4, of which 3 were waited for; matrix products, arithmetic and copies ran while one was open for 32% of the time, Pallas kernels for 0%

commit v1 on v0

v1 whole, which is shorter than its diff:
```python
import functools
import math

import jax
import jax.numpy as jnp
from jax import lax
from jax.experimental import pallas as pl
from jax.experimental.pallas import tpu as pltpu
from jax.sharding import PartitionSpec as P

HEAD_DIM = 128
LANES = 128
SLAB = 8
SPAN_OUT = 16
SPAN_IN = 8
EPS = 1e-06
BF16 = jnp.bfloat16
F32 = jnp.float32
VMEM = pl.BlockSpec(memory_space=pltpu.VMEM)


def to_slabs(source, target, first, rows):
    for group in range(SLAB):
        target[pl.ds(first * SLAB + group, rows, stride=SLAB), :] = source[
            :, group * LANES : (group + 1) * LANES
        ].astype(F32)


def slab(ref, index):
    return ref[pl.ds(pl.multiple_of(index * SLAB, SLAB), SLAB), :]


def add_taps(sums, x_ref, tap_ref, x_first, tap_first):
    taps = [slab(tap_ref, tap_first + d) for d in range(1 - SPAN_IN, SPAN_OUT)]
    sums = list(sums)
    for b in range(SPAN_IN):
        x = slab(x_ref, x_first + b)
        for a in range(SPAN_OUT):
            sums[a] = sums[a] + taps[a - b + SPAN_IN - 1] * x
    return tuple(sums)


def own_kernel(rows, span, mixed_ref, taps_ref, sums_ref, tap_ref, x_ref):
    tap_ref[pl.ds(0, SPAN_OUT * SLAB), :] = jnp.zeros((SPAN_OUT * SLAB, LANES), F32)
    tap_ref[pl.ds((SPAN_OUT + span) * SLAB, SPAN_OUT * SLAB), :] = jnp.zeros(
        (SPAN_OUT * SLAB, LANES), F32
    )
    to_slabs(taps_ref, tap_ref, SPAN_OUT, span)
    to_slabs(mixed_ref, x_ref, 0, rows)

    def block(t, _):
        def step(s, sums):
            return add_taps(
                sums, x_ref, tap_ref, s * SPAN_IN, SPAN_OUT + t * SPAN_OUT - s * SPAN_IN
            )

        sums = lax.fori_loop(
            0,
            (t + 1) * (SPAN_OUT // SPAN_IN),
            step,
            tuple(jnp.zeros((SLAB, LANES), F32) for _ in range(SPAN_OUT)),
        )
        for a in range(SPAN_OUT):
            sums_ref[
                pl.ds(pl.multiple_of((t * SPAN_OUT + a) * SLAB, SLAB), SLAB), :
            ] = sums[a]
        return 0

    lax.fori_loop(0, rows // SPAN_OUT, block, 0)


def rim_kernel(rows, span, rim_ref, sums_ref, tap_ref, gate_ref, hyena_ref, x_ref, full_ref):
    to_slabs(rim_ref, x_ref, 0, rows)

    def block(t, _):
        def step(s, sums):
            return add_taps(
                sums, x_ref, tap_ref, s * SPAN_IN, SPAN_OUT + rows + t * SPAN_OUT - s * SPAN_IN
            )

        sums = lax.fori_loop(
            t * (SPAN_OUT // SPAN_IN),
            rows // SPAN_IN,
            step,
            tuple(slab(sums_ref, t * SPAN_OUT + a) for a in range(SPAN_OUT)),
        )
        for a in range(SPAN_OUT):
            full_ref[
                pl.ds(pl.multiple_of((t * SPAN_OUT + a) * SLAB, SLAB), SLAB), :
            ] = sums[a]
        return 0

    lax.fori_loop(0, rows // SPAN_OUT, block, 0)
    for group in range(SLAB):
        lanes = slice(group * LANES, (group + 1) * LANES)
        hyena_ref[:, lanes] = (
            gate_ref[:, lanes].astype(F32) * full_ref[pl.ds(group, rows, stride=SLAB), :]
        ).astype(BF16)


def own_part(mixed, taps):
    rows, span = mixed.shape[0], taps.shape[0]
    return pl.pallas_call(
        functools.partial(own_kernel, rows, span),
        out_shape=(
            jax.ShapeDtypeStruct((rows * SLAB, LANES), F32),
            jax.ShapeDtypeStruct(((span + 2 * SPAN_OUT) * SLAB, LANES), F32),
        ),
        in_specs=[VMEM] * 2,
        out_specs=(VMEM, VMEM),
        scratch_shapes=[pltpu.VMEM((rows * SLAB, LANES), F32)],
        compiler_params=pltpu.CompilerParams(vmem_limit_bytes=16 << 20),
        cost_estimate=pl.CostEstimate(
            flops=rows * span * SLAB * LANES, bytes_accessed=1 << 21, transcendentals=0
        ),
        name="fir_own_rows",
    )(mixed, taps)


def rim_part(rim, sums, taps, gate):
    rows = gate.shape[0]
    span = taps.shape[0] // SLAB - 2 * SPAN_OUT
    return pl.pallas_call(
        functools.partial(rim_kernel, rows, span),
        out_shape=jax.ShapeDtypeStruct((rows, SLAB * LANES), BF16),
        in_specs=[VMEM] * 4,
        out_specs=VMEM,
        scratch_shapes=[pltpu.VMEM((rows * SLAB, LANES), F32)] * 2,
        compiler_params=pltpu.CompilerParams(vmem_limit_bytes=16 << 20),
        cost_estimate=pl.CostEstimate(
            flops=rows * span * SLAB * LANES, bytes_accessed=1 << 21, transcendentals=0
        ),
        name="fir_rim_rows",
    )(rim, sums, taps, gate)


def hyena_of(gate, mixed, rim, taps):
    rows, channels = gate.shape
    wide = SLAB * LANES
    pieces = []
    for first in range(0, channels, wide):
        cut = slice(first, min(first + wide, channels))

        def widened(value):
            part = value[:, cut]
            return jnp.pad(part, ((0, 0), (0, wide - part.shape[1])))

        sums, slabs = own_part(widened(mixed), widened(taps))
        piece = rim_part(widened(rim), sums, slabs, widened(gate))
        pieces.append(piece[:, : cut.stop - cut.start])
    return pieces[0] if len(pieces) == 1 else jnp.concatenate(pieces, axis=1)


def project(blocks, offsets, gain_ref, weight_ref, acc_ref, ssq_ref, me):
    width = weight_ref.shape[2]
    for block_ref, offset in zip(blocks, offsets):
        owner = jnp.bitwise_xor(me, offset)
        channels = block_ref.shape[1]
        hyena = block_ref[...].astype(F32)
        squares = hyena * hyena
        total = ssq_ref[...]
        for first in range(0, channels, LANES):
            total = total + squares[:, first : first + LANES]
        ssq_ref[...] = total
        scaled = (hyena * gain_ref[pl.ds(owner, 1), :]).astype(BF16)
        start = pl.multiple_of(owner * channels, channels)
        for which in range(3):
            acc_ref[:, which * width : (which + 1) * width] += jnp.dot(
                scaled,
                weight_ref[which, pl.ds(start, channels), :],
                preferred_element_type=F32,
            )


def first_kernel(offsets, me_ref, *refs):
    n = len(offsets)
    blocks, (gain_ref, weight_ref, acc_ref, ssq_ref) = refs[:n], refs[n:]
    acc_ref[...] = jnp.zeros_like(acc_ref)
    ssq_ref[...] = jnp.zeros_like(ssq_ref)
    project(blocks, offsets, gain_ref, weight_ref, acc_ref, ssq_ref, me_ref[0])


def last_kernel(offsets, model, me_ref, *refs):
    n = len(offsets)
    blocks, (gain_ref, weight_ref, acc_in, ssq_in), rest = refs[:n], refs[n : n + 4], refs[n + 4 :]
    outs, (acc_ref, ssq_ref) = rest[:-2], rest[-2:]
    acc_ref[...] = acc_in[...]
    ssq_ref[...] = ssq_in[...]
    project(blocks, offsets, gain_ref, weight_ref, acc_ref, ssq_ref, me_ref[0])
    msq = jnp.sum(ssq_ref[...], axis=1, keepdims=True) / model
    scale = lax.rsqrt(msq + EPS)
    rows = acc_ref.shape[0]
    width = weight_ref.shape[2]
    for k, out in enumerate(outs):
        head = jnp.bitwise_xor(me_ref[1], k)
        for which in range(3):
            lanes = pl.ds(pl.multiple_of(which * width + head * HEAD_DIM, LANES), HEAD_DIM)
            out[which * rows : (which + 1) * rows, :] = (acc_ref[:, lanes] * scale).astype(BF16)


def qkv_messages(mine, others, gain, weight, spot, model):
    rows = mine[0][1].shape[0]
    width = weight.shape[2]
    smem = pl.BlockSpec(memory_space=pltpu.SMEM)
    params = pltpu.CompilerParams(vmem_limit_bytes=24 << 20)
    acc_shape = jax.ShapeDtypeStruct((rows, 3 * width), F32)
    ssq_shape = jax.ShapeDtypeStruct((rows, LANES), F32)

    def cost(blocks):
        macs = len(blocks) * rows * blocks[0][1].shape[1] * 3 * width
        return pl.CostEstimate(
            flops=2 * macs, bytes_accessed=2 * macs // rows + (2 << 20), transcendentals=0
        )

    acc, ssq = pl.pallas_call(
        functools.partial(first_kernel, tuple(o for o, _ in mine)),
        out_shape=(acc_shape, ssq_shape),
        in_specs=[smem] + [VMEM] * (len(mine) + 2),
        out_specs=(VMEM, VMEM),
        compiler_params=params,
        cost_estimate=cost(mine),
        name="qkv_first_blocks",
    )(spot, *[b for _, b in mine], gain, weight)
    heads = width // HEAD_DIM
    return pl.pallas_call(
        functools.partial(last_kernel, tuple(o for o, _ in others), model),
        out_shape=tuple(
            jax.ShapeDtypeStruct((3 * rows, HEAD_DIM), BF16) for _ in range(heads)
        ),
        in_specs=[smem] + [VMEM] * (len(others) + 4),
        out_specs=tuple(VMEM for _ in range(heads)),
        scratch_shapes=[pltpu.VMEM(acc_shape.shape, F32), pltpu.VMEM(ssq_shape.shape, F32)],
        compiler_params=params,
        cost_estimate=cost(others),
        name="qkv_last_blocks",
    )(spot, *[b for _, b in others], gain, weight, acc, ssq)


def attend_kernel(rows, count, spot_ref, *refs):
    mine, theirs = refs[:count], refs[count : 2 * count]
    outs = refs[2 * count : 3 * count]
    key_ref, value_ref = refs[3 * count :]
    z, c = spot_ref[1], spot_ref[3]
    for k in range(count):
        for part, held in enumerate((mine[k], theirs[k])):
            spot = (k * 2 + part) * rows
            key_ref[spot : spot + rows, :] = held[rows : 2 * rows, :]
            value_ref[spot : spot + rows, :] = held[2 * rows : 3 * rows, :]
    total_rows = 2 * count * rows
    within = lax.broadcasted_iota(jnp.int32, (1, total_rows), 1)
    place = within // rows
    key_pos = (
        2 * jnp.bitwise_xor(place // 2, z) + jnp.bitwise_xor(place % 2, c)
    ) * rows + within % rows
    scale = 1.0 / math.sqrt(HEAD_DIM)
    for k in range(count):
        first = (2 * jnp.bitwise_xor(z, k) + c) * rows
        query_pos = first + lax.broadcasted_iota(jnp.int32, (rows, 1), 0)
        scores = (
            lax.dot_general(
                mine[k][:rows, :],
                key_ref[...],
                (((1,), (1,)), ((), ())),
                preferred_element_type=F32,
            )
            * scale
        )
        allowed = query_pos >= key_pos
        scores = jnp.where(allowed, scores, -1e30)
        top = jnp.max(scores, axis=1, keepdims=True)
        expo = jnp.exp(scores - top)
        total = jnp.sum(expo, axis=1, keepdims=True)
        summed = jnp.dot(expo.astype(BF16), value_ref[...], preferred_element_type=F32)
        outs[k][...] = (summed / total).astype(BF16)


def attend(mine, theirs, spot):
    count = len(mine)
    rows = mine[0].shape[0] // 3
    return pl.pallas_call(
        functools.partial(attend_kernel, rows, count),
        out_shape=tuple(jax.ShapeDtypeStruct((rows, HEAD_DIM), BF16) for _ in range(count)),
        in_specs=[pl.BlockSpec(memory_space=pltpu.SMEM)] + [VMEM] * (2 * count),
        out_specs=tuple(VMEM for _ in range(count)),
        scratch_shapes=[pltpu.VMEM((2 * count * rows, HEAD_DIM), BF16)] * 2,
        compiler_params=pltpu.CompilerParams(vmem_limit_bytes=24 << 20),
        name="attention",
    )(spot, *mine, *theirs)


def join_kernel(spot_ref, *refs):
    blocks, out = refs[:-1], refs[-1]
    for k, block in enumerate(blocks):
        head = jnp.bitwise_xor(spot_ref[1], k)
        out[:, pl.ds(pl.multiple_of(head * HEAD_DIM, LANES), HEAD_DIM)] = block[...]


def join(blocks, spot):
    rows = blocks[0].shape[0]
    return pl.pallas_call(
        join_kernel,
        out_shape=jax.ShapeDtypeStruct((rows, len(blocks) * HEAD_DIM), BF16),
        in_specs=[pl.BlockSpec(memory_space=pltpu.SMEM)] + [VMEM] * len(blocks),
        out_specs=VMEM,
        name="join_heads",
    )(spot, *blocks)


def gathered_attention(message, heads, rows):
    parts = jnp.stack([m.reshape(3, rows, HEAD_DIM) for m in message], axis=2)
    query, keys, values = parts[0], parts[1], parts[2]
    keys = lax.all_gather(keys, "ctx", axis=0, tiled=True)
    values = lax.all_gather(values, "ctx", axis=0, tiled=True)
    query_pos = lax.axis_index("ctx") * rows + jnp.arange(rows, dtype=jnp.int32)
    key_pos = jnp.arange(keys.shape[0], dtype=jnp.int32)
    scores = jnp.einsum("qhd,khd->hqk", query, keys, preferred_element_type=F32)
    allowed = (query_pos[:, None] >= key_pos[None, :])[None]
    scores = jnp.where(allowed, scores / math.sqrt(HEAD_DIM), -1e30)
    expo = jnp.where(allowed, jnp.exp(scores - jnp.max(scores, axis=2, keepdims=True)), 0.0)
    total = jnp.sum(expo, axis=2)
    summed = jnp.einsum("hqk,khd->qhd", expo.astype(BF16), values, preferred_element_type=F32)
    return (summed / total.T[:, :, None]).astype(BF16).reshape(rows, heads * HEAD_DIM)


def body(gate_in, conv_in, value_in, filter_taps, norm_gain, qkv_weight):
    rows, channels = gate_in.shape
    ctx, tp = lax.axis_size("ctx"), lax.axis_size("tp")
    at_ctx, at_tp = lax.axis_index("ctx"), lax.axis_index("tp")
    weight = jnp.transpose(qkv_weight, (1, 0, 2))
    heads = weight.shape[2] // HEAD_DIM
    model = weight.shape[1]
    chip_per_head = heads * 2 == ctx and heads & (heads - 1) == 0
    at_z = at_ctx // 2 if chip_per_head else jnp.zeros_like(at_ctx)
    spot = jnp.stack([at_tp, at_z, at_ctx % 2, at_tp % 2]).astype(jnp.int32)

    gain = lax.all_gather(norm_gain, "tp", axis=0)
    mixed = (conv_in.astype(F32) * value_in.astype(F32)).astype(BF16)
    rim = lax.ppermute(mixed, "ctx", [(i, i + 1) for i in range(ctx - 1)])
    hyena = hyena_of(gate_in, mixed, rim, filter_taps)

    def swapped(value, by):
        return lax.ppermute(value, "tp", [(i, i ^ by) for i in range(tp)])

    far = []
    by = tp // 2
    while by > 1:
        far = far + [(o ^ by, swapped(b, by)) for o, b in [(0, hyena)] + far]
        by //= 2
    mine = [(0, hyena), (1, swapped(hyena, 1))]
    others = far + [(o ^ 1, swapped(b, 1)) for o, b in far]
    messages = qkv_messages(mine, others, gain, weight, spot, model)
    if not chip_per_head:
        return gathered_attention(messages, heads, rows)

    def routed(value, k):
        pairs = []
        for z in range(ctx // 2):
            for y in range(2):
                for x in range(tp // 2):
                    for c in range(2):
                        source = (2 * z + y) * tp + 2 * x + c
                        pairs.append((source, (2 * (z ^ k) + c) * tp + 2 * x + y))
        return lax.ppermute(value, ("ctx", "tp"), pairs)

    held = [routed(messages[k], k) for k in range(heads)]
    theirs = [swapped(value, 1) for value in held]
    parts = attend(held, theirs, spot)
    return join([routed(parts[k], k) for k in range(heads)], spot)


def solution(mesh):
    placed = (
        P("ctx", "tp"),
        P("ctx", "tp"),
        P("ctx", "tp"),
        P(None, "tp"),
        P("tp"),
        P(None, None, "tp"),
    )
    return jax.shard_map(
        body, mesh=mesh, in_specs=placed, out_specs=P("ctx", "tp"), check_vma=False
    )
```

time: 332 us -> 73.2 us (0.22)
  matrix products: 109 us -> 0 us
  local copies, waits for them, and re-layouts: 112 us -> 10.2 us
  waiting for transfers between devices: 78 us -> 14.3 us
  starting transfers between devices: 4.26 us -> 28.7 us
  between operations: 14.6 us -> 0.15 us
  Pallas kernels: 0 us -> 13.2 us
  other arithmetic: 5.01 us -> 1.17 us
    dot_general x6 -> x0, matrix products: 109 us -> none  [the longest x1 92.6 us: causal_filter(): jnp.einsum('mksc,misc->kic', windows, weights_table, precision=lax.Precis...]
    gather x2 -> x0, local copies, waits for them, and re-layouts: 85.4 us -> none  [causal_filter(): taps[jnp.clip(tap_index, 0, span - 1)]]
    all_gather x3 -> x0, waiting for transfers between devices: 78 us -> none  [the longest x1 41.2 us: body(): value_piece = lax.all_gather(values, 'ctx', axis=0, tiled=True)]
    ppermute x1 -> x16, starting transfers between devices: 3.99 us -> 28.7 us  [the longest x8 17.7 us: routed(): return lax.ppermute(value, ('ctx', 'tp'), pairs)]
    ppermute x1 -> x16, waiting for transfers between devices: 0.01 us -> 14.3 us  [the longest x8 9.46 us: routed(): return lax.ppermute(value, ('ctx', 'tp'), pairs)]
    pallas_call x0 -> x6, Pallas kernels: none -> 13.2 us  [the longest x1 3.19 us: own_part(): pl.pallas_call(functools.partial(own_kernel, rows, span), out_shape=(jax....]
    unnamed x15 -> x18, local copies, waits for them, and re-layouts: 18.5 us -> 10.2 us
    another operation x4 -> x0, local copies, waits for them, and re-layouts: 6.8 us -> none  [the longest x2 6.68 us: causal_filter(): jnp.stack([blocks[offset:offset + out_blocks] for offset in range(reach_c...]
  transfers between devices with their start and end apart: 4 -> 16, of which waited for: 3 -> 8; matrix products, arithmetic and copies ran while one was open for 32% -> 0% of each run, Pallas kernels for 0% -> 7%
where the time goes in v1:
time: 73.2 us; the launch traced here: 72.8 us
  starting transfers between devices  28.7 us (39%)
  waiting for transfers between devices  14.3 us (20%)
  Pallas kernels  13.2 us (18%)
  local copies, waits for them, and re-layouts  10.2 us (14%)
  blocking collectives  5.1 us (7%)
  other arithmetic  1.17 us (2%)
    ppermute x8, starting transfers between devices, routed(): return lax.ppermute(value, ('ctx', 'tp'), pairs)  17.7 us
    unnamed x18, local copies, waits for them, and re-layouts  10.2 us
    ppermute x8, waiting for transfers between devices, routed(): return lax.ppermute(value, ('ctx', 'tp'), pairs)  9.46 us
    ppermute x7, starting transfers between devices, swapped(): return lax.ppermute(value, 'tp', [(i, i ^ by) for i in range(tp)])  7 us
    all_gather x1, blocking collectives, body(): gain = lax.all_gather(norm_gain, 'tp', axis=0)  5.1 us
    ppermute x7, waiting for transfers between devices, swapped(): return lax.ppermute(value, 'tp', [(i, i ^ by) for i in range(tp)])  4.16 us
    ppermute x1, starting transfers between devices, body(): rim = lax.ppermute(mixed, 'ctx', [(i, i + 1) for i in range(ctx - 1)])  3.99 us
    pallas_call x1, Pallas kernels, own_part(): pl.pallas_call(functools.partial(own_kernel, rows, span), out_shape=(jax....  3.19 us
  transfers between devices with their start and end apart: 16, of which 8 were waited for; matrix products, arithmetic and copies ran while one was open for 0% of the time, Pallas kernels for 7%

profile of v1, /device:TPU:1, one launch (start us, length us, event | category | flops | bytes accessed | tf_op | source)
XLA Modules:
  0.0 72.8 jit_solution(7878097651681827304)
XLA Ops:
  0.0 1.1 %multiply_convert_fusion.mixed_ref = bf16[128,1024]{1,0:T(8,128)(2,1)S(1)} fusion(bf16[128,1024]{1,0:T(8,128)(2,1)} %param.8, bf16[128,1024]{1,0:T(8,128)(2,1)} %param.7), kind=kLoop, calls=%fused_computation | loop fusion | flops 524288 | bytes 786432 | tf_op jit(solution)/shard_map/convert_element_type | solution.py:337
  1.1 4.0 %collective-permute-start = (bf16[128,1024]{1,0:T(8,128)(2,1)S(1)}, bf16[128,1024]{1,0:T(8,128)(2,1)S(1)}, u32[]{:S(2)}, u32[]{:S(2)}) collective-permute-start(bf16[128,1024]{1,0:T(8,128)(2,1)S(1)} %multiply_convert_fusion.mixed_ref), channel_id=1, source_target_pairs={{0,4},{4,8},{8,12},{12,16},{16,20},{20,24},{24,28},{1,5},{5,9},{9,... | collective-permute-start | bytes 786440 | tf_op jit(solution)/shard_map/ppermute | solution.py:338
  5.1 0.0 copy-start.2
  5.1 1.0 %copy-done.2 = f32[128,1024]{1,0:T(8,128)S(1)} copy-done((f32[128,1024]{1,0:T(8,128)S(1)}, f32[128,1024]{1,0:T(8,128)}, u32[]{:S(2)}) %copy-start.2) | copy-done | bytes 524312
  6.1 3.2 %fir_own_rows.1 = (f32[1024,128]{1,0:T(8,128)S(1)}, f32[1280,128]{1,0:T(8,128)S(1)}) custom-call(bf16[128,1024]{1,0:T(8,128)(2,1)S(1)} %multiply_convert_fusion.mixed_ref, f32[128,1024]{1,0:T(8,128)S(1)} %copy-done.2), custom_call_target="tpu_custom_call" | custom-call | flops 16777216 | bytes 2097152 | tf_op jit(solution)/shard_map/fir_own_rows/pallas_call | solution.py:103
  9.3 0.7 collective-permute-done.rim_ref
  10.0 0.0 copy-start.3
  10.0 0.9 %copy-done.3 = bf16[128,1024]{1,0:T(8,128)(2,1)S(1)} copy-done((bf16[128,1024]{1,0:T(8,128)(2,1)S(1)}, bf16[128,1024]{1,0:T(8,128)(2,1)}, u32[]{:S(2)}) %copy-start.3) | copy-done | bytes 262168
  11.0 3.2 %fir_rim_rows.1.refs_0_ = bf16[128,1024]{1,0:T(8,128)(2,1)S(1)} custom-call(bf16[128,1024]{1,0:T(8,128)(2,1)S(1)} %collective-permute-done.rim_ref, f32[1024,128]{1,0:T(8,128)S(1)} %get-tuple-element.17.sums_ref, f32[1280,128]{1,0:T(8,128)S(1)} %get-tuple-element.18.tap_ref, bf16[128,1024]{1,0:T(8,128)(2,1)S(1)} %copy-done.3), custom_call_target="tpu_custom_call" | custom-call | flops 16777216 | bytes 2097152 | tf_op jit(solution)/shard_map/fir_rim_rows/pallas_call | solution.py:123
  14.2 1.3 %collective-permute-start.1 = (bf16[128,1024]{1,0:T(8,128)(2,1)S(1)}, bf16[128,1024]{1,0:T(8,128)(2,1)S(1)}, u32[]{:S(2)}, u32[]{:S(2)}) collective-permute-start(bf16[128,1024]{1,0:T(8,128)(2,1)S(1)} %fir_rim_rows.1.refs_0_), channel_id=1, source_target_pairs={{0,2},{1,3},{2,0},{3,1},{4,6},{5,7},{6,4},{7,5},{8,10},{9,11},{10,... | collective-permute-start | bytes 786440 | tf_op jit(solution)/shard_map/ppermute | solution.py:342
  15.4 1.8 %collective-permute-start.3 = (bf16[128,1024]{1,0:T(8,128)(2,1)S(1)}, bf16[128,1024]{1,0:T(8,128)(2,1)S(1)}, u32[]{:S(2)}, u32[]{:S(2)}) collective-permute-start(bf16[128,1024]{1,0:T(8,128)(2,1)S(1)} %fir_rim_rows.1.refs_0_), channel_id=1, source_target_pairs={{0,1},{1,0},{2,3},{3,2},{4,5},{5,4},{6,7},{7,6},{8,9},{9,8},{10,11... | collective-permute-start | bytes 786440 | tf_op jit(solution)/shard_map/ppermute | solution.py:342
  17.3 3.2 %collective-permute-done.1.refs_0_ = bf16[128,1024]{1,0:T(8,128)(2,1)S(1)} collective-permute-done((bf16[128,1024]{1,0:T(8,128)(2,1)S(1)}, bf16[128,1024]{1,0:T(8,128)(2,1)S(1)}, u32[]{:S(2)}, u32[]{:S(2)}) %collective-permute-start.1) | collective-permute-done | bytes 262176 | tf_op jit(solution)/shard_map/ppermute | solution.py:342
  20.5 2.5 %collective-permute-start.2 = (bf16[128,1024]{1,0:T(8,128)(2,1)S(1)}, bf16[128,1024]{1,0:T(8,128)(2,1)S(1)}, u32[]{:S(2)}, u32[]{:S(2)}) collective-permute-start(bf16[128,1024]{1,0:T(8,128)(2,1)S(1)} %collective-permute-done.1.refs_0_), channel_id=1, source_target_pairs={{0,1},{1,0},{2,3},{3,2},{4,5},{5,4},{6,7},{7,6},{8,9},{9,8},{10,11... | collective-permute-start | bytes 786440 | tf_op jit(solution)/shard_map/ppermute | solution.py:342
  22.9 5.1 %all-gather = f32[4096]{0:T(1024)S(1)} all-gather(f32[1024]{0:T(1024)} %param.10), channel_id=2, replica_groups=mesh['ctx'=8,'tp'=4] {'tp'}, dimensions={0}, use_global_device_ids=true | all-gather | bytes 20480 | tf_op jit(solution)/shard_map/all_gather | solution.py:336
  28.1 0.1 pad_add_fusion.me_ref.spot_ref
  28.1 0.0 copy-start.4
  28.2 0.0 collective-permute-done.3.refs_1_
  28.2 0.0 copy-start
  28.2 4.6 %copy-done = bf16[4096,3,512]{2,0,1:T(8,128)(2,1)S(1)} copy-done((bf16[4096,3,512]{2,0,1:T(8,128)(2,1)S(1)}, bf16[4096,3,512]{2,0,1:T(8,128)(2,1)}, u32[]{:S(2)}) %copy-start) | copy-done | bytes 12582936
  32.7 0.0 copy-start.1
  32.7 1.6 %qkv_first_blocks.1 = (f32[128,1536]{1,0:T(8,128)S(1)}, f32[128,128]{1,0:T(8,128)S(1)}) custom-call(s32[4]{0:T(128)S(1)} %pad_add_fusion.me_ref.spot_ref, bf16[128,1024]{1,0:T(8,128)(2,1)S(1)} %fir_rim_rows.1.refs_0_, bf16[128,1024]{1,0:T(8,128)(2,1)S(1)} %collective-permute-done.3.refs_1_, f32[4,1024]{1,0:T(4,128)S(1)} %reshape.refs_2_, ...), custom_call_target="tpu_custom_call" | custom-call | flops 805306368 | bytes 8388608 | tf_op jit(solution)/shard_map/qkv_first_blocks/pallas_call | solution.py:215
  34.3 0.0 collective-permute-done.2.refs_1_
  34.3 3.0 %copy-done.1 = bf16[4096,3,512]{2,0,1:T(8,128)(2,1)S(1)} copy-done((bf16[4096,3,512]{2,0,1:T(8,128)(2,1)S(1)}, bf16[4096,3,512]{2,0,1:T(8,128)(2,1)}, u32[]{:S(2)}) %copy-start.1) | copy-done | bytes 12582936
  37.3 1.7 %qkv_last_blocks.1 = (bf16[384,128]{1,0:T(8,128)(2,1)S(1)}, bf16[384,128]{1,0:T(8,128)(2,1)S(1)}, bf16[384,128]{1,0:T(8,128)(2,1)S(1)}, bf16[384,128]{1,0:T(8,128)(2,1)S(1)}) custom-call(s32[4]{0:T(128)S(1)} %pad_add_fusion.me_ref.spot_ref, bf16[128,1024]{1,0:T(8,128)(2,1)S(1)} %collective-permute-done.1.refs_0_, ...), custom_call_target="tpu_custom_call" | custom-call | flops 805306368 | bytes 8388608 | tf_op jit(solution)/shard_map/qkv_last_blocks/pallas_call | solution.py:225
  39.0 4.4 %collective-permute-start.6 = (bf16[384,128]{1,0:T(8,128)(2,1)S(1)}, bf16[384,128]{1,0:T(8,128)(2,1)S(1)}, u32[]{:S(2)}, u32[]{:S(2)}) collective-permute-start(bf16[384,128]{1,0:T(8,128)(2,1)S(1)} %get-tuple-element.23), channel_id=1, source_target_pairs={{0,16},{1,20},{2,18},{3,22},{4,17},{5,21},{6,19},{7,23},{8,24},{9,... | collective-permute-start | bytes 294920 | tf_op jit(solution)/shard_map/ppermute | solution.py:363
  43.4 2.1 %collective-permute-start.7 = (bf16[384,128]{1,0:T(8,128)(2,1)S(1)}, bf16[384,128]{1,0:T(8,128)(2,1)S(1)}, u32[]{:S(2)}, u32[]{:S(2)}) collective-permute-start(bf16[384,128]{1,0:T(8,128)(2,1)S(1)} %get-tuple-element.24), channel_id=1, source_target_pairs={{0,24},{1,28},{2,26},{3,30},{4,25},{5,29},{6,27},{7,31},{8,16},{9,... | collective-permute-start | bytes 294920 | tf_op jit(solution)/shard_map/ppermute | solution.py:363
  45.5 2.3 %collective-permute-start.4 = (bf16[384,128]{1,0:T(8,128)(2,1)S(1)}, bf16[384,128]{1,0:T(8,128)(2,1)S(1)}, u32[]{:S(2)}, u32[]{:S(2)}) collective-permute-start(bf16[384,128]{1,0:T(8,128)(2,1)S(1)} %get-tuple-element.21), channel_id=1, source_target_pairs={{0,0},{1,4},{2,2},{3,6},{4,1},{5,5},{6,3},{7,7},{8,8},{9,12},{10,1... | collective-permute-start | bytes 294920 | tf_op jit(solution)/shard_map/ppermute | solution.py:363
  47.8 0.3 collective-permute-start.5
  48.1 2.6 %collective-permute-done.6.refs_2_ = bf16[384,128]{1,0:T(8,128)(2,1)S(1)} collective-permute-done((bf16[384,128]{1,0:T(8,128)(2,1)S(1)}, bf16[384,128]{1,0:T(8,128)(2,1)S(1)}, u32[]{:S(2)}, u32[]{:S(2)}) %collective-permute-start.6) | collective-permute-done | bytes 98336 | tf_op jit(solution)/shard_map/ppermute | solution.py:363
  50.7 0.9 %collective-permute-start.10 = (bf16[384,128]{1,0:T(8,128)(2,1)S(1)}, bf16[384,128]{1,0:T(8,128)(2,1)S(1)}, u32[]{:S(2)}, u32[]{:S(2)}) collective-permute-start(bf16[384,128]{1,0:T(8,128)(2,1)S(1)} %collective-permute-done.6.refs_2_), channel_id=1, source_target_pairs={{0,1},{1,0},{2,3},{3,2},{4,5},{5,4},{6,7},{7,6},{8,9},{9,8},{10,11... | collective-permute-start | bytes 294920 | tf_op jit(solution)/shard_map/ppermute | solution.py:342
  51.6 0.0 collective-permute-done.7.refs_3_
  51.6 0.0 collective-permute-start.11
  51.6 1.4 %collective-permute-done.4.refs_0_ = bf16[384,128]{1,0:T(8,128)(2,1)S(1)} collective-permute-done((bf16[384,128]{1,0:T(8,128)(2,1)S(1)}, bf16[384,128]{1,0:T(8,128)(2,1)S(1)}, u32[]{:S(2)}, u32[]{:S(2)}) %collective-permute-start.4) | collective-permute-done | bytes 98336 | tf_op jit(solution)/shard_map/ppermute | solution.py:363
  53.0 0.0 collective-permute-start.8
  53.0 0.0 collective-permute-done.5.refs_1_
  53.0 0.5 collective-permute-start.9
  53.5 0.0 collective-permute-done.10.refs_6_
  53.5 0.0 collective-permute-done.11.refs_7_
  53.5 0.8 %collective-permute-done.8.refs_4_ = bf16[384,128]{1,0:T(8,128)(2,1)S(1)} collective-permute-done((bf16[384,128]{1,0:T(8,128)(2,1)S(1)}, bf16[384,128]{1,0:T(8,128)(2,1)S(1)}, u32[]{:S(2)}, u32[]{:S(2)}) %collective-permute-start.8) | collective-permute-done | bytes 98336 | tf_op jit(solution)/shard_map/ppermute | solution.py:342
  54.3 0.2 collective-permute-done.9.refs_5_
  54.4 0.0 copy-done.4
  54.4 2.1 %attention.1 = (bf16[128,128]{1,0:T(8,128)(2,1)S(1)}, bf16[128,128]{1,0:T(8,128)(2,1)S(1)}, bf16[128,128]{1,0:T(8,128)(2,1)S(1)}, bf16[128,128]{1,0:T(8,128)(2,1)S(1)}) custom-call(s32[4]{0:T(128)S(1)} %pad_add_fusion.me_ref.spot_ref, bf16[384,128]{1,0:T(8,128)(2,1)S(1)} %collective-permute-done.4.refs_0_, ...), custom_call_target="tpu_custom_call" | custom-call | tf_op jit(solution)/shard_map/attention/pallas_call | solution.py:280
  56.6 3.4 %collective-permute-start.12 = (bf16[128,128]{1,0:T(8,128)(2,1)S(1)}, bf16[128,128]{1,0:T(8,128)(2,1)S(1)}, u32[]{:S(2)}, u32[]{:S(2)}) collective-permute-start(bf16[128,128]{1,0:T(8,128)(2,1)S(1)} %get-tuple-element.25), channel_id=1, source_target_pairs={{0,0},{1,4},{2,2},{3,6},{4,1},{5,5},{6,3},{7,7},{8,8},{9,12},{10,1... | collective-permute-start | bytes 98312 | tf_op jit(solution)/shard_map/ppermute | solution.py:363
  59.9 1.1 %collective-permute-start.13 = (bf16[128,128]{1,0:T(8,128)(2,1)S(1)}, bf16[128,128]{1,0:T(8,128)(2,1)S(1)}, u32[]{:S(2)}, u32[]{:S(2)}) collective-permute-start(bf16[128,128]{1,0:T(8,128)(2,1)S(1)} %get-tuple-element.26), channel_id=1, source_target_pairs={{0,8},{1,12},{2,10},{3,14},{4,9},{5,13},{6,11},{7,15},{8,0},{9,4},... | collective-permute-start | bytes 98312 | tf_op jit(solution)/shard_map/ppermute | solution.py:363
  61.0 3.6 %collective-permute-start.14 = (bf16[128,128]{1,0:T(8,128)(2,1)S(1)}, bf16[128,128]{1,0:T(8,128)(2,1)S(1)}, u32[]{:S(2)}, u32[]{:S(2)}) collective-permute-start(bf16[128,128]{1,0:T(8,128)(2,1)S(1)} %get-tuple-element.27), channel_id=1, source_target_pairs={{0,16},{1,20},{2,18},{3,22},{4,17},{5,21},{6,19},{7,23},{8,24},{9,... | collective-permute-start | bytes 98312 | tf_op jit(solution)/shard_map/ppermute | solution.py:363
  64.6 0.5 collective-permute-start.15
  65.2 0.0 collective-permute-done.12.refs_0_
  65.2 0.0 copy-start.5
  65.2 0.0 collective-permute-done.13.refs_1_
  65.2 0.0 copy-start.6
  65.2 1.7 %collective-permute-done.14.refs_2_ = bf16[128,128]{1,0:T(8,128)(2,1)S(1)} collective-permute-done((bf16[128,128]{1,0:T(8,128)(2,1)S(1)}, bf16[128,128]{1,0:T(8,128)(2,1)S(1)}, u32[]{:S(2)}, u32[]{:S(2)}) %collective-permute-start.14) | collective-permute-done | bytes 32800 | tf_op jit(solution)/shard_map/ppermute | solution.py:363
  66.9 0.0 copy-start.7
  66.9 3.8 %collective-permute-done.15.refs_3_ = bf16[128,128]{1,0:T(8,128)(2,1)S(1)} collective-permute-done((bf16[128,128]{1,0:T(8,128)(2,1)S(1)}, bf16[128,128]{1,0:T(8,128)(2,1)S(1)}, u32[]{:S(2)}, u32[]{:S(2)}) %collective-permute-start.15) | collective-permute-done | bytes 32800 | tf_op jit(solution)/shard_map/ppermute | solution.py:363
  70.7 0.0 copy-done.5
  70.7 0.0 copy-done.6
  70.7 0.0 copy-done.7
  70.7 0.0 copy-start.8
  70.7 0.6 copy-done.8
  71.3 1.5 %join_heads.1 = bf16[128,512]{1,0:T(8,128)(2,1)} custom-call(s32[4]{0:T(128)} %copy-done.4, bf16[128,128]{1,0:T(8,128)(2,1)} %copy-done.5, bf16[128,128]{1,0:T(8,128)(2,1)} %copy-done.6, bf16[128,128]{1,0:T(8,128)(2,1)} %copy-done.7, bf16[128,128]{1,0:T(8,128)(2,1)} %copy-done.8), custom_call_target="tpu_custom_call" | custom-call | tf_op jit(solution)/shard_map/join_heads/pallas_call | solution.py:300
  (1 shorter events, 0.0 us)
Async XLA Ops:
  1.1 8.9 %collective-permute-start = (bf16[128,1024]{1,0:T(8,128)(2,1)S(1)}, bf16[128,1024]{1,0:T(8,128)(2,1)S(1)}, u32[]{:S(2)}, u32[]{:S(2)}) collective-permute-start(bf16[128,1024]{1,0:T(8,128)(2,1)S(1)} %multiply_convert_fusion.mixed_ref), channel_id=1, source_target_pairs={{0,4},{4,8},{8,12},{12,16},{16,20},{20,24},{24,28},{1,5},{5,9},{9,... | collective-permute-start | bytes 786440 | tf_op jit(solution)/shard_map/ppermute | solution.py:338
  5.1 1.0 %copy-start.2 = (f32[128,1024]{1,0:T(8,128)S(1)}, f32[128,1024]{1,0:T(8,128)}, u32[]{:S(2)}) copy-start(f32[128,1024]{1,0:T(8,128)} %taps_ref.1) | copy-start | bytes 1572868
  10.0 0.9 %copy-start.3 = (bf16[128,1024]{1,0:T(8,128)(2,1)S(1)}, bf16[128,1024]{1,0:T(8,128)(2,1)}, u32[]{:S(2)}) copy-start(bf16[128,1024]{1,0:T(8,128)(2,1)} %gate_ref.1) | copy-start | bytes 786436
  14.2 6.3 %collective-permute-start.1 = (bf16[128,1024]{1,0:T(8,128)(2,1)S(1)}, bf16[128,1024]{1,0:T(8,128)(2,1)S(1)}, u32[]{:S(2)}, u32[]{:S(2)}) collective-permute-start(bf16[128,1024]{1,0:T(8,128)(2,1)S(1)} %fir_rim_rows.1.refs_0_), channel_id=1, source_target_pairs={{0,2},{1,3},{2,0},{3,1},{4,6},{5,7},{6,4},{7,5},{8,10},{9,11},{10,... | collective-permute-start | bytes 786440 | tf_op jit(solution)/shard_map/ppermute | solution.py:342
  15.4 12.7 %collective-permute-start.3 = (bf16[128,1024]{1,0:T(8,128)(2,1)S(1)}, bf16[128,1024]{1,0:T(8,128)(2,1)S(1)}, u32[]{:S(2)}, u32[]{:S(2)}) collective-permute-start(bf16[128,1024]{1,0:T(8,128)(2,1)S(1)} %fir_rim_rows.1.refs_0_), channel_id=1, source_target_pairs={{0,1},{1,0},{2,3},{3,2},{4,5},{5,4},{6,7},{7,6},{8,9},{9,8},{10,11... | collective-permute-start | bytes 786440 | tf_op jit(solution)/shard_map/ppermute | solution.py:342
  20.5 13.8 %collective-permute-start.2 = (bf16[128,1024]{1,0:T(8,128)(2,1)S(1)}, bf16[128,1024]{1,0:T(8,128)(2,1)S(1)}, u32[]{:S(2)}, u32[]{:S(2)}) collective-permute-start(bf16[128,1024]{1,0:T(8,128)(2,1)S(1)} %collective-permute-done.1.refs_0_), channel_id=1, source_target_pairs={{0,1},{1,0},{2,3},{3,2},{4,5},{5,4},{6,7},{7,6},{8,9},{9,8},{10,11... | collective-permute-start | bytes 786440 | tf_op jit(solution)/shard_map/ppermute | solution.py:342
  28.1 26.3 %copy-start.4 = (s32[4]{0:T(128)}, s32[4]{0:T(128)S(1)}, u32[]{:S(2)}) copy-start(s32[4]{0:T(128)S(1)} %pad_add_fusion.me_ref.spot_ref) | copy-start | bytes 52
  28.2 4.6 %copy-start = (bf16[4096,3,512]{2,0,1:T(8,128)(2,1)S(1)}, bf16[4096,3,512]{2,0,1:T(8,128)(2,1)}, u32[]{:S(2)}) copy-start(bf16[4096,3,512]{2,0,1:T(8,128)(2,1)} %param.11) | copy-start | bytes 37748740
  32.7 4.6 %copy-start.1 = (bf16[4096,3,512]{2,0,1:T(8,128)(2,1)S(1)}, bf16[4096,3,512]{2,0,1:T(8,128)(2,1)}, u32[]{:S(2)}) copy-start(bf16[4096,3,512]{2,0,1:T(8,128)(2,1)} %param.11) | copy-start | bytes 37748740
  39.0 11.7 %collective-permute-start.6 = (bf16[384,128]{1,0:T(8,128)(2,1)S(1)}, bf16[384,128]{1,0:T(8,128)(2,1)S(1)}, u32[]{:S(2)}, u32[]{:S(2)}) collective-permute-start(bf16[384,128]{1,0:T(8,128)(2,1)S(1)} %get-tuple-element.23), channel_id=1, source_target_pairs={{0,16},{1,20},{2,18},{3,22},{4,17},{5,21},{6,19},{7,23},{8,24},{9,... | collective-permute-start | bytes 294920 | tf_op jit(solution)/shard_map/ppermute | solution.py:363
  43.4 8.2 %collective-permute-start.7 = (bf16[384,128]{1,0:T(8,128)(2,1)S(1)}, bf16[384,128]{1,0:T(8,128)(2,1)S(1)}, u32[]{:S(2)}, u32[]{:S(2)}) collective-permute-start(bf16[384,128]{1,0:T(8,128)(2,1)S(1)} %get-tuple-element.24), channel_id=1, source_target_pairs={{0,24},{1,28},{2,26},{3,30},{4,25},{5,29},{6,27},{7,31},{8,16},{9,... | collective-permute-start | bytes 294920 | tf_op jit(solution)/shard_map/ppermute | solution.py:363
  45.5 7.5 %collective-permute-start.4 = (bf16[384,128]{1,0:T(8,128)(2,1)S(1)}, bf16[384,128]{1,0:T(8,128)(2,1)S(1)}, u32[]{:S(2)}, u32[]{:S(2)}) collective-permute-start(bf16[384,128]{1,0:T(8,128)(2,1)S(1)} %get-tuple-element.21), channel_id=1, source_target_pairs={{0,0},{1,4},{2,2},{3,6},{4,1},{5,5},{6,3},{7,7},{8,8},{9,12},{10,1... | collective-permute-start | bytes 294920 | tf_op jit(solution)/shard_map/ppermute | solution.py:363
  47.8 5.2 %collective-permute-start.5 = (bf16[384,128]{1,0:T(8,128)(2,1)S(1)}, bf16[384,128]{1,0:T(8,128)(2,1)S(1)}, u32[]{:S(2)}, u32[]{:S(2)}) collective-permute-start(bf16[384,128]{1,0:T(8,128)(2,1)S(1)} %get-tuple-element.22), channel_id=1, source_target_pairs={{0,8},{1,12},{2,10},{3,14},{4,9},{5,13},{6,11},{7,15},{8,0},{9,4},... | collective-permute-start | bytes 294920 | tf_op jit(solution)/shard_map/ppermute | solution.py:363
  50.7 2.8 %collective-permute-start.10 = (bf16[384,128]{1,0:T(8,128)(2,1)S(1)}, bf16[384,128]{1,0:T(8,128)(2,1)S(1)}, u32[]{:S(2)}, u32[]{:S(2)}) collective-permute-start(bf16[384,128]{1,0:T(8,128)(2,1)S(1)} %collective-permute-done.6.refs_2_), channel_id=1, source_target_pairs={{0,1},{1,0},{2,3},{3,2},{4,5},{5,4},{6,7},{7,6},{8,9},{9,8},{10,11... | collective-permute-start | bytes 294920 | tf_op jit(solution)/shard_map/ppermute | solution.py:342
  51.6 1.9 %collective-permute-start.11 = (bf16[384,128]{1,0:T(8,128)(2,1)S(1)}, bf16[384,128]{1,0:T(8,128)(2,1)S(1)}, u32[]{:S(2)}, u32[]{:S(2)}) collective-permute-start(bf16[384,128]{1,0:T(8,128)(2,1)S(1)} %collective-permute-done.7.refs_3_), channel_id=1, source_target_pairs={{0,1},{1,0},{2,3},{3,2},{4,5},{5,4},{6,7},{7,6},{8,9},{9,8},{10,11... | collective-permute-start | bytes 294920 | tf_op jit(solution)/shard_map/ppermute | solution.py:342
  53.0 1.3 %collective-permute-start.8 = (bf16[384,128]{1,0:T(8,128)(2,1)S(1)}, bf16[384,128]{1,0:T(8,128)(2,1)S(1)}, u32[]{:S(2)}, u32[]{:S(2)}) collective-permute-start(bf16[384,128]{1,0:T(8,128)(2,1)S(1)} %collective-permute-done.4.refs_0_), channel_id=1, source_target_pairs={{0,1},{1,0},{2,3},{3,2},{4,5},{5,4},{6,7},{7,6},{8,9},{9,8},{10,11... | collective-permute-start | bytes 294920 | tf_op jit(solution)/shard_map/ppermute | solution.py:342
  53.0 1.5 %collective-permute-start.9 = (bf16[384,128]{1,0:T(8,128)(2,1)S(1)}, bf16[384,128]{1,0:T(8,128)(2,1)S(1)}, u32[]{:S(2)}, u32[]{:S(2)}) collective-permute-start(bf16[384,128]{1,0:T(8,128)(2,1)S(1)} %collective-permute-done.5.refs_1_), channel_id=1, source_target_pairs={{0,1},{1,0},{2,3},{3,2},{4,5},{5,4},{6,7},{7,6},{8,9},{9,8},{10,11... | collective-permute-start | bytes 294920 | tf_op jit(solution)/shard_map/ppermute | solution.py:342
  56.6 8.6 %collective-permute-start.12 = (bf16[128,128]{1,0:T(8,128)(2,1)S(1)}, bf16[128,128]{1,0:T(8,128)(2,1)S(1)}, u32[]{:S(2)}, u32[]{:S(2)}) collective-permute-start(bf16[128,128]{1,0:T(8,128)(2,1)S(1)} %get-tuple-element.25), channel_id=1, source_target_pairs={{0,0},{1,4},{2,2},{3,6},{4,1},{5,5},{6,3},{7,7},{8,8},{9,12},{10,1... | collective-permute-start | bytes 98312 | tf_op jit(solution)/shard_map/ppermute | solution.py:363
  59.9 5.2 %collective-permute-start.13 = (bf16[128,128]{1,0:T(8,128)(2,1)S(1)}, bf16[128,128]{1,0:T(8,128)(2,1)S(1)}, u32[]{:S(2)}, u32[]{:S(2)}) collective-permute-start(bf16[128,128]{1,0:T(8,128)(2,1)S(1)} %get-tuple-element.26), channel_id=1, source_target_pairs={{0,8},{1,12},{2,10},{3,14},{4,9},{5,13},{6,11},{7,15},{8,0},{9,4},... | collective-permute-start | bytes 98312 | tf_op jit(solution)/shard_map/ppermute | solution.py:363
  61.0 5.8 %collective-permute-start.14 = (bf16[128,128]{1,0:T(8,128)(2,1)S(1)}, bf16[128,128]{1,0:T(8,128)(2,1)S(1)}, u32[]{:S(2)}, u32[]{:S(2)}) collective-permute-start(bf16[128,128]{1,0:T(8,128)(2,1)S(1)} %get-tuple-element.27), channel_id=1, source_target_pairs={{0,16},{1,20},{2,18},{3,22},{4,17},{5,21},{6,19},{7,23},{8,24},{9,... | collective-permute-start | bytes 98312 | tf_op jit(solution)/shard_map/ppermute | solution.py:363
  64.6 6.0 %collective-permute-start.15 = (bf16[128,128]{1,0:T(8,128)(2,1)S(1)}, bf16[128,128]{1,0:T(8,128)(2,1)S(1)}, u32[]{:S(2)}, u32[]{:S(2)}) collective-permute-start(bf16[128,128]{1,0:T(8,128)(2,1)S(1)} %get-tuple-element.28), channel_id=1, source_target_pairs={{0,24},{1,28},{2,26},{3,30},{4,25},{5,29},{6,27},{7,31},{8,16},{9,... | collective-permute-start | bytes 98312 | tf_op jit(solution)/shard_map/ppermute | solution.py:363
  65.2 5.5 %copy-start.5 = (bf16[128,128]{1,0:T(8,128)(2,1)}, bf16[128,128]{1,0:T(8,128)(2,1)S(1)}, u32[]{:S(2)}) copy-start(bf16[128,128]{1,0:T(8,128)(2,1)S(1)} %collective-permute-done.12.refs_0_) | copy-start | bytes 98308
  65.2 5.5 %copy-start.6 = (bf16[128,128]{1,0:T(8,128)(2,1)}, bf16[128,128]{1,0:T(8,128)(2,1)S(1)}, u32[]{:S(2)}) copy-start(bf16[128,128]{1,0:T(8,128)(2,1)S(1)} %collective-permute-done.13.refs_1_) | copy-start | bytes 98308
  66.9 3.8 %copy-start.7 = (bf16[128,128]{1,0:T(8,128)(2,1)}, bf16[128,128]{1,0:T(8,128)(2,1)S(1)}, u32[]{:S(2)}) copy-start(bf16[128,128]{1,0:T(8,128)(2,1)S(1)} %collective-permute-done.14.refs_2_) | copy-start | bytes 98308
  70.7 0.6 copy-start.8

commit v2 on v1

--- a/solution.py
+++ b/solution.py
@@ -40,13 +40,35 @@
     return tuple(sums)
 
 
-def own_kernel(rows, span, mixed_ref, taps_ref, sums_ref, tap_ref, x_ref):
+def own_kernel(
+    rows,
+    span,
+    mixed_ref,
+    taps_hbm,
+    gate_hbm,
+    weight_hbm,
+    sums_ref,
+    tap_ref,
+    gate_ref,
+    weight_ref,
+    x_ref,
+    taps_ref,
+    sems,
+):
+    copies = [
+        pltpu.make_async_copy(taps_hbm, taps_ref, sems.at[0]),
+        pltpu.make_async_copy(gate_hbm, gate_ref, sems.at[1]),
+        pltpu.make_async_copy(weight_hbm, weight_ref, sems.at[2]),
+    ]
+    for copy in copies:
+        copy.start()
     tap_ref[pl.ds(0, SPAN_OUT * SLAB), :] = jnp.zeros((SPAN_OUT * SLAB, LANES), F32)
     tap_ref[pl.ds((SPAN_OUT + span) * SLAB, SPAN_OUT * SLAB), :] = jnp.zeros(
         (SPAN_OUT * SLAB, LANES), F32
     )
+    to_slabs(mixed_ref, x_ref, 0, rows)
+    copies[0].wait()
     to_slabs(taps_ref, tap_ref, SPAN_OUT, span)
-    to_slabs(mixed_ref, x_ref, 0, rows)
 
     def block(t, _):
         def step(s, sums):
@@ -67,9 +89,11 @@
         return 0
 
     lax.fori_loop(0, rows // SPAN_OUT, block, 0)
-
-
-def rim_kernel(rows, span, rim_ref, sums_ref, tap_ref, gate_ref, hyena_ref, x_ref, full_ref):
+    for copy in copies[1:]:
+        copy.wait()
+
+
+def rim_kernel(rows, span, rim_ref, sums_ref, tap_ref, gate_ref, gain_ref, sent_ref, x_ref, full_ref):
     to_slabs(rim_ref, x_ref, 0, rows)
 
     def block(t, _):
@@ -91,82 +115,81 @@
         return 0
 
     lax.fori_loop(0, rows // SPAN_OUT, block, 0)
+    squares = jnp.zeros((rows, LANES), F32)
     for group in range(SLAB):
         lanes = slice(group * LANES, (group + 1) * LANES)
-        hyena_ref[:, lanes] = (
+        hyena = (
             gate_ref[:, lanes].astype(F32) * full_ref[pl.ds(group, rows, stride=SLAB), :]
-        ).astype(BF16)
-
-
-def own_part(mixed, taps):
+        ).astype(BF16).astype(F32)
+        squares = squares + hyena * hyena
+        sent_ref[:, lanes] = (hyena * gain_ref[:, lanes]).astype(BF16)
+    total = jnp.sum(squares, axis=1, keepdims=True)
+    pieces = []
+    for _ in range(3):
+        pieces.append(total.astype(BF16).astype(F32))
+        total = total - pieces[-1]
+    lane = lax.broadcasted_iota(jnp.int32, (rows, LANES), 1)
+    row = jnp.zeros((rows, LANES), F32)
+    for place, piece in enumerate(pieces):
+        row = jnp.where(lane == place, piece, row)
+    sent_ref[:, SLAB * LANES :] = row.astype(BF16)
+
+
+def own_part(mixed, taps, gate, weight):
     rows, span = mixed.shape[0], taps.shape[0]
+    wide = SLAB * LANES
+    hbm = pl.BlockSpec(memory_space=pltpu.HBM)
     return pl.pallas_call(
         functools.partial(own_kernel, rows, span),
         out_shape=(
             jax.ShapeDtypeStruct((rows * SLAB, LANES), F32),
             jax.ShapeDtypeStruct(((span + 2 * SPAN_OUT) * SLAB, LANES), F32),
+            jax.ShapeDtypeStruct(gate.shape, BF16),
+            jax.ShapeDtypeStruct(weight.shape, BF16),
         ),
-        in_specs=[VMEM] * 2,
-        out_specs=(VMEM, VMEM),
-        scratch_shapes=[pltpu.VMEM((rows * SLAB, LANES), F32)],
-        compiler_params=pltpu.CompilerParams(vmem_limit_bytes=16 << 20),
+        in_specs=[VMEM, hbm, hbm, hbm],
+        out_specs=(VMEM, VMEM, VMEM, VMEM),
+        scratch_shapes=[
+            pltpu.VMEM((rows * SLAB, LANES), F32),
+            pltpu.VMEM((span, wide), F32),
+            pltpu.SemaphoreType.DMA((3,)),
+        ],
+        compiler_params=pltpu.CompilerParams(vmem_limit_bytes=32 << 20),
         cost_estimate=pl.CostEstimate(
-            flops=rows * span * SLAB * LANES, bytes_accessed=1 << 21, transcendentals=0
+            flops=rows * span * wide, bytes_accessed=12 << 20, transcendentals=0
         ),
         name="fir_own_rows",
-    )(mixed, taps)
-
-
-def rim_part(rim, sums, taps, gate):
+    )(mixed, taps, gate, weight)
+
+
+def rim_part(rim, sums, taps, gate, gain):
     rows = gate.shape[0]
+    wide = SLAB * LANES
     span = taps.shape[0] // SLAB - 2 * SPAN_OUT
     return pl.pallas_call(
         functools.partial(rim_kernel, rows, span),
-        out_shape=jax.ShapeDtypeStruct((rows, SLAB * LANES), BF16),
-        in_specs=[VMEM] * 4,
+        out_shape=jax.ShapeDtypeStruct((rows, wide + LANES), BF16),
+        in_specs=[VMEM] * 5,
         out_specs=VMEM,
         scratch_shapes=[pltpu.VMEM((rows * SLAB, LANES), F32)] * 2,
         compiler_params=pltpu.CompilerParams(vmem_limit_bytes=16 << 20),
         cost_estimate=pl.CostEstimate(
-            flops=rows * span * SLAB * LANES, bytes_accessed=1 << 21, transcendentals=0
+            flops=rows * span * wide, bytes_accessed=1 << 21, transcendentals=0
         ),
         name="fir_rim_rows",
-    )(rim, sums, taps, gate)
-
-
-def hyena_of(gate, mixed, rim, taps):
-    rows, channels = gate.shape
-    wide = SLAB * LANES
-    pieces = []
-    for first in range(0, channels, wide):
-        cut = slice(first, min(first + wide, channels))
-
-        def widened(value):
-            part = value[:, cut]
-            return jnp.pad(part, ((0, 0), (0, wide - part.shape[1])))
-
-        sums, slabs = own_part(widened(mixed), widened(taps))
-        piece = rim_part(widened(rim), sums, slabs, widened(gate))
-        pieces.append(piece[:, : cut.stop - cut.start])
-    return pieces[0] if len(pieces) == 1 else jnp.concatenate(pieces, axis=1)
-
-
-def project(blocks, offsets, gain_ref, weight_ref, acc_ref, ssq_ref, me):
+    )(rim, sums, taps, gate, gain)
+
+
+def project(blocks, offsets, weight_ref, acc_ref, ssq_ref, me):
     width = weight_ref.shape[2]
     for block_ref, offset in zip(blocks, offsets):
         owner = jnp.bitwise_xor(me, offset)
-        channels = block_ref.shape[1]
-        hyena = block_ref[...].astype(F32)
-        squares = hyena * hyena
-        total = ssq_ref[...]
-        for first in range(0, channels, LANES):
-            total = total + squares[:, first : first + LANES]
-        ssq_ref[...] = total
-        scaled = (hyena * gain_ref[pl.ds(owner, 1), :]).astype(BF16)
+        channels = block_ref.shape[1] - LANES
+        ssq_ref[...] += block_ref[:, channels:].astype(F32)
         start = pl.multiple_of(owner * channels, channels)
         for which in range(3):
             acc_ref[:, which * width : (which + 1) * width] += jnp.dot(
-                scaled,
+                block_ref[:, :channels],
                 weight_ref[which, pl.ds(start, channels), :],
                 preferred_element_type=F32,
             )
@@ -174,19 +197,19 @@
 
 def first_kernel(offsets, me_ref, *refs):
     n = len(offsets)
-    blocks, (gain_ref, weight_ref, acc_ref, ssq_ref) = refs[:n], refs[n:]
+    blocks, (weight_ref, acc_ref, ssq_ref) = refs[:n], refs[n:]
     acc_ref[...] = jnp.zeros_like(acc_ref)
     ssq_ref[...] = jnp.zeros_like(ssq_ref)
-    project(blocks, offsets, gain_ref, weight_ref, acc_ref, ssq_ref, me_ref[0])
+    project(blocks, offsets, weight_ref, acc_ref, ssq_ref, me_ref[0])
 
 
 def last_kernel(offsets, model, me_ref, *refs):
     n = len(offsets)
-    blocks, (gain_ref, weight_ref, acc_in, ssq_in), rest = refs[:n], refs[n : n + 4], refs[n + 4 :]
+    blocks, (weight_ref, acc_in, ssq_in), rest = refs[:n], refs[n : n + 3], refs[n + 3 :]
     outs, (acc_ref, ssq_ref) = rest[:-2], rest[-2:]
     acc_ref[...] = acc_in[...]
     ssq_ref[...] = ssq_in[...]
-    project(blocks, offsets, gain_ref, weight_ref, acc_ref, ssq_ref, me_ref[0])
+    project(blocks, offsets, weight_ref, acc_ref, ssq_ref, me_ref[0])
     msq = jnp.sum(ssq_ref[...], axis=1, keepdims=True) / model
     scale = lax.rsqrt(msq + EPS)
     rows = acc_ref.shape[0]
@@ -198,7 +221,7 @@
             out[which * rows : (which + 1) * rows, :] = (acc_ref[:, lanes] * scale).astype(BF16)
 
 
-def qkv_messages(mine, others, gain, weight, spot, model):
+def qkv_messages(mine, others, weight, spot, model):
     rows = mine[0][1].shape[0]
     width = weight.shape[2]
     smem = pl.BlockSpec(memory_space=pltpu.SMEM)
@@ -215,25 +238,25 @@
     acc, ssq = pl.pallas_call(
         functools.partial(first_kernel, tuple(o for o, _ in mine)),
         out_shape=(acc_shape, ssq_shape),
-        in_specs=[smem] + [VMEM] * (len(mine) + 2),
+        in_specs=[smem] + [VMEM] * (len(mine) + 1),
         out_specs=(VMEM, VMEM),
         compiler_params=params,
         cost_estimate=cost(mine),
         name="qkv_first_blocks",
-    )(spot, *[b for _, b in mine], gain, weight)
+    )(spot, *[b for _, b in mine], weight)
     heads = width // HEAD_DIM
     return pl.pallas_call(
         functools.partial(last_kernel, tuple(o for o, _ in others), model),
         out_shape=tuple(
             jax.ShapeDtypeStruct((3 * rows, HEAD_DIM), BF16) for _ in range(heads)
         ),
-        in_specs=[smem] + [VMEM] * (len(others) + 4),
+        in_specs=[smem] + [VMEM] * (len(others) + 3),
         out_specs=tuple(VMEM for _ in range(heads)),
         scratch_shapes=[pltpu.VMEM(acc_shape.shape, F32), pltpu.VMEM(ssq_shape.shape, F32)],
         compiler_params=params,
         cost_estimate=cost(others),
         name="qkv_last_blocks",
-    )(spot, *[b for _, b in others], gain, weight, acc, ssq)
+    )(spot, *[b for _, b in others], weight, acc, ssq)
 
 
 def attend_kernel(rows, count, spot_ref, *refs):
@@ -302,6 +325,7 @@
         out_shape=jax.ShapeDtypeStruct((rows, len(blocks) * HEAD_DIM), BF16),
         in_specs=[pl.BlockSpec(memory_space=pltpu.SMEM)] + [VMEM] * len(blocks),
         out_specs=VMEM,
+        compiler_params=pltpu.CompilerParams(vmem_limit_bytes=4 << 20),
         name="join_heads",
     )(spot, *blocks)
 
@@ -333,10 +357,19 @@
     at_z = at_ctx // 2 if chip_per_head else jnp.zeros_like(at_ctx)
     spot = jnp.stack([at_tp, at_z, at_ctx % 2, at_tp % 2]).astype(jnp.int32)
 
-    gain = lax.all_gather(norm_gain, "tp", axis=0)
     mixed = (conv_in.astype(F32) * value_in.astype(F32)).astype(BF16)
     rim = lax.ppermute(mixed, "ctx", [(i, i + 1) for i in range(ctx - 1)])
-    hyena = hyena_of(gate_in, mixed, rim, filter_taps)
+    wide = SLAB * LANES
+
+    def widened(value):
+        return jnp.pad(value, ((0, 0), (0, wide - channels))) if channels < wide else value
+
+    sums, taps, gate, weight = own_part(
+        widened(mixed), widened(filter_taps), widened(gate_in), weight
+    )
+    sent = rim_part(widened(rim), sums, taps, gate, widened(norm_gain[None]))
+    if channels < wide:
+        sent = jnp.concatenate([sent[:, :channels], sent[:, wide:]], axis=1)
 
     def swapped(value, by):
         return lax.ppermute(value, "tp", [(i, i ^ by) for i in range(tp)])
@@ -344,11 +377,11 @@
     far = []
     by = tp // 2
     while by > 1:
-        far = far + [(o ^ by, swapped(b, by)) for o, b in [(0, hyena)] + far]
+        far = far + [(o ^ by, swapped(b, by)) for o, b in [(0, sent)] + far]
         by //= 2
-    mine = [(0, hyena), (1, swapped(hyena, 1))]
+    mine = [(0, sent), (1, swapped(sent, 1))]
     others = far + [(o ^ 1, swapped(b, 1)) for o, b in far]
-    messages = qkv_messages(mine, others, gain, weight, spot, model)
+    messages = qkv_messages(mine, others, weight, spot, model)
     if not chip_per_head:
         return gathered_attention(messages, heads, rows)
 

time: 73.2 us -> 67.6 us (0.923)
  blocking collectives: 5.1 us -> 0 us
  starting transfers between devices: 28.7 us -> 25.3 us
  Pallas kernels: 13.2 us -> 14.4 us
  local copies, waits for them, and re-layouts: 10.2 us -> 11.1 us
  waiting for transfers between devices: 14.3 us -> 15.2 us
    all_gather x1 -> x0, blocking collectives: 5.1 us -> none  [body(): gain = lax.all_gather(norm_gain, 'tp', axis=0)]
    ppermute x7, waiting for transfers between devices: 4.16 us -> 6.06 us  [swapped(): return lax.ppermute(value, 'tp', [(i, i ^ by) for i in range(tp)])]
    ppermute x8, starting transfers between devices: 17.7 us -> 15.9 us  [routed(): return lax.ppermute(value, ('ctx', 'tp'), pairs)]
    ppermute x7, starting transfers between devices: 7 us -> 5.4 us  [swapped(): return lax.ppermute(value, 'tp', [(i, i ^ by) for i in range(tp)])]
    pallas_call x1, Pallas kernels: 3.19 us -> 4.65 us  [own_part(): pl.pallas_call(functools.partial(own_kernel, rows, span), out_shape=(jax....]
    unnamed x18 -> x10, local copies, waits for them, and re-layouts: 10.2 us -> 11.1 us
  transfers between devices with their start and end apart: 16 -> 16, of which waited for: 8 -> 7; matrix products, arithmetic and copies ran while one was open for 0% -> 0% of each run, Pallas kernels for 7% -> 9%
where the time goes in v2:
time: 67.6 us; the launch traced here: 67.3 us
  starting transfers between devices  25.3 us (37%)
  waiting for transfers between devices  15.2 us (22%)
  Pallas kernels  14.4 us (21%)
  local copies, waits for them, and re-layouts  11.1 us (16%)
  other arithmetic  1.18 us (2%)
    ppermute x8, starting transfers between devices, routed(): return lax.ppermute(value, ('ctx', 'tp'), pairs)  15.9 us
    unnamed x10, local copies, waits for them, and re-layouts  11.1 us
    ppermute x8, waiting for transfers between devices, routed(): return lax.ppermute(value, ('ctx', 'tp'), pairs)  9.18 us
    ppermute x7, waiting for transfers between devices, swapped(): return lax.ppermute(value, 'tp', [(i, i ^ by) for i in range(tp)])  6.06 us
    ppermute x7, starting transfers between devices, swapped(): return lax.ppermute(value, 'tp', [(i, i ^ by) for i in range(tp)])  5.4 us
    pallas_call x1, Pallas kernels, own_part(): pl.pallas_call(functools.partial(own_kernel, rows, span), out_shape=(jax....  4.65 us
    ppermute x1, starting transfers between devices, body(): rim = lax.ppermute(mixed, 'ctx', [(i, i + 1) for i in range(ctx - 1)])  3.99 us
    pallas_call x1, Pallas kernels, rim_part(): pl.pallas_call(functools.partial(rim_kernel, rows, span), out_shape=jax.S...  3.24 us
  transfers between devices with their start and end apart: 16, of which 7 were waited for; matrix products, arithmetic and copies ran while one was open for 0% of the time, Pallas kernels for 9%

profile of v2, /device:TPU:1, one launch (start us, length us, event | category | flops | bytes accessed | tf_op | source)
XLA Modules:
  0.0 67.3 jit_solution(13816064958380041330)
XLA Ops:
  0.0 0.0 copy-start.4
  0.0 1.1 %multiply_convert_fusion.mixed_ref = bf16[128,1024]{1,0:T(8,128)(2,1)S(1)} fusion(bf16[128,1024]{1,0:T(8,128)(2,1)} %param.8, bf16[128,1024]{1,0:T(8,128)(2,1)} %param.7), kind=kLoop, calls=%fused_computation | loop fusion | flops 524288 | bytes 786432 | tf_op jit(solution)/shard_map/convert_element_type | solution.py:360
  1.1 4.0 %collective-permute-start = (bf16[128,1024]{1,0:T(8,128)(2,1)S(1)}, bf16[128,1024]{1,0:T(8,128)(2,1)S(1)}, u32[]{:S(2)}, u32[]{:S(2)}) collective-permute-start(bf16[128,1024]{1,0:T(8,128)(2,1)S(1)} %multiply_convert_fusion.mixed_ref), channel_id=1, source_target_pairs={{0,4},{4,8},{8,12},{12,16},{16,20},{20,24},{24,28},{1,5},{5,9},{9,... | collective-permute-start | bytes 786440 | tf_op jit(solution)/shard_map/ppermute | solution.py:361
  5.1 0.0 copy-start.2
  5.1 1.0 %copy-done.2 = f32[128,1024]{1,0:T(8,128)S(1)} copy-done((f32[128,1024]{1,0:T(8,128)S(1)}, f32[128,1024]{1,0:T(8,128)}, u32[]{:S(2)}) %copy-start.2) | copy-done | bytes 524312
  6.2 0.0 copy-start.3
  6.2 0.9 %copy-done.3 = bf16[128,1024]{1,0:T(8,128)(2,1)S(1)} copy-done((bf16[128,1024]{1,0:T(8,128)(2,1)S(1)}, bf16[128,1024]{1,0:T(8,128)(2,1)}, u32[]{:S(2)}) %copy-start.3) | copy-done | bytes 262168
  7.1 4.7 %fir_own_rows.1 = (f32[1024,128]{1,0:T(8,128)S(1)}, f32[1280,128]{1,0:T(8,128)S(1)}, bf16[128,1024]{1,0:T(8,128)(2,1)S(1)}, bf16[3,4096,512]{2,1,0:T(8,128)(2,1)S(1)}) custom-call(bf16[128,1024]{1,0:T(8,128)(2,1)S(1)} %multiply_convert_fusion.mixed_ref, f32[128,1024]{1,0:T(8,128)S(1)} %copy-done.2, bf16[128,1024]{1,0:T(8,128)(2,1)S(1)} %copy-done.3, ...), custom_call_target="tpu_custom_call" | custom-call | flops 16777216 | bytes 12582912 | tf_op jit(solution)/shard_map/fir_own_rows/pallas_call | solution.py:142
  11.8 0.0 copy-start
  11.8 4.5 %copy-done = bf16[3,4096,512]{2,1,0:T(8,128)(2,1)} copy-done((bf16[3,4096,512]{2,1,0:T(8,128)(2,1)}, bf16[3,4096,512]{2,1,0:T(8,128)(2,1)S(1)}, u32[]{:S(2)}) %copy-start) | copy-done | bytes 12582936
  16.3 0.0 collective-permute-done.rim_ref
  16.3 0.0 copy-done.4
  16.3 3.2 %fir_rim_rows.1.refs_0_ = bf16[128,1152]{1,0:T(8,128)(2,1)S(1)} custom-call(bf16[128,1024]{1,0:T(8,128)(2,1)S(1)} %collective-permute-done.rim_ref, f32[1024,128]{1,0:T(8,128)S(1)} %get-tuple-element.19.sums_ref, f32[1280,128]{1,0:T(8,128)S(1)} %get-tuple-element.20.tap_ref, bf16[128,1024]{1,0:T(8,128)(2,1)S(1)} %get-tuple-element.21.gate_ref, ...), custom_call_target="tpu_custom_call" | custom-call | flops 16777216 | bytes 2097152 | tf_op jit(solution)/shard_map/fir_rim_rows/pallas_call | solution.py:169
  19.5 1.3 %collective-permute-start.1 = (bf16[128,1152]{1,0:T(8,128)(2,1)S(1)}, bf16[128,1152]{1,0:T(8,128)(2,1)S(1)}, u32[]{:S(2)}, u32[]{:S(2)}) collective-permute-start(bf16[128,1152]{1,0:T(8,128)(2,1)S(1)} %fir_rim_rows.1.refs_0_), channel_id=1, source_target_pairs={{0,2},{1,3},{2,0},{3,1},{4,6},{5,7},{6,4},{7,5},{8,10},{9,11},{10,... | collective-permute-start | bytes 884744 | tf_op jit(solution)/shard_map/ppermute | solution.py:375
  20.8 1.2 %collective-permute-start.3 = (bf16[128,1152]{1,0:T(8,128)(2,1)S(1)}, bf16[128,1152]{1,0:T(8,128)(2,1)S(1)}, u32[]{:S(2)}, u32[]{:S(2)}) collective-permute-start(bf16[128,1152]{1,0:T(8,128)(2,1)S(1)} %fir_rim_rows.1.refs_0_), channel_id=1, source_target_pairs={{0,1},{1,0},{2,3},{3,2},{4,5},{5,4},{6,7},{7,6},{8,9},{9,8},{10,11... | collective-permute-start | bytes 884744 | tf_op jit(solution)/shard_map/ppermute | solution.py:375
  22.1 5.1 %collective-permute-done.1.refs_0_ = bf16[128,1152]{1,0:T(8,128)(2,1)S(1)} collective-permute-done((bf16[128,1152]{1,0:T(8,128)(2,1)S(1)}, bf16[128,1152]{1,0:T(8,128)(2,1)S(1)}, u32[]{:S(2)}, u32[]{:S(2)}) %collective-permute-start.1) | collective-permute-done | bytes 294944 | tf_op jit(solution)/shard_map/ppermute | solution.py:375
  27.2 1.9 %collective-permute-start.2 = (bf16[128,1152]{1,0:T(8,128)(2,1)S(1)}, bf16[128,1152]{1,0:T(8,128)(2,1)S(1)}, u32[]{:S(2)}, u32[]{:S(2)}) collective-permute-start(bf16[128,1152]{1,0:T(8,128)(2,1)S(1)} %collective-permute-done.1.refs_0_), channel_id=1, source_target_pairs={{0,1},{1,0},{2,3},{3,2},{4,5},{5,4},{6,7},{7,6},{8,9},{9,8},{10,11... | collective-permute-start | bytes 884744 | tf_op jit(solution)/shard_map/ppermute | solution.py:375
  29.0 0.1 pad_add_fusion.me_ref.spot_ref
  29.1 0.0 collective-permute-done.3.refs_1_
  29.1 0.0 copy-start.1
  29.1 4.6 %copy-done.1 = bf16[3,4096,512]{2,1,0:T(8,128)(2,1)S(1)} copy-done((bf16[3,4096,512]{2,1,0:T(8,128)(2,1)S(1)}, bf16[3,4096,512]{2,1,0:T(8,128)(2,1)}, u32[]{:S(2)}) %copy-start.1) | copy-done | bytes 12582936
  33.7 1.5 %qkv_first_blocks.1 = (f32[128,1536]{1,0:T(8,128)S(1)}, f32[128,128]{1,0:T(8,128)S(1)}) custom-call(s32[4]{0:T(128)S(1)} %pad_add_fusion.me_ref.spot_ref, bf16[128,1152]{1,0:T(8,128)(2,1)S(1)} %fir_rim_rows.1.refs_0_, bf16[128,1152]{1,0:T(8,128)(2,1)S(1)} %collective-permute-done.3.refs_1_, bf16[3,4096,512]{2,1,0:T(8,128)(2,1)S(1)} %copy-done.1), custom_call_target="tpu_custom_call" | custom-call | flops 905969664 | bytes 9175040 | tf_op jit(solution)/shard_map/qkv_first_blocks/pallas_call | solution.py:238
  35.2 0.0 collective-permute-done.2.refs_1_
  35.2 1.7 %qkv_last_blocks.1 = (bf16[384,128]{1,0:T(8,128)(2,1)S(1)}, bf16[384,128]{1,0:T(8,128)(2,1)S(1)}, bf16[384,128]{1,0:T(8,128)(2,1)S(1)}, bf16[384,128]{1,0:T(8,128)(2,1)S(1)}) custom-call(s32[4]{0:T(128)S(1)} %pad_add_fusion.me_ref.spot_ref, bf16[128,1152]{1,0:T(8,128)(2,1)S(1)} %collective-permute-done.1.refs_0_, ...), custom_call_target="tpu_custom_call" | custom-call | flops 905969664 | bytes 9175040 | tf_op jit(solution)/shard_map/qkv_last_blocks/pallas_call | solution.py:248
  36.9 3.2 %collective-permute-start.6 = (bf16[384,128]{1,0:T(8,128)(2,1)S(1)}, bf16[384,128]{1,0:T(8,128)(2,1)S(1)}, u32[]{:S(2)}, u32[]{:S(2)}) collective-permute-start(bf16[384,128]{1,0:T(8,128)(2,1)S(1)} %get-tuple-element.27), channel_id=1, source_target_pairs={{0,16},{1,20},{2,18},{3,22},{4,17},{5,21},{6,19},{7,23},{8,24},{9,... | collective-permute-start | bytes 294920 | tf_op jit(solution)/shard_map/ppermute | solution.py:396
  40.1 1.4 %collective-permute-start.7 = (bf16[384,128]{1,0:T(8,128)(2,1)S(1)}, bf16[384,128]{1,0:T(8,128)(2,1)S(1)}, u32[]{:S(2)}, u32[]{:S(2)}) collective-permute-start(bf16[384,128]{1,0:T(8,128)(2,1)S(1)} %get-tuple-element.28), channel_id=1, source_target_pairs={{0,24},{1,28},{2,26},{3,30},{4,25},{5,29},{6,27},{7,31},{8,16},{9,... | collective-permute-start | bytes 294920 | tf_op jit(solution)/shard_map/ppermute | solution.py:396
  41.5 3.0 %collective-permute-start.4 = (bf16[384,128]{1,0:T(8,128)(2,1)S(1)}, bf16[384,128]{1,0:T(8,128)(2,1)S(1)}, u32[]{:S(2)}, u32[]{:S(2)}) collective-permute-start(bf16[384,128]{1,0:T(8,128)(2,1)S(1)} %get-tuple-element.25), channel_id=1, source_target_pairs={{0,0},{1,4},{2,2},{3,6},{4,1},{5,5},{6,3},{7,7},{8,8},{9,12},{10,1... | collective-permute-start | bytes 294920 | tf_op jit(solution)/shard_map/ppermute | solution.py:396
  44.6 0.1 collective-permute-start.5
  44.6 3.4 %collective-permute-done.6.refs_2_ = bf16[384,128]{1,0:T(8,128)(2,1)S(1)} collective-permute-done((bf16[384,128]{1,0:T(8,128)(2,1)S(1)}, bf16[384,128]{1,0:T(8,128)(2,1)S(1)}, u32[]{:S(2)}, u32[]{:S(2)}) %collective-permute-start.6) | collective-permute-done | bytes 98336 | tf_op jit(solution)/shard_map/ppermute | solution.py:396
  48.1 0.0 collective-permute-start.10
  48.1 0.0 collective-permute-done.7.refs_3_
  48.1 0.5 collective-permute-start.11
  48.6 1.2 %collective-permute-done.4.refs_0_ = bf16[384,128]{1,0:T(8,128)(2,1)S(1)} collective-permute-done((bf16[384,128]{1,0:T(8,128)(2,1)S(1)}, bf16[384,128]{1,0:T(8,128)(2,1)S(1)}, u32[]{:S(2)}, u32[]{:S(2)}) %collective-permute-start.4) | collective-permute-done | bytes 98336 | tf_op jit(solution)/shard_map/ppermute | solution.py:396
  49.8 0.0 collective-permute-start.8
  49.8 0.0 collective-permute-done.5.refs_1_
  49.8 0.5 collective-permute-start.9
  50.3 0.0 collective-permute-done.10.refs_6_
  50.3 0.0 collective-permute-done.11.refs_7_
  50.3 0.8 %collective-permute-done.8.refs_4_ = bf16[384,128]{1,0:T(8,128)(2,1)S(1)} collective-permute-done((bf16[384,128]{1,0:T(8,128)(2,1)S(1)}, bf16[384,128]{1,0:T(8,128)(2,1)S(1)}, u32[]{:S(2)}, u32[]{:S(2)}) %collective-permute-start.8) | collective-permute-done | bytes 98336 | tf_op jit(solution)/shard_map/ppermute | solution.py:375
  51.1 0.2 collective-permute-done.9.refs_5_
  51.2 2.1 %attention.1 = (bf16[128,128]{1,0:T(8,128)(2,1)S(1)}, bf16[128,128]{1,0:T(8,128)(2,1)S(1)}, bf16[128,128]{1,0:T(8,128)(2,1)S(1)}, bf16[128,128]{1,0:T(8,128)(2,1)S(1)}) custom-call(s32[4]{0:T(128)S(1)} %pad_add_fusion.me_ref.spot_ref, bf16[384,128]{1,0:T(8,128)(2,1)S(1)} %collective-permute-done.4.refs_0_, ...), custom_call_target="tpu_custom_call" | custom-call | tf_op jit(solution)/shard_map/attention/pallas_call | solution.py:303
  53.3 2.9 %collective-permute-start.12 = (bf16[128,128]{1,0:T(8,128)(2,1)S(1)}, bf16[128,128]{1,0:T(8,128)(2,1)S(1)}, u32[]{:S(2)}, u32[]{:S(2)}) collective-permute-start(bf16[128,128]{1,0:T(8,128)(2,1)S(1)} %get-tuple-element.29), channel_id=1, source_target_pairs={{0,0},{1,4},{2,2},{3,6},{4,1},{5,5},{6,3},{7,7},{8,8},{9,12},{10,1... | collective-permute-start | bytes 98312 | tf_op jit(solution)/shard_map/ppermute | solution.py:396
  56.3 1.2 %collective-permute-start.13 = (bf16[128,128]{1,0:T(8,128)(2,1)S(1)}, bf16[128,128]{1,0:T(8,128)(2,1)S(1)}, u32[]{:S(2)}, u32[]{:S(2)}) collective-permute-start(bf16[128,128]{1,0:T(8,128)(2,1)S(1)} %get-tuple-element.30), channel_id=1, source_target_pairs={{0,8},{1,12},{2,10},{3,14},{4,9},{5,13},{6,11},{7,15},{8,0},{9,4},... | collective-permute-start | bytes 98312 | tf_op jit(solution)/shard_map/ppermute | solution.py:396
  57.5 2.6 %collective-permute-start.14 = (bf16[128,128]{1,0:T(8,128)(2,1)S(1)}, bf16[128,128]{1,0:T(8,128)(2,1)S(1)}, u32[]{:S(2)}, u32[]{:S(2)}) collective-permute-start(bf16[128,128]{1,0:T(8,128)(2,1)S(1)} %get-tuple-element.31), channel_id=1, source_target_pairs={{0,16},{1,20},{2,18},{3,22},{4,17},{5,21},{6,19},{7,23},{8,24},{9,... | collective-permute-start | bytes 98312 | tf_op jit(solution)/shard_map/ppermute | solution.py:396
  60.0 1.5 %collective-permute-start.15 = (bf16[128,128]{1,0:T(8,128)(2,1)S(1)}, bf16[128,128]{1,0:T(8,128)(2,1)S(1)}, u32[]{:S(2)}, u32[]{:S(2)}) collective-permute-start(bf16[128,128]{1,0:T(8,128)(2,1)S(1)} %get-tuple-element.32), channel_id=1, source_target_pairs={{0,24},{1,28},{2,26},{3,30},{4,25},{5,29},{6,27},{7,31},{8,16},{9,... | collective-permute-start | bytes 98312 | tf_op jit(solution)/shard_map/ppermute | solution.py:396
  61.5 0.0 collective-permute-done.12.refs_0_
  61.5 0.0 collective-permute-done.13.refs_1_
  61.5 1.4 %collective-permute-done.14.refs_2_ = bf16[128,128]{1,0:T(8,128)(2,1)S(1)} collective-permute-done((bf16[128,128]{1,0:T(8,128)(2,1)S(1)}, bf16[128,128]{1,0:T(8,128)(2,1)S(1)}, u32[]{:S(2)}, u32[]{:S(2)}) %collective-permute-start.14) | collective-permute-done | bytes 32800 | tf_op jit(solution)/shard_map/ppermute | solution.py:396
  62.9 3.2 %collective-permute-done.15.refs_3_ = bf16[128,128]{1,0:T(8,128)(2,1)S(1)} collective-permute-done((bf16[128,128]{1,0:T(8,128)(2,1)S(1)}, bf16[128,128]{1,0:T(8,128)(2,1)S(1)}, u32[]{:S(2)}, u32[]{:S(2)}) %collective-permute-start.15) | collective-permute-done | bytes 32800 | tf_op jit(solution)/shard_map/ppermute | solution.py:396
  66.1 1.2 %join_heads.1 = bf16[128,512]{1,0:T(8,128)(2,1)} custom-call(s32[4]{0:T(128)S(1)} %pad_add_fusion.me_ref.spot_ref, bf16[128,128]{1,0:T(8,128)(2,1)S(1)} %collective-permute-done.12.refs_0_, bf16[128,128]{1,0:T(8,128)(2,1)S(1)} %collective-permute-done.13.refs_1_, bf16[128,128]{1,0:T(8,128)(2,1)S(1)} %collective-permute-done.14.refs_2_, ...), custom_call_target="tpu_custom_call" | custom-call | tf_op jit(solution)/shard_map/join_heads/pallas_call | solution.py:323
Async XLA Ops:
  0.0 16.3 %copy-start.4 = (f32[1024]{0:T(1024)S(1)}, f32[1024]{0:T(1024)}, u32[]{:S(2)}) copy-start(f32[1024]{0:T(1024)} %param.10) | copy-start | bytes 12292
  1.1 15.2 %collective-permute-start = (bf16[128,1024]{1,0:T(8,128)(2,1)S(1)}, bf16[128,1024]{1,0:T(8,128)(2,1)S(1)}, u32[]{:S(2)}, u32[]{:S(2)}) collective-permute-start(bf16[128,1024]{1,0:T(8,128)(2,1)S(1)} %multiply_convert_fusion.mixed_ref), channel_id=1, source_target_pairs={{0,4},{4,8},{8,12},{12,16},{16,20},{20,24},{24,28},{1,5},{5,9},{9,... | collective-permute-start | bytes 786440 | tf_op jit(solution)/shard_map/ppermute | solution.py:361
  5.1 1.0 %copy-start.2 = (f32[128,1024]{1,0:T(8,128)S(1)}, f32[128,1024]{1,0:T(8,128)}, u32[]{:S(2)}) copy-start(f32[128,1024]{1,0:T(8,128)} %taps_hbm.1) | copy-start | bytes 1572868
  6.2 0.9 %copy-start.3 = (bf16[128,1024]{1,0:T(8,128)(2,1)S(1)}, bf16[128,1024]{1,0:T(8,128)(2,1)}, u32[]{:S(2)}) copy-start(bf16[128,1024]{1,0:T(8,128)(2,1)} %gate_hbm.1) | copy-start | bytes 786436
  11.8 4.5 %copy-start = (bf16[3,4096,512]{2,1,0:T(8,128)(2,1)}, bf16[3,4096,512]{2,1,0:T(8,128)(2,1)S(1)}, u32[]{:S(2)}) copy-start(bf16[3,4096,512]{2,1,0:T(8,128)(2,1)S(1)} %get-tuple-element.22.refs_2_) | copy-start | bytes 37748740
  19.5 7.6 %collective-permute-start.1 = (bf16[128,1152]{1,0:T(8,128)(2,1)S(1)}, bf16[128,1152]{1,0:T(8,128)(2,1)S(1)}, u32[]{:S(2)}, u32[]{:S(2)}) collective-permute-start(bf16[128,1152]{1,0:T(8,128)(2,1)S(1)} %fir_rim_rows.1.refs_0_), channel_id=1, source_target_pairs={{0,2},{1,3},{2,0},{3,1},{4,6},{5,7},{6,4},{7,5},{8,10},{9,11},{10,... | collective-permute-start | bytes 884744 | tf_op jit(solution)/shard_map/ppermute | solution.py:375
  20.8 8.3 %collective-permute-start.3 = (bf16[128,1152]{1,0:T(8,128)(2,1)S(1)}, bf16[128,1152]{1,0:T(8,128)(2,1)S(1)}, u32[]{:S(2)}, u32[]{:S(2)}) collective-permute-start(bf16[128,1152]{1,0:T(8,128)(2,1)S(1)} %fir_rim_rows.1.refs_0_), channel_id=1, source_target_pairs={{0,1},{1,0},{2,3},{3,2},{4,5},{5,4},{6,7},{7,6},{8,9},{9,8},{10,11... | collective-permute-start | bytes 884744 | tf_op jit(solution)/shard_map/ppermute | solution.py:375
  27.2 8.1 %collective-permute-start.2 = (bf16[128,1152]{1,0:T(8,128)(2,1)S(1)}, bf16[128,1152]{1,0:T(8,128)(2,1)S(1)}, u32[]{:S(2)}, u32[]{:S(2)}) collective-permute-start(bf16[128,1152]{1,0:T(8,128)(2,1)S(1)} %collective-permute-done.1.refs_0_), channel_id=1, source_target_pairs={{0,1},{1,0},{2,3},{3,2},{4,5},{5,4},{6,7},{7,6},{8,9},{9,8},{10,11... | collective-permute-start | bytes 884744 | tf_op jit(solution)/shard_map/ppermute | solution.py:375
  29.1 4.6 %copy-start.1 = (bf16[3,4096,512]{2,1,0:T(8,128)(2,1)S(1)}, bf16[3,4096,512]{2,1,0:T(8,128)(2,1)}, u32[]{:S(2)}) copy-start(bf16[3,4096,512]{2,1,0:T(8,128)(2,1)} %copy-done) | copy-start | bytes 37748740
  36.9 11.1 %collective-permute-start.6 = (bf16[384,128]{1,0:T(8,128)(2,1)S(1)}, bf16[384,128]{1,0:T(8,128)(2,1)S(1)}, u32[]{:S(2)}, u32[]{:S(2)}) collective-permute-start(bf16[384,128]{1,0:T(8,128)(2,1)S(1)} %get-tuple-element.27), channel_id=1, source_target_pairs={{0,16},{1,20},{2,18},{3,22},{4,17},{5,21},{6,19},{7,23},{8,24},{9,... | collective-permute-start | bytes 294920 | tf_op jit(solution)/shard_map/ppermute | solution.py:396
  40.1 7.9 %collective-permute-start.7 = (bf16[384,128]{1,0:T(8,128)(2,1)S(1)}, bf16[384,128]{1,0:T(8,128)(2,1)S(1)}, u32[]{:S(2)}, u32[]{:S(2)}) collective-permute-start(bf16[384,128]{1,0:T(8,128)(2,1)S(1)} %get-tuple-element.28), channel_id=1, source_target_pairs={{0,24},{1,28},{2,26},{3,30},{4,25},{5,29},{6,27},{7,31},{8,16},{9,... | collective-permute-start | bytes 294920 | tf_op jit(solution)/shard_map/ppermute | solution.py:396
  41.5 8.2 %collective-permute-start.4 = (bf16[384,128]{1,0:T(8,128)(2,1)S(1)}, bf16[384,128]{1,0:T(8,128)(2,1)S(1)}, u32[]{:S(2)}, u32[]{:S(2)}) collective-permute-start(bf16[384,128]{1,0:T(8,128)(2,1)S(1)} %get-tuple-element.25), channel_id=1, source_target_pairs={{0,0},{1,4},{2,2},{3,6},{4,1},{5,5},{6,3},{7,7},{8,8},{9,12},{10,1... | collective-permute-start | bytes 294920 | tf_op jit(solution)/shard_map/ppermute | solution.py:396
  44.6 5.2 %collective-permute-start.5 = (bf16[384,128]{1,0:T(8,128)(2,1)S(1)}, bf16[384,128]{1,0:T(8,128)(2,1)S(1)}, u32[]{:S(2)}, u32[]{:S(2)}) collective-permute-start(bf16[384,128]{1,0:T(8,128)(2,1)S(1)} %get-tuple-element.26), channel_id=1, source_target_pairs={{0,8},{1,12},{2,10},{3,14},{4,9},{5,13},{6,11},{7,15},{8,0},{9,4},... | collective-permute-start | bytes 294920 | tf_op jit(solution)/shard_map/ppermute | solution.py:396
  48.1 2.2 %collective-permute-start.10 = (bf16[384,128]{1,0:T(8,128)(2,1)S(1)}, bf16[384,128]{1,0:T(8,128)(2,1)S(1)}, u32[]{:S(2)}, u32[]{:S(2)}) collective-permute-start(bf16[384,128]{1,0:T(8,128)(2,1)S(1)} %collective-permute-done.6.refs_2_), channel_id=1, source_target_pairs={{0,1},{1,0},{2,3},{3,2},{4,5},{5,4},{6,7},{7,6},{8,9},{9,8},{10,11... | collective-permute-start | bytes 294920 | tf_op jit(solution)/shard_map/ppermute | solution.py:375
  48.1 2.2 %collective-permute-start.11 = (bf16[384,128]{1,0:T(8,128)(2,1)S(1)}, bf16[384,128]{1,0:T(8,128)(2,1)S(1)}, u32[]{:S(2)}, u32[]{:S(2)}) collective-permute-start(bf16[384,128]{1,0:T(8,128)(2,1)S(1)} %collective-permute-done.7.refs_3_), channel_id=1, source_target_pairs={{0,1},{1,0},{2,3},{3,2},{4,5},{5,4},{6,7},{7,6},{8,9},{9,8},{10,11... | collective-permute-start | bytes 294920 | tf_op jit(solution)/shard_map/ppermute | solution.py:375
  49.8 1.3 %collective-permute-start.8 = (bf16[384,128]{1,0:T(8,128)(2,1)S(1)}, bf16[384,128]{1,0:T(8,128)(2,1)S(1)}, u32[]{:S(2)}, u32[]{:S(2)}) collective-permute-start(bf16[384,128]{1,0:T(8,128)(2,1)S(1)} %collective-permute-done.4.refs_0_), channel_id=1, source_target_pairs={{0,1},{1,0},{2,3},{3,2},{4,5},{5,4},{6,7},{7,6},{8,9},{9,8},{10,11... | collective-permute-start | bytes 294920 | tf_op jit(solution)/shard_map/ppermute | solution.py:375
  49.8 1.5 %collective-permute-start.9 = (bf16[384,128]{1,0:T(8,128)(2,1)S(1)}, bf16[384,128]{1,0:T(8,128)(2,1)S(1)}, u32[]{:S(2)}, u32[]{:S(2)}) collective-permute-start(bf16[384,128]{1,0:T(8,128)(2,1)S(1)} %collective-permute-done.5.refs_1_), channel_id=1, source_target_pairs={{0,1},{1,0},{2,3},{3,2},{4,5},{5,4},{6,7},{7,6},{8,9},{9,8},{10,11... | collective-permute-start | bytes 294920 | tf_op jit(solution)/shard_map/ppermute | solution.py:375
  53.3 8.2 %collective-permute-start.12 = (bf16[128,128]{1,0:T(8,128)(2,1)S(1)}, bf16[128,128]{1,0:T(8,128)(2,1)S(1)}, u32[]{:S(2)}, u32[]{:S(2)}) collective-permute-start(bf16[128,128]{1,0:T(8,128)(2,1)S(1)} %get-tuple-element.29), channel_id=1, source_target_pairs={{0,0},{1,4},{2,2},{3,6},{4,1},{5,5},{6,3},{7,7},{8,8},{9,12},{10,1... | collective-permute-start | bytes 98312 | tf_op jit(solution)/shard_map/ppermute | solution.py:396
  56.3 5.2 %collective-permute-start.13 = (bf16[128,128]{1,0:T(8,128)(2,1)S(1)}, bf16[128,128]{1,0:T(8,128)(2,1)S(1)}, u32[]{:S(2)}, u32[]{:S(2)}) collective-permute-start(bf16[128,128]{1,0:T(8,128)(2,1)S(1)} %get-tuple-element.30), channel_id=1, source_target_pairs={{0,8},{1,12},{2,10},{3,14},{4,9},{5,13},{6,11},{7,15},{8,0},{9,4},... | collective-permute-start | bytes 98312 | tf_op jit(solution)/shard_map/ppermute | solution.py:396
  57.5 5.4 %collective-permute-start.14 = (bf16[128,128]{1,0:T(8,128)(2,1)S(1)}, bf16[128,128]{1,0:T(8,128)(2,1)S(1)}, u32[]{:S(2)}, u32[]{:S(2)}) collective-permute-start(bf16[128,128]{1,0:T(8,128)(2,1)S(1)} %get-tuple-element.31), channel_id=1, source_target_pairs={{0,16},{1,20},{2,18},{3,22},{4,17},{5,21},{6,19},{7,23},{8,24},{9,... | collective-permute-start | bytes 98312 | tf_op jit(solution)/shard_map/ppermute | solution.py:396
  60.0 6.0 %collective-permute-start.15 = (bf16[128,128]{1,0:T(8,128)(2,1)S(1)}, bf16[128,128]{1,0:T(8,128)(2,1)S(1)}, u32[]{:S(2)}, u32[]{:S(2)}) collective-permute-start(bf16[128,128]{1,0:T(8,128)(2,1)S(1)} %get-tuple-element.32), channel_id=1, source_target_pairs={{0,24},{1,28},{2,26},{3,30},{4,25},{5,29},{6,27},{7,31},{8,16},{9,... | collective-permute-start | bytes 98312 | tf_op jit(solution)/shard_map/ppermute | solution.py:396

commit v3 on v2

--- a/solution.py
+++ b/solution.py
@@ -195,36 +195,35 @@
             )
 
 
-def first_kernel(offsets, me_ref, *refs):
+def first_kernel(offsets, *refs):
     n = len(offsets)
     blocks, (weight_ref, acc_ref, ssq_ref) = refs[:n], refs[n:]
     acc_ref[...] = jnp.zeros_like(acc_ref)
     ssq_ref[...] = jnp.zeros_like(ssq_ref)
-    project(blocks, offsets, weight_ref, acc_ref, ssq_ref, me_ref[0])
-
-
-def last_kernel(offsets, model, me_ref, *refs):
+    project(blocks, offsets, weight_ref, acc_ref, ssq_ref, lax.axis_index("tp"))
+
+
+def last_kernel(offsets, model, spread, *refs):
     n = len(offsets)
     blocks, (weight_ref, acc_in, ssq_in), rest = refs[:n], refs[n : n + 3], refs[n + 3 :]
     outs, (acc_ref, ssq_ref) = rest[:-2], rest[-2:]
     acc_ref[...] = acc_in[...]
     ssq_ref[...] = ssq_in[...]
-    project(blocks, offsets, weight_ref, acc_ref, ssq_ref, me_ref[0])
+    project(blocks, offsets, weight_ref, acc_ref, ssq_ref, lax.axis_index("tp"))
     msq = jnp.sum(ssq_ref[...], axis=1, keepdims=True) / model
     scale = lax.rsqrt(msq + EPS)
     rows = acc_ref.shape[0]
     width = weight_ref.shape[2]
     for k, out in enumerate(outs):
-        head = jnp.bitwise_xor(me_ref[1], k)
+        head = jnp.bitwise_xor(lax.axis_index("ctx") // 2, k) if spread else k
         for which in range(3):
             lanes = pl.ds(pl.multiple_of(which * width + head * HEAD_DIM, LANES), HEAD_DIM)
             out[which * rows : (which + 1) * rows, :] = (acc_ref[:, lanes] * scale).astype(BF16)
 
 
-def qkv_messages(mine, others, weight, spot, model):
+def qkv_messages(mine, others, weight, model, spread):
     rows = mine[0][1].shape[0]
     width = weight.shape[2]
-    smem = pl.BlockSpec(memory_space=pltpu.SMEM)
     params = pltpu.CompilerParams(vmem_limit_bytes=24 << 20)
     acc_shape = jax.ShapeDtypeStruct((rows, 3 * width), F32)
     ssq_shape = jax.ShapeDtypeStruct((rows, LANES), F32)
@@ -238,32 +237,32 @@
     acc, ssq = pl.pallas_call(
         functools.partial(first_kernel, tuple(o for o, _ in mine)),
         out_shape=(acc_shape, ssq_shape),
-        in_specs=[smem] + [VMEM] * (len(mine) + 1),
+        in_specs=[VMEM] * (len(mine) + 1),
         out_specs=(VMEM, VMEM),
         compiler_params=params,
         cost_estimate=cost(mine),
         name="qkv_first_blocks",
-    )(spot, *[b for _, b in mine], weight)
+    )(*[b for _, b in mine], weight)
     heads = width // HEAD_DIM
     return pl.pallas_call(
-        functools.partial(last_kernel, tuple(o for o, _ in others), model),
+        functools.partial(last_kernel, tuple(o for o, _ in others), model, spread),
         out_shape=tuple(
             jax.ShapeDtypeStruct((3 * rows, HEAD_DIM), BF16) for _ in range(heads)
         ),
-        in_specs=[smem] + [VMEM] * (len(others) + 3),
+        in_specs=[VMEM] * (len(others) + 3),
         out_specs=tuple(VMEM for _ in range(heads)),
         scratch_shapes=[pltpu.VMEM(acc_shape.shape, F32), pltpu.VMEM(ssq_shape.shape, F32)],
         compiler_params=params,
         cost_estimate=cost(others),
         name="qkv_last_blocks",
-    )(spot, *[b for _, b in others], weight, acc, ssq)
-
-
-def attend_kernel(rows, count, spot_ref, *refs):
+    )(*[b for _, b in others], weight, acc, ssq)
+
+
+def attend_kernel(rows, count, *refs):
     mine, theirs = refs[:count], refs[count : 2 * count]
     outs = refs[2 * count : 3 * count]
     key_ref, value_ref = refs[3 * count :]
-    z, c = spot_ref[1], spot_ref[3]
+    z, c = lax.axis_index("ctx") // 2, lax.axis_index("tp") % 2
     for k in range(count):
         for part, held in enumerate((mine[k], theirs[k])):
             spot = (k * 2 + part) * rows
@@ -297,37 +296,37 @@
         outs[k][...] = (summed / total).astype(BF16)
 
 
-def attend(mine, theirs, spot):
+def attend(mine, theirs):
     count = len(mine)
     rows = mine[0].shape[0] // 3
     return pl.pallas_call(
         functools.partial(attend_kernel, rows, count),
         out_shape=tuple(jax.ShapeDtypeStruct((rows, HEAD_DIM), BF16) for _ in range(count)),
-        in_specs=[pl.BlockSpec(memory_space=pltpu.SMEM)] + [VMEM] * (2 * count),
+        in_specs=[VMEM] * (2 * count),
         out_specs=tuple(VMEM for _ in range(count)),
         scratch_shapes=[pltpu.VMEM((2 * count * rows, HEAD_DIM), BF16)] * 2,
         compiler_params=pltpu.CompilerParams(vmem_limit_bytes=24 << 20),
         name="attention",
-    )(spot, *mine, *theirs)
-
-
-def join_kernel(spot_ref, *refs):
+    )(*mine, *theirs)
+
+
+def join_kernel(*refs):
     blocks, out = refs[:-1], refs[-1]
     for k, block in enumerate(blocks):
-        head = jnp.bitwise_xor(spot_ref[1], k)
+        head = jnp.bitwise_xor(lax.axis_index("ctx") // 2, k)
         out[:, pl.ds(pl.multiple_of(head * HEAD_DIM, LANES), HEAD_DIM)] = block[...]
 
 
-def join(blocks, spot):
+def join(blocks):
     rows = blocks[0].shape[0]
     return pl.pallas_call(
         join_kernel,
         out_shape=jax.ShapeDtypeStruct((rows, len(blocks) * HEAD_DIM), BF16),
-        in_specs=[pl.BlockSpec(memory_space=pltpu.SMEM)] + [VMEM] * len(blocks),
+        in_specs=[VMEM] * len(blocks),
         out_specs=VMEM,
         compiler_params=pltpu.CompilerParams(vmem_limit_bytes=4 << 20),
         name="join_heads",
-    )(spot, *blocks)
+    )(*blocks)
 
 
 def gathered_attention(message, heads, rows):
@@ -349,13 +348,10 @@
 def body(gate_in, conv_in, value_in, filter_taps, norm_gain, qkv_weight):
     rows, channels = gate_in.shape
     ctx, tp = lax.axis_size("ctx"), lax.axis_size("tp")
-    at_ctx, at_tp = lax.axis_index("ctx"), lax.axis_index("tp")
     weight = jnp.transpose(qkv_weight, (1, 0, 2))
     heads = weight.shape[2] // HEAD_DIM
     model = weight.shape[1]
     chip_per_head = heads * 2 == ctx and heads & (heads - 1) == 0
-    at_z = at_ctx // 2 if chip_per_head else jnp.zeros_like(at_ctx)
-    spot = jnp.stack([at_tp, at_z, at_ctx % 2, at_tp % 2]).astype(jnp.int32)
 
     mixed = (conv_in.astype(F32) * value_in.astype(F32)).astype(BF16)
     rim = lax.ppermute(mixed, "ctx", [(i, i + 1) for i in range(ctx - 1)])
@@ -381,7 +377,7 @@
         by //= 2
     mine = [(0, sent), (1, swapped(sent, 1))]
     others = far + [(o ^ 1, swapped(b, 1)) for o, b in far]
-    messages = qkv_messages(mine, others, weight, spot, model)
+    messages = qkv_messages(mine, others, weight, model, chip_per_head)
     if not chip_per_head:
         return gathered_attention(messages, heads, rows)
 
@@ -397,8 +393,8 @@
 
     held = [routed(messages[k], k) for k in range(heads)]
     theirs = [swapped(value, 1) for value in held]
-    parts = attend(held, theirs, spot)
-    return join([routed(parts[k], k) for k in range(heads)], spot)
+    parts = attend(held, theirs)
+    return join([routed(parts[k], k) for k in range(heads)])
 
 
 def solution(mesh):

time: 67.6 us -> 57.5 us (0.85)
  local copies, waits for them, and re-layouts: 11.1 us -> 1.99 us
  Pallas kernels: 14.4 us -> 12.2 us
  waiting for transfers between devices: 15.2 us -> 16.5 us
    unnamed x10 -> x6, local copies, waits for them, and re-layouts: 11.1 us -> 1.99 us
    ppermute x8, waiting for transfers between devices: 9.18 us -> 10 us  [routed(): return lax.ppermute(value, ('ctx', 'tp'), pairs)]
  transfers between devices with their start and end apart: 16 -> 16, of which waited for: 7 -> 9; matrix products, arithmetic and copies ran while one was open for 0% -> 0% of each run, Pallas kernels for 9% -> 10%
where the time goes in v3:
time: 57.5 us; the launch traced here: 57.2 us
  starting transfers between devices  25.2 us (44%)
  waiting for transfers between devices  16.5 us (29%)
  Pallas kernels  12.2 us (21%)
  local copies, waits for them, and re-layouts  1.99 us (3%)
  other arithmetic  1.11 us (2%)
    ppermute x8, starting transfers between devices, routed(): return lax.ppermute(value, ('ctx', 'tp'), pairs)  16.2 us
    ppermute x8, waiting for transfers between devices, routed(): return lax.ppermute(value, ('ctx', 'tp'), pairs)  10 us
    ppermute x7, waiting for transfers between devices, swapped(): return lax.ppermute(value, 'tp', [(i, i ^ by) for i in range(tp)])  6.52 us
    ppermute x7, starting transfers between devices, swapped(): return lax.ppermute(value, 'tp', [(i, i ^ by) for i in range(tp)])  5.01 us
    pallas_call x1, Pallas kernels, own_part(): pl.pallas_call(functools.partial(own_kernel, rows, span), out_shape=(jax....  4.65 us
    ppermute x1, starting transfers between devices, body(): rim = lax.ppermute(mixed, 'ctx', [(i, i + 1) for i in range(ctx - 1)])  3.99 us
    pallas_call x1, Pallas kernels, rim_part(): pl.pallas_call(functools.partial(rim_kernel, rows, span), out_shape=jax.S...  3.24 us
    unnamed x6, local copies, waits for them, and re-layouts  1.99 us
  transfers between devices with their start and end apart: 16, of which 9 were waited for; matrix products, arithmetic and copies ran while one was open for 0% of the time, Pallas kernels for 10%

profile of v3, /device:TPU:1, one launch (start us, length us, event | category | flops | bytes accessed | tf_op | source)
XLA Modules:
  0.0 57.2 jit_solution(5044125340774616547)
XLA Ops:
  0.0 0.0 copy-start.2
  0.0 1.1 %multiply_convert_fusion.mixed_ref = bf16[128,1024]{1,0:T(8,128)(2,1)S(1)} fusion(bf16[128,1024]{1,0:T(8,128)(2,1)} %param.8, bf16[128,1024]{1,0:T(8,128)(2,1)} %param.7), kind=kLoop, calls=%fused_computation | loop fusion | flops 524288 | bytes 786432 | tf_op jit(solution)/shard_map/convert_element_type | solution.py:356
  1.1 4.0 %collective-permute-start = (bf16[128,1024]{1,0:T(8,128)(2,1)S(1)}, bf16[128,1024]{1,0:T(8,128)(2,1)S(1)}, u32[]{:S(2)}, u32[]{:S(2)}) collective-permute-start(bf16[128,1024]{1,0:T(8,128)(2,1)S(1)} %multiply_convert_fusion.mixed_ref), channel_id=1, source_target_pairs={{0,4},{4,8},{8,12},{12,16},{16,20},{20,24},{24,28},{1,5},{5,9},{9,... | collective-permute-start | bytes 786440 | tf_op jit(solution)/shard_map/ppermute | solution.py:357
  5.1 0.0 copy-start
  5.1 1.0 %copy-done = f32[128,1024]{1,0:T(8,128)S(1)} copy-done((f32[128,1024]{1,0:T(8,128)S(1)}, f32[128,1024]{1,0:T(8,128)}, u32[]{:S(2)}) %copy-start) | copy-done | bytes 524312
  6.2 0.0 copy-start.1
  6.2 0.9 %copy-done.1 = bf16[128,1024]{1,0:T(8,128)(2,1)S(1)} copy-done((bf16[128,1024]{1,0:T(8,128)(2,1)S(1)}, bf16[128,1024]{1,0:T(8,128)(2,1)}, u32[]{:S(2)}) %copy-start.1) | copy-done | bytes 262168
  7.1 4.7 %fir_own_rows.1 = (f32[1024,128]{1,0:T(8,128)S(1)}, f32[1280,128]{1,0:T(8,128)S(1)}, bf16[128,1024]{1,0:T(8,128)(2,1)S(1)}, bf16[3,4096,512]{2,1,0:T(8,128)(2,1)S(1)}) custom-call(bf16[128,1024]{1,0:T(8,128)(2,1)S(1)} %multiply_convert_fusion.mixed_ref, f32[128,1024]{1,0:T(8,128)S(1)} %copy-done, bf16[128,1024]{1,0:T(8,128)(2,1)S(1)} %copy-done.1, ...), custom_call_target="tpu_custom_call" | custom-call | flops 16777216 | bytes 12582912 | tf_op jit(solution)/shard_map/fir_own_rows/pallas_call | solution.py:142
  11.8 0.0 collective-permute-done.rim_ref
  11.8 0.0 copy-done.2
  11.8 3.2 %fir_rim_rows.1.refs_0_ = bf16[128,1152]{1,0:T(8,128)(2,1)S(1)} custom-call(bf16[128,1024]{1,0:T(8,128)(2,1)S(1)} %collective-permute-done.rim_ref, f32[1024,128]{1,0:T(8,128)S(1)} %get-tuple-element.19.sums_ref, f32[1280,128]{1,0:T(8,128)S(1)} %get-tuple-element.20.tap_ref, bf16[128,1024]{1,0:T(8,128)(2,1)S(1)} %get-tuple-element.21.gate_ref, ...), custom_call_target="tpu_custom_call" | custom-call | flops 16777216 | bytes 2097152 | tf_op jit(solution)/shard_map/fir_rim_rows/pallas_call | solution.py:169
  15.0 1.3 %collective-permute-start.1 = (bf16[128,1152]{1,0:T(8,128)(2,1)S(1)}, bf16[128,1152]{1,0:T(8,128)(2,1)S(1)}, u32[]{:S(2)}, u32[]{:S(2)}) collective-permute-start(bf16[128,1152]{1,0:T(8,128)(2,1)S(1)} %fir_rim_rows.1.refs_0_), channel_id=1, source_target_pairs={{0,2},{1,3},{2,0},{3,1},{4,6},{5,7},{6,4},{7,5},{8,10},{9,11},{10,... | collective-permute-start | bytes 884744 | tf_op jit(solution)/shard_map/ppermute | solution.py:371
  16.3 1.2 %collective-permute-start.3 = (bf16[128,1152]{1,0:T(8,128)(2,1)S(1)}, bf16[128,1152]{1,0:T(8,128)(2,1)S(1)}, u32[]{:S(2)}, u32[]{:S(2)}) collective-permute-start(bf16[128,1152]{1,0:T(8,128)(2,1)S(1)} %fir_rim_rows.1.refs_0_), channel_id=1, source_target_pairs={{0,1},{1,0},{2,3},{3,2},{4,5},{5,4},{6,7},{7,6},{8,9},{9,8},{10,11... | collective-permute-start | bytes 884744 | tf_op jit(solution)/shard_map/ppermute | solution.py:371
  17.6 5.1 %collective-permute-done.1.refs_0_ = bf16[128,1152]{1,0:T(8,128)(2,1)S(1)} collective-permute-done((bf16[128,1152]{1,0:T(8,128)(2,1)S(1)}, bf16[128,1152]{1,0:T(8,128)(2,1)S(1)}, u32[]{:S(2)}, u32[]{:S(2)}) %collective-permute-start.1) | collective-permute-done | bytes 294944 | tf_op jit(solution)/shard_map/ppermute | solution.py:371
  22.7 1.9 %collective-permute-start.2 = (bf16[128,1152]{1,0:T(8,128)(2,1)S(1)}, bf16[128,1152]{1,0:T(8,128)(2,1)S(1)}, u32[]{:S(2)}, u32[]{:S(2)}) collective-permute-start(bf16[128,1152]{1,0:T(8,128)(2,1)S(1)} %collective-permute-done.1.refs_0_), channel_id=1, source_target_pairs={{0,1},{1,0},{2,3},{3,2},{4,5},{5,4},{6,7},{7,6},{8,9},{9,8},{10,11... | collective-permute-start | bytes 884744 | tf_op jit(solution)/shard_map/ppermute | solution.py:371
  24.5 0.0 collective-permute-done.3.refs_1_
  24.5 1.0 %qkv_first_blocks.1 = (f32[128,1536]{1,0:T(8,128)S(1)}, f32[128,128]{1,0:T(8,128)S(1)}) custom-call(bf16[128,1152]{1,0:T(8,128)(2,1)S(1)} %fir_rim_rows.1.refs_0_, bf16[128,1152]{1,0:T(8,128)(2,1)S(1)} %collective-permute-done.3.refs_1_, bf16[3,4096,512]{2,1,0:T(8,128)(2,1)S(1)} %get-tuple-element.22.refs_2_), custom_call_target="tpu_custom_call" | custom-call | flops 905969664 | bytes 9175040 | tf_op jit(solution)/shard_map/qkv_first_blocks/pallas_call | solution.py:237
  25.5 0.2 collective-permute-done.2.refs_1_
  25.7 1.1 %qkv_last_blocks.1 = (bf16[384,128]{1,0:T(8,128)(2,1)S(1)}, bf16[384,128]{1,0:T(8,128)(2,1)S(1)}, bf16[384,128]{1,0:T(8,128)(2,1)S(1)}, bf16[384,128]{1,0:T(8,128)(2,1)S(1)}) custom-call(bf16[128,1152]{1,0:T(8,128)(2,1)S(1)} %collective-permute-done.1.refs_0_, bf16[128,1152]{1,0:T(8,128)(2,1)S(1)} %collective-permute-done.2.refs_1_, ...), custom_call_target="tpu_custom_call" | custom-call | flops 905969664 | bytes 9175040 | tf_op jit(solution)/shard_map/qkv_last_blocks/pallas_call | solution.py:247
  26.8 3.6 %collective-permute-start.6 = (bf16[384,128]{1,0:T(8,128)(2,1)S(1)}, bf16[384,128]{1,0:T(8,128)(2,1)S(1)}, u32[]{:S(2)}, u32[]{:S(2)}) collective-permute-start(bf16[384,128]{1,0:T(8,128)(2,1)S(1)} %get-tuple-element.27), channel_id=1, source_target_pairs={{0,16},{1,20},{2,18},{3,22},{4,17},{5,21},{6,19},{7,23},{8,24},{9,... | collective-permute-start | bytes 294920 | tf_op jit(solution)/shard_map/ppermute | solution.py:392
  30.4 1.2 %collective-permute-start.7 = (bf16[384,128]{1,0:T(8,128)(2,1)S(1)}, bf16[384,128]{1,0:T(8,128)(2,1)S(1)}, u32[]{:S(2)}, u32[]{:S(2)}) collective-permute-start(bf16[384,128]{1,0:T(8,128)(2,1)S(1)} %get-tuple-element.28), channel_id=1, source_target_pairs={{0,24},{1,28},{2,26},{3,30},{4,25},{5,29},{6,27},{7,31},{8,16},{9,... | collective-permute-start | bytes 294920 | tf_op jit(solution)/shard_map/ppermute | solution.py:392
  31.6 3.3 %collective-permute-start.4 = (bf16[384,128]{1,0:T(8,128)(2,1)S(1)}, bf16[384,128]{1,0:T(8,128)(2,1)S(1)}, u32[]{:S(2)}, u32[]{:S(2)}) collective-permute-start(bf16[384,128]{1,0:T(8,128)(2,1)S(1)} %get-tuple-element.25), channel_id=1, source_target_pairs={{0,0},{1,4},{2,2},{3,6},{4,1},{5,5},{6,3},{7,7},{8,8},{9,12},{10,1... | collective-permute-start | bytes 294920 | tf_op jit(solution)/shard_map/ppermute | solution.py:392
  34.8 0.1 collective-permute-start.5
  34.9 3.1 %collective-permute-done.6.refs_2_ = bf16[384,128]{1,0:T(8,128)(2,1)S(1)} collective-permute-done((bf16[384,128]{1,0:T(8,128)(2,1)S(1)}, bf16[384,128]{1,0:T(8,128)(2,1)S(1)}, u32[]{:S(2)}, u32[]{:S(2)}) %collective-permute-start.6) | collective-permute-done | bytes 98336 | tf_op jit(solution)/shard_map/ppermute | solution.py:392
  38.0 0.0 collective-permute-start.10
  38.0 0.0 collective-permute-done.7.refs_3_
  38.0 0.5 collective-permute-start.11
  38.5 0.5 collective-permute-done.4.refs_0_
  39.0 0.0 collective-permute-start.8
  39.0 0.8 %collective-permute-done.5.refs_1_ = bf16[384,128]{1,0:T(8,128)(2,1)S(1)} collective-permute-done((bf16[384,128]{1,0:T(8,128)(2,1)S(1)}, bf16[384,128]{1,0:T(8,128)(2,1)S(1)}, u32[]{:S(2)}, u32[]{:S(2)}) %collective-permute-start.5) | collective-permute-done | bytes 98336 | tf_op jit(solution)/shard_map/ppermute | solution.py:392
  39.9 0.1 collective-permute-start.9
  40.0 0.0 collective-permute-done.10.refs_6_
  40.0 0.0 collective-permute-done.11.refs_7_
  40.0 0.3 collective-permute-done.8.refs_4_
  40.3 0.8 %collective-permute-done.9.refs_5_ = bf16[384,128]{1,0:T(8,128)(2,1)S(1)} collective-permute-done((bf16[384,128]{1,0:T(8,128)(2,1)S(1)}, bf16[384,128]{1,0:T(8,128)(2,1)S(1)}, u32[]{:S(2)}, u32[]{:S(2)}) %collective-permute-start.9) | collective-permute-done | bytes 98336 | tf_op jit(solution)/shard_map/ppermute | solution.py:371
  41.2 1.6 %attention.1 = (bf16[128,128]{1,0:T(8,128)(2,1)S(1)}, bf16[128,128]{1,0:T(8,128)(2,1)S(1)}, bf16[128,128]{1,0:T(8,128)(2,1)S(1)}, bf16[128,128]{1,0:T(8,128)(2,1)S(1)}) custom-call(bf16[384,128]{1,0:T(8,128)(2,1)S(1)} %collective-permute-done.4.refs_0_, bf16[384,128]{1,0:T(8,128)(2,1)S(1)} %collective-permute-done.5.refs_1_, ...), custom_call_target="tpu_custom_call" | custom-call | tf_op jit(solution)/shard_map/attention/pallas_call | solution.py:302
  42.7 3.3 %collective-permute-start.12 = (bf16[128,128]{1,0:T(8,128)(2,1)S(1)}, bf16[128,128]{1,0:T(8,128)(2,1)S(1)}, u32[]{:S(2)}, u32[]{:S(2)}) collective-permute-start(bf16[128,128]{1,0:T(8,128)(2,1)S(1)} %get-tuple-element.29), channel_id=1, source_target_pairs={{0,0},{1,4},{2,2},{3,6},{4,1},{5,5},{6,3},{7,7},{8,8},{9,12},{10,1... | collective-permute-start | bytes 98312 | tf_op jit(solution)/shard_map/ppermute | solution.py:392
  46.0 1.0 %collective-permute-start.13 = (bf16[128,128]{1,0:T(8,128)(2,1)S(1)}, bf16[128,128]{1,0:T(8,128)(2,1)S(1)}, u32[]{:S(2)}, u32[]{:S(2)}) collective-permute-start(bf16[128,128]{1,0:T(8,128)(2,1)S(1)} %get-tuple-element.30), channel_id=1, source_target_pairs={{0,8},{1,12},{2,10},{3,14},{4,9},{5,13},{6,11},{7,15},{8,0},{9,4},... | collective-permute-start | bytes 98312 | tf_op jit(solution)/shard_map/ppermute | solution.py:392
  47.0 3.5 %collective-permute-start.14 = (bf16[128,128]{1,0:T(8,128)(2,1)S(1)}, bf16[128,128]{1,0:T(8,128)(2,1)S(1)}, u32[]{:S(2)}, u32[]{:S(2)}) collective-permute-start(bf16[128,128]{1,0:T(8,128)(2,1)S(1)} %get-tuple-element.31), channel_id=1, source_target_pairs={{0,16},{1,20},{2,18},{3,22},{4,17},{5,21},{6,19},{7,23},{8,24},{9,... | collective-permute-start | bytes 98312 | tf_op jit(solution)/shard_map/ppermute | solution.py:392
  50.5 0.4 collective-permute-start.15
  50.9 0.0 collective-permute-done.12.refs_0_
  50.9 0.0 collective-permute-done.13.refs_1_
  50.9 1.8 %collective-permute-done.14.refs_2_ = bf16[128,128]{1,0:T(8,128)(2,1)S(1)} collective-permute-done((bf16[128,128]{1,0:T(8,128)(2,1)S(1)}, bf16[128,128]{1,0:T(8,128)(2,1)S(1)}, u32[]{:S(2)}, u32[]{:S(2)}) %collective-permute-start.14) | collective-permute-done | bytes 32800 | tf_op jit(solution)/shard_map/ppermute | solution.py:392
  52.8 3.8 %collective-permute-done.15.refs_3_ = bf16[128,128]{1,0:T(8,128)(2,1)S(1)} collective-permute-done((bf16[128,128]{1,0:T(8,128)(2,1)S(1)}, bf16[128,128]{1,0:T(8,128)(2,1)S(1)}, u32[]{:S(2)}, u32[]{:S(2)}) %collective-permute-start.15) | collective-permute-done | bytes 32800 | tf_op jit(solution)/shard_map/ppermute | solution.py:392
  56.5 0.7 %join_heads.1 = bf16[128,512]{1,0:T(8,128)(2,1)} custom-call(bf16[128,128]{1,0:T(8,128)(2,1)S(1)} %collective-permute-done.12.refs_0_, bf16[128,128]{1,0:T(8,128)(2,1)S(1)} %collective-permute-done.13.refs_1_, bf16[128,128]{1,0:T(8,128)(2,1)S(1)} %collective-permute-done.14.refs_2_, bf16[128,128]{1,0:T(8,128)(2,1)S(1)} %collective-permute-done.15.refs_3_), custom_call_target="tpu_custom_call" | custom-call | tf_op jit(solution)/shard_map/join_heads/pallas_call | solution.py:322
Async XLA Ops:
  0.0 11.8 %copy-start.2 = (f32[1024]{0:T(1024)S(1)}, f32[1024]{0:T(1024)}, u32[]{:S(2)}) copy-start(f32[1024]{0:T(1024)} %param.10) | copy-start | bytes 12292
  1.1 10.7 %collective-permute-start = (bf16[128,1024]{1,0:T(8,128)(2,1)S(1)}, bf16[128,1024]{1,0:T(8,128)(2,1)S(1)}, u32[]{:S(2)}, u32[]{:S(2)}) collective-permute-start(bf16[128,1024]{1,0:T(8,128)(2,1)S(1)} %multiply_convert_fusion.mixed_ref), channel_id=1, source_target_pairs={{0,4},{4,8},{8,12},{12,16},{16,20},{20,24},{24,28},{1,5},{5,9},{9,... | collective-permute-start | bytes 786440 | tf_op jit(solution)/shard_map/ppermute | solution.py:357
  5.1 1.0 %copy-start = (f32[128,1024]{1,0:T(8,128)S(1)}, f32[128,1024]{1,0:T(8,128)}, u32[]{:S(2)}) copy-start(f32[128,1024]{1,0:T(8,128)} %taps_hbm.1) | copy-start | bytes 1572868
  6.2 0.9 %copy-start.1 = (bf16[128,1024]{1,0:T(8,128)(2,1)S(1)}, bf16[128,1024]{1,0:T(8,128)(2,1)}, u32[]{:S(2)}) copy-start(bf16[128,1024]{1,0:T(8,128)(2,1)} %gate_hbm.1) | copy-start | bytes 786436
  15.0 7.6 %collective-permute-start.1 = (bf16[128,1152]{1,0:T(8,128)(2,1)S(1)}, bf16[128,1152]{1,0:T(8,128)(2,1)S(1)}, u32[]{:S(2)}, u32[]{:S(2)}) collective-permute-start(bf16[128,1152]{1,0:T(8,128)(2,1)S(1)} %fir_rim_rows.1.refs_0_), channel_id=1, source_target_pairs={{0,2},{1,3},{2,0},{3,1},{4,6},{5,7},{6,4},{7,5},{8,10},{9,11},{10,... | collective-permute-start | bytes 884744 | tf_op jit(solution)/shard_map/ppermute | solution.py:371
  16.3 8.2 %collective-permute-start.3 = (bf16[128,1152]{1,0:T(8,128)(2,1)S(1)}, bf16[128,1152]{1,0:T(8,128)(2,1)S(1)}, u32[]{:S(2)}, u32[]{:S(2)}) collective-permute-start(bf16[128,1152]{1,0:T(8,128)(2,1)S(1)} %fir_rim_rows.1.refs_0_), channel_id=1, source_target_pairs={{0,1},{1,0},{2,3},{3,2},{4,5},{5,4},{6,7},{7,6},{8,9},{9,8},{10,11... | collective-permute-start | bytes 884744 | tf_op jit(solution)/shard_map/ppermute | solution.py:371
  22.7 3.1 %collective-permute-start.2 = (bf16[128,1152]{1,0:T(8,128)(2,1)S(1)}, bf16[128,1152]{1,0:T(8,128)(2,1)S(1)}, u32[]{:S(2)}, u32[]{:S(2)}) collective-permute-start(bf16[128,1152]{1,0:T(8,128)(2,1)S(1)} %collective-permute-done.1.refs_0_), channel_id=1, source_target_pairs={{0,1},{1,0},{2,3},{3,2},{4,5},{5,4},{6,7},{7,6},{8,9},{9,8},{10,11... | collective-permute-start | bytes 884744 | tf_op jit(solution)/shard_map/ppermute | solution.py:371
  26.8 11.1 %collective-permute-start.6 = (bf16[384,128]{1,0:T(8,128)(2,1)S(1)}, bf16[384,128]{1,0:T(8,128)(2,1)S(1)}, u32[]{:S(2)}, u32[]{:S(2)}) collective-permute-start(bf16[384,128]{1,0:T(8,128)(2,1)S(1)} %get-tuple-element.27), channel_id=1, source_target_pairs={{0,16},{1,20},{2,18},{3,22},{4,17},{5,21},{6,19},{7,23},{8,24},{9,... | collective-permute-start | bytes 294920 | tf_op jit(solution)/shard_map/ppermute | solution.py:392
  30.4 7.6 %collective-permute-start.7 = (bf16[384,128]{1,0:T(8,128)(2,1)S(1)}, bf16[384,128]{1,0:T(8,128)(2,1)S(1)}, u32[]{:S(2)}, u32[]{:S(2)}) collective-permute-start(bf16[384,128]{1,0:T(8,128)(2,1)S(1)} %get-tuple-element.28), channel_id=1, source_target_pairs={{0,24},{1,28},{2,26},{3,30},{4,25},{5,29},{6,27},{7,31},{8,16},{9,... | collective-permute-start | bytes 294920 | tf_op jit(solution)/shard_map/ppermute | solution.py:392
  31.6 7.4 %collective-permute-start.4 = (bf16[384,128]{1,0:T(8,128)(2,1)S(1)}, bf16[384,128]{1,0:T(8,128)(2,1)S(1)}, u32[]{:S(2)}, u32[]{:S(2)}) collective-permute-start(bf16[384,128]{1,0:T(8,128)(2,1)S(1)} %get-tuple-element.25), channel_id=1, source_target_pairs={{0,0},{1,4},{2,2},{3,6},{4,1},{5,5},{6,3},{7,7},{8,8},{9,12},{10,1... | collective-permute-start | bytes 294920 | tf_op jit(solution)/shard_map/ppermute | solution.py:392
  34.8 5.0 %collective-permute-start.5 = (bf16[384,128]{1,0:T(8,128)(2,1)S(1)}, bf16[384,128]{1,0:T(8,128)(2,1)S(1)}, u32[]{:S(2)}, u32[]{:S(2)}) collective-permute-start(bf16[384,128]{1,0:T(8,128)(2,1)S(1)} %get-tuple-element.26), channel_id=1, source_target_pairs={{0,8},{1,12},{2,10},{3,14},{4,9},{5,13},{6,11},{7,15},{8,0},{9,4},... | collective-permute-start | bytes 294920 | tf_op jit(solution)/shard_map/ppermute | solution.py:392
  38.0 2.0 %collective-permute-start.10 = (bf16[384,128]{1,0:T(8,128)(2,1)S(1)}, bf16[384,128]{1,0:T(8,128)(2,1)S(1)}, u32[]{:S(2)}, u32[]{:S(2)}) collective-permute-start(bf16[384,128]{1,0:T(8,128)(2,1)S(1)} %collective-permute-done.6.refs_2_), channel_id=1, source_target_pairs={{0,1},{1,0},{2,3},{3,2},{4,5},{5,4},{6,7},{7,6},{8,9},{9,8},{10,11... | collective-permute-start | bytes 294920 | tf_op jit(solution)/shard_map/ppermute | solution.py:371
  38.0 2.0 %collective-permute-start.11 = (bf16[384,128]{1,0:T(8,128)(2,1)S(1)}, bf16[384,128]{1,0:T(8,128)(2,1)S(1)}, u32[]{:S(2)}, u32[]{:S(2)}) collective-permute-start(bf16[384,128]{1,0:T(8,128)(2,1)S(1)} %collective-permute-done.7.refs_3_), channel_id=1, source_target_pairs={{0,1},{1,0},{2,3},{3,2},{4,5},{5,4},{6,7},{7,6},{8,9},{9,8},{10,11... | collective-permute-start | bytes 294920 | tf_op jit(solution)/shard_map/ppermute | solution.py:371
  39.0 1.3 %collective-permute-start.8 = (bf16[384,128]{1,0:T(8,128)(2,1)S(1)}, bf16[384,128]{1,0:T(8,128)(2,1)S(1)}, u32[]{:S(2)}, u32[]{:S(2)}) collective-permute-start(bf16[384,128]{1,0:T(8,128)(2,1)S(1)} %collective-permute-done.4.refs_0_), channel_id=1, source_target_pairs={{0,1},{1,0},{2,3},{3,2},{4,5},{5,4},{6,7},{7,6},{8,9},{9,8},{10,11... | collective-permute-start | bytes 294920 | tf_op jit(solution)/shard_map/ppermute | solution.py:371
  39.9 1.3 %collective-permute-start.9 = (bf16[384,128]{1,0:T(8,128)(2,1)S(1)}, bf16[384,128]{1,0:T(8,128)(2,1)S(1)}, u32[]{:S(2)}, u32[]{:S(2)}) collective-permute-start(bf16[384,128]{1,0:T(8,128)(2,1)S(1)} %collective-permute-done.5.refs_1_), channel_id=1, source_target_pairs={{0,1},{1,0},{2,3},{3,2},{4,5},{5,4},{6,7},{7,6},{8,9},{9,8},{10,11... | collective-permute-start | bytes 294920 | tf_op jit(solution)/shard_map/ppermute | solution.py:371
  42.7 8.2 %collective-permute-start.12 = (bf16[128,128]{1,0:T(8,128)(2,1)S(1)}, bf16[128,128]{1,0:T(8,128)(2,1)S(1)}, u32[]{:S(2)}, u32[]{:S(2)}) collective-permute-start(bf16[128,128]{1,0:T(8,128)(2,1)S(1)} %get-tuple-element.29), channel_id=1, source_target_pairs={{0,0},{1,4},{2,2},{3,6},{4,1},{5,5},{6,3},{7,7},{8,8},{9,12},{10,1... | collective-permute-start | bytes 98312 | tf_op jit(solution)/shard_map/ppermute | solution.py:392
  46.0 4.9 %collective-permute-start.13 = (bf16[128,128]{1,0:T(8,128)(2,1)S(1)}, bf16[128,128]{1,0:T(8,128)(2,1)S(1)}, u32[]{:S(2)}, u32[]{:S(2)}) collective-permute-start(bf16[128,128]{1,0:T(8,128)(2,1)S(1)} %get-tuple-element.30), channel_id=1, source_target_pairs={{0,8},{1,12},{2,10},{3,14},{4,9},{5,13},{6,11},{7,15},{8,0},{9,4},... | collective-permute-start | bytes 98312 | tf_op jit(solution)/shard_map/ppermute | solution.py:392
  47.0 5.7 %collective-permute-start.14 = (bf16[128,128]{1,0:T(8,128)(2,1)S(1)}, bf16[128,128]{1,0:T(8,128)(2,1)S(1)}, u32[]{:S(2)}, u32[]{:S(2)}) collective-permute-start(bf16[128,128]{1,0:T(8,128)(2,1)S(1)} %get-tuple-element.31), channel_id=1, source_target_pairs={{0,16},{1,20},{2,18},{3,22},{4,17},{5,21},{6,19},{7,23},{8,24},{9,... | collective-permute-start | bytes 98312 | tf_op jit(solution)/shard_map/ppermute | solution.py:392
  50.5 6.0 %collective-permute-start.15 = (bf16[128,128]{1,0:T(8,128)(2,1)S(1)}, bf16[128,128]{1,0:T(8,128)(2,1)S(1)}, u32[]{:S(2)}, u32[]{:S(2)}) collective-permute-start(bf16[128,128]{1,0:T(8,128)(2,1)S(1)} %get-tuple-element.32), channel_id=1, source_target_pairs={{0,24},{1,28},{2,26},{3,30},{4,25},{5,29},{6,27},{7,31},{8,16},{9,... | collective-permute-start | bytes 98312 | tf_op jit(solution)/shard_map/ppermute | solution.py:392

commit v4 on v0

v4 whole, which is shorter than its diff:
```python
import functools
import math

import jax
import jax.numpy as jnp
from jax import lax
from jax.experimental import pallas as pl
from jax.experimental.pallas import tpu as pltpu
from jax.sharding import PartitionSpec as P

HEAD_DIM = 128
LANES = 128
SLAB = 8
PHASES = 4
SUBS = 9
HELD = 8
EPS = 1e-06
BF16 = jnp.bfloat16
F32 = jnp.float32
VMEM = pl.BlockSpec(memory_space=pltpu.VMEM)
HBM = pl.BlockSpec(memory_space=pltpu.HBM)


def params(mib):
    return pltpu.CompilerParams(vmem_limit_bytes=mib << 20)


LATE = 1 << 28


def cost(weight=1024):
    return pl.CostEstimate(flops=0, bytes_accessed=weight, transcendentals=0)


def slabs(count):
    return jax.ShapeDtypeStruct((count * SLAB, LANES), F32)


def slab_scratch(count):
    return pltpu.VMEM((count * SLAB, LANES), F32)


def at(index):
    if not isinstance(index, int):
        return pl.ds(pl.multiple_of(index * SLAB, SLAB), SLAB)
    return pl.ds(index * SLAB, SLAB)


def to_slabs(source, target):
    for group in range(SLAB):
        target[pl.ds(group, source.shape[0], stride=SLAB), :] = source[
            :, group * LANES : (group + 1) * LANES
        ].astype(F32)


def to_subs(source, count, target):
    for n in range(count):
        x0, x1, x2, x3 = (source[at(PHASES * n + p), :] for p in range(PHASES))
        low, high = x0 + x1, x2 + x3
        for s, value in enumerate((x0, x2, x0 + x2, x1, x3, x1 + x3, low, high, low + high)):
            target[at(s * count + n), :] = value


def accumulate(sums, first, lag, taps, tap_at, x_ref, x_at, x_first, x_count, span):
    sums = list(sums)
    for start in range(x_first, x_first + x_count, HELD):
        places = range(start, min(start + HELD, x_first + x_count))
        used = {}
        for i in places:
            x = x_ref[at(x_at + (i - x_first)), :]
            for k in range(len(sums)):
                j = lag + first + k - i
                if 0 <= j < span:
                    if j not in used:
                        used[j] = taps[at(tap_at + j), :]
                    sums[k] = sums[k] + used[j] * x
    return sums


def finish(z_ref, count, full_ref):
    def z(s, k):
        return z_ref[at(s * (count + 1) + k), :]

    before = [z(s, 0) for s in range(SUBS)]
    for n in range(count):
        now = [z(s, n + 1) for s in range(SUBS)]

        def even(s):
            return now[s] + before[s + 1]

        def odd(s, held):
            return held[s + 2] - held[s] - held[s + 1]

        a_even, a_odd, b_even, b_odd = even(0), odd(0, now), even(3), odd(3, now)
        full_ref[at(PHASES * n), :] = a_even + odd(3, before)
        full_ref[at(PHASES * n + 1), :] = even(6) - a_even - b_even
        full_ref[at(PHASES * n + 2), :] = a_odd + b_even
        full_ref[at(PHASES * n + 3), :] = odd(6, now) - a_odd - b_odd
        before = now


def emit(full_ref, gate_ref, first, gain_ref, sent_ref):
    rows = sent_ref.shape[0]
    squares = jnp.zeros((rows, LANES), F32)
    for group in range(SLAB):
        lanes = slice(group * LANES, (group + 1) * LANES)
        hyena = (
            (
                gate_ref[first : first + rows, lanes].astype(F32)
                * full_ref[pl.ds(group, rows, stride=SLAB), :]
            )
            .astype(BF16)
            .astype(F32)
        )
        squares = squares + hyena * hyena
        sent_ref[:, lanes] = (hyena * gain_ref[:, lanes]).astype(BF16)
    total = jnp.sum(squares, axis=1, keepdims=True)
    pieces = []
    for _ in range(3):
        pieces.append(total.astype(BF16).astype(F32))
        total = total - pieces[-1]
    lane = lax.broadcasted_iota(jnp.int32, (rows, LANES), 1)
    row = jnp.zeros((rows, LANES), F32)
    for place, piece in enumerate(pieces):
        row = jnp.where(lane == place, piece, row)
    sent_ref[:, SLAB * LANES :] = row.astype(BF16)


def own_kernel(
    mixed_ref,
    taps_hbm,
    gate_hbm,
    weight_hbm,
    sums_low,
    sums_high,
    tap_subs,
    gate_ref,
    weight_ref,
    taps_ref,
    slab_ref,
    x_subs,
    sems,
):
    rows, span = mixed_ref.shape[0], taps_ref.shape[0]
    quarter, eighth = rows // PHASES, rows // PHASES // 2
    tap_quarter = span // PHASES
    blocks = lax.axis_size("tp")
    channels = weight_ref.shape[1] // blocks
    copies = [
        pltpu.make_async_copy(taps_hbm, taps_ref, sems.at[0]),
        pltpu.make_async_copy(gate_hbm, gate_ref, sems.at[1]),
    ] + [
        own_weights(weight_hbm, weight_ref, o, channels, sems.at[2 + o]) for o in range(blocks)
    ]
    for copy in copies:
        copy.start()
    to_slabs(mixed_ref, slab_ref)
    to_subs(slab_ref, quarter, x_subs)
    copies[0].wait()
    to_slabs(taps_ref, slab_ref)
    to_subs(slab_ref, tap_quarter, tap_subs)

    def sub(s, _):
        zero = jnp.zeros((SLAB, LANES), F32)
        sums_low[at(s * eighth), :] = zero
        for first in (0, eighth):
            sums = accumulate(
                [zero] * eighth, first, 0, tap_subs, s * tap_quarter, x_subs, s * quarter,
                0, first + eighth, tap_quarter,
            )
            for k, value in enumerate(sums):
                n = first + k
                if n < eighth - 1:
                    sums_low[at(s * eighth + n + 1), :] = value
                else:
                    sums_high[at(s * (eighth + 1) + n + 1 - eighth), :] = value
        return 0

    lax.fori_loop(0, SUBS, sub, 0)
    for copy in copies[1:]:
        copy.wait()


def own_weights(weight_hbm, weight_ref, offset, channels, sem):
    owner = jnp.bitwise_xor(lax.axis_index("tp"), offset)
    return pltpu.make_async_copy(
        weight_hbm.at[:, pl.ds(pl.multiple_of(owner * channels, channels), channels), :],
        weight_ref.at[:, pl.ds(offset * channels, channels), :],
        sem,
    )


def own_part(mixed, taps, gate, weight, tp):
    rows, span = mixed.shape[0], taps.shape[0]
    quarter = rows // PHASES
    eighth = quarter // 2
    return pl.pallas_call(
        own_kernel,
        out_shape=(
            slabs(SUBS * eighth),
            slabs(SUBS * (eighth + 1)),
            slabs(SUBS * span // PHASES),
            jax.ShapeDtypeStruct(gate.shape, BF16),
            jax.ShapeDtypeStruct(weight.shape, BF16),
        ),
        in_specs=[VMEM, HBM, HBM, HBM],
        out_specs=(VMEM,) * 5,
        scratch_shapes=[
            pltpu.VMEM(taps.shape, F32),
            slab_scratch(max(rows, span)),
            slab_scratch(SUBS * quarter),
            pltpu.SemaphoreType.DMA((2 + tp,)),
        ],
        compiler_params=params(24),
        cost_estimate=cost(),
        name="fir_own_rows",
    )(mixed, *(pltpu.with_memory_space_constraint(v, pltpu.HBM) for v in (taps, gate, weight)))


def high_kernel(
    rim_ref, sums_ref, tap_subs, gate_ref, gain_ref, sent_ref, x_subs, last_ref, slab_ref, z_ref
):
    rows = sent_ref.shape[0]
    eighth = rows // PHASES
    tap_quarter = tap_subs.shape[0] // SLAB // SUBS
    to_slabs(rim_ref.at[pl.ds(rows, rows)], slab_ref)
    to_subs(slab_ref, eighth, x_subs)

    def sub(s, _):
        at_z = s * (eighth + 1)
        sums = [sums_ref[at(at_z + k), :] for k in range(eighth + 1)]
        sums = accumulate(
            sums, eighth - 1, 2 * eighth, tap_subs, s * tap_quarter, x_subs, s * eighth,
            eighth, eighth, tap_quarter,
        )
        for k, value in enumerate(sums):
            z_ref[at(at_z + k), :] = value
        last_ref[at(s), :] = sums[0]
        return 0

    lax.fori_loop(0, SUBS, sub, 0)
    finish(z_ref, eighth, slab_ref)
    emit(slab_ref, gate_ref, rows, gain_ref, sent_ref)


def high_part(rim, sums, taps, gate, gain):
    rows = rim.shape[0] // 2
    eighth = rows // PHASES
    return pl.pallas_call(
        high_kernel,
        out_shape=(
            jax.ShapeDtypeStruct((rows, (SLAB + 1) * LANES), BF16),
            slabs(SUBS * eighth),
            slabs(SUBS),
        ),
        in_specs=[VMEM] * 5,
        out_specs=(VMEM,) * 3,
        scratch_shapes=[slab_scratch(rows), slab_scratch(SUBS * (eighth + 1))],
        compiler_params=params(16),
        cost_estimate=cost(),
        name="fir_later_rows",
    )(rim, sums, taps, gate, gain)


def low_kernel(
    rim_ref,
    sums_ref,
    x_high,
    last_ref,
    tap_subs,
    gate_ref,
    gain_ref,
    sent_ref,
    slab_ref,
    x_subs,
    z_ref,
):
    rows = sent_ref.shape[0]
    eighth = rows // PHASES
    tap_quarter = tap_subs.shape[0] // SLAB // SUBS
    to_slabs(rim_ref.at[pl.ds(0, rows)], slab_ref)
    to_subs(slab_ref, eighth, x_subs)

    def sub(s, _):
        sums = [sums_ref[at(s * eighth + k), :] for k in range(eighth)]
        for x_ref, first in ((x_high, eighth), (x_subs, 0)):
            sums = accumulate(
                sums, -1, 2 * eighth, tap_subs, s * tap_quarter, x_ref, s * eighth,
                first, eighth, tap_quarter,
            )
        for k, value in enumerate(sums + [last_ref[at(s), :]]):
            z_ref[at(s * (eighth + 1) + k), :] = value
        return 0

    lax.fori_loop(0, SUBS, sub, 0)
    finish(z_ref, eighth, slab_ref)
    emit(slab_ref, gate_ref, 0, gain_ref, sent_ref)


def low_part(rim, sums, x_high, last, taps, gate, gain):
    rows = rim.shape[0] // 2
    eighth = rows // PHASES
    return pl.pallas_call(
        low_kernel,
        out_shape=jax.ShapeDtypeStruct((rows, (SLAB + 1) * LANES), BF16),
        in_specs=[VMEM] * 7,
        out_specs=VMEM,
        scratch_shapes=[
            slab_scratch(rows),
            slab_scratch(SUBS * eighth),
            slab_scratch(SUBS * (eighth + 1)),
        ],
        compiler_params=params(16),
        cost_estimate=cost(),
        name="fir_earlier_rows",
    )(rim, sums, x_high, last, taps, gate, gain)


def project(blocks, first, weight_ref, acc_ref, ssq_ref):
    width = weight_ref.shape[2]
    whole = [jnp.concatenate([low[...], high[...]], axis=0) for low, high in blocks]
    channels = whole[0].shape[1] - LANES
    for block in whole:
        ssq_ref[...] += block[:, channels:].astype(F32)
    for which in range(3):
        lanes = slice(which * width, (which + 1) * width)
        total = acc_ref[:, lanes]
        for place, block in enumerate(whole, first):
            total = total + jnp.dot(
                block[:, :channels],
                weight_ref[which, place * channels : (place + 1) * channels, :],
                preferred_element_type=F32,
            )
        acc_ref[:, lanes] = total


def first_kernel(*refs):
    blocks = ((refs[0], refs[1]), (refs[2], refs[3]))
    weight_ref, acc_ref, ssq_ref = refs[4:]
    acc_ref[...] = jnp.zeros_like(acc_ref)
    ssq_ref[...] = jnp.zeros_like(ssq_ref)
    project(blocks, 0, weight_ref, acc_ref, ssq_ref)


def first_projection(mine, weight):
    rows = 2 * mine[0][0].shape[0]
    return pl.pallas_call(
        first_kernel,
        out_shape=(
            jax.ShapeDtypeStruct((rows, 3 * weight.shape[2]), F32),
            jax.ShapeDtypeStruct((rows, LANES), F32),
        ),
        in_specs=[VMEM] * 5,
        out_specs=(VMEM,) * 2,
        compiler_params=params(24),
        cost_estimate=cost(),
        name="projections_near",
    )(*mine[0], *mine[1], weight)


def last_kernel(count, model, layout, *refs):
    blocks = [(refs[2 * n], refs[2 * n + 1]) for n in range(count)]
    weight_ref, acc_in, ssq_in = refs[2 * count : 2 * count + 3]
    outs, (acc_ref, ssq_ref) = refs[2 * count + 3 : -2], refs[-2:]
    acc_ref[...] = acc_in[...]
    ssq_ref[...] = ssq_in[...]
    project(blocks, 2, weight_ref, acc_ref, ssq_ref)
    msq = jnp.sum(ssq_ref[...], axis=1, keepdims=True) / model
    scale = lax.rsqrt(msq + EPS)
    rows = acc_ref.shape[0]
    width = weight_ref.shape[2]
    heads = width // HEAD_DIM
    place = lax.axis_index("ctx") % heads
    kept = {}
    for out, parts in zip(outs, layout):
        for spot, (which, k) in enumerate(parts):
            if (which, k) not in kept:
                head = jnp.bitwise_xor(place, k)
                lanes = pl.ds(pl.multiple_of(which * width + head * HEAD_DIM, LANES), HEAD_DIM)
                kept[which, k] = (acc_ref[:, lanes] * scale).astype(BF16)
            out[spot * rows : (spot + 1) * rows, :] = kept[which, k]


def last_projection(others, weight, acc, ssq, model, layout):
    rows = acc.shape[0]
    return pl.pallas_call(
        functools.partial(last_kernel, len(others), model, layout),
        out_shape=tuple(
            jax.ShapeDtypeStruct((len(parts) * rows, HEAD_DIM), BF16) for parts in layout
        ),
        in_specs=[VMEM] * (2 * len(others) + 3),
        out_specs=(VMEM,) * len(layout),
        scratch_shapes=[pltpu.VMEM(acc.shape, F32), pltpu.VMEM(ssq.shape, F32)],
        compiler_params=params(24),
        cost_estimate=cost(),
        name="projections_far",
    )(*[half for pair in others for half in pair], weight, acc, ssq)


def earlier_kernel(*refs):
    blocks, (key_ref, value_ref) = refs[:-2], refs[-2:]
    rows = blocks[0].shape[0] // 2
    for k, block in enumerate(blocks):
        key_ref[k * rows : (k + 1) * rows, :] = block[:rows, :]
        value_ref[k * rows : (k + 1) * rows, :] = block[rows:, :]


def earlier_group(blocks):
    shape = jax.ShapeDtypeStruct((blocks[0].shape[0] // 2 * len(blocks), HEAD_DIM), BF16)
    return pl.pallas_call(
        earlier_kernel,
        out_shape=(shape, shape),
        in_specs=[VMEM] * len(blocks),
        out_specs=(VMEM, VMEM),
        compiler_params=params(4),
        cost_estimate=cost(LATE),
        name="earlier_keys",
    )(*blocks)


def attend_kernel(rows, count, *refs):
    mine, (old_keys, old_values), outs = refs[:count], refs[count : count + 2], refs[count + 2 : -2]
    key_ref, value_ref = refs[-2:]
    place = lax.axis_index("ctx")
    group, p = place // count, place % count
    key_ref[: count * rows, :] = old_keys[...]
    value_ref[: count * rows, :] = old_values[...]
    for k in range(count):
        spot = slice((count + k) * rows, (count + k + 1) * rows)
        key_ref[spot, :] = mine[k][rows : 2 * rows, :]
        value_ref[spot, :] = mine[k][2 * rows : 3 * rows, :]
    column = lax.broadcasted_iota(jnp.int32, (1, 2 * count * rows), 1)
    block = jnp.bitwise_xor(column // rows % count, p)
    first = jnp.where(column < count * rows, jnp.where(group > 0, 0, 2 * count), group * count)
    key_pos = (first + block) * rows + column % rows
    scale = 1.0 / math.sqrt(HEAD_DIM)
    for k in range(count):
        start = (group * count + jnp.bitwise_xor(p, k)) * rows
        query_pos = start + lax.broadcasted_iota(jnp.int32, (rows, 1), 0)
        scores = (
            lax.dot_general(
                mine[k][:rows, :],
                key_ref[...],
                (((1,), (1,)), ((), ())),
                preferred_element_type=F32,
            )
            * scale
        )
        scores = jnp.where(query_pos >= key_pos, scores, -1e30)
        top = jnp.max(scores, axis=1, keepdims=True)
        expo = jnp.exp(scores - top)
        total = jnp.sum(expo, axis=1, keepdims=True)
        summed = jnp.dot(expo.astype(BF16), value_ref[...], preferred_element_type=F32)
        outs[k][...] = (summed / total).astype(BF16)


def attend(mine, earlier):
    count = len(mine)
    rows = mine[0].shape[0] // 3
    return pl.pallas_call(
        functools.partial(attend_kernel, rows, count),
        out_shape=tuple(jax.ShapeDtypeStruct((rows, HEAD_DIM), BF16) for _ in range(count)),
        in_specs=[VMEM] * (count + 2),
        out_specs=(VMEM,) * count,
        scratch_shapes=[pltpu.VMEM((2 * count * rows, HEAD_DIM), BF16)] * 2,
        compiler_params=params(24),
        cost_estimate=cost(),
        name="attention",
    )(*mine, *earlier)


def join_kernel(*refs):
    blocks, out = refs[:-1], refs[-1]
    for k, block in enumerate(blocks):
        head = jnp.bitwise_xor(lax.axis_index("ctx") % len(blocks), k)
        out[:, pl.ds(pl.multiple_of(head * HEAD_DIM, LANES), HEAD_DIM)] = block[...]


def join(blocks):
    rows = blocks[0].shape[0]
    return pl.pallas_call(
        join_kernel,
        out_shape=jax.ShapeDtypeStruct((rows, len(blocks) * HEAD_DIM), BF16),
        in_specs=[VMEM] * len(blocks),
        out_specs=VMEM,
        compiler_params=params(4),
        name="join_heads",
    )(*blocks)


def gathered_attention(message, heads, rows):
    order = jnp.bitwise_xor(lax.axis_index("ctx") % heads, jnp.arange(heads))
    query, keys, values = (
        m.reshape(heads, rows, HEAD_DIM)[order].transpose(1, 0, 2) for m in message
    )
    keys = lax.all_gather(keys, "ctx", axis=0, tiled=True)
    values = lax.all_gather(values, "ctx", axis=0, tiled=True)
    query_pos = lax.axis_index("ctx") * rows + jnp.arange(rows, dtype=jnp.int32)
    key_pos = jnp.arange(keys.shape[0], dtype=jnp.int32)
    scores = jnp.einsum("qhd,khd->hqk", query, keys, preferred_element_type=F32)
    allowed = (query_pos[:, None] >= key_pos[None, :])[None]
    scores = jnp.where(allowed, scores / math.sqrt(HEAD_DIM), -1e30)
    expo = jnp.where(allowed, jnp.exp(scores - jnp.max(scores, axis=2, keepdims=True)), 0.0)
    total = jnp.sum(expo, axis=2)
    summed = jnp.einsum("hqk,khd->qhd", expo.astype(BF16), values, preferred_element_type=F32)
    return (summed / total.T[:, :, None]).astype(BF16).reshape(rows, heads * HEAD_DIM)


def body(gate_in, conv_in, value_in, filter_taps, norm_gain, qkv_weight):
    rows, channels = gate_in.shape
    ctx, tp = lax.axis_size("ctx"), lax.axis_size("tp")
    weight = jnp.transpose(qkv_weight, (1, 0, 2))
    heads = weight.shape[2] // HEAD_DIM
    model = weight.shape[1]
    two_groups = heads == 4 and ctx == 2 * heads

    wide = SLAB * LANES

    def widened(value):
        return jnp.pad(value, ((0, 0), (0, wide - channels))) if channels < wide else value

    def narrowed(sent):
        if channels == wide:
            return sent
        return jnp.concatenate([sent[:, :channels], sent[:, wide:]], axis=1)

    def swapped(value, by):
        return lax.ppermute(value, "tp", [(i, i ^ by) for i in range(tp)])

    mixed = (conv_in.astype(F32) * value_in.astype(F32)).astype(BF16)
    rim = widened(lax.ppermute(mixed, "ctx", [(i, i + 1) for i in range(ctx - 1)]))
    gain = widened(norm_gain[None])
    sums_low, sums_high, taps, gate, weight = own_part(
        widened(mixed), widened(filter_taps), widened(gate_in), weight, tp
    )
    sent_high, x_high, last = high_part(rim, sums_high, taps, gate, gain)
    sent_high = narrowed(sent_high)
    near_high = swapped(sent_high, 1)
    rim, near_high = lax.optimization_barrier((rim, near_high))
    sent_low = narrowed(low_part(rim, sums_low, x_high, last, taps, gate, gain))
    sent = (sent_low, sent_high)

    far = []
    by = tp // 2
    while by > 1:
        far = far + [
            (o ^ by, tuple(swapped(part, by) for part in pair)) for o, pair in [(0, sent)] + far
        ]
        by //= 2
    mine = (sent, (swapped(sent_low, 1), near_high))
    acc, ssq = first_projection(mine, weight)
    places, pairs = [o for o, _ in far], [pair for _, pair in far]
    last_low, acc = lax.optimization_barrier((pairs[-1][0], acc))
    pairs[-1] = (last_low, pairs[-1][1])
    others = []
    for o, pair in sorted(zip(places, pairs), key=lambda item: item[0]):
        others += [pair, tuple(swapped(part, 1) for part in pair)]

    def parts(first, *which):
        return tuple((w, k) for k in which for w in range(first, 3))

    if not two_groups:
        layout = tuple(tuple((w, k) for k in range(heads)) for w in range(3))
        return gathered_attention(
            last_projection(others, weight, acc, ssq, model, layout), heads, rows
        )
    layout = tuple(parts(first, k) for first in (1, 0) for k in range(heads))
    sent = last_projection(others, weight, acc, ssq, model, layout)
    onward, inside = sent[:heads], sent[heads:]

    def within(value, k):
        return lax.ppermute(value, "ctx", [(i, i ^ k) for i in range(ctx)]) if k else value

    earlier = [
        lax.ppermute(onward[k], "ctx", [(i, heads + (i ^ k)) for i in range(heads)])
        for k in range(heads)
    ]
    held = [within(inside[k], k) for k in range(heads)]
    done = attend(held, earlier_group(earlier))
    return join([within(done[k], k) for k in range(heads - 1, -1, -1)][::-1])


def solution(mesh):
    placed = (
        P("ctx", "tp"),
        P("ctx", "tp"),
        P("ctx", "tp"),
        P(None, "tp"),
        P("tp"),
        P(None, None, "tp"),
    )
    return jax.shard_map(
        body, mesh=mesh, in_specs=placed, out_specs=P("ctx", "tp"), check_vma=False
    )
```

time: 332 us -> 55 us (0.17)
  the two profiles are of different devices: /device:TPU:1 before, /device:TPU:18 now
where the time goes in v4:
time: 55 us; the launch traced here: 54.8 us
  waiting for transfers between devices  23.4 us (43%)
  starting transfers between devices  18.7 us (34%)
  Pallas kernels  11.4 us (21%)
  other arithmetic  1.11 us (2%)
    ppermute x4, waiting for transfers between devices, body(): lax.ppermute(onward[k], 'ctx', [(i, heads + (i ^ k)) for i in range(heads)])  9.45 us
    ppermute x6, starting transfers between devices, within(): lax.ppermute(value, 'ctx', [(i, i ^ k) for i in range(ctx)])  8.52 us
    ppermute x6, waiting for transfers between devices, swapped(): return lax.ppermute(value, 'tp', [(i, i ^ by) for i in range(tp)])  6.74 us
    ppermute x4, starting transfers between devices, body(): lax.ppermute(onward[k], 'ctx', [(i, heads + (i ^ k)) for i in range(heads)])  5.15 us
    pallas_call x1, Pallas kernels, own_part(): pl.pallas_call(own_kernel, out_shape=(slabs(SUBS * eighth), slabs(SUBS *...  4.96 us
    ppermute x6, waiting for transfers between devices, within(): lax.ppermute(value, 'ctx', [(i, i ^ k) for i in range(ctx)])  4.76 us
    ppermute x1, starting transfers between devices, body(): lax.ppermute(mixed, 'ctx', [(i, i + 1) for i in range(ctx - 1)])  3.43 us
    ppermute x1, waiting for transfers between devices, body(): lax.ppermute(mixed, 'ctx', [(i, i + 1) for i in range(ctx - 1)])  2.43 us
  transfers between devices with their start and end apart: 17, of which 11 were waited for; matrix products, arithmetic and copies ran while one was open for 0% of the time, Pallas kernels for 14%

profile of v4, /device:TPU:18, one launch (start us, length us, event | category | flops | bytes accessed | tf_op | source)
XLA Modules:
  0.0 54.8 jit_solution(11254266786058000900)
XLA Ops:
  0.0 0.0 copy-start
  0.0 1.1 %multiply_convert_fusion.mixed_ref = bf16[128,1024]{1,0:T(8,128)(2,1)S(1)} fusion(bf16[128,1024]{1,0:T(8,128)(2,1)} %param.8, bf16[128,1024]{1,0:T(8,128)(2,1)} %param.7), kind=kLoop, calls=%fused_computation | loop fusion | flops 524288 | bytes 786432 | tf_op jit(solution)/shard_map/convert_element_type | solution.py:530
  1.1 3.4 %collective-permute-start = (bf16[128,1024]{1,0:T(8,128)(2,1)S(1)}, bf16[128,1024]{1,0:T(8,128)(2,1)S(1)}, u32[]{:S(2)}, u32[]{:S(2)}) collective-permute-start(bf16[128,1024]{1,0:T(8,128)(2,1)S(1)} %multiply_convert_fusion.mixed_ref), channel_id=1, source_target_pairs={{0,4},{4,8},{8,12},{12,16},{16,20},{20,24},{24,28},{1,5},{5,9},{9,... | collective-permute-start | bytes 786440 | tf_op jit(solution)/shard_map/ppermute | solution.py:531
  4.6 5.0 %fir_own_rows.1 = (f32[1152,128]{1,0:T(8,128)S(1)}, f32[1224,128]{1,0:T(8,128)S(1)}, f32[2304,128]{1,0:T(8,128)S(1)}, bf16[128,1024]{1,0:T(8,128)(2,1)S(1)}, bf16[3,4096,512]{2,1,0:T(8,128)(2,1)S(1)}) custom-call(bf16[128,1024]{1,0:T(8,128)(2,1)S(1)} %multiply_convert_fusion.mixed_ref, f32[128,1024]{1,0:T(8,128)} %taps_hbm.1, bf16[128,1024]{1,0:T(8,128)(2,1)} %gate_hbm.1, ...), custom_call_target="tpu_custom_call" | custom-call | bytes 1024 | tf_op jit(solution)/shard_map/fir_own_rows/pallas_call | solution.py:197
  9.5 2.4 %collective-permute-done.rim_ref = bf16[128,1024]{1,0:T(8,128)(2,1)S(1)} collective-permute-done((bf16[128,1024]{1,0:T(8,128)(2,1)S(1)}, bf16[128,1024]{1,0:T(8,128)(2,1)S(1)}, u32[]{:S(2)}, u32[]{:S(2)}) %collective-permute-start) | collective-permute-done | bytes 262176 | tf_op jit(solution)/shard_map/ppermute | solution.py:531
  12.0 0.0 copy-done
  12.0 0.7 %fir_later_rows.1 = (bf16[64,1152]{1,0:T(8,128)(2,1)S(1)}, f32[1152,128]{1,0:T(8,128)S(1)}, f32[72,128]{1,0:T(8,128)S(1)}) custom-call(bf16[128,1024]{1,0:T(8,128)(2,1)S(1)} %collective-permute-done.rim_ref, f32[1224,128]{1,0:T(8,128)S(1)} %get-tuple-element.33.sums_ref, f32[2304,128]{1,0:T(8,128)S(1)} %get-tuple-element.34.tap_subs, ...), custom_call_target="tpu_custom_call" | custom-call | bytes 1024 | tf_op jit(solution)/shard_map/fir_later_rows/pallas_call | solution.py:249
  12.6 0.1 collective-permute-start.1
  12.7 0.6 %collective-permute-start.4 = (bf16[64,1152]{1,0:T(8,128)(2,1)S(1)}, bf16[64,1152]{1,0:T(8,128)(2,1)S(1)}, u32[]{:S(2)}, u32[]{:S(2)}) collective-permute-start(bf16[64,1152]{1,0:T(8,128)(2,1)S(1)} %get-tuple-element.36.refs_1_), channel_id=1, source_target_pairs={{0,2},{1,3},{2,0},{3,1},{4,6},{5,7},{6,4},{7,5},{8,10},{9,11},{10,... | collective-permute-start | bytes 442376 | tf_op jit(solution)/shard_map/ppermute | solution.py:528
  13.3 0.8 %collective-permute-done.1.refs_3_ = bf16[64,1152]{1,0:T(8,128)(2,1)S(1)} collective-permute-done((bf16[64,1152]{1,0:T(8,128)(2,1)S(1)}, bf16[64,1152]{1,0:T(8,128)(2,1)S(1)}, u32[]{:S(2)}, u32[]{:S(2)}) %collective-permute-start.1) | collective-permute-done | bytes 147488 | tf_op jit(solution)/shard_map/ppermute | solution.py:528
  14.1 1.5 %fir_earlier_rows.1.refs_0_ = bf16[64,1152]{1,0:T(8,128)(2,1)S(1)} custom-call(bf16[128,1024]{1,0:T(8,128)(2,1)S(1)} %collective-permute-done.rim_ref, f32[1152,128]{1,0:T(8,128)S(1)} %get-tuple-element.38.sums_ref, f32[1152,128]{1,0:T(8,128)S(1)} %get-tuple-element.39.x_high, f32[72,128]{1,0:T(8,128)S(1)} %get-tuple-element.40.last_ref, ...), custom_call_target="tpu_custom_call" | custom-call | bytes 1024 | tf_op jit(solution)/shard_map/fir_earlier_rows/pallas_call | solution.py:303
  15.6 0.2 collective-permute-start.3
  15.8 0.8 %collective-permute-start.2 = (bf16[64,1152]{1,0:T(8,128)(2,1)S(1)}, bf16[64,1152]{1,0:T(8,128)(2,1)S(1)}, u32[]{:S(2)}, u32[]{:S(2)}) collective-permute-start(bf16[64,1152]{1,0:T(8,128)(2,1)S(1)} %fir_earlier_rows.1.refs_0_), channel_id=1, source_target_pairs={{0,2},{1,3},{2,0},{3,1},{4,6},{5,7},{6,4},{7,5},{8,10},{9,11},{10,... | collective-permute-start | bytes 442376 | tf_op jit(solution)/shard_map/ppermute | solution.py:528
  16.5 2.6 %collective-permute-done.4.refs_1_ = bf16[64,1152]{1,0:T(8,128)(2,1)S(1)} collective-permute-done((bf16[64,1152]{1,0:T(8,128)(2,1)S(1)}, bf16[64,1152]{1,0:T(8,128)(2,1)S(1)}, u32[]{:S(2)}, u32[]{:S(2)}) %collective-permute-start.4) | collective-permute-done | bytes 147488 | tf_op jit(solution)/shard_map/ppermute | solution.py:528
  19.2 0.0 collective-permute-start.6
  19.2 0.0 collective-permute-done.3.refs_2_
  19.2 1.0 %projections_near.1 = (f32[128,1536]{1,0:T(8,128)S(1)}, f32[128,128]{1,0:T(8,128)S(1)}) custom-call(bf16[64,1152]{1,0:T(8,128)(2,1)S(1)} %fir_earlier_rows.1.refs_0_, bf16[64,1152]{1,0:T(8,128)(2,1)S(1)} %get-tuple-element.36.refs_1_, bf16[64,1152]{1,0:T(8,128)(2,1)S(1)} %collective-permute-done.3.refs_2_, ...), custom_call_target="tpu_custom_call" | custom-call | bytes 1024 | tf_op jit(solution)/shard_map/projections_near/pallas_call | solution.py:347
  20.1 2.0 %collective-permute-done.2.refs_0_ = bf16[64,1152]{1,0:T(8,128)(2,1)S(1)} collective-permute-done((bf16[64,1152]{1,0:T(8,128)(2,1)S(1)}, bf16[64,1152]{1,0:T(8,128)(2,1)S(1)}, u32[]{:S(2)}, u32[]{:S(2)}) %collective-permute-start.2) | collective-permute-done | bytes 147488 | tf_op jit(solution)/shard_map/ppermute | solution.py:528
  22.1 0.0 collective-permute-start.5
  22.1 0.0 collective-permute-done.6.refs_3_
  22.1 1.4 %collective-permute-done.5.refs_2_ = bf16[64,1152]{1,0:T(8,128)(2,1)S(1)} collective-permute-done((bf16[64,1152]{1,0:T(8,128)(2,1)S(1)}, bf16[64,1152]{1,0:T(8,128)(2,1)S(1)}, u32[]{:S(2)}, u32[]{:S(2)}) %collective-permute-start.5) | collective-permute-done | bytes 147488 | tf_op jit(solution)/shard_map/ppermute | solution.py:528
  23.5 1.1 %projections_far.1 = (bf16[256,128]{1,0:T(8,128)(2,1)S(1)}, bf16[256,128]{1,0:T(8,128)(2,1)S(1)}, bf16[256,128]{1,0:T(8,128)(2,1)S(1)}, bf16[256,128]{1,0:T(8,12...) custom-call(bf16[64,1152]{1,0:T(8,128)(2,1)S(1)} %collective-permute, ...), custom_call_target="tpu_custom_call" | custom-call | bytes 1024 | tf_op jit(solution)/shard_map/projections_far/pallas_call | solution.py:386
  24.6 1.3 %collective-permute-start.10 = (bf16[256,128]{1,0:T(8,128)(2,1)S(1)}, bf16[256,128]{1,0:T(8,128)(2,1)S(1)}, u32[]{:S(2)}, u32[]{:S(2)}) collective-permute-start(bf16[256,128]{1,0:T(8,128)(2,1)S(1)} %get-tuple-element.51), channel_id=1, source_target_pairs={{0,16},{4,20},{8,24},{12,28},{1,17},{5,21},{9,25},{13,29},{2,18},{... | collective-permute-start | bytes 196616 | tf_op jit(solution)/shard_map/ppermute | solution.py:575
  25.9 1.3 %collective-permute-start.11 = (bf16[256,128]{1,0:T(8,128)(2,1)S(1)}, bf16[256,128]{1,0:T(8,128)(2,1)S(1)}, u32[]{:S(2)}, u32[]{:S(2)}) collective-permute-start(bf16[256,128]{1,0:T(8,128)(2,1)S(1)} %get-tuple-element.52), channel_id=1, source_target_pairs={{0,20},{4,16},{8,28},{12,24},{1,21},{5,17},{9,29},{13,25},{2,22},{... | collective-permute-start | bytes 196616 | tf_op jit(solution)/shard_map/ppermute | solution.py:575
  27.2 0.7 %collective-permute-start.7 = (bf16[384,128]{1,0:T(8,128)(2,1)S(1)}, bf16[384,128]{1,0:T(8,128)(2,1)S(1)}, u32[]{:S(2)}, u32[]{:S(2)}) collective-permute-start(bf16[384,128]{1,0:T(8,128)(2,1)S(1)} %get-tuple-element.48), channel_id=1, source_target_pairs={{0,4},{4,0},{8,12},{12,8},{16,20},{20,16},{24,28},{28,24},{1,5},{5... | collective-permute-start | bytes 294920 | tf_op jit(solution)/shard_map/ppermute | solution.py:572
  27.9 1.6 %collective-permute-start.8 = (bf16[384,128]{1,0:T(8,128)(2,1)S(1)}, bf16[384,128]{1,0:T(8,128)(2,1)S(1)}, u32[]{:S(2)}, u32[]{:S(2)}) collective-permute-start(bf16[384,128]{1,0:T(8,128)(2,1)S(1)} %get-tuple-element.49), channel_id=1, source_target_pairs={{0,8},{4,12},{8,0},{12,4},{16,24},{20,28},{24,16},{28,20},{1,9},{5... | collective-permute-start | bytes 294920 | tf_op jit(solution)/shard_map/ppermute | solution.py:572
  29.5 1.3 %collective-permute-start.9 = (bf16[384,128]{1,0:T(8,128)(2,1)S(1)}, bf16[384,128]{1,0:T(8,128)(2,1)S(1)}, u32[]{:S(2)}, u32[]{:S(2)}) collective-permute-start(bf16[384,128]{1,0:T(8,128)(2,1)S(1)} %get-tuple-element.50), channel_id=1, source_target_pairs={{0,12},{4,8},{8,4},{12,0},{16,28},{20,24},{24,20},{28,16},{1,13},{... | collective-permute-start | bytes 294920 | tf_op jit(solution)/shard_map/ppermute | solution.py:572
  30.8 1.1 %collective-permute-done.10.refs_0_ = bf16[256,128]{1,0:T(8,128)(2,1)S(1)} collective-permute-done((bf16[256,128]{1,0:T(8,128)(2,1)S(1)}, bf16[256,128]{1,0:T(8,128)(2,1)S(1)}, u32[]{:S(2)}, u32[]{:S(2)}) %collective-permute-start.10) | collective-permute-done | bytes 65568 | tf_op jit(solution)/shard_map/ppermute | solution.py:575
  31.9 1.3 %collective-permute-start.12 = (bf16[256,128]{1,0:T(8,128)(2,1)S(1)}, bf16[256,128]{1,0:T(8,128)(2,1)S(1)}, u32[]{:S(2)}, u32[]{:S(2)}) collective-permute-start(bf16[256,128]{1,0:T(8,128)(2,1)S(1)} %get-tuple-element.53), channel_id=1, source_target_pairs={{0,24},{4,28},{8,16},{12,20},{1,25},{5,29},{9,17},{13,21},{2,26},{... | collective-permute-start | bytes 196616 | tf_op jit(solution)/shard_map/ppermute | solution.py:575
  33.2 1.3 %collective-permute-done.11.refs_1_ = bf16[256,128]{1,0:T(8,128)(2,1)S(1)} collective-permute-done((bf16[256,128]{1,0:T(8,128)(2,1)S(1)}, bf16[256,128]{1,0:T(8,128)(2,1)S(1)}, u32[]{:S(2)}, u32[]{:S(2)}) %collective-permute-start.11) | collective-permute-done | bytes 65568 | tf_op jit(solution)/shard_map/ppermute | solution.py:575
  34.5 1.3 %collective-permute-start.13 = (bf16[256,128]{1,0:T(8,128)(2,1)S(1)}, bf16[256,128]{1,0:T(8,128)(2,1)S(1)}, u32[]{:S(2)}, u32[]{:S(2)}) collective-permute-start(bf16[256,128]{1,0:T(8,128)(2,1)S(1)} %get-tuple-element.54), channel_id=1, source_target_pairs={{0,28},{4,24},{8,20},{12,16},{1,29},{5,25},{9,21},{13,17},{2,30},{... | collective-permute-start | bytes 196616 | tf_op jit(solution)/shard_map/ppermute | solution.py:575
  35.8 2.4 %collective-permute-done.12.refs_2_ = bf16[256,128]{1,0:T(8,128)(2,1)S(1)} collective-permute-done((bf16[256,128]{1,0:T(8,128)(2,1)S(1)}, bf16[256,128]{1,0:T(8,128)(2,1)S(1)}, u32[]{:S(2)}, u32[]{:S(2)}) %collective-permute-start.12) | collective-permute-done | bytes 65568 | tf_op jit(solution)/shard_map/ppermute | solution.py:575
  38.2 4.6 %collective-permute-done.13.refs_3_ = bf16[256,128]{1,0:T(8,128)(2,1)S(1)} collective-permute-done((bf16[256,128]{1,0:T(8,128)(2,1)S(1)}, bf16[256,128]{1,0:T(8,128)(2,1)S(1)}, u32[]{:S(2)}, u32[]{:S(2)}) %collective-permute-start.13) | collective-permute-done | bytes 65568 | tf_op jit(solution)/shard_map/ppermute | solution.py:575
  42.8 0.0 collective-permute-done.7.refs_1_
  42.8 0.0 collective-permute-done.8.refs_2_
  42.8 0.0 collective-permute-done.9.refs_3_
  42.8 1.6 %attention.1 = (bf16[128,128]{1,0:T(8,128)(2,1)S(1)}, bf16[128,128]{1,0:T(8,128)(2,1)S(1)}, bf16[128,128]{1,0:T(8,128)(2,1)S(1)}, bf16[128,128]{1,0:T(8,128)(2,1)S(1)}) custom-call(bf16[384,128]{1,0:T(8,128)(2,1)S(1)} %get-tuple-element.47.refs_0_, bf16[384,128]{1,0:T(8,128)(2,1)S(1)} %collective-permute-done.7.refs_1_, ...), custom_call_target="tpu_custom_call" | custom-call | bytes 1024 | tf_op jit(solution)/shard_map/attention/pallas_call | solution.py:460
  44.4 0.1 collective-permute-start.14
  44.5 4.8 %collective-permute-start.15 = (bf16[128,128]{1,0:T(8,128)(2,1)S(1)}, bf16[128,128]{1,0:T(8,128)(2,1)S(1)}, u32[]{:S(2)}, u32[]{:S(2)}) collective-permute-start(bf16[128,128]{1,0:T(8,128)(2,1)S(1)} %get-tuple-element.59), channel_id=1, source_target_pairs={{0,8},{4,12},{8,0},{12,4},{16,24},{20,28},{24,16},{28,20},{1,9},{5... | collective-permute-start | bytes 98312 | tf_op jit(solution)/shard_map/ppermute | solution.py:572
  49.3 0.1 collective-permute-start.16
  49.4 0.0 collective-permute-done.14.refs_1_
  49.4 1.8 %collective-permute-done.15.refs_2_ = bf16[128,128]{1,0:T(8,128)(2,1)S(1)} collective-permute-done((bf16[128,128]{1,0:T(8,128)(2,1)S(1)}, bf16[128,128]{1,0:T(8,128)(2,1)S(1)}, u32[]{:S(2)}, u32[]{:S(2)}) %collective-permute-start.15) | collective-permute-done | bytes 32800 | tf_op jit(solution)/shard_map/ppermute | solution.py:572
  51.2 2.9 %collective-permute-done.16.refs_3_ = bf16[128,128]{1,0:T(8,128)(2,1)S(1)} collective-permute-done((bf16[128,128]{1,0:T(8,128)(2,1)S(1)}, bf16[128,128]{1,0:T(8,128)(2,1)S(1)}, u32[]{:S(2)}, u32[]{:S(2)}) %collective-permute-start.16) | collective-permute-done | bytes 32800 | tf_op jit(solution)/shard_map/ppermute | solution.py:572
  54.1 0.7 %join_heads.1 = bf16[128,512]{1,0:T(8,128)(2,1)} custom-call(bf16[128,128]{1,0:T(8,128)(2,1)S(1)} %get-tuple-element.57.refs_0_, bf16[128,128]{1,0:T(8,128)(2,1)S(1)} %collective-permute-done.14.refs_1_, bf16[128,128]{1,0:T(8,128)(2,1)S(1)} %collective-permute-done.15.refs_2_, bf16[128,128]{1,0:T(8,128)(2,1)S(1)} %collective-permute-done.16.refs_3_), custom_call_target="tpu_custom_call" | custom-call | tf_op jit(solution)/shard_map/join_heads/pallas_call | solution.py:481
  (1 shorter events, 0.0 us)
Async XLA Ops:
  0.0 12.0 %copy-start = (f32[1024]{0:T(1024)S(1)}, f32[1024]{0:T(1024)}, u32[]{:S(2)}) copy-start(f32[1024]{0:T(1024)} %param.10) | copy-start | bytes 12292
  1.1 10.8 %collective-permute-start = (bf16[128,1024]{1,0:T(8,128)(2,1)S(1)}, bf16[128,1024]{1,0:T(8,128)(2,1)S(1)}, u32[]{:S(2)}, u32[]{:S(2)}) collective-permute-start(bf16[128,1024]{1,0:T(8,128)(2,1)S(1)} %multiply_convert_fusion.mixed_ref), channel_id=1, source_target_pairs={{0,4},{4,8},{8,12},{12,16},{16,20},{20,24},{24,28},{1,5},{5,9},{9,... | collective-permute-start | bytes 786440 | tf_op jit(solution)/shard_map/ppermute | solution.py:531
  12.6 1.4 %collective-permute-start.1 = (bf16[64,1152]{1,0:T(8,128)(2,1)S(1)}, bf16[64,1152]{1,0:T(8,128)(2,1)S(1)}, u32[]{:S(2)}, u32[]{:S(2)}) collective-permute-start(bf16[64,1152]{1,0:T(8,128)(2,1)S(1)} %get-tuple-element.36.refs_1_), channel_id=1, source_target_pairs={{0,1},{1,0},{2,3},{3,2},{4,5},{5,4},{6,7},{7,6},{8,9},{9,8},{10,11... | collective-permute-start | bytes 442376 | tf_op jit(solution)/shard_map/ppermute | solution.py:528
  12.7 6.4 %collective-permute-start.4 = (bf16[64,1152]{1,0:T(8,128)(2,1)S(1)}, bf16[64,1152]{1,0:T(8,128)(2,1)S(1)}, u32[]{:S(2)}, u32[]{:S(2)}) collective-permute-start(bf16[64,1152]{1,0:T(8,128)(2,1)S(1)} %get-tuple-element.36.refs_1_), channel_id=1, source_target_pairs={{0,2},{1,3},{2,0},{3,1},{4,6},{5,7},{6,4},{7,5},{8,10},{9,11},{10,... | collective-permute-start | bytes 442376 | tf_op jit(solution)/shard_map/ppermute | solution.py:528
  15.6 3.6 %collective-permute-start.3 = (bf16[64,1152]{1,0:T(8,128)(2,1)S(1)}, bf16[64,1152]{1,0:T(8,128)(2,1)S(1)}, u32[]{:S(2)}, u32[]{:S(2)}) collective-permute-start(bf16[64,1152]{1,0:T(8,128)(2,1)S(1)} %fir_earlier_rows.1.refs_0_), channel_id=1, source_target_pairs={{0,1},{1,0},{2,3},{3,2},{4,5},{5,4},{6,7},{7,6},{8,9},{9,8},{10,11... | collective-permute-start | bytes 442376 | tf_op jit(solution)/shard_map/ppermute | solution.py:528
  15.8 6.4 %collective-permute-start.2 = (bf16[64,1152]{1,0:T(8,128)(2,1)S(1)}, bf16[64,1152]{1,0:T(8,128)(2,1)S(1)}, u32[]{:S(2)}, u32[]{:S(2)}) collective-permute-start(bf16[64,1152]{1,0:T(8,128)(2,1)S(1)} %fir_earlier_rows.1.refs_0_), channel_id=1, source_target_pairs={{0,2},{1,3},{2,0},{3,1},{4,6},{5,7},{6,4},{7,5},{8,10},{9,11},{10,... | collective-permute-start | bytes 442376 | tf_op jit(solution)/shard_map/ppermute | solution.py:528
  19.2 3.0 %collective-permute-start.6 = (bf16[64,1152]{1,0:T(8,128)(2,1)S(1)}, bf16[64,1152]{1,0:T(8,128)(2,1)S(1)}, u32[]{:S(2)}, u32[]{:S(2)}) collective-permute-start(bf16[64,1152]{1,0:T(8,128)(2,1)S(1)} %collective-permute-done.4.refs_1_), channel_id=1, source_target_pairs={{0,1},{1,0},{2,3},{3,2},{4,5},{5,4},{6,7},{7,6},{8,9},{9,8},{10,11... | collective-permute-start | bytes 442376 | tf_op jit(solution)/shard_map/ppermute | solution.py:528
  22.1 1.4 %collective-permute-start.5 = (bf16[64,1152]{1,0:T(8,128)(2,1)S(1)}, bf16[64,1152]{1,0:T(8,128)(2,1)S(1)}, u32[]{:S(2)}, u32[]{:S(2)}) collective-permute-start(bf16[64,1152]{1,0:T(8,128)(2,1)S(1)} %collective-permute-done.2.refs_0_), channel_id=1, source_target_pairs={{0,1},{1,0},{2,3},{3,2},{4,5},{5,4},{6,7},{7,6},{8,9},{9,8},{10,11... | collective-permute-start | bytes 442376 | tf_op jit(solution)/shard_map/ppermute | solution.py:528
  24.6 7.3 %collective-permute-start.10 = (bf16[256,128]{1,0:T(8,128)(2,1)S(1)}, bf16[256,128]{1,0:T(8,128)(2,1)S(1)}, u32[]{:S(2)}, u32[]{:S(2)}) collective-permute-start(bf16[256,128]{1,0:T(8,128)(2,1)S(1)} %get-tuple-element.51), channel_id=1, source_target_pairs={{0,16},{4,20},{8,24},{12,28},{1,17},{5,21},{9,25},{13,29},{2,18},{... | collective-permute-start | bytes 196616 | tf_op jit(solution)/shard_map/ppermute | solution.py:575
  25.9 8.6 %collective-permute-start.11 = (bf16[256,128]{1,0:T(8,128)(2,1)S(1)}, bf16[256,128]{1,0:T(8,128)(2,1)S(1)}, u32[]{:S(2)}, u32[]{:S(2)}) collective-permute-start(bf16[256,128]{1,0:T(8,128)(2,1)S(1)} %get-tuple-element.52), channel_id=1, source_target_pairs={{0,20},{4,16},{8,28},{12,24},{1,21},{5,17},{9,29},{13,25},{2,22},{... | collective-permute-start | bytes 196616 | tf_op jit(solution)/shard_map/ppermute | solution.py:575
  27.2 15.6 %collective-permute-start.7 = (bf16[384,128]{1,0:T(8,128)(2,1)S(1)}, bf16[384,128]{1,0:T(8,128)(2,1)S(1)}, u32[]{:S(2)}, u32[]{:S(2)}) collective-permute-start(bf16[384,128]{1,0:T(8,128)(2,1)S(1)} %get-tuple-element.48), channel_id=1, source_target_pairs={{0,4},{4,0},{8,12},{12,8},{16,20},{20,16},{24,28},{28,24},{1,5},{5... | collective-permute-start | bytes 294920 | tf_op jit(solution)/shard_map/ppermute | solution.py:572
  27.9 14.9 %collective-permute-start.8 = (bf16[384,128]{1,0:T(8,128)(2,1)S(1)}, bf16[384,128]{1,0:T(8,128)(2,1)S(1)}, u32[]{:S(2)}, u32[]{:S(2)}) collective-permute-start(bf16[384,128]{1,0:T(8,128)(2,1)S(1)} %get-tuple-element.49), channel_id=1, source_target_pairs={{0,8},{4,12},{8,0},{12,4},{16,24},{20,28},{24,16},{28,20},{1,9},{5... | collective-permute-start | bytes 294920 | tf_op jit(solution)/shard_map/ppermute | solution.py:572
  29.5 13.4 %collective-permute-start.9 = (bf16[384,128]{1,0:T(8,128)(2,1)S(1)}, bf16[384,128]{1,0:T(8,128)(2,1)S(1)}, u32[]{:S(2)}, u32[]{:S(2)}) collective-permute-start(bf16[384,128]{1,0:T(8,128)(2,1)S(1)} %get-tuple-element.50), channel_id=1, source_target_pairs={{0,12},{4,8},{8,4},{12,0},{16,28},{20,24},{24,20},{28,16},{1,13},{... | collective-permute-start | bytes 294920 | tf_op jit(solution)/shard_map/ppermute | solution.py:572
  31.9 6.3 %collective-permute-start.12 = (bf16[256,128]{1,0:T(8,128)(2,1)S(1)}, bf16[256,128]{1,0:T(8,128)(2,1)S(1)}, u32[]{:S(2)}, u32[]{:S(2)}) collective-permute-start(bf16[256,128]{1,0:T(8,128)(2,1)S(1)} %get-tuple-element.53), channel_id=1, source_target_pairs={{0,24},{4,28},{8,16},{12,20},{1,25},{5,29},{9,17},{13,21},{2,26},{... | collective-permute-start | bytes 196616 | tf_op jit(solution)/shard_map/ppermute | solution.py:575
  34.5 8.3 %collective-permute-start.13 = (bf16[256,128]{1,0:T(8,128)(2,1)S(1)}, bf16[256,128]{1,0:T(8,128)(2,1)S(1)}, u32[]{:S(2)}, u32[]{:S(2)}) collective-permute-start(bf16[256,128]{1,0:T(8,128)(2,1)S(1)} %get-tuple-element.54), channel_id=1, source_target_pairs={{0,28},{4,24},{8,20},{12,16},{1,29},{5,25},{9,21},{13,17},{2,30},{... | collective-permute-start | bytes 196616 | tf_op jit(solution)/shard_map/ppermute | solution.py:575
  44.4 5.0 %collective-permute-start.14 = (bf16[128,128]{1,0:T(8,128)(2,1)S(1)}, bf16[128,128]{1,0:T(8,128)(2,1)S(1)}, u32[]{:S(2)}, u32[]{:S(2)}) collective-permute-start(bf16[128,128]{1,0:T(8,128)(2,1)S(1)} %get-tuple-element.58), channel_id=1, source_target_pairs={{0,4},{4,0},{8,12},{12,8},{16,20},{20,16},{24,28},{28,24},{1,5},{5... | collective-permute-start | bytes 98312 | tf_op jit(solution)/shard_map/ppermute | solution.py:572
  44.5 6.7 %collective-permute-start.15 = (bf16[128,128]{1,0:T(8,128)(2,1)S(1)}, bf16[128,128]{1,0:T(8,128)(2,1)S(1)}, u32[]{:S(2)}, u32[]{:S(2)}) collective-permute-start(bf16[128,128]{1,0:T(8,128)(2,1)S(1)} %get-tuple-element.59), channel_id=1, source_target_pairs={{0,8},{4,12},{8,0},{12,4},{16,24},{20,28},{24,16},{28,20},{1,9},{5... | collective-permute-start | bytes 98312 | tf_op jit(solution)/shard_map/ppermute | solution.py:572
  49.3 4.8 %collective-permute-start.16 = (bf16[128,128]{1,0:T(8,128)(2,1)S(1)}, bf16[128,128]{1,0:T(8,128)(2,1)S(1)}, u32[]{:S(2)}, u32[]{:S(2)}) collective-permute-start(bf16[128,128]{1,0:T(8,128)(2,1)S(1)} %get-tuple-element.60), channel_id=1, source_target_pairs={{0,12},{4,8},{8,4},{12,0},{16,28},{20,24},{24,20},{28,16},{1,13},{... | collective-permute-start | bytes 98312 | tf_op jit(solution)/shard_map/ppermute | solution.py:572

commit v5 on v4

--- a/solution.py
+++ b/solution.py
@@ -25,11 +25,8 @@
     return pltpu.CompilerParams(vmem_limit_bytes=mib << 20)
 
 
-LATE = 1 << 28
-
-
-def cost(weight=1024):
-    return pl.CostEstimate(flops=0, bytes_accessed=weight, transcendentals=0)
+def cost():
+    return pl.CostEstimate(flops=0, bytes_accessed=1024, transcendentals=0)
 
 
 def slabs(count):
@@ -358,7 +355,7 @@
     )(*mine[0], *mine[1], weight)
 
 
-def last_kernel(count, model, layout, *refs):
+def last_kernel(count, model, spread, *refs):
     blocks = [(refs[2 * n], refs[2 * n + 1]) for n in range(count)]
     weight_ref, acc_in, ssq_in = refs[2 * count : 2 * count + 3]
     outs, (acc_ref, ssq_ref) = refs[2 * count + 3 : -2], refs[-2:]
@@ -370,26 +367,24 @@
     rows = acc_ref.shape[0]
     width = weight_ref.shape[2]
     heads = width // HEAD_DIM
-    place = lax.axis_index("ctx") % heads
-    kept = {}
-    for out, parts in zip(outs, layout):
-        for spot, (which, k) in enumerate(parts):
-            if (which, k) not in kept:
-                head = jnp.bitwise_xor(place, k)
-                lanes = pl.ds(pl.multiple_of(which * width + head * HEAD_DIM, LANES), HEAD_DIM)
-                kept[which, k] = (acc_ref[:, lanes] * scale).astype(BF16)
-            out[spot * rows : (spot + 1) * rows, :] = kept[which, k]
-
-
-def last_projection(others, weight, acc, ssq, model, layout):
+    place = lax.axis_index("ctx") // 2 if spread else 0
+    for n, out in enumerate(outs):
+        head = jnp.bitwise_xor(place, heads - 1 - n)
+        for which in range(3):
+            lanes = pl.ds(pl.multiple_of(which * width + head * HEAD_DIM, LANES), HEAD_DIM)
+            out[which * rows : (which + 1) * rows, :] = (acc_ref[:, lanes] * scale).astype(BF16)
+
+
+def last_projection(others, weight, acc, ssq, model, spread):
     rows = acc.shape[0]
-    return pl.pallas_call(
-        functools.partial(last_kernel, len(others), model, layout),
+    heads = weight.shape[2] // HEAD_DIM
+    return pl.pallas_call(
+        functools.partial(last_kernel, len(others), model, spread),
         out_shape=tuple(
-            jax.ShapeDtypeStruct((len(parts) * rows, HEAD_DIM), BF16) for parts in layout
+            jax.ShapeDtypeStruct((3 * rows, HEAD_DIM), BF16) for _ in range(heads)
         ),
         in_specs=[VMEM] * (2 * len(others) + 3),
-        out_specs=(VMEM,) * len(layout),
+        out_specs=(VMEM,) * heads,
         scratch_shapes=[pltpu.VMEM(acc.shape, F32), pltpu.VMEM(ssq.shape, F32)],
         compiler_params=params(24),
         cost_estimate=cost(),
@@ -397,82 +392,78 @@
     )(*[half for pair in others for half in pair], weight, acc, ssq)
 
 
-def earlier_kernel(*refs):
-    blocks, (key_ref, value_ref) = refs[:-2], refs[-2:]
-    rows = blocks[0].shape[0] // 2
+def pack_kernel(*refs):
+    blocks, out = refs[:-1], refs[-1]
+    rows = blocks[0].shape[0] // 3
+    half = len(blocks) * rows
     for k, block in enumerate(blocks):
-        key_ref[k * rows : (k + 1) * rows, :] = block[:rows, :]
-        value_ref[k * rows : (k + 1) * rows, :] = block[rows:, :]
-
-
-def earlier_group(blocks):
-    shape = jax.ShapeDtypeStruct((blocks[0].shape[0] // 2 * len(blocks), HEAD_DIM), BF16)
-    return pl.pallas_call(
-        earlier_kernel,
-        out_shape=(shape, shape),
+        out[k * rows : (k + 1) * rows, :] = block[rows : 2 * rows, :]
+        out[half + k * rows : half + (k + 1) * rows, :] = block[2 * rows :, :]
+
+
+def packed(blocks):
+    rows = blocks[0].shape[0] // 3
+    return pl.pallas_call(
+        pack_kernel,
+        out_shape=jax.ShapeDtypeStruct((2 * len(blocks) * rows, HEAD_DIM), BF16),
         in_specs=[VMEM] * len(blocks),
-        out_specs=(VMEM, VMEM),
+        out_specs=VMEM,
         compiler_params=params(4),
-        cost_estimate=cost(LATE),
-        name="earlier_keys",
+        cost_estimate=cost(),
+        name="pack_keys",
     )(*blocks)
 
 
-def attend_kernel(rows, count, *refs):
-    mine, (old_keys, old_values), outs = refs[:count], refs[count : count + 2], refs[count + 2 : -2]
-    key_ref, value_ref = refs[-2:]
-    place = lax.axis_index("ctx")
-    group, p = place // count, place % count
-    key_ref[: count * rows, :] = old_keys[...]
-    value_ref[: count * rows, :] = old_values[...]
-    for k in range(count):
-        spot = slice((count + k) * rows, (count + k + 1) * rows)
-        key_ref[spot, :] = mine[k][rows : 2 * rows, :]
-        value_ref[spot, :] = mine[k][2 * rows : 3 * rows, :]
-    column = lax.broadcasted_iota(jnp.int32, (1, 2 * count * rows), 1)
-    block = jnp.bitwise_xor(column // rows % count, p)
-    first = jnp.where(column < count * rows, jnp.where(group > 0, 0, 2 * count), group * count)
-    key_pos = (first + block) * rows + column % rows
+def attend_kernel(count, *refs):
+    blocks, sides, outs = refs[:count], refs[count : count + 2], refs[count + 2 :]
+    rows = outs[0].shape[0]
+    half = count * rows
+    z, c = lax.axis_index("ctx") // 2, lax.axis_index("tp") % 2
+    column = lax.broadcasted_iota(jnp.int32, (1, half), 1)
+    even = 2 * jnp.bitwise_xor(column // rows, z) * rows + column % rows
     scale = 1.0 / math.sqrt(HEAD_DIM)
-    for k in range(count):
-        start = (group * count + jnp.bitwise_xor(p, k)) * rows
+    for n, block in enumerate(blocks):
+        k = count - 1 - n
+        start = (2 * jnp.bitwise_xor(z, k) + c) * rows
         query_pos = start + lax.broadcasted_iota(jnp.int32, (rows, 1), 0)
-        scores = (
-            lax.dot_general(
-                mine[k][:rows, :],
-                key_ref[...],
+        scores = []
+        for side, core in zip(sides, (c, 1 - c)):
+            product = lax.dot_general(
+                block[:rows, :],
+                side[:half, :],
                 (((1,), (1,)), ((), ())),
                 preferred_element_type=F32,
             )
-            * scale
+            allowed = query_pos >= even + core * rows
+            scores.append(jnp.where(allowed, product * scale, -1e30))
+        top = jnp.maximum(*(jnp.max(part, axis=1, keepdims=True) for part in scores))
+        expo = [jnp.exp(part - top) for part in scores]
+        total = sum(jnp.sum(part, axis=1, keepdims=True) for part in expo)
+        summed = sum(
+            jnp.dot(part.astype(BF16), side[half:, :], preferred_element_type=F32)
+            for part, side in zip(expo, sides)
         )
-        scores = jnp.where(query_pos >= key_pos, scores, -1e30)
-        top = jnp.max(scores, axis=1, keepdims=True)
-        expo = jnp.exp(scores - top)
-        total = jnp.sum(expo, axis=1, keepdims=True)
-        summed = jnp.dot(expo.astype(BF16), value_ref[...], preferred_element_type=F32)
-        outs[k][...] = (summed / total).astype(BF16)
-
-
-def attend(mine, earlier):
-    count = len(mine)
-    rows = mine[0].shape[0] // 3
-    return pl.pallas_call(
-        functools.partial(attend_kernel, rows, count),
+        outs[n][...] = (summed / total).astype(BF16)
+
+
+def attend(blocks, mine, theirs):
+    count = len(blocks)
+    rows = blocks[0].shape[0] // 3
+    return pl.pallas_call(
+        functools.partial(attend_kernel, count),
         out_shape=tuple(jax.ShapeDtypeStruct((rows, HEAD_DIM), BF16) for _ in range(count)),
         in_specs=[VMEM] * (count + 2),
         out_specs=(VMEM,) * count,
-        scratch_shapes=[pltpu.VMEM((2 * count * rows, HEAD_DIM), BF16)] * 2,
         compiler_params=params(24),
         cost_estimate=cost(),
         name="attention",
-    )(*mine, *earlier)
+    )(*blocks, mine, theirs)
 
 
 def join_kernel(*refs):
     blocks, out = refs[:-1], refs[-1]
-    for k, block in enumerate(blocks):
-        head = jnp.bitwise_xor(lax.axis_index("ctx") % len(blocks), k)
+    for n, block in enumerate(blocks):
+        head = jnp.bitwise_xor(lax.axis_index("ctx") // 2, len(blocks) - 1 - n)
         out[:, pl.ds(pl.multiple_of(head * HEAD_DIM, LANES), HEAD_DIM)] = block[...]
 
 
@@ -484,15 +475,14 @@
         in_specs=[VMEM] * len(blocks),
         out_specs=VMEM,
         compiler_params=params(4),
+        cost_estimate=cost(),
         name="join_heads",
     )(*blocks)
 
 
 def gathered_attention(message, heads, rows):
-    order = jnp.bitwise_xor(lax.axis_index("ctx") % heads, jnp.arange(heads))
-    query, keys, values = (
-        m.reshape(heads, rows, HEAD_DIM)[order].transpose(1, 0, 2) for m in message
-    )
+    parts = jnp.stack([m.reshape(3, rows, HEAD_DIM) for m in message], axis=2)
+    query, keys, values = parts[0], parts[1], parts[2]
     keys = lax.all_gather(keys, "ctx", axis=0, tiled=True)
     values = lax.all_gather(values, "ctx", axis=0, tiled=True)
     query_pos = lax.axis_index("ctx") * rows + jnp.arange(rows, dtype=jnp.int32)
@@ -512,7 +502,7 @@
     weight = jnp.transpose(qkv_weight, (1, 0, 2))
     heads = weight.shape[2] // HEAD_DIM
     model = weight.shape[1]
-    two_groups = heads == 4 and ctx == 2 * heads
+    chip_per_head = heads * 2 == ctx and heads & (heads - 1) == 0
 
     wide = SLAB * LANES
 
@@ -555,29 +545,25 @@
     others = []
     for o, pair in sorted(zip(places, pairs), key=lambda item: item[0]):
         others += [pair, tuple(swapped(part, 1) for part in pair)]
-
-    def parts(first, *which):
-        return tuple((w, k) for k in which for w in range(first, 3))
-
-    if not two_groups:
-        layout = tuple(tuple((w, k) for k in range(heads)) for w in range(3))
-        return gathered_attention(
-            last_projection(others, weight, acc, ssq, model, layout), heads, rows
-        )
-    layout = tuple(parts(first, k) for first in (1, 0) for k in range(heads))
-    sent = last_projection(others, weight, acc, ssq, model, layout)
-    onward, inside = sent[:heads], sent[heads:]
-
-    def within(value, k):
-        return lax.ppermute(value, "ctx", [(i, i ^ k) for i in range(ctx)]) if k else value
-
-    earlier = [
-        lax.ppermute(onward[k], "ctx", [(i, heads + (i ^ k)) for i in range(heads)])
-        for k in range(heads)
-    ]
-    held = [within(inside[k], k) for k in range(heads)]
-    done = attend(held, earlier_group(earlier))
-    return join([within(done[k], k) for k in range(heads - 1, -1, -1)][::-1])
+    messages = last_projection(others, weight, acc, ssq, model, chip_per_head)
+    if not chip_per_head:
+        return gathered_attention(messages[::-1], heads, rows)
+
+    def routed(value, k):
+        pairs = []
+        for z in range(ctx // 2):
+            for y in range(2):
+                for x in range(tp // 2):
+                    for c in range(2):
+                        source = (2 * z + y) * tp + 2 * x + c
+                        pairs.append((source, (2 * (z ^ k) + c) * tp + 2 * x + y))
+        return lax.ppermute(value, ("ctx", "tp"), pairs)
+
+    order = range(heads - 1, -1, -1)
+    held = [routed(value, k) for value, k in zip(messages, order)]
+    mine = packed(held[::-1])
+    done = attend(held, mine, swapped(mine, 1))
+    return join([routed(value, k) for value, k in zip(done, order)])
 
 
 def solution(mesh):

time: 55 us -> 53.1 us (0.965)
  the two profiles are of different devices: /device:TPU:18 before, /device:TPU:1 now
where the time goes in v5:
time: 53.1 us; the launch traced here: 52.9 us
  starting transfers between devices  28.3 us (53%)
  waiting for transfers between devices  11.9 us (22%)
  Pallas kernels  11.4 us (21%)
  other arithmetic  1.11 us (2%)
    ppermute x8, starting transfers between devices, routed(): return lax.ppermute(value, ('ctx', 'tp'), pairs)  17.4 us
    ppermute x8, waiting for transfers between devices, routed(): return lax.ppermute(value, ('ctx', 'tp'), pairs)  7.21 us
    ppermute x7, starting transfers between devices, swapped(): return lax.ppermute(value, 'tp', [(i, i ^ by) for i in range(tp)])  6.89 us
    pallas_call x1, Pallas kernels, own_part(): pl.pallas_call(own_kernel, out_shape=(slabs(SUBS * eighth), slabs(SUBS *...  4.96 us
    ppermute x7, waiting for transfers between devices, swapped(): return lax.ppermute(value, 'tp', [(i, i ^ by) for i in range(tp)])  4.71 us
    ppermute x1, starting transfers between devices, body(): lax.ppermute(mixed, 'ctx', [(i, i + 1) for i in range(ctx - 1)])  3.99 us
    pallas_call x1, Pallas kernels, attend(): pl.pallas_call(functools.partial(attend_kernel, count), out_shape=tuple((...  1.55 us
    pallas_call x1, Pallas kernels, low_part(): pl.pallas_call(low_kernel, out_shape=jax.ShapeDtypeStruct((rows, (SLAB +...  1.49 us
  transfers between devices with their start and end apart: 16, of which 7 were waited for; matrix products, arithmetic and copies ran while one was open for 0% of the time, Pallas kernels for 14%

profile of v5, /device:TPU:1, one launch (start us, length us, event | category | flops | bytes accessed | tf_op | source)
XLA Modules:
  0.0 52.9 jit_solution(10135600786615439617)
XLA Ops:
  0.0 0.0 copy-start
  0.0 1.1 %multiply_convert_fusion.mixed_ref = bf16[128,1024]{1,0:T(8,128)(2,1)S(1)} fusion(bf16[128,1024]{1,0:T(8,128)(2,1)} %param.8, bf16[128,1024]{1,0:T(8,128)(2,1)} %param.7), kind=kLoop, calls=%fused_computation | loop fusion | flops 524288 | bytes 786432 | tf_op jit(solution)/shard_map/convert_element_type | solution.py:520
  1.1 4.0 %collective-permute-start = (bf16[128,1024]{1,0:T(8,128)(2,1)S(1)}, bf16[128,1024]{1,0:T(8,128)(2,1)S(1)}, u32[]{:S(2)}, u32[]{:S(2)}) collective-permute-start(bf16[128,1024]{1,0:T(8,128)(2,1)S(1)} %multiply_convert_fusion.mixed_ref), channel_id=1, source_target_pairs={{0,4},{4,8},{8,12},{12,16},{16,20},{20,24},{24,28},{1,5},{5,9},{9,... | collective-permute-start | bytes 786440 | tf_op jit(solution)/shard_map/ppermute | solution.py:521
  5.1 5.0 %fir_own_rows.1 = (f32[1152,128]{1,0:T(8,128)S(1)}, f32[1224,128]{1,0:T(8,128)S(1)}, f32[2304,128]{1,0:T(8,128)S(1)}, bf16[128,1024]{1,0:T(8,128)(2,1)S(1)}, bf16[3,4096,512]{2,1,0:T(8,128)(2,1)S(1)}) custom-call(bf16[128,1024]{1,0:T(8,128)(2,1)S(1)} %multiply_convert_fusion.mixed_ref, f32[128,1024]{1,0:T(8,128)} %taps_hbm.1, bf16[128,1024]{1,0:T(8,128)(2,1)} %gate_hbm.1, ...), custom_call_target="tpu_custom_call" | custom-call | bytes 1024 | tf_op jit(solution)/shard_map/fir_own_rows/pallas_call | solution.py:194
  10.1 0.0 collective-permute-done.rim_ref
  10.1 0.0 copy-done
  10.1 0.7 %fir_later_rows.1 = (bf16[64,1152]{1,0:T(8,128)(2,1)S(1)}, f32[1152,128]{1,0:T(8,128)S(1)}, f32[72,128]{1,0:T(8,128)S(1)}) custom-call(bf16[128,1024]{1,0:T(8,128)(2,1)S(1)} %collective-permute-done.rim_ref, f32[1224,128]{1,0:T(8,128)S(1)} %get-tuple-element.27.sums_ref, f32[2304,128]{1,0:T(8,128)S(1)} %get-tuple-element.28.tap_subs, ...), custom_call_target="tpu_custom_call" | custom-call | bytes 1024 | tf_op jit(solution)/shard_map/fir_later_rows/pallas_call | solution.py:246
  10.8 1.6 %collective-permute-start.1 = (bf16[64,1152]{1,0:T(8,128)(2,1)S(1)}, bf16[64,1152]{1,0:T(8,128)(2,1)S(1)}, u32[]{:S(2)}, u32[]{:S(2)}) collective-permute-start(bf16[64,1152]{1,0:T(8,128)(2,1)S(1)} %get-tuple-element.30.refs_1_), channel_id=1, source_target_pairs={{0,1},{1,0},{2,3},{3,2},{4,5},{5,4},{6,7},{7,6},{8,9},{9,8},{10,11... | collective-permute-start | bytes 442376 | tf_op jit(solution)/shard_map/ppermute | solution.py:518
  12.3 1.2 %collective-permute-start.4 = (bf16[64,1152]{1,0:T(8,128)(2,1)S(1)}, bf16[64,1152]{1,0:T(8,128)(2,1)S(1)}, u32[]{:S(2)}, u32[]{:S(2)}) collective-permute-start(bf16[64,1152]{1,0:T(8,128)(2,1)S(1)} %get-tuple-element.30.refs_1_), channel_id=1, source_target_pairs={{0,2},{1,3},{2,0},{3,1},{4,6},{5,7},{6,4},{7,5},{8,10},{9,11},{10,... | collective-permute-start | bytes 442376 | tf_op jit(solution)/shard_map/ppermute | solution.py:518
  13.6 0.0 collective-permute-done.1.refs_3_
  13.6 1.5 %fir_earlier_rows.1.refs_0_ = bf16[64,1152]{1,0:T(8,128)(2,1)S(1)} custom-call(bf16[128,1024]{1,0:T(8,128)(2,1)S(1)} %collective-permute-done.rim_ref, f32[1152,128]{1,0:T(8,128)S(1)} %get-tuple-element.32.sums_ref, f32[1152,128]{1,0:T(8,128)S(1)} %get-tuple-element.33.x_high, f32[72,128]{1,0:T(8,128)S(1)} %get-tuple-element.34.last_ref, ...), custom_call_target="tpu_custom_call" | custom-call | bytes 1024 | tf_op jit(solution)/shard_map/fir_earlier_rows/pallas_call | solution.py:300
  15.1 0.4 collective-permute-start.3
  15.5 1.0 %collective-permute-start.2 = (bf16[64,1152]{1,0:T(8,128)(2,1)S(1)}, bf16[64,1152]{1,0:T(8,128)(2,1)S(1)}, u32[]{:S(2)}, u32[]{:S(2)}) collective-permute-start(bf16[64,1152]{1,0:T(8,128)(2,1)S(1)} %fir_earlier_rows.1.refs_0_), channel_id=1, source_target_pairs={{0,2},{1,3},{2,0},{3,1},{4,6},{5,7},{6,4},{7,5},{8,10},{9,11},{10,... | collective-permute-start | bytes 442376 | tf_op jit(solution)/shard_map/ppermute | solution.py:518
  16.5 1.3 %collective-permute-done.4.refs_1_ = bf16[64,1152]{1,0:T(8,128)(2,1)S(1)} collective-permute-done((bf16[64,1152]{1,0:T(8,128)(2,1)S(1)}, bf16[64,1152]{1,0:T(8,128)(2,1)S(1)}, u32[]{:S(2)}, u32[]{:S(2)}) %collective-permute-start.4) | collective-permute-done | bytes 147488 | tf_op jit(solution)/shard_map/ppermute | solution.py:518
  17.8 0.8 %collective-permute-start.6 = (bf16[64,1152]{1,0:T(8,128)(2,1)S(1)}, bf16[64,1152]{1,0:T(8,128)(2,1)S(1)}, u32[]{:S(2)}, u32[]{:S(2)}) collective-permute-start(bf16[64,1152]{1,0:T(8,128)(2,1)S(1)} %collective-permute-done.4.refs_1_), channel_id=1, source_target_pairs={{0,1},{1,0},{2,3},{3,2},{4,5},{5,4},{6,7},{7,6},{8,9},{9,8},{10,11... | collective-permute-start | bytes 442376 | tf_op jit(solution)/shard_map/ppermute | solution.py:518
  18.6 0.0 collective-permute-done.3.refs_2_
  18.6 1.0 %projections_near.1 = (f32[128,1536]{1,0:T(8,128)S(1)}, f32[128,128]{1,0:T(8,128)S(1)}) custom-call(bf16[64,1152]{1,0:T(8,128)(2,1)S(1)} %fir_earlier_rows.1.refs_0_, bf16[64,1152]{1,0:T(8,128)(2,1)S(1)} %get-tuple-element.30.refs_1_, bf16[64,1152]{1,0:T(8,128)(2,1)S(1)} %collective-permute-done.3.refs_2_, ...), custom_call_target="tpu_custom_call" | custom-call | bytes 1024 | tf_op jit(solution)/shard_map/projections_near/pallas_call | solution.py:344
  19.6 1.2 %collective-permute-done.2.refs_0_ = bf16[64,1152]{1,0:T(8,128)(2,1)S(1)} collective-permute-done((bf16[64,1152]{1,0:T(8,128)(2,1)S(1)}, bf16[64,1152]{1,0:T(8,128)(2,1)S(1)}, u32[]{:S(2)}, u32[]{:S(2)}) %collective-permute-start.2) | collective-permute-done | bytes 147488 | tf_op jit(solution)/shard_map/ppermute | solution.py:518
  20.9 0.9 %collective-permute-start.5 = (bf16[64,1152]{1,0:T(8,128)(2,1)S(1)}, bf16[64,1152]{1,0:T(8,128)(2,1)S(1)}, u32[]{:S(2)}, u32[]{:S(2)}) collective-permute-start(bf16[64,1152]{1,0:T(8,128)(2,1)S(1)} %collective-permute-done.2.refs_0_), channel_id=1, source_target_pairs={{0,1},{1,0},{2,3},{3,2},{4,5},{5,4},{6,7},{7,6},{8,9},{9,8},{10,11... | collective-permute-start | bytes 442376 | tf_op jit(solution)/shard_map/ppermute | solution.py:518
  21.8 0.0 collective-permute-done.6.refs_3_
  21.8 1.0 %collective-permute-done.5.refs_2_ = bf16[64,1152]{1,0:T(8,128)(2,1)S(1)} collective-permute-done((bf16[64,1152]{1,0:T(8,128)(2,1)S(1)}, bf16[64,1152]{1,0:T(8,128)(2,1)S(1)}, u32[]{:S(2)}, u32[]{:S(2)}) %collective-permute-start.5) | collective-permute-done | bytes 147488 | tf_op jit(solution)/shard_map/ppermute | solution.py:518
  22.8 1.1 %projections_far.1 = (bf16[384,128]{1,0:T(8,128)(2,1)S(1)}, bf16[384,128]{1,0:T(8,128)(2,1)S(1)}, bf16[384,128]{1,0:T(8,128)(2,1)S(1)}, bf16[384,128]{1,0:T(8,128)(2,1)S(1)}) custom-call(bf16[64,1152]{1,0:T(8,128)(2,1)S(1)} %collective-permute-done.2.refs_0_, bf16[64,1152]{1,0:T(8,128)(2,1)S(1)} %collective-permute-done.4.refs_1_, ...), custom_call_target="tpu_custom_call" | custom-call | bytes 1024 | tf_op jit(solution)/shard_map/projections_far/pallas_call | solution.py:381
  23.9 5.6 %collective-permute-start.7 = (bf16[384,128]{1,0:T(8,128)(2,1)S(1)}, bf16[384,128]{1,0:T(8,128)(2,1)S(1)}, u32[]{:S(2)}, u32[]{:S(2)}) collective-permute-start(bf16[384,128]{1,0:T(8,128)(2,1)S(1)} %get-tuple-element.41), channel_id=1, source_target_pairs={{0,24},{1,28},{2,26},{3,30},{4,25},{5,29},{6,27},{7,31},{8,16},{9,... | collective-permute-start | bytes 294920 | tf_op jit(solution)/shard_map/ppermute | solution.py:560
  29.4 0.0 collective-permute-start.8
  29.5 1.4 %collective-permute-start.9 = (bf16[384,128]{1,0:T(8,128)(2,1)S(1)}, bf16[384,128]{1,0:T(8,128)(2,1)S(1)}, u32[]{:S(2)}, u32[]{:S(2)}) collective-permute-start(bf16[384,128]{1,0:T(8,128)(2,1)S(1)} %get-tuple-element.43), channel_id=1, source_target_pairs={{0,8},{1,12},{2,10},{3,14},{4,9},{5,13},{6,11},{7,15},{8,0},{9,4},... | collective-permute-start | bytes 294920 | tf_op jit(solution)/shard_map/ppermute | solution.py:560
  30.8 2.3 %collective-permute-start.10 = (bf16[384,128]{1,0:T(8,128)(2,1)S(1)}, bf16[384,128]{1,0:T(8,128)(2,1)S(1)}, u32[]{:S(2)}, u32[]{:S(2)}) collective-permute-start(bf16[384,128]{1,0:T(8,128)(2,1)S(1)} %get-tuple-element.44), channel_id=1, source_target_pairs={{0,0},{1,4},{2,2},{3,6},{4,1},{5,5},{6,3},{7,7},{8,8},{9,12},{10,1... | collective-permute-start | bytes 294920 | tf_op jit(solution)/shard_map/ppermute | solution.py:560
  33.2 0.0 collective-permute-done.7.refs_3_.refs_0_
  33.2 4.6 %collective-permute-done.8.refs_2_.refs_1_ = bf16[384,128]{1,0:T(8,128)(2,1)S(1)} collective-permute-done((bf16[384,128]{1,0:T(8,128)(2,1)S(1)}, bf16[384,128]{1,0:T(8,128)(2,1)S(1)}, u32[]{:S(2)}, u32[]{:S(2)}) %collective-permute-start.8) | collective-permute-done | bytes 98336 | tf_op jit(solution)/shard_map/ppermute | solution.py:560
  37.8 0.0 collective-permute-done.9.refs_1_.refs_2_
  37.8 0.0 collective-permute-done.10.refs_0_.refs_3_
  37.9 0.9 %collective-permute-start.11 = (bf16[1024,128]{1,0:T(8,128)(2,1)S(1)}, bf16[1024,128]{1,0:T(8,128)(2,1)S(1)}, u32[]{:S(2)}, u32[]{:S(2)}) collective-permute-start(bf16[1024,128]{1,0:T(8,128)(2,1)S(1)} %pack_keys.1.refs_4_), channel_id=1, source_target_pairs={{0,1},{1,0},{2,3},{3,2},{4,5},{5,4},{6,7},{7,6},{8,9},{9,8},{10,11... | collective-permute-start | bytes 786440 | tf_op jit(solution)/shard_map/ppermute | solution.py:518
  38.8 1.2 %collective-permute-done.11.refs_5_ = bf16[1024,128]{1,0:T(8,128)(2,1)S(1)} collective-permute-done((bf16[1024,128]{1,0:T(8,128)(2,1)S(1)}, bf16[1024,128]{1,0:T(8,128)(2,1)S(1)}, u32[]{:S(2)}, u32[]{:S(2)}) %collective-permute-start.11) | collective-permute-done | bytes 262176 | tf_op jit(solution)/shard_map/ppermute | solution.py:518
  39.9 1.6 %attention.1 = (bf16[128,128]{1,0:T(8,128)(2,1)S(1)}, bf16[128,128]{1,0:T(8,128)(2,1)S(1)}, bf16[128,128]{1,0:T(8,128)(2,1)S(1)}, bf16[128,128]{1,0:T(8,128)(2,1)S(1)}) custom-call(bf16[384,128]{1,0:T(8,128)(2,1)S(1)} %collective-permute-done.7.refs_3_.refs_0_, bf16[384,128]{1,0:T(8,128)(2,1)S(1)} %collective-permute-done.8.refs_2_.refs_1_, ...), custom_call_target="tpu_custom_call" | custom-call | bytes 1024 | tf_op jit(solution)/shard_map/attention/pallas_call | solution.py:452
  41.5 3.4 %collective-permute-start.12 = (bf16[128,128]{1,0:T(8,128)(2,1)S(1)}, bf16[128,128]{1,0:T(8,128)(2,1)S(1)}, u32[]{:S(2)}, u32[]{:S(2)}) collective-permute-start(bf16[128,128]{1,0:T(8,128)(2,1)S(1)} %get-tuple-element.45), channel_id=1, source_target_pairs={{0,24},{1,28},{2,26},{3,30},{4,25},{5,29},{6,27},{7,31},{8,16},{9,... | collective-permute-start | bytes 98312 | tf_op jit(solution)/shard_map/ppermute | solution.py:560
  44.9 0.0 collective-permute-start.13
  44.9 2.1 %collective-permute-start.14 = (bf16[128,128]{1,0:T(8,128)(2,1)S(1)}, bf16[128,128]{1,0:T(8,128)(2,1)S(1)}, u32[]{:S(2)}, u32[]{:S(2)}) collective-permute-start(bf16[128,128]{1,0:T(8,128)(2,1)S(1)} %get-tuple-element.47), channel_id=1, source_target_pairs={{0,8},{1,12},{2,10},{3,14},{4,9},{5,13},{6,11},{7,15},{8,0},{9,4},... | collective-permute-start | bytes 98312 | tf_op jit(solution)/shard_map/ppermute | solution.py:560
  47.0 2.6 %collective-permute-start.15 = (bf16[128,128]{1,0:T(8,128)(2,1)S(1)}, bf16[128,128]{1,0:T(8,128)(2,1)S(1)}, u32[]{:S(2)}, u32[]{:S(2)}) collective-permute-start(bf16[128,128]{1,0:T(8,128)(2,1)S(1)} %get-tuple-element.48), channel_id=1, source_target_pairs={{0,0},{1,4},{2,2},{3,6},{4,1},{5,5},{6,3},{7,7},{8,8},{9,12},{10,1... | collective-permute-start | bytes 98312 | tf_op jit(solution)/shard_map/ppermute | solution.py:560
  49.6 0.0 collective-permute-done.12.refs_0_
  49.7 0.3 collective-permute-done.13.refs_1_
  50.0 0.0 collective-permute-done.14.refs_2_
  50.0 2.2 %collective-permute-done.15.refs_3_ = bf16[128,128]{1,0:T(8,128)(2,1)S(1)} collective-permute-done((bf16[128,128]{1,0:T(8,128)(2,1)S(1)}, bf16[128,128]{1,0:T(8,128)(2,1)S(1)}, u32[]{:S(2)}, u32[]{:S(2)}) %collective-permute-start.15) | collective-permute-done | bytes 32800 | tf_op jit(solution)/shard_map/ppermute | solution.py:560
  52.2 0.7 %join_heads.1 = bf16[128,512]{1,0:T(8,128)(2,1)} custom-call(bf16[128,128]{1,0:T(8,128)(2,1)S(1)} %collective-permute-done.12.refs_0_, bf16[128,128]{1,0:T(8,128)(2,1)S(1)} %collective-permute-done.13.refs_1_, bf16[128,128]{1,0:T(8,128)(2,1)S(1)} %collective-permute-done.14.refs_2_, bf16[128,128]{1,0:T(8,128)(2,1)S(1)} %collective-permute-done.15.refs_3_), custom_call_target="tpu_custom_call" | custom-call | bytes 1024 | tf_op jit(solution)/shard_map/join_heads/pallas_call | solution.py:472
  (1 shorter events, 0.0 us)
Async XLA Ops:
  0.0 10.1 %copy-start = (f32[1024]{0:T(1024)S(1)}, f32[1024]{0:T(1024)}, u32[]{:S(2)}) copy-start(f32[1024]{0:T(1024)} %param.10) | copy-start | bytes 12292
  1.1 9.0 %collective-permute-start = (bf16[128,1024]{1,0:T(8,128)(2,1)S(1)}, bf16[128,1024]{1,0:T(8,128)(2,1)S(1)}, u32[]{:S(2)}, u32[]{:S(2)}) collective-permute-start(bf16[128,1024]{1,0:T(8,128)(2,1)S(1)} %multiply_convert_fusion.mixed_ref), channel_id=1, source_target_pairs={{0,4},{4,8},{8,12},{12,16},{16,20},{20,24},{24,28},{1,5},{5,9},{9,... | collective-permute-start | bytes 786440 | tf_op jit(solution)/shard_map/ppermute | solution.py:521
  10.8 2.8 %collective-permute-start.1 = (bf16[64,1152]{1,0:T(8,128)(2,1)S(1)}, bf16[64,1152]{1,0:T(8,128)(2,1)S(1)}, u32[]{:S(2)}, u32[]{:S(2)}) collective-permute-start(bf16[64,1152]{1,0:T(8,128)(2,1)S(1)} %get-tuple-element.30.refs_1_), channel_id=1, source_target_pairs={{0,1},{1,0},{2,3},{3,2},{4,5},{5,4},{6,7},{7,6},{8,9},{9,8},{10,11... | collective-permute-start | bytes 442376 | tf_op jit(solution)/shard_map/ppermute | solution.py:518
  12.3 5.4 %collective-permute-start.4 = (bf16[64,1152]{1,0:T(8,128)(2,1)S(1)}, bf16[64,1152]{1,0:T(8,128)(2,1)S(1)}, u32[]{:S(2)}, u32[]{:S(2)}) collective-permute-start(bf16[64,1152]{1,0:T(8,128)(2,1)S(1)} %get-tuple-element.30.refs_1_), channel_id=1, source_target_pairs={{0,2},{1,3},{2,0},{3,1},{4,6},{5,7},{6,4},{7,5},{8,10},{9,11},{10,... | collective-permute-start | bytes 442376 | tf_op jit(solution)/shard_map/ppermute | solution.py:518
  15.1 3.6 %collective-permute-start.3 = (bf16[64,1152]{1,0:T(8,128)(2,1)S(1)}, bf16[64,1152]{1,0:T(8,128)(2,1)S(1)}, u32[]{:S(2)}, u32[]{:S(2)}) collective-permute-start(bf16[64,1152]{1,0:T(8,128)(2,1)S(1)} %fir_earlier_rows.1.refs_0_), channel_id=1, source_target_pairs={{0,1},{1,0},{2,3},{3,2},{4,5},{5,4},{6,7},{7,6},{8,9},{9,8},{10,11... | collective-permute-start | bytes 442376 | tf_op jit(solution)/shard_map/ppermute | solution.py:518
  15.5 5.4 %collective-permute-start.2 = (bf16[64,1152]{1,0:T(8,128)(2,1)S(1)}, bf16[64,1152]{1,0:T(8,128)(2,1)S(1)}, u32[]{:S(2)}, u32[]{:S(2)}) collective-permute-start(bf16[64,1152]{1,0:T(8,128)(2,1)S(1)} %fir_earlier_rows.1.refs_0_), channel_id=1, source_target_pairs={{0,2},{1,3},{2,0},{3,1},{4,6},{5,7},{6,4},{7,5},{8,10},{9,11},{10,... | collective-permute-start | bytes 442376 | tf_op jit(solution)/shard_map/ppermute | solution.py:518
  17.8 4.0 %collective-permute-start.6 = (bf16[64,1152]{1,0:T(8,128)(2,1)S(1)}, bf16[64,1152]{1,0:T(8,128)(2,1)S(1)}, u32[]{:S(2)}, u32[]{:S(2)}) collective-permute-start(bf16[64,1152]{1,0:T(8,128)(2,1)S(1)} %collective-permute-done.4.refs_1_), channel_id=1, source_target_pairs={{0,1},{1,0},{2,3},{3,2},{4,5},{5,4},{6,7},{7,6},{8,9},{9,8},{10,11... | collective-permute-start | bytes 442376 | tf_op jit(solution)/shard_map/ppermute | solution.py:518
  20.9 1.9 %collective-permute-start.5 = (bf16[64,1152]{1,0:T(8,128)(2,1)S(1)}, bf16[64,1152]{1,0:T(8,128)(2,1)S(1)}, u32[]{:S(2)}, u32[]{:S(2)}) collective-permute-start(bf16[64,1152]{1,0:T(8,128)(2,1)S(1)} %collective-permute-done.2.refs_0_), channel_id=1, source_target_pairs={{0,1},{1,0},{2,3},{3,2},{4,5},{5,4},{6,7},{7,6},{8,9},{9,8},{10,11... | collective-permute-start | bytes 442376 | tf_op jit(solution)/shard_map/ppermute | solution.py:518
  23.9 9.3 %collective-permute-start.7 = (bf16[384,128]{1,0:T(8,128)(2,1)S(1)}, bf16[384,128]{1,0:T(8,128)(2,1)S(1)}, u32[]{:S(2)}, u32[]{:S(2)}) collective-permute-start(bf16[384,128]{1,0:T(8,128)(2,1)S(1)} %get-tuple-element.41), channel_id=1, source_target_pairs={{0,24},{1,28},{2,26},{3,30},{4,25},{5,29},{6,27},{7,31},{8,16},{9,... | collective-permute-start | bytes 294920 | tf_op jit(solution)/shard_map/ppermute | solution.py:560
  29.4 8.4 %collective-permute-start.8 = (bf16[384,128]{1,0:T(8,128)(2,1)S(1)}, bf16[384,128]{1,0:T(8,128)(2,1)S(1)}, u32[]{:S(2)}, u32[]{:S(2)}) collective-permute-start(bf16[384,128]{1,0:T(8,128)(2,1)S(1)} %get-tuple-element.42), channel_id=1, source_target_pairs={{0,16},{1,20},{2,18},{3,22},{4,17},{5,21},{6,19},{7,23},{8,24},{9,... | collective-permute-start | bytes 294920 | tf_op jit(solution)/shard_map/ppermute | solution.py:560
  29.5 8.4 %collective-permute-start.9 = (bf16[384,128]{1,0:T(8,128)(2,1)S(1)}, bf16[384,128]{1,0:T(8,128)(2,1)S(1)}, u32[]{:S(2)}, u32[]{:S(2)}) collective-permute-start(bf16[384,128]{1,0:T(8,128)(2,1)S(1)} %get-tuple-element.43), channel_id=1, source_target_pairs={{0,8},{1,12},{2,10},{3,14},{4,9},{5,13},{6,11},{7,15},{8,0},{9,4},... | collective-permute-start | bytes 294920 | tf_op jit(solution)/shard_map/ppermute | solution.py:560
  30.8 7.0 %collective-permute-start.10 = (bf16[384,128]{1,0:T(8,128)(2,1)S(1)}, bf16[384,128]{1,0:T(8,128)(2,1)S(1)}, u32[]{:S(2)}, u32[]{:S(2)}) collective-permute-start(bf16[384,128]{1,0:T(8,128)(2,1)S(1)} %get-tuple-element.44), channel_id=1, source_target_pairs={{0,0},{1,4},{2,2},{3,6},{4,1},{5,5},{6,3},{7,7},{8,8},{9,12},{10,1... | collective-permute-start | bytes 294920 | tf_op jit(solution)/shard_map/ppermute | solution.py:560
  37.9 2.1 %collective-permute-start.11 = (bf16[1024,128]{1,0:T(8,128)(2,1)S(1)}, bf16[1024,128]{1,0:T(8,128)(2,1)S(1)}, u32[]{:S(2)}, u32[]{:S(2)}) collective-permute-start(bf16[1024,128]{1,0:T(8,128)(2,1)S(1)} %pack_keys.1.refs_4_), channel_id=1, source_target_pairs={{0,1},{1,0},{2,3},{3,2},{4,5},{5,4},{6,7},{7,6},{8,9},{9,8},{10,11... | collective-permute-start | bytes 786440 | tf_op jit(solution)/shard_map/ppermute | solution.py:518
  41.5 8.2 %collective-permute-start.12 = (bf16[128,128]{1,0:T(8,128)(2,1)S(1)}, bf16[128,128]{1,0:T(8,128)(2,1)S(1)}, u32[]{:S(2)}, u32[]{:S(2)}) collective-permute-start(bf16[128,128]{1,0:T(8,128)(2,1)S(1)} %get-tuple-element.45), channel_id=1, source_target_pairs={{0,24},{1,28},{2,26},{3,30},{4,25},{5,29},{6,27},{7,31},{8,16},{9,... | collective-permute-start | bytes 98312 | tf_op jit(solution)/shard_map/ppermute | solution.py:560
  44.9 5.1 %collective-permute-start.13 = (bf16[128,128]{1,0:T(8,128)(2,1)S(1)}, bf16[128,128]{1,0:T(8,128)(2,1)S(1)}, u32[]{:S(2)}, u32[]{:S(2)}) collective-permute-start(bf16[128,128]{1,0:T(8,128)(2,1)S(1)} %get-tuple-element.46), channel_id=1, source_target_pairs={{0,16},{1,20},{2,18},{3,22},{4,17},{5,21},{6,19},{7,23},{8,24},{9,... | collective-permute-start | bytes 98312 | tf_op jit(solution)/shard_map/ppermute | solution.py:560
  44.9 5.1 %collective-permute-start.14 = (bf16[128,128]{1,0:T(8,128)(2,1)S(1)}, bf16[128,128]{1,0:T(8,128)(2,1)S(1)}, u32[]{:S(2)}, u32[]{:S(2)}) collective-permute-start(bf16[128,128]{1,0:T(8,128)(2,1)S(1)} %get-tuple-element.47), channel_id=1, source_target_pairs={{0,8},{1,12},{2,10},{3,14},{4,9},{5,13},{6,11},{7,15},{8,0},{9,4},... | collective-permute-start | bytes 98312 | tf_op jit(solution)/shard_map/ppermute | solution.py:560
  47.0 5.2 %collective-permute-start.15 = (bf16[128,128]{1,0:T(8,128)(2,1)S(1)}, bf16[128,128]{1,0:T(8,128)(2,1)S(1)}, u32[]{:S(2)}, u32[]{:S(2)}) collective-permute-start(bf16[128,128]{1,0:T(8,128)(2,1)S(1)} %get-tuple-element.48), channel_id=1, source_target_pairs={{0,0},{1,4},{2,2},{3,6},{4,1},{5,5},{6,3},{7,7},{8,8},{9,12},{10,1... | collective-permute-start | bytes 98312 | tf_op jit(solution)/shard_map/ppermute | solution.py:560

commit v6 on v5

--- a/solution.py
+++ b/solution.py
@@ -313,7 +313,7 @@
     )(rim, sums, x_high, last, taps, gate, gain)
 
 
-def project(blocks, first, weight_ref, acc_ref, ssq_ref):
+def project(blocks, places, weight_ref, acc_ref, ssq_ref):
     width = weight_ref.shape[2]
     whole = [jnp.concatenate([low[...], high[...]], axis=0) for low, high in blocks]
     channels = whole[0].shape[1] - LANES
@@ -322,7 +322,7 @@
     for which in range(3):
         lanes = slice(which * width, (which + 1) * width)
         total = acc_ref[:, lanes]
-        for place, block in enumerate(whole, first):
+        for place, block in zip(places, whole):
             total = total + jnp.dot(
                 block[:, :channels],
                 weight_ref[which, place * channels : (place + 1) * channels, :],
@@ -331,37 +331,39 @@
         acc_ref[:, lanes] = total
 
 
-def first_kernel(*refs):
-    blocks = ((refs[0], refs[1]), (refs[2], refs[3]))
-    weight_ref, acc_ref, ssq_ref = refs[4:]
-    acc_ref[...] = jnp.zeros_like(acc_ref)
-    ssq_ref[...] = jnp.zeros_like(ssq_ref)
-    project(blocks, 0, weight_ref, acc_ref, ssq_ref)
-
-
-def first_projection(mine, weight):
-    rows = 2 * mine[0][0].shape[0]
-    return pl.pallas_call(
-        first_kernel,
+def partial_kernel(places, fresh, *refs):
+    count = len(places)
+    blocks = [(refs[2 * n], refs[2 * n + 1]) for n in range(count)]
+    weight_ref, *before, acc_ref, ssq_ref = refs[2 * count :]
+    acc_ref[...] = jnp.zeros_like(acc_ref) if fresh else before[0][...]
+    ssq_ref[...] = jnp.zeros_like(ssq_ref) if fresh else before[1][...]
+    project(blocks, places, weight_ref, acc_ref, ssq_ref)
+
+
+def part_projection(blocks, weight, before=()):
+    rows = 2 * blocks[0][1][0].shape[0]
+    return pl.pallas_call(
+        functools.partial(partial_kernel, tuple(place for place, _ in blocks), not before),
         out_shape=(
             jax.ShapeDtypeStruct((rows, 3 * weight.shape[2]), F32),
             jax.ShapeDtypeStruct((rows, LANES), F32),
         ),
-        in_specs=[VMEM] * 5,
+        in_specs=[VMEM] * (2 * len(blocks) + 1 + len(before)),
         out_specs=(VMEM,) * 2,
         compiler_params=params(24),
         cost_estimate=cost(),
-        name="projections_near",
-    )(*mine[0], *mine[1], weight)
-
-
-def last_kernel(count, model, spread, *refs):
+        name="projections_part",
+    )(*[half for _, pair in blocks for half in pair], weight, *before)
+
+
+def last_kernel(places, model, spread, *refs):
+    count = len(places)
     blocks = [(refs[2 * n], refs[2 * n + 1]) for n in range(count)]
     weight_ref, acc_in, ssq_in = refs[2 * count : 2 * count + 3]
     outs, (acc_ref, ssq_ref) = refs[2 * count + 3 : -2], refs[-2:]
     acc_ref[...] = acc_in[...]
     ssq_ref[...] = ssq_in[...]
-    project(blocks, 2, weight_ref, acc_ref, ssq_ref)
+    project(blocks, places, weight_ref, acc_ref, ssq_ref)
     msq = jnp.sum(ssq_ref[...], axis=1, keepdims=True) / model
     scale = lax.rsqrt(msq + EPS)
     rows = acc_ref.shape[0]
@@ -375,89 +377,106 @@
             out[which * rows : (which + 1) * rows, :] = (acc_ref[:, lanes] * scale).astype(BF16)
 
 
-def last_projection(others, weight, acc, ssq, model, spread):
+def last_projection(blocks, weight, acc, ssq, model, spread):
     rows = acc.shape[0]
     heads = weight.shape[2] // HEAD_DIM
     return pl.pallas_call(
-        functools.partial(last_kernel, len(others), model, spread),
+        functools.partial(last_kernel, tuple(place for place, _ in blocks), model, spread),
         out_shape=tuple(
             jax.ShapeDtypeStruct((3 * rows, HEAD_DIM), BF16) for _ in range(heads)
         ),
-        in_specs=[VMEM] * (2 * len(others) + 3),
+        in_specs=[VMEM] * (2 * len(blocks) + 3),
         out_specs=(VMEM,) * heads,
         scratch_shapes=[pltpu.VMEM(acc.shape, F32), pltpu.VMEM(ssq.shape, F32)],
         compiler_params=params(24),
         cost_estimate=cost(),
-        name="projections_far",
-    )(*[half for pair in others for half in pair], weight, acc, ssq)
-
-
-def pack_kernel(*refs):
-    blocks, out = refs[:-1], refs[-1]
+        name="projections_last",
+    )(*[half for _, pair in blocks for half in pair], weight, acc, ssq)
+
+
+def scores_of(query, keys, rows, y):
+    place = lax.axis_index("ctx")
+
+    def base(shape, axis, of_y):
+        index = lax.broadcasted_iota(jnp.int32, shape, axis)
+        block = 2 * jnp.bitwise_xor(index // rows, place // 2) + of_y
+        return block * rows + index % rows
+
+    product = lax.dot_general(
+        query, keys, (((1,), (1,)), ((), ())), preferred_element_type=F32
+    ) * (1.0 / math.sqrt(HEAD_DIM))
+    query_base = base((query.shape[0], 1), 0, place % 2)
+    key_base = base((1, keys.shape[0]), 1, y)
+    return jnp.where(query_base >= key_base, product, -1e30)
+
+
+def own_y_kernel(*refs):
+    blocks, outs = refs[:-6], refs[-6:]
+    query_ref, top_ref, total_ref, summed_ref, key_ref, value_ref = outs
     rows = blocks[0].shape[0] // 3
-    half = len(blocks) * rows
-    for k, block in enumerate(blocks):
-        out[k * rows : (k + 1) * rows, :] = block[rows : 2 * rows, :]
-        out[half + k * rows : half + (k + 1) * rows, :] = block[2 * rows :, :]
-
-
-def packed(blocks):
-    rows = blocks[0].shape[0] // 3
-    return pl.pallas_call(
-        pack_kernel,
-        out_shape=jax.ShapeDtypeStruct((2 * len(blocks) * rows, HEAD_DIM), BF16),
+    for n, block in enumerate(blocks):
+        spot = slice(n * rows, (n + 1) * rows)
+        query_ref[spot, :] = block[:rows, :]
+        key_ref[spot, :] = block[rows : 2 * rows, :]
+        value_ref[spot, :] = block[2 * rows :, :]
+    scores = scores_of(query_ref[...], key_ref[...], rows, lax.axis_index("ctx") % 2)
+    top = jnp.max(scores, axis=1, keepdims=True)
+    expo = jnp.exp(scores - top)
+    top_ref[...] = jnp.broadcast_to(top, top_ref.shape)
+    total_ref[...] = jnp.broadcast_to(jnp.sum(expo, axis=1, keepdims=True), total_ref.shape)
+    summed_ref[...] = jnp.dot(expo.astype(BF16), value_ref[...], preferred_element_type=F32)
+
+
+def attend_own_y(blocks):
+    length = len(blocks) * blocks[0].shape[0] // 3
+    query = jax.ShapeDtypeStruct((length, HEAD_DIM), BF16)
+    shape = jax.ShapeDtypeStruct((length, LANES), F32)
+    return pl.pallas_call(
+        own_y_kernel,
+        out_shape=(query, shape, shape, shape),
         in_specs=[VMEM] * len(blocks),
-        out_specs=VMEM,
-        compiler_params=params(4),
-        cost_estimate=cost(),
-        name="pack_keys",
+        out_specs=(VMEM,) * 4,
+        scratch_shapes=[pltpu.VMEM((length, HEAD_DIM), BF16)] * 2,
+        compiler_params=params(16),
+        cost_estimate=cost(),
+        name="attention_own_y",
     )(*blocks)
 
 
-def attend_kernel(count, *refs):
-    blocks, sides, outs = refs[:count], refs[count : count + 2], refs[count + 2 :]
+def other_y_kernel(count, *refs):
+    others, (query_ref, top_ref, total_ref, summed_ref) = refs[:count], refs[count : count + 4]
+    outs, (key_ref, value_ref) = refs[count + 4 : -2], refs[-2:]
     rows = outs[0].shape[0]
-    half = count * rows
-    z, c = lax.axis_index("ctx") // 2, lax.axis_index("tp") % 2
-    column = lax.broadcasted_iota(jnp.int32, (1, half), 1)
-    even = 2 * jnp.bitwise_xor(column // rows, z) * rows + column % rows
-    scale = 1.0 / math.sqrt(HEAD_DIM)
-    for n, block in enumerate(blocks):
-        k = count - 1 - n
-        start = (2 * jnp.bitwise_xor(z, k) + c) * rows
-        query_pos = start + lax.broadcasted_iota(jnp.int32, (rows, 1), 0)
-        scores = []
-        for side, core in zip(sides, (c, 1 - c)):
-            product = lax.dot_general(
-                block[:rows, :],
-                side[:half, :],
-                (((1,), (1,)), ((), ())),
-                preferred_element_type=F32,
-            )
-            allowed = query_pos >= even + core * rows
-            scores.append(jnp.where(allowed, product * scale, -1e30))
-        top = jnp.maximum(*(jnp.max(part, axis=1, keepdims=True) for part in scores))
-        expo = [jnp.exp(part - top) for part in scores]
-        total = sum(jnp.sum(part, axis=1, keepdims=True) for part in expo)
-        summed = sum(
-            jnp.dot(part.astype(BF16), side[half:, :], preferred_element_type=F32)
-            for part, side in zip(expo, sides)
-        )
-        outs[n][...] = (summed / total).astype(BF16)
-
-
-def attend(blocks, mine, theirs):
-    count = len(blocks)
-    rows = blocks[0].shape[0] // 3
-    return pl.pallas_call(
-        functools.partial(attend_kernel, count),
+    for n, other in enumerate(others):
+        key_ref[n * rows : (n + 1) * rows, :] = other[:rows, :]
+        value_ref[n * rows : (n + 1) * rows, :] = other[rows:, :]
+    scores = scores_of(query_ref[...], key_ref[...], rows, 1 - lax.axis_index("ctx") % 2)
+    before = top_ref[...]
+    top = jnp.maximum(before[:, :1], jnp.max(scores, axis=1, keepdims=True))
+    expo = jnp.exp(scores - top)
+    fade = jnp.exp(before - top)
+    total = total_ref[...] * fade + jnp.sum(expo, axis=1, keepdims=True)
+    summed = summed_ref[...] * fade + jnp.dot(
+        expo.astype(BF16), value_ref[...], preferred_element_type=F32
+    )
+    attended = (summed / total).astype(BF16)
+    for n, out in enumerate(reversed(outs)):
+        out[...] = attended[n * rows : (n + 1) * rows, :]
+
+
+def attend_other_y(others, state):
+    count = len(others)
+    rows = others[0].shape[0] // 2
+    return pl.pallas_call(
+        functools.partial(other_y_kernel, count),
         out_shape=tuple(jax.ShapeDtypeStruct((rows, HEAD_DIM), BF16) for _ in range(count)),
-        in_specs=[VMEM] * (count + 2),
+        in_specs=[VMEM] * (count + 4),
         out_specs=(VMEM,) * count,
-        compiler_params=params(24),
-        cost_estimate=cost(),
-        name="attention",
-    )(*blocks, mine, theirs)
+        scratch_shapes=[pltpu.VMEM((count * rows, HEAD_DIM), BF16)] * 2,
+        compiler_params=params(16),
+        cost_estimate=cost(),
+        name="attention_other_y",
+    )(*others, *state)
 
 
 def join_kernel(*refs):
@@ -534,36 +553,31 @@
     by = tp // 2
     while by > 1:
         far = far + [
-            (o ^ by, tuple(swapped(part, by) for part in pair)) for o, pair in [(0, sent)] + far
+            (o ^ by ^ 1, tuple(swapped(part, by ^ 1) for part in pair))
+            for o, pair in [(0, sent)] + far
         ]
         by //= 2
-    mine = (sent, (swapped(sent_low, 1), near_high))
-    acc, ssq = first_projection(mine, weight)
-    places, pairs = [o for o, _ in far], [pair for _, pair in far]
-    last_low, acc = lax.optimization_barrier((pairs[-1][0], acc))
-    pairs[-1] = (last_low, pairs[-1][1])
-    others = []
-    for o, pair in sorted(zip(places, pairs), key=lambda item: item[0]):
-        others += [pair, tuple(swapped(part, 1) for part in pair)]
-    messages = last_projection(others, weight, acc, ssq, model, chip_per_head)
+    acc, ssq = part_projection([(0, sent), (1, (swapped(sent_low, 1), near_high))], weight)
+    last_low, acc = lax.optimization_barrier((far[-1][1][0], acc))
+    far[-1] = (far[-1][0], (last_low, far[-1][1][1]))
+    swaps = [(o ^ 1, tuple(swapped(part, 1) for part in pair)) for o, pair in far]
+    acc, ssq = part_projection(far, weight, (acc, ssq))
+    messages = last_projection(swaps, weight, acc, ssq, model, chip_per_head)
     if not chip_per_head:
         return gathered_attention(messages[::-1], heads, rows)
 
-    def routed(value, k):
-        pairs = []
-        for z in range(ctx // 2):
-            for y in range(2):
-                for x in range(tp // 2):
-                    for c in range(2):
-                        source = (2 * z + y) * tp + 2 * x + c
-                        pairs.append((source, (2 * (z ^ k) + c) * tp + 2 * x + y))
+    def over_z(value, k):
+        pairs = [(i * tp + t, (i ^ (2 * k)) * tp + (t ^ 1)) for i in range(ctx) for t in range(tp)]
         return lax.ppermute(value, ("ctx", "tp"), pairs)
 
+    def over_y(value):
+        return lax.ppermute(value, "ctx", [(i, i ^ 1) for i in range(ctx)])
+
     order = range(heads - 1, -1, -1)
-    held = [routed(value, k) for value, k in zip(messages, order)]
-    mine = packed(held[::-1])
-    done = attend(held, mine, swapped(mine, 1))
-    return join([routed(value, k) for value, k in zip(done, order)])
+    held = [over_z(value, k) for value, k in zip(messages, order)]
+    others = [over_y(value[rows:]) for value in held]
+    done = attend_other_y(others[::-1], attend_own_y(held[::-1]))
+    return join([over_z(value, k) for value, k in zip(done, order)])
 
 
 def solution(mesh):

time: 53.1 us -> 51 us (0.960)
  starting transfers between devices: 28.3 us -> 21.9 us
  waiting for transfers between devices: 11.9 us -> 15.9 us
    ppermute x8 -> x12, waiting for transfers between devices: 7.21 us -> 11.8 us  [the longest x8 9.65 us: over_z(): return lax.ppermute(value, ('ctx', 'tp'), pairs)]
    ppermute x8 -> x12, starting transfers between devices: 17.4 us -> 13.4 us  [the longest x8 10.3 us: over_z(): return lax.ppermute(value, ('ctx', 'tp'), pairs)]
    ppermute x7 -> x6, starting transfers between devices: 6.89 us -> 4.49 us  [swapped(): return lax.ppermute(value, 'tp', [(i, i ^ by) for i in range(tp)])]
    ppermute x7 -> x6, waiting for transfers between devices: 4.71 us -> 4.09 us  [swapped(): return lax.ppermute(value, 'tp', [(i, i ^ by) for i in range(tp)])]
    pallas_call x4 -> x5, Pallas kernels: 3.63 us -> 4.03 us  [the longest x2 1.55 us: part_projection(): pl.pallas_call(functools.partial(partial_kernel, tuple((place for place,...]
  transfers between devices with their start and end apart: 16 -> 19, of which waited for: 7 -> 8; matrix products, arithmetic and copies ran while one was open for 0% -> 0% of each run, Pallas kernels for 14% -> 17%
where the time goes in v6:
time: 51 us; the launch traced here: 50.9 us
  starting transfers between devices  21.9 us (43%)
  waiting for transfers between devices  15.9 us (31%)
  Pallas kernels  11.8 us (23%)
  other arithmetic  1.11 us (2%)
    ppermute x8, starting transfers between devices, over_z(): return lax.ppermute(value, ('ctx', 'tp'), pairs)  10.3 us
    ppermute x8, waiting for transfers between devices, over_z(): return lax.ppermute(value, ('ctx', 'tp'), pairs)  9.65 us
    pallas_call x1, Pallas kernels, own_part(): pl.pallas_call(own_kernel, out_shape=(slabs(SUBS * eighth), slabs(SUBS *...  4.96 us
    ppermute x6, starting transfers between devices, swapped(): return lax.ppermute(value, 'tp', [(i, i ^ by) for i in range(tp)])  4.49 us
    ppermute x6, waiting for transfers between devices, swapped(): return lax.ppermute(value, 'tp', [(i, i ^ by) for i in range(tp)])  4.09 us
    ppermute x1, starting transfers between devices, body(): lax.ppermute(mixed, 'ctx', [(i, i + 1) for i in range(ctx - 1)])  3.99 us
    ppermute x4, starting transfers between devices, over_y(): return lax.ppermute(value, 'ctx', [(i, i ^ 1) for i in range(ctx)])  3.13 us
    ppermute x4, waiting for transfers between devices, over_y(): return lax.ppermute(value, 'ctx', [(i, i ^ 1) for i in range(ctx)])  2.11 us
  transfers between devices with their start and end apart: 19, of which 8 were waited for; matrix products, arithmetic and copies ran while one was open for 0% of the time, Pallas kernels for 17%

profile of v6, /device:TPU:1, one launch (start us, length us, event | category | flops | bytes accessed | tf_op | source)
XLA Modules:
  0.0 50.9 jit_solution(16468011257312724466)
XLA Ops:
  0.0 0.0 copy-start
  0.0 1.1 %multiply_convert_fusion.mixed_ref = bf16[128,1024]{1,0:T(8,128)(2,1)S(1)} fusion(bf16[128,1024]{1,0:T(8,128)(2,1)} %param.8, bf16[128,1024]{1,0:T(8,128)(2,1)} %param.7), kind=kLoop, calls=%fused_computation | loop fusion | flops 524288 | bytes 786432 | tf_op jit(solution)/shard_map/convert_element_type | solution.py:539
  1.1 4.0 %collective-permute-start = (bf16[128,1024]{1,0:T(8,128)(2,1)S(1)}, bf16[128,1024]{1,0:T(8,128)(2,1)S(1)}, u32[]{:S(2)}, u32[]{:S(2)}) collective-permute-start(bf16[128,1024]{1,0:T(8,128)(2,1)S(1)} %multiply_convert_fusion.mixed_ref), channel_id=1, source_target_pairs={{0,4},{4,8},{8,12},{12,16},{16,20},{20,24},{24,28},{1,5},{5,9},{9,... | collective-permute-start | bytes 786440 | tf_op jit(solution)/shard_map/ppermute | solution.py:540
  5.1 5.0 %fir_own_rows.1 = (f32[1152,128]{1,0:T(8,128)S(1)}, f32[1224,128]{1,0:T(8,128)S(1)}, f32[2304,128]{1,0:T(8,128)S(1)}, bf16[128,1024]{1,0:T(8,128)(2,1)S(1)}, bf16[3,4096,512]{2,1,0:T(8,128)(2,1)S(1)}) custom-call(bf16[128,1024]{1,0:T(8,128)(2,1)S(1)} %multiply_convert_fusion.mixed_ref, f32[128,1024]{1,0:T(8,128)} %taps_hbm.1, bf16[128,1024]{1,0:T(8,128)(2,1)} %gate_hbm.1, ...), custom_call_target="tpu_custom_call" | custom-call | bytes 1024 | tf_op jit(solution)/shard_map/fir_own_rows/pallas_call | solution.py:194
  10.1 0.0 collective-permute-done.rim_ref
  10.1 0.0 copy-done
  10.1 0.7 %fir_later_rows.1 = (bf16[64,1152]{1,0:T(8,128)(2,1)S(1)}, f32[1152,128]{1,0:T(8,128)S(1)}, f32[72,128]{1,0:T(8,128)S(1)}) custom-call(bf16[128,1024]{1,0:T(8,128)(2,1)S(1)} %collective-permute-done.rim_ref, f32[1224,128]{1,0:T(8,128)S(1)} %get-tuple-element.33.sums_ref, f32[2304,128]{1,0:T(8,128)S(1)} %get-tuple-element.34.tap_subs, ...), custom_call_target="tpu_custom_call" | custom-call | bytes 1024 | tf_op jit(solution)/shard_map/fir_later_rows/pallas_call | solution.py:246
  10.8 1.6 %collective-permute-start.1 = (bf16[64,1152]{1,0:T(8,128)(2,1)S(1)}, bf16[64,1152]{1,0:T(8,128)(2,1)S(1)}, u32[]{:S(2)}, u32[]{:S(2)}) collective-permute-start(bf16[64,1152]{1,0:T(8,128)(2,1)S(1)} %get-tuple-element.36.refs_1_), channel_id=1, source_target_pairs={{0,1},{1,0},{2,3},{3,2},{4,5},{5,4},{6,7},{7,6},{8,9},{9,8},{10,11... | collective-permute-start | bytes 442376 | tf_op jit(solution)/shard_map/ppermute | solution.py:537
  12.3 1.2 %collective-permute-start.5 = (bf16[64,1152]{1,0:T(8,128)(2,1)S(1)}, bf16[64,1152]{1,0:T(8,128)(2,1)S(1)}, u32[]{:S(2)}, u32[]{:S(2)}) collective-permute-start(bf16[64,1152]{1,0:T(8,128)(2,1)S(1)} %get-tuple-element.36.refs_1_), channel_id=1, source_target_pairs={{0,3},{1,2},{2,1},{3,0},{4,7},{5,6},{6,5},{7,4},{8,11},{9,10},{10,... | collective-permute-start | bytes 442376 | tf_op jit(solution)/shard_map/ppermute | solution.py:537
  13.5 0.0 collective-permute-done.1.refs_3_
  13.5 1.5 %fir_earlier_rows.1.refs_0_ = bf16[64,1152]{1,0:T(8,128)(2,1)S(1)} custom-call(bf16[128,1024]{1,0:T(8,128)(2,1)S(1)} %collective-permute-done.rim_ref, f32[1152,128]{1,0:T(8,128)S(1)} %get-tuple-element.38.sums_ref, f32[1152,128]{1,0:T(8,128)S(1)} %get-tuple-element.39.x_high, f32[72,128]{1,0:T(8,128)S(1)} %get-tuple-element.40.last_ref, ...), custom_call_target="tpu_custom_call" | custom-call | bytes 1024 | tf_op jit(solution)/shard_map/fir_earlier_rows/pallas_call | solution.py:300
  15.0 0.5 %collective-permute-start.3 = (bf16[64,1152]{1,0:T(8,128)(2,1)S(1)}, bf16[64,1152]{1,0:T(8,128)(2,1)S(1)}, u32[]{:S(2)}, u32[]{:S(2)}) collective-permute-start(bf16[64,1152]{1,0:T(8,128)(2,1)S(1)} %fir_earlier_rows.1.refs_0_), channel_id=1, source_target_pairs={{0,1},{1,0},{2,3},{3,2},{4,5},{5,4},{6,7},{7,6},{8,9},{9,8},{10,11... | collective-permute-start | bytes 442376 | tf_op jit(solution)/shard_map/ppermute | solution.py:537
  15.5 1.0 %collective-permute-start.2 = (bf16[64,1152]{1,0:T(8,128)(2,1)S(1)}, bf16[64,1152]{1,0:T(8,128)(2,1)S(1)}, u32[]{:S(2)}, u32[]{:S(2)}) collective-permute-start(bf16[64,1152]{1,0:T(8,128)(2,1)S(1)} %fir_earlier_rows.1.refs_0_), channel_id=1, source_target_pairs={{0,3},{1,2},{2,1},{3,0},{4,7},{5,6},{6,5},{7,4},{8,11},{9,10},{10,... | collective-permute-start | bytes 442376 | tf_op jit(solution)/shard_map/ppermute | solution.py:537
  16.5 1.4 %collective-permute-done.5.refs_1_ = bf16[64,1152]{1,0:T(8,128)(2,1)S(1)} collective-permute-done((bf16[64,1152]{1,0:T(8,128)(2,1)S(1)}, bf16[64,1152]{1,0:T(8,128)(2,1)S(1)}, u32[]{:S(2)}, u32[]{:S(2)}) %collective-permute-start.5) | collective-permute-done | bytes 147488 | tf_op jit(solution)/shard_map/ppermute | solution.py:537
  17.9 0.1 collective-permute-start.6
  18.0 0.0 collective-permute-done.3.refs_2_
  18.0 1.0 %projections_part.2 = (f32[128,1536]{1,0:T(8,128)S(1)}, f32[128,128]{1,0:T(8,128)S(1)}) custom-call(bf16[64,1152]{1,0:T(8,128)(2,1)S(1)} %fir_earlier_rows.1.refs_0_, bf16[64,1152]{1,0:T(8,128)(2,1)S(1)} %get-tuple-element.36.refs_1_, bf16[64,1152]{1,0:T(8,128)(2,1)S(1)} %collective-permute-done.3.refs_2_, ...), custom_call_target="tpu_custom_call" | custom-call | bytes 1024 | tf_op jit(solution)/shard_map/projections_part/pallas_call | solution.py:345
  19.0 2.1 %collective-permute-done.2.refs_0_ = bf16[64,1152]{1,0:T(8,128)(2,1)S(1)} collective-permute-done((bf16[64,1152]{1,0:T(8,128)(2,1)S(1)}, bf16[64,1152]{1,0:T(8,128)(2,1)S(1)}, u32[]{:S(2)}, u32[]{:S(2)}) %collective-permute-start.2) | collective-permute-done | bytes 147488 | tf_op jit(solution)/shard_map/ppermute | solution.py:537
  21.1 0.1 collective-permute-start.4
  21.2 0.6 %projections_part.3 = (f32[128,1536]{1,0:T(8,128)S(1)}, f32[128,128]{1,0:T(8,128)S(1)}) custom-call(bf16[64,1152]{1,0:T(8,128)(2,1)S(1)} %collective-permute-done.2.refs_0_, bf16[64,1152]{1,0:T(8,128)(2,1)S(1)} %collective-permute-done.5.refs_1_, bf16[3,4096,512]{2,1,0:T(8,128)(2,1)S(1)} %get-tuple-element.42.refs_4_.refs_2_, ...), custom_call_target="tpu_custom_call" | custom-call | bytes 1024 | tf_op jit(solution)/shard_map/projections_part/pallas_call | solution.py:345
  21.8 0.0 collective-permute-done.6.refs_1_
  21.8 0.7 %collective-permute-done.4.refs_0_ = bf16[64,1152]{1,0:T(8,128)(2,1)S(1)} collective-permute-done((bf16[64,1152]{1,0:T(8,128)(2,1)S(1)}, bf16[64,1152]{1,0:T(8,128)(2,1)S(1)}, u32[]{:S(2)}, u32[]{:S(2)}) %collective-permute-start.4) | collective-permute-done | bytes 147488 | tf_op jit(solution)/shard_map/ppermute | solution.py:537
  22.4 0.7 %projections_last.1 = (bf16[384,128]{1,0:T(8,128)(2,1)S(1)}, bf16[384,128]{1,0:T(8,128)(2,1)S(1)}, bf16[384,128]{1,0:T(8,128)(2,1)S(1)}, bf16[384,128]{1,0:T(8,128)(2,1)S(1)}) custom-call(bf16[64,1152]{1,0:T(8,128)(2,1)S(1)} %collective-permute-done.4.refs_0_, bf16[64,1152]{1,0:T(8,128)(2,1)S(1)} %collective-permute-done.6.refs_1_, ...), custom_call_target="tpu_custom_call" | custom-call | bytes 1024 | tf_op jit(solution)/shard_map/projections_last/pallas_call | solution.py:383
  23.1 0.2 collective-permute-start.7
  23.3 3.4 %collective-permute-start.9 = (bf16[384,128]{1,0:T(8,128)(2,1)S(1)}, bf16[384,128]{1,0:T(8,128)(2,1)S(1)}, u32[]{:S(2)}, u32[]{:S(2)}) collective-permute-start(bf16[384,128]{1,0:T(8,128)(2,1)S(1)} %get-tuple-element.50), channel_id=1, source_target_pairs={{0,9},{1,8},{2,11},{3,10},{4,13},{5,12},{6,15},{7,14},{8,1},{9,0},... | collective-permute-start | bytes 294920 | tf_op jit(solution)/shard_map/ppermute | solution.py:571
  26.7 2.4 %collective-permute-start.11 = (bf16[384,128]{1,0:T(8,128)(2,1)S(1)}, bf16[384,128]{1,0:T(8,128)(2,1)S(1)}, u32[]{:S(2)}, u32[]{:S(2)}) collective-permute-start(bf16[384,128]{1,0:T(8,128)(2,1)S(1)} %get-tuple-element.51), channel_id=1, source_target_pairs={{0,17},{1,16},{2,19},{3,18},{4,21},{5,20},{6,23},{7,22},{8,25},{9,... | collective-permute-start | bytes 294920 | tf_op jit(solution)/shard_map/ppermute | solution.py:571
  29.1 0.0 collective-permute-start.13
  29.1 0.0 collective-permute-done.7.refs_0_
  29.1 0.6 %collective-permute-start.8 = (bf16[256,128]{1,0:T(8,128)(2,1)S(1)}, bf16[256,128]{1,0:T(8,128)(2,1)S(1)}, u32[]{:S(2)}, u32[]{:S(2)}) collective-permute-start(bf16[256,128]{1,0:T(8,128)(2,1)S(1)} %slice.16), channel_id=1, source_target_pairs={{0,4},{4,0},{8,12},{12,8},{16,20},{20,16},{24,28},{28,24},{1,5},{5... | collective-permute-start | bytes 196616 | tf_op jit(solution)/shard_map/ppermute | solution.py:574
  29.7 0.0 collective-permute-done.9.refs_1_
  29.7 1.0 %collective-permute-start.10 = (bf16[256,128]{1,0:T(8,128)(2,1)S(1)}, bf16[256,128]{1,0:T(8,128)(2,1)S(1)}, u32[]{:S(2)}, u32[]{:S(2)}) collective-permute-start(bf16[256,128]{1,0:T(8,128)(2,1)S(1)} %slice.17), channel_id=1, source_target_pairs={{0,4},{4,0},{8,12},{12,8},{16,20},{20,16},{24,28},{28,24},{1,5},{5... | collective-permute-start | bytes 196616 | tf_op jit(solution)/shard_map/ppermute | solution.py:574
  30.7 6.2 %collective-permute-done.11.refs_2_ = bf16[384,128]{1,0:T(8,128)(2,1)S(1)} collective-permute-done((bf16[384,128]{1,0:T(8,128)(2,1)S(1)}, bf16[384,128]{1,0:T(8,128)(2,1)S(1)}, u32[]{:S(2)}, u32[]{:S(2)}) %collective-permute-start.11) | collective-permute-done | bytes 98336 | tf_op jit(solution)/shard_map/ppermute | solution.py:571
  36.9 0.3 collective-permute-start.12
  37.2 0.0 collective-permute-done.13.refs_3_
  37.3 1.2 %collective-permute-start.14 = (bf16[256,128]{1,0:T(8,128)(2,1)S(1)}, bf16[256,128]{1,0:T(8,128)(2,1)S(1)}, u32[]{:S(2)}, u32[]{:S(2)}) collective-permute-start(bf16[256,128]{1,0:T(8,128)(2,1)S(1)} %slice.19), channel_id=1, source_target_pairs={{0,4},{4,0},{8,12},{12,8},{16,20},{20,16},{24,28},{28,24},{1,5},{5... | collective-permute-start | bytes 196616 | tf_op jit(solution)/shard_map/ppermute | solution.py:574
  38.4 0.8 %attention_own_y.1 = (bf16[512,128]{1,0:T(8,128)(2,1)S(1)}, f32[512,128]{1,0:T(8,128)S(1)}, f32[512,128]{1,0:T(8,128)S(1)}, f32[512,128]{1,0:T(8,128)S(1)}) custom-call(bf16[384,128]{1,0:T(8,128)(2,1)S(1)} %collective-permute-done.7.refs_0_, bf16[384,128]{1,0:T(8,128)(2,1)S(1)} %collective-permute-done.9.refs_1_, ...), custom_call_target="tpu_custom_call" | custom-call | bytes 1024 | tf_op jit(solution)/shard_map/attention_own_y/pallas_call | solution.py:434
  39.3 0.0 collective-permute-done.8.refs_0_
  39.3 0.0 collective-permute-done.10.refs_1_
  39.3 1.4 %collective-permute-done.12.refs_2_ = bf16[256,128]{1,0:T(8,128)(2,1)S(1)} collective-permute-done((bf16[256,128]{1,0:T(8,128)(2,1)S(1)}, bf16[256,128]{1,0:T(8,128)(2,1)S(1)}, u32[]{:S(2)}, u32[]{:S(2)}) %collective-permute-start.12) | collective-permute-done | bytes 65568 | tf_op jit(solution)/shard_map/ppermute | solution.py:574
  40.8 0.7 %collective-permute-done.14.refs_3_ = bf16[256,128]{1,0:T(8,128)(2,1)S(1)} collective-permute-done((bf16[256,128]{1,0:T(8,128)(2,1)S(1)}, bf16[256,128]{1,0:T(8,128)(2,1)S(1)}, u32[]{:S(2)}, u32[]{:S(2)}) %collective-permute-start.14) | collective-permute-done | bytes 65568 | tf_op jit(solution)/shard_map/ppermute | solution.py:574
  41.4 0.9 %attention_other_y.1 = (bf16[128,128]{1,0:T(8,128)(2,1)S(1)}, bf16[128,128]{1,0:T(8,128)(2,1)S(1)}, bf16[128,128]{1,0:T(8,128)(2,1)S(1)}, bf16[128,128]{1,0:T(8,128)(2,1)S(1)}) custom-call(bf16[256,128]{1,0:T(8,128)(2,1)S(1)} %collective-permute-done.8.refs_0_, bf16[256,128]{1,0:T(8,128)(2,1)S(1)} %collective-permute-done.10.refs_1_, ...), custom_call_target="tpu_custom_call" | custom-call | bytes 1024 | tf_op jit(solution)/shard_map/attention_other_y/pallas_call | solution.py:470
  42.4 3.6 %collective-permute-start.15 = (bf16[128,128]{1,0:T(8,128)(2,1)S(1)}, bf16[128,128]{1,0:T(8,128)(2,1)S(1)}, u32[]{:S(2)}, u32[]{:S(2)}) collective-permute-start(bf16[128,128]{1,0:T(8,128)(2,1)S(1)} %get-tuple-element.57), channel_id=1, source_target_pairs={{0,25},{1,24},{2,27},{3,26},{4,29},{5,28},{6,31},{7,30},{8,17},{9,... | collective-permute-start | bytes 98312 | tf_op jit(solution)/shard_map/ppermute | solution.py:571
  45.9 0.0 collective-permute-start.16
  45.9 0.4 collective-permute-start.17
  46.4 0.3 collective-permute-start.18
  46.7 0.9 %collective-permute-done.15.refs_0_ = bf16[128,128]{1,0:T(8,128)(2,1)S(1)} collective-permute-done((bf16[128,128]{1,0:T(8,128)(2,1)S(1)}, bf16[128,128]{1,0:T(8,128)(2,1)S(1)}, u32[]{:S(2)}, u32[]{:S(2)}) %collective-permute-start.15) | collective-permute-done | bytes 32800 | tf_op jit(solution)/shard_map/ppermute | solution.py:571
  47.6 2.6 %collective-permute-done.16.refs_1_ = bf16[128,128]{1,0:T(8,128)(2,1)S(1)} collective-permute-done((bf16[128,128]{1,0:T(8,128)(2,1)S(1)}, bf16[128,128]{1,0:T(8,128)(2,1)S(1)}, u32[]{:S(2)}, u32[]{:S(2)}) %collective-permute-start.16) | collective-permute-done | bytes 32800 | tf_op jit(solution)/shard_map/ppermute | solution.py:571
  50.2 0.0 collective-permute-done.17.refs_2_
  50.2 0.0 collective-permute-done.18.refs_3_
  50.2 0.7 %join_heads.1 = bf16[128,512]{1,0:T(8,128)(2,1)} custom-call(bf16[128,128]{1,0:T(8,128)(2,1)S(1)} %collective-permute-done.15.refs_0_, bf16[128,128]{1,0:T(8,128)(2,1)S(1)} %collective-permute-done.16.refs_1_, bf16[128,128]{1,0:T(8,128)(2,1)S(1)} %collective-permute-done.17.refs_2_, bf16[128,128]{1,0:T(8,128)(2,1)S(1)} %collective-permute-done.18.refs_3_), custom_call_target="tpu_custom_call" | custom-call | bytes 1024 | tf_op jit(solution)/shard_map/join_heads/pallas_call | solution.py:491
  (4 shorter events, 0.0 us)
Async XLA Ops:
  0.0 10.1 %copy-start = (f32[1024]{0:T(1024)S(1)}, f32[1024]{0:T(1024)}, u32[]{:S(2)}) copy-start(f32[1024]{0:T(1024)} %param.10) | copy-start | bytes 12292
  1.1 9.0 %collective-permute-start = (bf16[128,1024]{1,0:T(8,128)(2,1)S(1)}, bf16[128,1024]{1,0:T(8,128)(2,1)S(1)}, u32[]{:S(2)}, u32[]{:S(2)}) collective-permute-start(bf16[128,1024]{1,0:T(8,128)(2,1)S(1)} %multiply_convert_fusion.mixed_ref), channel_id=1, source_target_pairs={{0,4},{4,8},{8,12},{12,16},{16,20},{20,24},{24,28},{1,5},{5,9},{9,... | collective-permute-start | bytes 786440 | tf_op jit(solution)/shard_map/ppermute | solution.py:540
  10.8 2.7 %collective-permute-start.1 = (bf16[64,1152]{1,0:T(8,128)(2,1)S(1)}, bf16[64,1152]{1,0:T(8,128)(2,1)S(1)}, u32[]{:S(2)}, u32[]{:S(2)}) collective-permute-start(bf16[64,1152]{1,0:T(8,128)(2,1)S(1)} %get-tuple-element.36.refs_1_), channel_id=1, source_target_pairs={{0,1},{1,0},{2,3},{3,2},{4,5},{5,4},{6,7},{7,6},{8,9},{9,8},{10,11... | collective-permute-start | bytes 442376 | tf_op jit(solution)/shard_map/ppermute | solution.py:537
  12.3 5.5 %collective-permute-start.5 = (bf16[64,1152]{1,0:T(8,128)(2,1)S(1)}, bf16[64,1152]{1,0:T(8,128)(2,1)S(1)}, u32[]{:S(2)}, u32[]{:S(2)}) collective-permute-start(bf16[64,1152]{1,0:T(8,128)(2,1)S(1)} %get-tuple-element.36.refs_1_), channel_id=1, source_target_pairs={{0,3},{1,2},{2,1},{3,0},{4,7},{5,6},{6,5},{7,4},{8,11},{9,10},{10,... | collective-permute-start | bytes 442376 | tf_op jit(solution)/shard_map/ppermute | solution.py:537
  15.0 3.0 %collective-permute-start.3 = (bf16[64,1152]{1,0:T(8,128)(2,1)S(1)}, bf16[64,1152]{1,0:T(8,128)(2,1)S(1)}, u32[]{:S(2)}, u32[]{:S(2)}) collective-permute-start(bf16[64,1152]{1,0:T(8,128)(2,1)S(1)} %fir_earlier_rows.1.refs_0_), channel_id=1, source_target_pairs={{0,1},{1,0},{2,3},{3,2},{4,5},{5,4},{6,7},{7,6},{8,9},{9,8},{10,11... | collective-permute-start | bytes 442376 | tf_op jit(solution)/shard_map/ppermute | solution.py:537
  15.5 5.5 %collective-permute-start.2 = (bf16[64,1152]{1,0:T(8,128)(2,1)S(1)}, bf16[64,1152]{1,0:T(8,128)(2,1)S(1)}, u32[]{:S(2)}, u32[]{:S(2)}) collective-permute-start(bf16[64,1152]{1,0:T(8,128)(2,1)S(1)} %fir_earlier_rows.1.refs_0_), channel_id=1, source_target_pairs={{0,3},{1,2},{2,1},{3,0},{4,7},{5,6},{6,5},{7,4},{8,11},{9,10},{10,... | collective-permute-start | bytes 442376 | tf_op jit(solution)/shard_map/ppermute | solution.py:537
  17.9 3.9 %collective-permute-start.6 = (bf16[64,1152]{1,0:T(8,128)(2,1)S(1)}, bf16[64,1152]{1,0:T(8,128)(2,1)S(1)}, u32[]{:S(2)}, u32[]{:S(2)}) collective-permute-start(bf16[64,1152]{1,0:T(8,128)(2,1)S(1)} %collective-permute-done.5.refs_1_), channel_id=1, source_target_pairs={{0,1},{1,0},{2,3},{3,2},{4,5},{5,4},{6,7},{7,6},{8,9},{9,8},{10,11... | collective-permute-start | bytes 442376 | tf_op jit(solution)/shard_map/ppermute | solution.py:537
  21.1 1.4 %collective-permute-start.4 = (bf16[64,1152]{1,0:T(8,128)(2,1)S(1)}, bf16[64,1152]{1,0:T(8,128)(2,1)S(1)}, u32[]{:S(2)}, u32[]{:S(2)}) collective-permute-start(bf16[64,1152]{1,0:T(8,128)(2,1)S(1)} %collective-permute-done.2.refs_0_), channel_id=1, source_target_pairs={{0,1},{1,0},{2,3},{3,2},{4,5},{5,4},{6,7},{7,6},{8,9},{9,8},{10,11... | collective-permute-start | bytes 442376 | tf_op jit(solution)/shard_map/ppermute | solution.py:537
  23.1 6.0 %collective-permute-start.7 = (bf16[384,128]{1,0:T(8,128)(2,1)S(1)}, bf16[384,128]{1,0:T(8,128)(2,1)S(1)}, u32[]{:S(2)}, u32[]{:S(2)}) collective-permute-start(bf16[384,128]{1,0:T(8,128)(2,1)S(1)} %get-tuple-element.49), channel_id=1, source_target_pairs={{0,1},{1,0},{2,3},{3,2},{4,5},{5,4},{6,7},{7,6},{8,9},{9,8},{10,11... | collective-permute-start | bytes 294920 | tf_op jit(solution)/shard_map/ppermute | solution.py:571
  23.3 6.4 %collective-permute-start.9 = (bf16[384,128]{1,0:T(8,128)(2,1)S(1)}, bf16[384,128]{1,0:T(8,128)(2,1)S(1)}, u32[]{:S(2)}, u32[]{:S(2)}) collective-permute-start(bf16[384,128]{1,0:T(8,128)(2,1)S(1)} %get-tuple-element.50), channel_id=1, source_target_pairs={{0,9},{1,8},{2,11},{3,10},{4,13},{5,12},{6,15},{7,14},{8,1},{9,0},... | collective-permute-start | bytes 294920 | tf_op jit(solution)/shard_map/ppermute | solution.py:571
  26.7 10.1 %collective-permute-start.11 = (bf16[384,128]{1,0:T(8,128)(2,1)S(1)}, bf16[384,128]{1,0:T(8,128)(2,1)S(1)}, u32[]{:S(2)}, u32[]{:S(2)}) collective-permute-start(bf16[384,128]{1,0:T(8,128)(2,1)S(1)} %get-tuple-element.51), channel_id=1, source_target_pairs={{0,17},{1,16},{2,19},{3,18},{4,21},{5,20},{6,23},{7,22},{8,25},{9,... | collective-permute-start | bytes 294920 | tf_op jit(solution)/shard_map/ppermute | solution.py:571
  29.1 8.1 %collective-permute-start.13 = (bf16[384,128]{1,0:T(8,128)(2,1)S(1)}, bf16[384,128]{1,0:T(8,128)(2,1)S(1)}, u32[]{:S(2)}, u32[]{:S(2)}) collective-permute-start(bf16[384,128]{1,0:T(8,128)(2,1)S(1)} %get-tuple-element.52), channel_id=1, source_target_pairs={{0,25},{1,24},{2,27},{3,26},{4,29},{5,28},{6,31},{7,30},{8,17},{9,... | collective-permute-start | bytes 294920 | tf_op jit(solution)/shard_map/ppermute | solution.py:571
  29.1 10.2 %collective-permute-start.8 = (bf16[256,128]{1,0:T(8,128)(2,1)S(1)}, bf16[256,128]{1,0:T(8,128)(2,1)S(1)}, u32[]{:S(2)}, u32[]{:S(2)}) collective-permute-start(bf16[256,128]{1,0:T(8,128)(2,1)S(1)} %slice.16), channel_id=1, source_target_pairs={{0,4},{4,0},{8,12},{12,8},{16,20},{20,16},{24,28},{28,24},{1,5},{5... | collective-permute-start | bytes 196616 | tf_op jit(solution)/shard_map/ppermute | solution.py:574
  29.7 9.6 %collective-permute-start.10 = (bf16[256,128]{1,0:T(8,128)(2,1)S(1)}, bf16[256,128]{1,0:T(8,128)(2,1)S(1)}, u32[]{:S(2)}, u32[]{:S(2)}) collective-permute-start(bf16[256,128]{1,0:T(8,128)(2,1)S(1)} %slice.17), channel_id=1, source_target_pairs={{0,4},{4,0},{8,12},{12,8},{16,20},{20,16},{24,28},{28,24},{1,5},{5... | collective-permute-start | bytes 196616 | tf_op jit(solution)/shard_map/ppermute | solution.py:574
  36.9 3.9 %collective-permute-start.12 = (bf16[256,128]{1,0:T(8,128)(2,1)S(1)}, bf16[256,128]{1,0:T(8,128)(2,1)S(1)}, u32[]{:S(2)}, u32[]{:S(2)}) collective-permute-start(bf16[256,128]{1,0:T(8,128)(2,1)S(1)} %slice.18), channel_id=1, source_target_pairs={{0,4},{4,0},{8,12},{12,8},{16,20},{20,16},{24,28},{28,24},{1,5},{5... | collective-permute-start | bytes 196616 | tf_op jit(solution)/shard_map/ppermute | solution.py:574
  37.3 4.2 %collective-permute-start.14 = (bf16[256,128]{1,0:T(8,128)(2,1)S(1)}, bf16[256,128]{1,0:T(8,128)(2,1)S(1)}, u32[]{:S(2)}, u32[]{:S(2)}) collective-permute-start(bf16[256,128]{1,0:T(8,128)(2,1)S(1)} %slice.19), channel_id=1, source_target_pairs={{0,4},{4,0},{8,12},{12,8},{16,20},{20,16},{24,28},{28,24},{1,5},{5... | collective-permute-start | bytes 196616 | tf_op jit(solution)/shard_map/ppermute | solution.py:574
  42.4 5.2 %collective-permute-start.15 = (bf16[128,128]{1,0:T(8,128)(2,1)S(1)}, bf16[128,128]{1,0:T(8,128)(2,1)S(1)}, u32[]{:S(2)}, u32[]{:S(2)}) collective-permute-start(bf16[128,128]{1,0:T(8,128)(2,1)S(1)} %get-tuple-element.57), channel_id=1, source_target_pairs={{0,25},{1,24},{2,27},{3,26},{4,29},{5,28},{6,31},{7,30},{8,17},{9,... | collective-permute-start | bytes 98312 | tf_op jit(solution)/shard_map/ppermute | solution.py:571
  45.9 4.2 %collective-permute-start.16 = (bf16[128,128]{1,0:T(8,128)(2,1)S(1)}, bf16[128,128]{1,0:T(8,128)(2,1)S(1)}, u32[]{:S(2)}, u32[]{:S(2)}) collective-permute-start(bf16[128,128]{1,0:T(8,128)(2,1)S(1)} %get-tuple-element.58), channel_id=1, source_target_pairs={{0,17},{1,16},{2,19},{3,18},{4,21},{5,20},{6,23},{7,22},{8,25},{9,... | collective-permute-start | bytes 98312 | tf_op jit(solution)/shard_map/ppermute | solution.py:571
  45.9 4.2 %collective-permute-start.17 = (bf16[128,128]{1,0:T(8,128)(2,1)S(1)}, bf16[128,128]{1,0:T(8,128)(2,1)S(1)}, u32[]{:S(2)}, u32[]{:S(2)}) collective-permute-start(bf16[128,128]{1,0:T(8,128)(2,1)S(1)} %get-tuple-element.59), channel_id=1, source_target_pairs={{0,9},{1,8},{2,11},{3,10},{4,13},{5,12},{6,15},{7,14},{8,1},{9,0},... | collective-permute-start | bytes 98312 | tf_op jit(solution)/shard_map/ppermute | solution.py:571
  46.4 3.8 %collective-permute-start.18 = (bf16[128,128]{1,0:T(8,128)(2,1)S(1)}, bf16[128,128]{1,0:T(8,128)(2,1)S(1)}, u32[]{:S(2)}, u32[]{:S(2)}) collective-permute-start(bf16[128,128]{1,0:T(8,128)(2,1)S(1)} %get-tuple-element.60), channel_id=1, source_target_pairs={{0,1},{1,0},{2,3},{3,2},{4,5},{5,4},{6,7},{7,6},{8,9},{9,8},{10,11... | collective-permute-start | bytes 98312 | tf_op jit(solution)/shard_map/ppermute | solution.py:571

commit v7 on v6

--- a/solution.py
+++ b/solution.py
@@ -394,32 +394,41 @@
     )(*[half for _, pair in blocks for half in pair], weight, acc, ssq)
 
 
-def scores_of(query, keys, rows, y):
-    place = lax.axis_index("ctx")
-
-    def base(shape, axis, of_y):
-        index = lax.broadcasted_iota(jnp.int32, shape, axis)
-        block = 2 * jnp.bitwise_xor(index // rows, place // 2) + of_y
-        return block * rows + index % rows
-
+def base_of(shape, axis, rows, y):
+    index = lax.broadcasted_iota(jnp.int32, shape, axis)
+    block = 2 * jnp.bitwise_xor(index // rows, lax.axis_index("ctx") // 2) + y
+    return block * rows + index % rows
+
+
+def scores_of(query, keys, rows, key_base):
     product = lax.dot_general(
         query, keys, (((1,), (1,)), ((), ())), preferred_element_type=F32
     ) * (1.0 / math.sqrt(HEAD_DIM))
-    query_base = base((query.shape[0], 1), 0, place % 2)
-    key_base = base((1, keys.shape[0]), 1, y)
+    query_base = base_of((query.shape[0], 1), 0, rows, lax.axis_index("ctx") % 2)
     return jnp.where(query_base >= key_base, product, -1e30)
 
 
-def own_y_kernel(*refs):
-    blocks, outs = refs[:-6], refs[-6:]
-    query_ref, top_ref, total_ref, summed_ref, key_ref, value_ref = outs
+def most_kernel(count, *refs):
+    blocks, others = refs[:count], refs[count : 2 * count - 1]
+    query_ref, top_ref, total_ref, summed_ref, key_ref, value_ref = refs[2 * count - 1 :]
     rows = blocks[0].shape[0] // 3
     for n, block in enumerate(blocks):
         spot = slice(n * rows, (n + 1) * rows)
         query_ref[spot, :] = block[:rows, :]
         key_ref[spot, :] = block[rows : 2 * rows, :]
         value_ref[spot, :] = block[2 * rows :, :]
-    scores = scores_of(query_ref[...], key_ref[...], rows, lax.axis_index("ctx") % 2)
+    for n, other in enumerate(others, count):
+        key_ref[n * rows : (n + 1) * rows, :] = other[:rows, :]
+        value_ref[n * rows : (n + 1) * rows, :] = other[rows:, :]
+    y = lax.axis_index("ctx") % 2
+    key_base = jnp.concatenate(
+        [
+            base_of((1, count * rows), 1, rows, y),
+            base_of((1, (count - 1) * rows), 1, rows, 1 - y),
+        ],
+        axis=1,
+    )
+    scores = scores_of(query_ref[...], key_ref[...], rows, key_base)
     top = jnp.max(scores, axis=1, keepdims=True)
     expo = jnp.exp(scores - top)
     top_ref[...] = jnp.broadcast_to(top, top_ref.shape)
@@ -427,56 +436,53 @@
     summed_ref[...] = jnp.dot(expo.astype(BF16), value_ref[...], preferred_element_type=F32)
 
 
-def attend_own_y(blocks):
-    length = len(blocks) * blocks[0].shape[0] // 3
-    query = jax.ShapeDtypeStruct((length, HEAD_DIM), BF16)
-    shape = jax.ShapeDtypeStruct((length, LANES), F32)
-    return pl.pallas_call(
-        own_y_kernel,
-        out_shape=(query, shape, shape, shape),
-        in_specs=[VMEM] * len(blocks),
+def attend_most(blocks, others):
+    count = len(blocks)
+    rows = blocks[0].shape[0] // 3
+    keys = pltpu.VMEM(((2 * count - 1) * rows, HEAD_DIM), BF16)
+    shape = jax.ShapeDtypeStruct((count * rows, LANES), F32)
+    return pl.pallas_call(
+        functools.partial(most_kernel, count),
+        out_shape=(jax.ShapeDtypeStruct((count * rows, HEAD_DIM), BF16), shape, shape, shape),
+        in_specs=[VMEM] * (2 * count - 1),
         out_specs=(VMEM,) * 4,
-        scratch_shapes=[pltpu.VMEM((length, HEAD_DIM), BF16)] * 2,
+        scratch_shapes=[keys, keys],
         compiler_params=params(16),
         cost_estimate=cost(),
-        name="attention_own_y",
-    )(*blocks)
-
-
-def other_y_kernel(count, *refs):
-    others, (query_ref, top_ref, total_ref, summed_ref) = refs[:count], refs[count : count + 4]
-    outs, (key_ref, value_ref) = refs[count + 4 : -2], refs[-2:]
+        name="attention_most",
+    )(*blocks, *others)
+
+
+def rest_kernel(other_ref, query_ref, top_ref, total_ref, summed_ref, *outs):
+    count = len(outs)
     rows = outs[0].shape[0]
-    for n, other in enumerate(others):
-        key_ref[n * rows : (n + 1) * rows, :] = other[:rows, :]
-        value_ref[n * rows : (n + 1) * rows, :] = other[rows:, :]
-    scores = scores_of(query_ref[...], key_ref[...], rows, 1 - lax.axis_index("ctx") % 2)
+    y = lax.axis_index("ctx") % 2
+    key_base = base_of((1, count * rows), 1, rows, 1 - y)[:, (count - 1) * rows :]
+    scores = scores_of(query_ref[...], other_ref[:rows, :], rows, key_base)
     before = top_ref[...]
     top = jnp.maximum(before[:, :1], jnp.max(scores, axis=1, keepdims=True))
     expo = jnp.exp(scores - top)
     fade = jnp.exp(before - top)
     total = total_ref[...] * fade + jnp.sum(expo, axis=1, keepdims=True)
     summed = summed_ref[...] * fade + jnp.dot(
-        expo.astype(BF16), value_ref[...], preferred_element_type=F32
+        expo.astype(BF16), other_ref[rows:, :], preferred_element_type=F32
     )
     attended = (summed / total).astype(BF16)
     for n, out in enumerate(reversed(outs)):
         out[...] = attended[n * rows : (n + 1) * rows, :]
 
 
-def attend_other_y(others, state):
-    count = len(others)
-    rows = others[0].shape[0] // 2
-    return pl.pallas_call(
-        functools.partial(other_y_kernel, count),
+def attend_rest(other, state, count):
+    rows = other.shape[0] // 2
+    return pl.pallas_call(
+        rest_kernel,
         out_shape=tuple(jax.ShapeDtypeStruct((rows, HEAD_DIM), BF16) for _ in range(count)),
-        in_specs=[VMEM] * (count + 4),
+        in_specs=[VMEM] * 5,
         out_specs=(VMEM,) * count,
-        scratch_shapes=[pltpu.VMEM((count * rows, HEAD_DIM), BF16)] * 2,
         compiler_params=params(16),
         cost_estimate=cost(),
-        name="attention_other_y",
-    )(*others, *state)
+        name="attention_rest",
+    )(other, *state)
 
 
 def join_kernel(*refs):
@@ -576,7 +582,8 @@
     order = range(heads - 1, -1, -1)
     held = [over_z(value, k) for value, k in zip(messages, order)]
     others = [over_y(value[rows:]) for value in held]
-    done = attend_other_y(others[::-1], attend_own_y(held[::-1]))
+    held, others = held[::-1], others[::-1]
+    done = attend_rest(others[-1], attend_most(held, others[:-1]), heads)
     return join([over_z(value, k) for value, k in zip(done, order)])
 
 

time: 51 us -> 50.8 us (level)
  transfers between devices with their start and end apart: 19 -> 19, of which waited for: 8 -> 7; matrix products, arithmetic and copies ran while one was open for 0% -> 0% of each run, Pallas kernels for 17% -> 18%
where the time goes in v7:
time: 50.8 us; the launch traced here: 50.6 us
  starting transfers between devices  21.9 us (43%)
  waiting for transfers between devices  15.6 us (31%)
  Pallas kernels  11.9 us (23%)
  other arithmetic  1.11 us (2%)
    ppermute x8, starting transfers between devices, over_z(): return lax.ppermute(value, ('ctx', 'tp'), pairs)  10.3 us
    ppermute x8, waiting for transfers between devices, over_z(): return lax.ppermute(value, ('ctx', 'tp'), pairs)  9.18 us
    pallas_call x1, Pallas kernels, own_part(): pl.pallas_call(own_kernel, out_shape=(slabs(SUBS * eighth), slabs(SUBS *...  4.96 us
    ppermute x6, starting transfers between devices, swapped(): return lax.ppermute(value, 'tp', [(i, i ^ by) for i in range(tp)])  4.49 us
    ppermute x6, waiting for transfers between devices, swapped(): return lax.ppermute(value, 'tp', [(i, i ^ by) for i in range(tp)])  4.09 us
    ppermute x1, starting transfers between devices, body(): lax.ppermute(mixed, 'ctx', [(i, i + 1) for i in range(ctx - 1)])  3.99 us
    ppermute x4, starting transfers between devices, over_y(): return lax.ppermute(value, 'ctx', [(i, i ^ 1) for i in range(ctx)])  3.13 us
    ppermute x4, waiting for transfers between devices, over_y(): return lax.ppermute(value, 'ctx', [(i, i ^ 1) for i in range(ctx)])  2.32 us
  transfers between devices with their start and end apart: 19, of which 7 were waited for; matrix products, arithmetic and copies ran while one was open for 0% of the time, Pallas kernels for 18%

profile of v7, /device:TPU:1, one launch (start us, length us, event | category | flops | bytes accessed | tf_op | source)
XLA Modules:
  0.0 50.6 jit_solution(1540230993637667131)
XLA Ops:
  0.0 0.0 copy-start
  0.0 1.1 %multiply_convert_fusion.mixed_ref = bf16[128,1024]{1,0:T(8,128)(2,1)S(1)} fusion(bf16[128,1024]{1,0:T(8,128)(2,1)} %param.8, bf16[128,1024]{1,0:T(8,128)(2,1)} %param.7), kind=kLoop, calls=%fused_computation | loop fusion | flops 524288 | bytes 786432 | tf_op jit(solution)/shard_map/convert_element_type | solution.py:545
  1.1 4.0 %collective-permute-start = (bf16[128,1024]{1,0:T(8,128)(2,1)S(1)}, bf16[128,1024]{1,0:T(8,128)(2,1)S(1)}, u32[]{:S(2)}, u32[]{:S(2)}) collective-permute-start(bf16[128,1024]{1,0:T(8,128)(2,1)S(1)} %multiply_convert_fusion.mixed_ref), channel_id=1, source_target_pairs={{0,4},{4,8},{8,12},{12,16},{16,20},{20,24},{24,28},{1,5},{5,9},{9,... | collective-permute-start | bytes 786440 | tf_op jit(solution)/shard_map/ppermute | solution.py:546
  5.1 5.0 %fir_own_rows.1 = (f32[1152,128]{1,0:T(8,128)S(1)}, f32[1224,128]{1,0:T(8,128)S(1)}, f32[2304,128]{1,0:T(8,128)S(1)}, bf16[128,1024]{1,0:T(8,128)(2,1)S(1)}, bf16[3,4096,512]{2,1,0:T(8,128)(2,1)S(1)}) custom-call(bf16[128,1024]{1,0:T(8,128)(2,1)S(1)} %multiply_convert_fusion.mixed_ref, f32[128,1024]{1,0:T(8,128)} %taps_hbm.1, bf16[128,1024]{1,0:T(8,128)(2,1)} %gate_hbm.1, ...), custom_call_target="tpu_custom_call" | custom-call | bytes 1024 | tf_op jit(solution)/shard_map/fir_own_rows/pallas_call | solution.py:194
  10.1 0.0 collective-permute-done.rim_ref
  10.1 0.0 copy-done
  10.1 0.7 %fir_later_rows.1 = (bf16[64,1152]{1,0:T(8,128)(2,1)S(1)}, f32[1152,128]{1,0:T(8,128)S(1)}, f32[72,128]{1,0:T(8,128)S(1)}) custom-call(bf16[128,1024]{1,0:T(8,128)(2,1)S(1)} %collective-permute-done.rim_ref, f32[1224,128]{1,0:T(8,128)S(1)} %get-tuple-element.33.sums_ref, f32[2304,128]{1,0:T(8,128)S(1)} %get-tuple-element.34.tap_subs, ...), custom_call_target="tpu_custom_call" | custom-call | bytes 1024 | tf_op jit(solution)/shard_map/fir_later_rows/pallas_call | solution.py:246
  10.8 1.6 %collective-permute-start.1 = (bf16[64,1152]{1,0:T(8,128)(2,1)S(1)}, bf16[64,1152]{1,0:T(8,128)(2,1)S(1)}, u32[]{:S(2)}, u32[]{:S(2)}) collective-permute-start(bf16[64,1152]{1,0:T(8,128)(2,1)S(1)} %get-tuple-element.36.refs_1_), channel_id=1, source_target_pairs={{0,1},{1,0},{2,3},{3,2},{4,5},{5,4},{6,7},{7,6},{8,9},{9,8},{10,11... | collective-permute-start | bytes 442376 | tf_op jit(solution)/shard_map/ppermute | solution.py:543
  12.3 1.2 %collective-permute-start.5 = (bf16[64,1152]{1,0:T(8,128)(2,1)S(1)}, bf16[64,1152]{1,0:T(8,128)(2,1)S(1)}, u32[]{:S(2)}, u32[]{:S(2)}) collective-permute-start(bf16[64,1152]{1,0:T(8,128)(2,1)S(1)} %get-tuple-element.36.refs_1_), channel_id=1, source_target_pairs={{0,3},{1,2},{2,1},{3,0},{4,7},{5,6},{6,5},{7,4},{8,11},{9,10},{10,... | collective-permute-start | bytes 442376 | tf_op jit(solution)/shard_map/ppermute | solution.py:543
  13.5 0.0 collective-permute-done.1.refs_3_
  13.5 1.5 %fir_earlier_rows.1.refs_0_ = bf16[64,1152]{1,0:T(8,128)(2,1)S(1)} custom-call(bf16[128,1024]{1,0:T(8,128)(2,1)S(1)} %collective-permute-done.rim_ref, f32[1152,128]{1,0:T(8,128)S(1)} %get-tuple-element.38.sums_ref, f32[1152,128]{1,0:T(8,128)S(1)} %get-tuple-element.39.x_high, f32[72,128]{1,0:T(8,128)S(1)} %get-tuple-element.40.last_ref, ...), custom_call_target="tpu_custom_call" | custom-call | bytes 1024 | tf_op jit(solution)/shard_map/fir_earlier_rows/pallas_call | solution.py:300
  15.0 0.5 %collective-permute-start.3 = (bf16[64,1152]{1,0:T(8,128)(2,1)S(1)}, bf16[64,1152]{1,0:T(8,128)(2,1)S(1)}, u32[]{:S(2)}, u32[]{:S(2)}) collective-permute-start(bf16[64,1152]{1,0:T(8,128)(2,1)S(1)} %fir_earlier_rows.1.refs_0_), channel_id=1, source_target_pairs={{0,1},{1,0},{2,3},{3,2},{4,5},{5,4},{6,7},{7,6},{8,9},{9,8},{10,11... | collective-permute-start | bytes 442376 | tf_op jit(solution)/shard_map/ppermute | solution.py:543
  15.5 1.0 %collective-permute-start.2 = (bf16[64,1152]{1,0:T(8,128)(2,1)S(1)}, bf16[64,1152]{1,0:T(8,128)(2,1)S(1)}, u32[]{:S(2)}, u32[]{:S(2)}) collective-permute-start(bf16[64,1152]{1,0:T(8,128)(2,1)S(1)} %fir_earlier_rows.1.refs_0_), channel_id=1, source_target_pairs={{0,3},{1,2},{2,1},{3,0},{4,7},{5,6},{6,5},{7,4},{8,11},{9,10},{10,... | collective-permute-start | bytes 442376 | tf_op jit(solution)/shard_map/ppermute | solution.py:543
  16.5 1.4 %collective-permute-done.5.refs_1_ = bf16[64,1152]{1,0:T(8,128)(2,1)S(1)} collective-permute-done((bf16[64,1152]{1,0:T(8,128)(2,1)S(1)}, bf16[64,1152]{1,0:T(8,128)(2,1)S(1)}, u32[]{:S(2)}, u32[]{:S(2)}) %collective-permute-start.5) | collective-permute-done | bytes 147488 | tf_op jit(solution)/shard_map/ppermute | solution.py:543
  17.9 0.1 collective-permute-start.6
  18.0 0.0 collective-permute-done.3.refs_2_
  18.0 1.0 %projections_part.2 = (f32[128,1536]{1,0:T(8,128)S(1)}, f32[128,128]{1,0:T(8,128)S(1)}) custom-call(bf16[64,1152]{1,0:T(8,128)(2,1)S(1)} %fir_earlier_rows.1.refs_0_, bf16[64,1152]{1,0:T(8,128)(2,1)S(1)} %get-tuple-element.36.refs_1_, bf16[64,1152]{1,0:T(8,128)(2,1)S(1)} %collective-permute-done.3.refs_2_, ...), custom_call_target="tpu_custom_call" | custom-call | bytes 1024 | tf_op jit(solution)/shard_map/projections_part/pallas_call | solution.py:345
  19.0 2.1 %collective-permute-done.2.refs_0_ = bf16[64,1152]{1,0:T(8,128)(2,1)S(1)} collective-permute-done((bf16[64,1152]{1,0:T(8,128)(2,1)S(1)}, bf16[64,1152]{1,0:T(8,128)(2,1)S(1)}, u32[]{:S(2)}, u32[]{:S(2)}) %collective-permute-start.2) | collective-permute-done | bytes 147488 | tf_op jit(solution)/shard_map/ppermute | solution.py:543
  21.1 0.1 collective-permute-start.4
  21.2 0.6 %projections_part.3 = (f32[128,1536]{1,0:T(8,128)S(1)}, f32[128,128]{1,0:T(8,128)S(1)}) custom-call(bf16[64,1152]{1,0:T(8,128)(2,1)S(1)} %collective-permute-done.2.refs_0_, bf16[64,1152]{1,0:T(8,128)(2,1)S(1)} %collective-permute-done.5.refs_1_, bf16[3,4096,512]{2,1,0:T(8,128)(2,1)S(1)} %get-tuple-element.42.refs_4_.refs_2_, ...), custom_call_target="tpu_custom_call" | custom-call | bytes 1024 | tf_op jit(solution)/shard_map/projections_part/pallas_call | solution.py:345
  21.8 0.0 collective-permute-done.6.refs_1_
  21.8 0.7 %collective-permute-done.4.refs_0_ = bf16[64,1152]{1,0:T(8,128)(2,1)S(1)} collective-permute-done((bf16[64,1152]{1,0:T(8,128)(2,1)S(1)}, bf16[64,1152]{1,0:T(8,128)(2,1)S(1)}, u32[]{:S(2)}, u32[]{:S(2)}) %collective-permute-start.4) | collective-permute-done | bytes 147488 | tf_op jit(solution)/shard_map/ppermute | solution.py:543
  22.4 0.7 %projections_last.1 = (bf16[384,128]{1,0:T(8,128)(2,1)S(1)}, bf16[384,128]{1,0:T(8,128)(2,1)S(1)}, bf16[384,128]{1,0:T(8,128)(2,1)S(1)}, bf16[384,128]{1,0:T(8,128)(2,1)S(1)}) custom-call(bf16[64,1152]{1,0:T(8,128)(2,1)S(1)} %collective-permute-done.4.refs_0_, bf16[64,1152]{1,0:T(8,128)(2,1)S(1)} %collective-permute-done.6.refs_1_, ...), custom_call_target="tpu_custom_call" | custom-call | bytes 1024 | tf_op jit(solution)/shard_map/projections_last/pallas_call | solution.py:383
  23.1 0.2 collective-permute-start.9
  23.3 3.4 %collective-permute-start.10 = (bf16[384,128]{1,0:T(8,128)(2,1)S(1)}, bf16[384,128]{1,0:T(8,128)(2,1)S(1)}, u32[]{:S(2)}, u32[]{:S(2)}) collective-permute-start(bf16[384,128]{1,0:T(8,128)(2,1)S(1)} %get-tuple-element.51), channel_id=1, source_target_pairs={{0,9},{1,8},{2,11},{3,10},{4,13},{5,12},{6,15},{7,14},{8,1},{9,0},... | collective-permute-start | bytes 294920 | tf_op jit(solution)/shard_map/ppermute | solution.py:577
  26.7 2.4 %collective-permute-start.11 = (bf16[384,128]{1,0:T(8,128)(2,1)S(1)}, bf16[384,128]{1,0:T(8,128)(2,1)S(1)}, u32[]{:S(2)}, u32[]{:S(2)}) collective-permute-start(bf16[384,128]{1,0:T(8,128)(2,1)S(1)} %get-tuple-element.52), channel_id=1, source_target_pairs={{0,17},{1,16},{2,19},{3,18},{4,21},{5,20},{6,23},{7,22},{8,25},{9,... | collective-permute-start | bytes 294920 | tf_op jit(solution)/shard_map/ppermute | solution.py:577
  29.1 0.0 collective-permute-start.7
  29.1 0.0 collective-permute-done.9.refs_0_
  29.1 0.6 %collective-permute-start.12 = (bf16[256,128]{1,0:T(8,128)(2,1)S(1)}, bf16[256,128]{1,0:T(8,128)(2,1)S(1)}, u32[]{:S(2)}, u32[]{:S(2)}) collective-permute-start(bf16[256,128]{1,0:T(8,128)(2,1)S(1)} %slice.17), channel_id=1, source_target_pairs={{0,4},{4,0},{8,12},{12,8},{16,20},{20,16},{24,28},{28,24},{1,5},{5... | collective-permute-start | bytes 196616 | tf_op jit(solution)/shard_map/ppermute | solution.py:580
  29.7 0.0 collective-permute-done.10.refs_1_
  29.7 1.0 %collective-permute-start.13 = (bf16[256,128]{1,0:T(8,128)(2,1)S(1)}, bf16[256,128]{1,0:T(8,128)(2,1)S(1)}, u32[]{:S(2)}, u32[]{:S(2)}) collective-permute-start(bf16[256,128]{1,0:T(8,128)(2,1)S(1)} %slice.18), channel_id=1, source_target_pairs={{0,4},{4,0},{8,12},{12,8},{16,20},{20,16},{24,28},{28,24},{1,5},{5... | collective-permute-start | bytes 196616 | tf_op jit(solution)/shard_map/ppermute | solution.py:580
  30.7 6.2 %collective-permute-done.11.refs_2_ = bf16[384,128]{1,0:T(8,128)(2,1)S(1)} collective-permute-done((bf16[384,128]{1,0:T(8,128)(2,1)S(1)}, bf16[384,128]{1,0:T(8,128)(2,1)S(1)}, u32[]{:S(2)}, u32[]{:S(2)}) %collective-permute-start.11) | collective-permute-done | bytes 98336 | tf_op jit(solution)/shard_map/ppermute | solution.py:577
  36.9 0.3 collective-permute-start.14
  37.2 0.0 collective-permute-done.7.refs_3_
  37.3 1.2 %collective-permute-start.8 = (bf16[256,128]{1,0:T(8,128)(2,1)S(1)}, bf16[256,128]{1,0:T(8,128)(2,1)S(1)}, u32[]{:S(2)}, u32[]{:S(2)}) collective-permute-start(bf16[256,128]{1,0:T(8,128)(2,1)S(1)} %slice.16), channel_id=1, source_target_pairs={{0,4},{4,0},{8,12},{12,8},{16,20},{20,16},{24,28},{28,24},{1,5},{5... | collective-permute-start | bytes 196616 | tf_op jit(solution)/shard_map/ppermute | solution.py:580
  38.4 0.0 collective-permute-done.12.refs_4_
  38.4 0.0 collective-permute-done.13.refs_5_
  38.4 2.3 %collective-permute-done.14.refs_6_ = bf16[256,128]{1,0:T(8,128)(2,1)S(1)} collective-permute-done((bf16[256,128]{1,0:T(8,128)(2,1)S(1)}, bf16[256,128]{1,0:T(8,128)(2,1)S(1)}, u32[]{:S(2)}, u32[]{:S(2)}) %collective-permute-start.14) | collective-permute-done | bytes 65568 | tf_op jit(solution)/shard_map/ppermute | solution.py:580
  40.8 1.3 %attention_most.1 = (bf16[512,128]{1,0:T(8,128)(2,1)S(1)}, f32[512,128]{1,0:T(8,128)S(1)}, f32[512,128]{1,0:T(8,128)S(1)}, f32[512,128]{1,0:T(8,128)S(1)}) custom-call(bf16[384,128]{1,0:T(8,128)(2,1)S(1)} %collective-permute-done.9.refs_0_, bf16[384,128]{1,0:T(8,128)(2,1)S(1)} %collective-permute-done.10.refs_1_, ...), custom_call_target="tpu_custom_call" | custom-call | bytes 1024 | tf_op jit(solution)/shard_map/attention_most/pallas_call | solution.py:444
  42.1 0.0 collective-permute-done.8.other_ref
  42.1 0.5 %attention_rest.1 = (bf16[128,128]{1,0:T(8,128)(2,1)S(1)}, bf16[128,128]{1,0:T(8,128)(2,1)S(1)}, bf16[128,128]{1,0:T(8,128)(2,1)S(1)}, bf16[128,128]{1,0:T(8,128)(2,1)S(1)}) custom-call(bf16[256,128]{1,0:T(8,128)(2,1)S(1)} %collective-permute-done.8.other_ref, bf16[512,128]{1,0:T(8,128)(2,1)S(1)} %get-tuple-element.53.query_ref, ...), custom_call_target="tpu_custom_call" | custom-call | bytes 1024 | tf_op jit(solution)/shard_map/attention_rest/pallas_call | solution.py:477
  42.6 3.1 %collective-permute-start.15 = (bf16[128,128]{1,0:T(8,128)(2,1)S(1)}, bf16[128,128]{1,0:T(8,128)(2,1)S(1)}, u32[]{:S(2)}, u32[]{:S(2)}) collective-permute-start(bf16[128,128]{1,0:T(8,128)(2,1)S(1)} %get-tuple-element.57), channel_id=1, source_target_pairs={{0,25},{1,24},{2,27},{3,26},{4,29},{5,28},{6,31},{7,30},{8,17},{9,... | collective-permute-start | bytes 98312 | tf_op jit(solution)/shard_map/ppermute | solution.py:577
  45.7 0.0 collective-permute-start.16
  45.7 0.3 collective-permute-start.17
  46.0 1.0 %collective-permute-start.18 = (bf16[128,128]{1,0:T(8,128)(2,1)S(1)}, bf16[128,128]{1,0:T(8,128)(2,1)S(1)}, u32[]{:S(2)}, u32[]{:S(2)}) collective-permute-start(bf16[128,128]{1,0:T(8,128)(2,1)S(1)} %get-tuple-element.60), channel_id=1, source_target_pairs={{0,1},{1,0},{2,3},{3,2},{4,5},{5,4},{6,7},{7,6},{8,9},{9,8},{10,11... | collective-permute-start | bytes 98312 | tf_op jit(solution)/shard_map/ppermute | solution.py:577
  46.9 0.9 %collective-permute-done.15.refs_0_ = bf16[128,128]{1,0:T(8,128)(2,1)S(1)} collective-permute-done((bf16[128,128]{1,0:T(8,128)(2,1)S(1)}, bf16[128,128]{1,0:T(8,128)(2,1)S(1)}, u32[]{:S(2)}, u32[]{:S(2)}) %collective-permute-start.15) | collective-permute-done | bytes 32800 | tf_op jit(solution)/shard_map/ppermute | solution.py:577
  47.8 2.1 %collective-permute-done.16.refs_1_ = bf16[128,128]{1,0:T(8,128)(2,1)S(1)} collective-permute-done((bf16[128,128]{1,0:T(8,128)(2,1)S(1)}, bf16[128,128]{1,0:T(8,128)(2,1)S(1)}, u32[]{:S(2)}, u32[]{:S(2)}) %collective-permute-start.16) | collective-permute-done | bytes 32800 | tf_op jit(solution)/shard_map/ppermute | solution.py:577
  49.9 0.0 collective-permute-done.17.refs_2_
  49.9 0.0 collective-permute-done.18.refs_3_
  49.9 0.7 %join_heads.1 = bf16[128,512]{1,0:T(8,128)(2,1)} custom-call(bf16[128,128]{1,0:T(8,128)(2,1)S(1)} %collective-permute-done.15.refs_0_, bf16[128,128]{1,0:T(8,128)(2,1)S(1)} %collective-permute-done.16.refs_1_, bf16[128,128]{1,0:T(8,128)(2,1)S(1)} %collective-permute-done.17.refs_2_, bf16[128,128]{1,0:T(8,128)(2,1)S(1)} %collective-permute-done.18.refs_3_), custom_call_target="tpu_custom_call" | custom-call | bytes 1024 | tf_op jit(solution)/shard_map/join_heads/pallas_call | solution.py:497
  (4 shorter events, 0.0 us)
Async XLA Ops:
  0.0 10.1 %copy-start = (f32[1024]{0:T(1024)S(1)}, f32[1024]{0:T(1024)}, u32[]{:S(2)}) copy-start(f32[1024]{0:T(1024)} %param.10) | copy-start | bytes 12292
  1.1 9.0 %collective-permute-start = (bf16[128,1024]{1,0:T(8,128)(2,1)S(1)}, bf16[128,1024]{1,0:T(8,128)(2,1)S(1)}, u32[]{:S(2)}, u32[]{:S(2)}) collective-permute-start(bf16[128,1024]{1,0:T(8,128)(2,1)S(1)} %multiply_convert_fusion.mixed_ref), channel_id=1, source_target_pairs={{0,4},{4,8},{8,12},{12,16},{16,20},{20,24},{24,28},{1,5},{5,9},{9,... | collective-permute-start | bytes 786440 | tf_op jit(solution)/shard_map/ppermute | solution.py:546
  10.8 2.7 %collective-permute-start.1 = (bf16[64,1152]{1,0:T(8,128)(2,1)S(1)}, bf16[64,1152]{1,0:T(8,128)(2,1)S(1)}, u32[]{:S(2)}, u32[]{:S(2)}) collective-permute-start(bf16[64,1152]{1,0:T(8,128)(2,1)S(1)} %get-tuple-element.36.refs_1_), channel_id=1, source_target_pairs={{0,1},{1,0},{2,3},{3,2},{4,5},{5,4},{6,7},{7,6},{8,9},{9,8},{10,11... | collective-permute-start | bytes 442376 | tf_op jit(solution)/shard_map/ppermute | solution.py:543
  12.3 5.5 %collective-permute-start.5 = (bf16[64,1152]{1,0:T(8,128)(2,1)S(1)}, bf16[64,1152]{1,0:T(8,128)(2,1)S(1)}, u32[]{:S(2)}, u32[]{:S(2)}) collective-permute-start(bf16[64,1152]{1,0:T(8,128)(2,1)S(1)} %get-tuple-element.36.refs_1_), channel_id=1, source_target_pairs={{0,3},{1,2},{2,1},{3,0},{4,7},{5,6},{6,5},{7,4},{8,11},{9,10},{10,... | collective-permute-start | bytes 442376 | tf_op jit(solution)/shard_map/ppermute | solution.py:543
  15.0 3.0 %collective-permute-start.3 = (bf16[64,1152]{1,0:T(8,128)(2,1)S(1)}, bf16[64,1152]{1,0:T(8,128)(2,1)S(1)}, u32[]{:S(2)}, u32[]{:S(2)}) collective-permute-start(bf16[64,1152]{1,0:T(8,128)(2,1)S(1)} %fir_earlier_rows.1.refs_0_), channel_id=1, source_target_pairs={{0,1},{1,0},{2,3},{3,2},{4,5},{5,4},{6,7},{7,6},{8,9},{9,8},{10,11... | collective-permute-start | bytes 442376 | tf_op jit(solution)/shard_map/ppermute | solution.py:543
  15.5 5.5 %collective-permute-start.2 = (bf16[64,1152]{1,0:T(8,128)(2,1)S(1)}, bf16[64,1152]{1,0:T(8,128)(2,1)S(1)}, u32[]{:S(2)}, u32[]{:S(2)}) collective-permute-start(bf16[64,1152]{1,0:T(8,128)(2,1)S(1)} %fir_earlier_rows.1.refs_0_), channel_id=1, source_target_pairs={{0,3},{1,2},{2,1},{3,0},{4,7},{5,6},{6,5},{7,4},{8,11},{9,10},{10,... | collective-permute-start | bytes 442376 | tf_op jit(solution)/shard_map/ppermute | solution.py:543
  17.9 3.9 %collective-permute-start.6 = (bf16[64,1152]{1,0:T(8,128)(2,1)S(1)}, bf16[64,1152]{1,0:T(8,128)(2,1)S(1)}, u32[]{:S(2)}, u32[]{:S(2)}) collective-permute-start(bf16[64,1152]{1,0:T(8,128)(2,1)S(1)} %collective-permute-done.5.refs_1_), channel_id=1, source_target_pairs={{0,1},{1,0},{2,3},{3,2},{4,5},{5,4},{6,7},{7,6},{8,9},{9,8},{10,11... | collective-permute-start | bytes 442376 | tf_op jit(solution)/shard_map/ppermute | solution.py:543
  21.1 1.4 %collective-permute-start.4 = (bf16[64,1152]{1,0:T(8,128)(2,1)S(1)}, bf16[64,1152]{1,0:T(8,128)(2,1)S(1)}, u32[]{:S(2)}, u32[]{:S(2)}) collective-permute-start(bf16[64,1152]{1,0:T(8,128)(2,1)S(1)} %collective-permute-done.2.refs_0_), channel_id=1, source_target_pairs={{0,1},{1,0},{2,3},{3,2},{4,5},{5,4},{6,7},{7,6},{8,9},{9,8},{10,11... | collective-permute-start | bytes 442376 | tf_op jit(solution)/shard_map/ppermute | solution.py:543
  23.1 6.0 %collective-permute-start.9 = (bf16[384,128]{1,0:T(8,128)(2,1)S(1)}, bf16[384,128]{1,0:T(8,128)(2,1)S(1)}, u32[]{:S(2)}, u32[]{:S(2)}) collective-permute-start(bf16[384,128]{1,0:T(8,128)(2,1)S(1)} %get-tuple-element.50), channel_id=1, source_target_pairs={{0,1},{1,0},{2,3},{3,2},{4,5},{5,4},{6,7},{7,6},{8,9},{9,8},{10,11... | collective-permute-start | bytes 294920 | tf_op jit(solution)/shard_map/ppermute | solution.py:577
  23.3 6.4 %collective-permute-start.10 = (bf16[384,128]{1,0:T(8,128)(2,1)S(1)}, bf16[384,128]{1,0:T(8,128)(2,1)S(1)}, u32[]{:S(2)}, u32[]{:S(2)}) collective-permute-start(bf16[384,128]{1,0:T(8,128)(2,1)S(1)} %get-tuple-element.51), channel_id=1, source_target_pairs={{0,9},{1,8},{2,11},{3,10},{4,13},{5,12},{6,15},{7,14},{8,1},{9,0},... | collective-permute-start | bytes 294920 | tf_op jit(solution)/shard_map/ppermute | solution.py:577
  26.7 10.1 %collective-permute-start.11 = (bf16[384,128]{1,0:T(8,128)(2,1)S(1)}, bf16[384,128]{1,0:T(8,128)(2,1)S(1)}, u32[]{:S(2)}, u32[]{:S(2)}) collective-permute-start(bf16[384,128]{1,0:T(8,128)(2,1)S(1)} %get-tuple-element.52), channel_id=1, source_target_pairs={{0,17},{1,16},{2,19},{3,18},{4,21},{5,20},{6,23},{7,22},{8,25},{9,... | collective-permute-start | bytes 294920 | tf_op jit(solution)/shard_map/ppermute | solution.py:577
  29.1 8.1 %collective-permute-start.7 = (bf16[384,128]{1,0:T(8,128)(2,1)S(1)}, bf16[384,128]{1,0:T(8,128)(2,1)S(1)}, u32[]{:S(2)}, u32[]{:S(2)}) collective-permute-start(bf16[384,128]{1,0:T(8,128)(2,1)S(1)} %get-tuple-element.49), channel_id=1, source_target_pairs={{0,25},{1,24},{2,27},{3,26},{4,29},{5,28},{6,31},{7,30},{8,17},{9,... | collective-permute-start | bytes 294920 | tf_op jit(solution)/shard_map/ppermute | solution.py:577
  29.1 9.3 %collective-permute-start.12 = (bf16[256,128]{1,0:T(8,128)(2,1)S(1)}, bf16[256,128]{1,0:T(8,128)(2,1)S(1)}, u32[]{:S(2)}, u32[]{:S(2)}) collective-permute-start(bf16[256,128]{1,0:T(8,128)(2,1)S(1)} %slice.17), channel_id=1, source_target_pairs={{0,4},{4,0},{8,12},{12,8},{16,20},{20,16},{24,28},{28,24},{1,5},{5... | collective-permute-start | bytes 196616 | tf_op jit(solution)/shard_map/ppermute | solution.py:580
  29.7 8.7 %collective-permute-start.13 = (bf16[256,128]{1,0:T(8,128)(2,1)S(1)}, bf16[256,128]{1,0:T(8,128)(2,1)S(1)}, u32[]{:S(2)}, u32[]{:S(2)}) collective-permute-start(bf16[256,128]{1,0:T(8,128)(2,1)S(1)} %slice.18), channel_id=1, source_target_pairs={{0,4},{4,0},{8,12},{12,8},{16,20},{20,16},{24,28},{28,24},{1,5},{5... | collective-permute-start | bytes 196616 | tf_op jit(solution)/shard_map/ppermute | solution.py:580
  36.9 3.9 %collective-permute-start.14 = (bf16[256,128]{1,0:T(8,128)(2,1)S(1)}, bf16[256,128]{1,0:T(8,128)(2,1)S(1)}, u32[]{:S(2)}, u32[]{:S(2)}) collective-permute-start(bf16[256,128]{1,0:T(8,128)(2,1)S(1)} %slice.19), channel_id=1, source_target_pairs={{0,4},{4,0},{8,12},{12,8},{16,20},{20,16},{24,28},{28,24},{1,5},{5... | collective-permute-start | bytes 196616 | tf_op jit(solution)/shard_map/ppermute | solution.py:580
  37.3 4.8 %collective-permute-start.8 = (bf16[256,128]{1,0:T(8,128)(2,1)S(1)}, bf16[256,128]{1,0:T(8,128)(2,1)S(1)}, u32[]{:S(2)}, u32[]{:S(2)}) collective-permute-start(bf16[256,128]{1,0:T(8,128)(2,1)S(1)} %slice.16), channel_id=1, source_target_pairs={{0,4},{4,0},{8,12},{12,8},{16,20},{20,16},{24,28},{28,24},{1,5},{5... | collective-permute-start | bytes 196616 | tf_op jit(solution)/shard_map/ppermute | solution.py:580
  42.6 5.2 %collective-permute-start.15 = (bf16[128,128]{1,0:T(8,128)(2,1)S(1)}, bf16[128,128]{1,0:T(8,128)(2,1)S(1)}, u32[]{:S(2)}, u32[]{:S(2)}) collective-permute-start(bf16[128,128]{1,0:T(8,128)(2,1)S(1)} %get-tuple-element.57), channel_id=1, source_target_pairs={{0,25},{1,24},{2,27},{3,26},{4,29},{5,28},{6,31},{7,30},{8,17},{9,... | collective-permute-start | bytes 98312 | tf_op jit(solution)/shard_map/ppermute | solution.py:577
  45.7 4.2 %collective-permute-start.16 = (bf16[128,128]{1,0:T(8,128)(2,1)S(1)}, bf16[128,128]{1,0:T(8,128)(2,1)S(1)}, u32[]{:S(2)}, u32[]{:S(2)}) collective-permute-start(bf16[128,128]{1,0:T(8,128)(2,1)S(1)} %get-tuple-element.58), channel_id=1, source_target_pairs={{0,17},{1,16},{2,19},{3,18},{4,21},{5,20},{6,23},{7,22},{8,25},{9,... | collective-permute-start | bytes 98312 | tf_op jit(solution)/shard_map/ppermute | solution.py:577
  45.7 4.2 %collective-permute-start.17 = (bf16[128,128]{1,0:T(8,128)(2,1)S(1)}, bf16[128,128]{1,0:T(8,128)(2,1)S(1)}, u32[]{:S(2)}, u32[]{:S(2)}) collective-permute-start(bf16[128,128]{1,0:T(8,128)(2,1)S(1)} %get-tuple-element.59), channel_id=1, source_target_pairs={{0,9},{1,8},{2,11},{3,10},{4,13},{5,12},{6,15},{7,14},{8,1},{9,0},... | collective-permute-start | bytes 98312 | tf_op jit(solution)/shard_map/ppermute | solution.py:577
  46.0 4.0 %collective-permute-start.18 = (bf16[128,128]{1,0:T(8,128)(2,1)S(1)}, bf16[128,128]{1,0:T(8,128)(2,1)S(1)}, u32[]{:S(2)}, u32[]{:S(2)}) collective-permute-start(bf16[128,128]{1,0:T(8,128)(2,1)S(1)} %get-tuple-element.60), channel_id=1, source_target_pairs={{0,1},{1,0},{2,3},{3,2},{4,5},{5,4},{6,7},{7,6},{8,9},{9,8},{10,11... | collective-permute-start | bytes 98312 | tf_op jit(solution)/shard_map/ppermute | solution.py:577

commit v8 on v7

--- a/solution.py
+++ b/solution.py
@@ -14,6 +14,7 @@
 PHASES = 4
 SUBS = 9
 HELD = 8
+PAD = 16
 EPS = 1e-06
 BF16 = jnp.bfloat16
 F32 = jnp.float32
@@ -123,37 +124,88 @@
     sent_ref[:, SLAB * LANES :] = row.astype(BF16)
 
 
-def own_kernel(
-    mixed_ref,
+def mixed_kernel(
+    conv_hbm,
+    value_hbm,
     taps_hbm,
     gate_hbm,
+    high_ref,
+    low_ref,
+    taps_ref,
+    gate_ref,
+    conv_ref,
+    value_ref,
+    sems,
+):
+    half = high_ref.shape[0]
+    pairs = (
+        (conv_hbm, conv_ref),
+        (value_hbm, value_ref),
+        (taps_hbm, taps_ref),
+        (gate_hbm, gate_ref),
+    )
+    copies = [
+        pltpu.make_async_copy(source, target, sems.at[n])
+        for n, (source, target) in enumerate(pairs)
+    ]
+    for copy in copies:
+        copy.start()
+    for copy in copies[:2]:
+        copy.wait()
+    mixed = (conv_ref[...].astype(F32) * value_ref[...].astype(F32)).astype(BF16)
+    high_ref[...] = mixed[half:, :]
+    low_ref[...] = mixed[: low_ref.shape[0], :]
+    for copy in copies[2:]:
+        copy.wait()
+
+
+def mixed_halves(conv, value, taps, gate):
+    rows, channels = conv.shape
+    half = rows // 2
+    arrays = (conv, value, taps, gate)
+    return pl.pallas_call(
+        mixed_kernel,
+        out_shape=(
+            jax.ShapeDtypeStruct((half, channels), BF16),
+            jax.ShapeDtypeStruct((half + PAD, channels), BF16),
+            jax.ShapeDtypeStruct(taps.shape, F32),
+            jax.ShapeDtypeStruct(gate.shape, BF16),
+        ),
+        in_specs=[HBM] * 4,
+        out_specs=(VMEM,) * 4,
+        scratch_shapes=[
+            pltpu.VMEM(conv.shape, BF16),
+            pltpu.VMEM(conv.shape, BF16),
+            pltpu.SemaphoreType.DMA((4,)),
+        ],
+        compiler_params=params(8),
+        cost_estimate=cost(),
+        name="conv_times_value",
+    )(*(pltpu.with_memory_space_constraint(v, pltpu.HBM) for v in arrays))
+
+
+def own_kernel(
+    low_ref,
+    high_ref,
+    taps_ref,
     weight_hbm,
     sums_low,
     sums_high,
     tap_subs,
-    gate_ref,
     weight_ref,
-    taps_ref,
     slab_ref,
     x_subs,
     sems,
 ):
-    rows, span = mixed_ref.shape[0], taps_ref.shape[0]
-    quarter, eighth = rows // PHASES, rows // PHASES // 2
+    half, span = high_ref.shape[0], taps_ref.shape[0]
+    quarter, eighth = 2 * half // PHASES, half // PHASES
     tap_quarter = span // PHASES
-    blocks = lax.axis_size("tp")
-    channels = weight_ref.shape[1] // blocks
-    copies = [
-        pltpu.make_async_copy(taps_hbm, taps_ref, sems.at[0]),
-        pltpu.make_async_copy(gate_hbm, gate_ref, sems.at[1]),
-    ] + [
-        own_weights(weight_hbm, weight_ref, o, channels, sems.at[2 + o]) for o in range(blocks)
-    ]
+    copies = weight_copies(weight_hbm, weight_ref, (0,), sems)
     for copy in copies:
         copy.start()
-    to_slabs(mixed_ref, slab_ref)
+    to_slabs(low_ref.at[pl.ds(0, half)], slab_ref.at[pl.ds(0, half * SLAB)])
+    to_slabs(high_ref, slab_ref.at[pl.ds(half * SLAB, half * SLAB)])
     to_subs(slab_ref, quarter, x_subs)
-    copies[0].wait()
     to_slabs(taps_ref, slab_ref)
     to_subs(slab_ref, tap_quarter, tap_subs)
 
@@ -174,21 +226,31 @@
         return 0
 
     lax.fori_loop(0, SUBS, sub, 0)
-    for copy in copies[1:]:
+    for copy in copies:
         copy.wait()
 
 
-def own_weights(weight_hbm, weight_ref, offset, channels, sem):
-    owner = jnp.bitwise_xor(lax.axis_index("tp"), offset)
-    return pltpu.make_async_copy(
-        weight_hbm.at[:, pl.ds(pl.multiple_of(owner * channels, channels), channels), :],
-        weight_ref.at[:, pl.ds(offset * channels, channels), :],
-        sem,
-    )
-
-
-def own_part(mixed, taps, gate, weight, tp):
-    rows, span = mixed.shape[0], taps.shape[0]
+def weight_copies(weight_hbm, weight_ref, offsets, sems):
+    copies = []
+    channels = weight_ref.shape[1] // len(offsets)
+    for n, offset in enumerate(offsets):
+        owner = jnp.bitwise_xor(lax.axis_index("tp"), offset)
+        copies.append(
+            pltpu.make_async_copy(
+                weight_hbm.at[:, pl.ds(pl.multiple_of(owner * channels, channels), channels), :],
+                weight_ref.at[:, pl.ds(n * channels, channels), :],
+                sems.at[n],
+            )
+        )
+    return copies
+
+
+def weight_rows(weight, count, channels):
+    return jax.ShapeDtypeStruct((3, count * channels, weight.shape[2]), BF16)
+
+
+def own_part(low, high, taps, weight, channels):
+    rows, span = 2 * high.shape[0], taps.shape[0]
     quarter = rows // PHASES
     eighth = quarter // 2
     return pl.pallas_call(
@@ -197,21 +259,19 @@
             slabs(SUBS * eighth),
             slabs(SUBS * (eighth + 1)),
             slabs(SUBS * span // PHASES),
-            jax.ShapeDtypeStruct(gate.shape, BF16),
-            jax.ShapeDtypeStruct(weight.shape, BF16),
+            weight_rows(weight, 1, channels),
         ),
-        in_specs=[VMEM, HBM, HBM, HBM],
-        out_specs=(VMEM,) * 5,
+        in_specs=[VMEM] * 3 + [HBM],
+        out_specs=(VMEM,) * 4,
         scratch_shapes=[
-            pltpu.VMEM(taps.shape, F32),
             slab_scratch(max(rows, span)),
             slab_scratch(SUBS * quarter),
-            pltpu.SemaphoreType.DMA((2 + tp,)),
+            pltpu.SemaphoreType.DMA((1,)),
         ],
-        compiler_params=params(24),
+        compiler_params=params(16),
         cost_estimate=cost(),
         name="fir_own_rows",
-    )(mixed, *(pltpu.with_memory_space_constraint(v, pltpu.HBM) for v in (taps, gate, weight)))
+    )(low, high, taps, pltpu.with_memory_space_constraint(weight, pltpu.HBM))
 
 
 def high_kernel(
@@ -220,7 +280,7 @@
     rows = sent_ref.shape[0]
     eighth = rows // PHASES
     tap_quarter = tap_subs.shape[0] // SLAB // SUBS
-    to_slabs(rim_ref.at[pl.ds(rows, rows)], slab_ref)
+    to_slabs(rim_ref, slab_ref)
     to_subs(slab_ref, eighth, x_subs)
 
     def sub(s, _):
@@ -241,7 +301,7 @@
 
 
 def high_part(rim, sums, taps, gate, gain):
-    rows = rim.shape[0] // 2
+    rows = rim.shape[0]
     eighth = rows // PHASES
     return pl.pallas_call(
         high_kernel,
@@ -260,6 +320,7 @@
 
 
 def low_kernel(
+    offsets,
     rim_ref,
     sums_ref,
     x_high,
@@ -267,11 +328,17 @@
     tap_subs,
     gate_ref,
     gain_ref,
+    weight_hbm,
     sent_ref,
+    weight_ref,
     slab_ref,
     x_subs,
     z_ref,
+    sems,
 ):
+    copies = weight_copies(weight_hbm, weight_ref, offsets, sems)
+    for copy in copies:
+        copy.start()
     rows = sent_ref.shape[0]
     eighth = rows // PHASES
     tap_quarter = tap_subs.shape[0] // SLAB // SUBS
@@ -292,29 +359,44 @@
     lax.fori_loop(0, SUBS, sub, 0)
     finish(z_ref, eighth, slab_ref)
     emit(slab_ref, gate_ref, 0, gain_ref, sent_ref)
-
-
-def low_part(rim, sums, x_high, last, taps, gate, gain):
-    rows = rim.shape[0] // 2
+    for copy in copies:
+        copy.wait()
+
+
+def low_part(rim, sums, x_high, last, taps, gate, gain, weight, offsets, channels):
+    rows = gate.shape[0] // 2
     eighth = rows // PHASES
     return pl.pallas_call(
-        low_kernel,
-        out_shape=jax.ShapeDtypeStruct((rows, (SLAB + 1) * LANES), BF16),
-        in_specs=[VMEM] * 7,
-        out_specs=VMEM,
+        functools.partial(low_kernel, offsets),
+        out_shape=(
+            jax.ShapeDtypeStruct((rows, (SLAB + 1) * LANES), BF16),
+            weight_rows(weight, len(offsets), channels),
+        ),
+        in_specs=[VMEM] * 7 + [HBM],
+        out_specs=(VMEM, VMEM),
         scratch_shapes=[
             slab_scratch(rows),
             slab_scratch(SUBS * eighth),
             slab_scratch(SUBS * (eighth + 1)),
+            pltpu.SemaphoreType.DMA((len(offsets),)),
         ],
         compiler_params=params(16),
         cost_estimate=cost(),
         name="fir_earlier_rows",
-    )(rim, sums, x_high, last, taps, gate, gain)
-
-
-def project(blocks, places, weight_ref, acc_ref, ssq_ref):
-    width = weight_ref.shape[2]
+    )(
+        rim,
+        sums,
+        x_high,
+        last,
+        taps,
+        gate,
+        gain,
+        pltpu.with_memory_space_constraint(weight, pltpu.HBM),
+    )
+
+
+def project(blocks, weight_refs, acc_ref, ssq_ref):
+    width = weight_refs[0].shape[2]
     whole = [jnp.concatenate([low[...], high[...]], axis=0) for low, high in blocks]
     channels = whole[0].shape[1] - LANES
     for block in whole:
@@ -322,48 +404,95 @@
     for which in range(3):
         lanes = slice(which * width, (which + 1) * width)
         total = acc_ref[:, lanes]
-        for place, block in zip(places, whole):
+        for ref, block in zip(weight_refs, whole):
             total = total + jnp.dot(
                 block[:, :channels],
-                weight_ref[which, place * channels : (place + 1) * channels, :],
+                ref[which],
                 preferred_element_type=F32,
             )
         acc_ref[:, lanes] = total
 
 
-def partial_kernel(places, fresh, *refs):
-    count = len(places)
+def split_rows(weight_ref, count):
+    channels = weight_ref.shape[1] // count
+    return [weight_ref.at[:, pl.ds(n * channels, channels), :] for n in range(count)]
+
+
+def near_kernel(far, last, *refs):
+    blocks = [(refs[0], refs[1]), (refs[2], refs[3])]
+    own_ref, beside_ref, weight_hbm, acc_ref, ssq_ref, far_ref, last_ref, far_sems, last_sems = (
+        refs[4:]
+    )
+    copies = weight_copies(weight_hbm, far_ref, far, far_sems)
+    copies += weight_copies(weight_hbm, last_ref, last, last_sems)
+    for copy in copies:
+        copy.start()
+    acc_ref[...] = jnp.zeros_like(acc_ref)
+    ssq_ref[...] = jnp.zeros_like(ssq_ref)
+    project(blocks, [own_ref, beside_ref], acc_ref, ssq_ref)
+    for copy in copies:
+        copy.wait()
+
+
+def near_projection(mine, beside, own_weight, beside_weight, weight, far, last):
+    rows = 2 * mine[0].shape[0]
+    channels, width = own_weight.shape[1:]
+    return pl.pallas_call(
+        functools.partial(near_kernel, far, last),
+        out_shape=(
+            jax.ShapeDtypeStruct((rows, 3 * width), F32),
+            jax.ShapeDtypeStruct((rows, LANES), F32),
+            weight_rows(weight, len(far), channels),
+            weight_rows(weight, len(last), channels),
+        ),
+        in_specs=[VMEM] * 6 + [HBM],
+        out_specs=(VMEM,) * 4,
+        scratch_shapes=[
+            pltpu.SemaphoreType.DMA((len(far),)),
+            pltpu.SemaphoreType.DMA((len(last),)),
+        ],
+        compiler_params=params(16),
+        cost_estimate=cost(),
+        name="projections_near",
+    )(
+        *mine,
+        *beside,
+        own_weight,
+        beside_weight,
+        pltpu.with_memory_space_constraint(weight, pltpu.HBM),
+    )
+
+
+def partial_kernel(count, *refs):
     blocks = [(refs[2 * n], refs[2 * n + 1]) for n in range(count)]
-    weight_ref, *before, acc_ref, ssq_ref = refs[2 * count :]
-    acc_ref[...] = jnp.zeros_like(acc_ref) if fresh else before[0][...]
-    ssq_ref[...] = jnp.zeros_like(ssq_ref) if fresh else before[1][...]
-    project(blocks, places, weight_ref, acc_ref, ssq_ref)
-
-
-def part_projection(blocks, weight, before=()):
-    rows = 2 * blocks[0][1][0].shape[0]
-    return pl.pallas_call(
-        functools.partial(partial_kernel, tuple(place for place, _ in blocks), not before),
+    weight_ref, acc_in, ssq_in, acc_ref, ssq_ref = refs[2 * count :]
+    acc_ref[...] = acc_in[...]
+    ssq_ref[...] = ssq_in[...]
+    project(blocks, split_rows(weight_ref, count), acc_ref, ssq_ref)
+
+
+def part_projection(blocks, weight, acc, ssq):
+    return pl.pallas_call(
+        functools.partial(partial_kernel, len(blocks)),
         out_shape=(
-            jax.ShapeDtypeStruct((rows, 3 * weight.shape[2]), F32),
-            jax.ShapeDtypeStruct((rows, LANES), F32),
+            jax.ShapeDtypeStruct(acc.shape, F32),
+            jax.ShapeDtypeStruct(ssq.shape, F32),
         ),
-        in_specs=[VMEM] * (2 * len(blocks) + 1 + len(before)),
+        in_specs=[VMEM] * (2 * len(blocks) + 3),
         out_specs=(VMEM,) * 2,
         compiler_params=params(24),
         cost_estimate=cost(),
-        name="projections_part",
-    )(*[half for _, pair in blocks for half in pair], weight, *before)
-
-
-def last_kernel(places, model, spread, *refs):
-    count = len(places)
+        name="projections_far",
+    )(*[half for pair in blocks for half in pair], weight, acc, ssq)
+
+
+def last_kernel(count, model, spread, *refs):
     blocks = [(refs[2 * n], refs[2 * n + 1]) for n in range(count)]
     weight_ref, acc_in, ssq_in = refs[2 * count : 2 * count + 3]
     outs, (acc_ref, ssq_ref) = refs[2 * count + 3 : -2], refs[-2:]
     acc_ref[...] = acc_in[...]
     ssq_ref[...] = ssq_in[...]
-    project(blocks, places, weight_ref, acc_ref, ssq_ref)
+    project(blocks, split_rows(weight_ref, count), acc_ref, ssq_ref)
     msq = jnp.sum(ssq_ref[...], axis=1, keepdims=True) / model
     scale = lax.rsqrt(msq + EPS)
     rows = acc_ref.shape[0]
@@ -381,7 +510,7 @@
     rows = acc.shape[0]
     heads = weight.shape[2] // HEAD_DIM
     return pl.pallas_call(
-        functools.partial(last_kernel, tuple(place for place, _ in blocks), model, spread),
+        functools.partial(last_kernel, len(blocks), model, spread),
         out_shape=tuple(
             jax.ShapeDtypeStruct((3 * rows, HEAD_DIM), BF16) for _ in range(heads)
         ),
@@ -391,7 +520,7 @@
         compiler_params=params(24),
         cost_estimate=cost(),
         name="projections_last",
-    )(*[half for _, pair in blocks for half in pair], weight, acc, ssq)
+    )(*[half for pair in blocks for half in pair], weight, acc, ssq)
 
 
 def base_of(shape, axis, rows, y):
@@ -542,33 +671,44 @@
     def swapped(value, by):
         return lax.ppermute(value, "tp", [(i, i ^ by) for i in range(tp)])
 
-    mixed = (conv_in.astype(F32) * value_in.astype(F32)).astype(BF16)
-    rim = widened(lax.ppermute(mixed, "ctx", [(i, i + 1) for i in range(ctx - 1)]))
+    high, low, taps, gate = mixed_halves(
+        *(widened(v) for v in (conv_in, value_in, filter_taps, gate_in))
+    )
+    rim_high, rim_low = (
+        lax.ppermute(part, "ctx", [(i, i + 1) for i in range(ctx - 1)]) for part in (high, low)
+    )
     gain = widened(norm_gain[None])
-    sums_low, sums_high, taps, gate, weight = own_part(
-        widened(mixed), widened(filter_taps), widened(gate_in), weight, tp
-    )
-    sent_high, x_high, last = high_part(rim, sums_high, taps, gate, gain)
+    sums_low, sums_high, taps, own_weight = own_part(low, high, taps, weight, channels)
+    sent_high, x_high, last = high_part(rim_high, sums_high, taps, gate, gain)
+    steps = [(tp >> n) ^ 1 for n in range(1, tp.bit_length() - 1)]
+    offsets = []
+    for by in steps:
+        offsets += [o ^ by for o in [0] + offsets]
     sent_high = narrowed(sent_high)
     near_high = swapped(sent_high, 1)
-    rim, near_high = lax.optimization_barrier((rim, near_high))
-    sent_low = narrowed(low_part(rim, sums_low, x_high, last, taps, gate, gain))
+    x_high, near_high = lax.optimization_barrier((x_high, near_high))
+    sent_low, beside_weight = low_part(
+        rim_low, sums_low, x_high, last, taps, gate, gain, weight, (1,), channels
+    )
+    sent_low = narrowed(sent_low)
     sent = (sent_low, sent_high)
-
     far = []
-    by = tp // 2
-    while by > 1:
-        far = far + [
-            (o ^ by ^ 1, tuple(swapped(part, by ^ 1) for part in pair))
-            for o, pair in [(0, sent)] + far
-        ]
-        by //= 2
-    acc, ssq = part_projection([(0, sent), (1, (swapped(sent_low, 1), near_high))], weight)
-    last_low, acc = lax.optimization_barrier((far[-1][1][0], acc))
-    far[-1] = (far[-1][0], (last_low, far[-1][1][1]))
-    swaps = [(o ^ 1, tuple(swapped(part, 1) for part in pair)) for o, pair in far]
-    acc, ssq = part_projection(far, weight, (acc, ssq))
-    messages = last_projection(swaps, weight, acc, ssq, model, chip_per_head)
+    for by in steps:
+        far += [tuple(swapped(part, by) for part in pair) for pair in [sent] + far]
+    acc, ssq, far_weight, last_weight = near_projection(
+        sent,
+        (swapped(sent_low, 1), near_high),
+        own_weight,
+        beside_weight,
+        weight,
+        tuple(offsets),
+        tuple(o ^ 1 for o in offsets),
+    )
+    last_low, acc = lax.optimization_barrier((far[-1][0], acc))
+    far[-1] = (last_low, far[-1][1])
+    swaps = [tuple(swapped(part, 1) for part in pair) for pair in far]
+    acc, ssq = part_projection(far, far_weight, acc, ssq)
+    messages = last_projection(swaps, last_weight, acc, ssq, model, chip_per_head)
     if not chip_per_head:
         return gathered_attention(messages[::-1], heads, rows)
 

time: 50.8 us -> 50.2 us (0.988)
  waiting for transfers between devices: 15.6 us -> 12.7 us
  starting transfers between devices: 21.9 us -> 23.7 us
  Pallas kernels: 11.9 us -> 13.4 us
  other arithmetic: 1.11 us -> 0 us
    pallas_call x4 -> x5, Pallas kernels: 3.73 us -> 8.21 us  [the longest x1 3.69 us: near_projection(): pl.pallas_call(functools.partial(near_kernel, far, last), out_shape=(jax....]
    ppermute x1 -> x2, starting transfers between devices: 3.99 us -> 7.13 us  [body(): lax.ppermute(part, 'ctx', [(i, i + 1) for i in range(ctx - 1)])]
    pallas_call x1, Pallas kernels: 4.96 us -> 1.95 us  [own_part(): pl.pallas_call(own_kernel, out_shape=(slabs(SUBS * eighth), slabs(SUBS *...]
    ppermute x6, waiting for transfers between devices: 4.09 us -> 1.3 us  [swapped(): return lax.ppermute(value, 'tp', [(i, i ^ by) for i in range(tp)])]
    ppermute x8, starting transfers between devices: 10.3 us -> 8.76 us  [over_z(): return lax.ppermute(value, ('ctx', 'tp'), pairs)]
    convert_element_type x1 -> x0, other arithmetic: 1.11 us -> none  [body(): mixed = (conv_in.astype(F32) * value_in.astype(F32)).astype(BF16)]
  transfers between devices with their start and end apart: 19 -> 20, of which waited for: 7 -> 6; matrix products, arithmetic and copies ran while one was open for 0% -> 0% of each run, Pallas kernels for 18% -> 20%
where the time goes in v8:
time: 50.2 us; the launch traced here: 50 us
  starting transfers between devices  23.7 us (47%)
  Pallas kernels  13.4 us (27%)
  waiting for transfers between devices  12.7 us (25%)
    ppermute x8, waiting for transfers between devices, over_z(): return lax.ppermute(value, ('ctx', 'tp'), pairs)  9.04 us
    ppermute x8, starting transfers between devices, over_z(): return lax.ppermute(value, ('ctx', 'tp'), pairs)  8.76 us
    ppermute x2, starting transfers between devices, body(): lax.ppermute(part, 'ctx', [(i, i + 1) for i in range(ctx - 1)])  7.13 us
    ppermute x6, starting transfers between devices, swapped(): return lax.ppermute(value, 'tp', [(i, i ^ by) for i in range(tp)])  4.57 us
    pallas_call x1, Pallas kernels, near_projection(): pl.pallas_call(functools.partial(near_kernel, far, last), out_shape=(jax....  3.69 us
    ppermute x4, starting transfers between devices, over_y(): return lax.ppermute(value, 'ctx', [(i, i ^ 1) for i in range(ctx)])  3.26 us
    ppermute x4, waiting for transfers between devices, over_y(): return lax.ppermute(value, 'ctx', [(i, i ^ 1) for i in range(ctx)])  2.32 us
    pallas_call x1, Pallas kernels, own_part(): pl.pallas_call(own_kernel, out_shape=(slabs(SUBS * eighth), slabs(SUBS *...  1.95 us
  transfers between devices with their start and end apart: 20, of which 6 were waited for; matrix products, arithmetic and copies ran while one was open for 0% of the time, Pallas kernels for 20%

profile of v8, /device:TPU:1, one launch (start us, length us, event | category | flops | bytes accessed | tf_op | source)
XLA Modules:
  0.0 50.0 jit_solution(7757857720847963179)
XLA Ops:
  0.0 1.3 %conv_times_value.1 = (bf16[64,1024]{1,0:T(8,128)(2,1)S(1)}, bf16[80,1024]{1,0:T(8,128)(2,1)S(1)}, f32[128,1024]{1,0:T(8,128)S(1)}, bf16[128,1024]{1,0:T(8,128)(2,1)S(1)}) custom-call(bf16[128,1024]{1,0:T(8,128)(2,1)} %conv_hbm.1, bf16[128,1024]{1,0:T(8,128)(2,1)} %value_hbm.1, f32[128,1024]{1,0:T(8,128)} %taps_hbm.1, bf16[128,1024]{1,0:T(8,128)(2,1)} %gate_hbm.1), custom_call_target="tpu_custom_call" | custom-call | bytes 1024 | tf_op jit(solution)/shard_map/conv_times_value/pallas_call | solution.py:166
  1.3 4.0 %collective-permute-start.1 = (bf16[64,1024]{1,0:T(8,128)(2,1)S(1)}, bf16[64,1024]{1,0:T(8,128)(2,1)S(1)}, u32[]{:S(2)}, u32[]{:S(2)}) collective-permute-start(bf16[64,1024]{1,0:T(8,128)(2,1)S(1)} %get-tuple-element.41.high_ref), channel_id=1, source_target_pairs={{0,4},{4,8},{8,12},{12,16},{16,20},{20,24},{24,28},{1,5},{5,9},{9,... | collective-permute-start | bytes 393224 | tf_op jit(solution)/shard_map/ppermute | solution.py:678
  5.3 3.1 %collective-permute-start = (bf16[80,1024]{1,0:T(8,128)(2,1)S(1)}, bf16[80,1024]{1,0:T(8,128)(2,1)S(1)}, u32[]{:S(2)}, u32[]{:S(2)}) collective-permute-start(bf16[80,1024]{1,0:T(8,128)(2,1)S(1)} %get-tuple-element.40.low_ref), channel_id=1, source_target_pairs={{0,4},{4,8},{8,12},{12,16},{16,20},{20,24},{24,28},{1,5},{5,9},{9,... | collective-permute-start | bytes 491528 | tf_op jit(solution)/shard_map/ppermute | solution.py:678
  8.5 0.0 copy-start
  8.5 2.0 %fir_own_rows.1 = (f32[1152,128]{1,0:T(8,128)S(1)}, f32[1224,128]{1,0:T(8,128)S(1)}, f32[2304,128]{1,0:T(8,128)S(1)}, bf16[3,1024,512]{2,1,0:T(8,128)(2,1)S(1)}) custom-call(bf16[80,1024]{1,0:T(8,128)(2,1)S(1)} %get-tuple-element.40.low_ref, bf16[64,1024]{1,0:T(8,128)(2,1)S(1)} %get-tuple-element.41.high_ref, f32[128,1024]{1,0:T(8,128)S(1)} %get-tuple-element.42.taps_ref, ...), custom_call_target="tpu_custom_call" | custom-call | bytes 1024 | tf_op jit(solution)/shard_map/fir_own_rows/pallas_call | solution.py:256
  10.4 0.0 collective-permute-done.1.rim_ref
  10.4 0.0 copy-done
  10.4 0.7 %fir_later_rows.1 = (bf16[64,1152]{1,0:T(8,128)(2,1)S(1)}, f32[1152,128]{1,0:T(8,128)S(1)}, f32[72,128]{1,0:T(8,128)S(1)}) custom-call(bf16[64,1024]{1,0:T(8,128)(2,1)S(1)} %collective-permute-done.1.rim_ref, f32[1224,128]{1,0:T(8,128)S(1)} %get-tuple-element.44.sums_ref, f32[2304,128]{1,0:T(8,128)S(1)} %get-tuple-element.45.tap_subs, ...), custom_call_target="tpu_custom_call" | custom-call | bytes 1024 | tf_op jit(solution)/shard_map/fir_later_rows/pallas_call | solution.py:306
  11.1 1.3 %collective-permute-start.2 = (bf16[64,1152]{1,0:T(8,128)(2,1)S(1)}, bf16[64,1152]{1,0:T(8,128)(2,1)S(1)}, u32[]{:S(2)}, u32[]{:S(2)}) collective-permute-start(bf16[64,1152]{1,0:T(8,128)(2,1)S(1)} %get-tuple-element.48.refs_1_), channel_id=1, source_target_pairs={{0,1},{1,0},{2,3},{3,2},{4,5},{5,4},{6,7},{7,6},{8,9},{9,8},{10,11... | collective-permute-start | bytes 442376 | tf_op jit(solution)/shard_map/ppermute | solution.py:672
  12.4 1.2 %collective-permute-start.6 = (bf16[64,1152]{1,0:T(8,128)(2,1)S(1)}, bf16[64,1152]{1,0:T(8,128)(2,1)S(1)}, u32[]{:S(2)}, u32[]{:S(2)}) collective-permute-start(bf16[64,1152]{1,0:T(8,128)(2,1)S(1)} %get-tuple-element.48.refs_1_), channel_id=1, source_target_pairs={{0,3},{1,2},{2,1},{3,0},{4,7},{5,6},{6,5},{7,4},{8,11},{9,10},{10,... | collective-permute-start | bytes 442376 | tf_op jit(solution)/shard_map/ppermute | solution.py:672
  13.6 0.0 collective-permute-done.2.refs_3_
  13.6 0.0 collective-permute-done.rim_ref
  13.6 2.0 %fir_earlier_rows.1 = (bf16[64,1152]{1,0:T(8,128)(2,1)S(1)}, bf16[3,1024,512]{2,1,0:T(8,128)(2,1)S(1)}) custom-call(bf16[80,1024]{1,0:T(8,128)(2,1)S(1)} %collective-permute-done.rim_ref, f32[1152,128]{1,0:T(8,128)S(1)} %get-tuple-element.43.sums_ref, f32[1152,128]{1,0:T(8,128)S(1)} %get-tuple-element.49.x_high, f32[72,128]{1,0:T(8,128)S(1)} %get-tuple-element.50.last_ref, ...), custom_call_target="tpu_custom_call" | custom-call | bytes 1024 | tf_op jit(solution)/shard_map/fir_earlier_rows/pallas_call | solution.py:369
  15.6 0.5 %collective-permute-start.4 = (bf16[64,1152]{1,0:T(8,128)(2,1)S(1)}, bf16[64,1152]{1,0:T(8,128)(2,1)S(1)}, u32[]{:S(2)}, u32[]{:S(2)}) collective-permute-start(bf16[64,1152]{1,0:T(8,128)(2,1)S(1)} %get-tuple-element.51.refs_0_), channel_id=1, source_target_pairs={{0,1},{1,0},{2,3},{3,2},{4,5},{5,4},{6,7},{7,6},{8,9},{9,8},{10,11... | collective-permute-start | bytes 442376 | tf_op jit(solution)/shard_map/ppermute | solution.py:672
  16.1 1.0 %collective-permute-start.3 = (bf16[64,1152]{1,0:T(8,128)(2,1)S(1)}, bf16[64,1152]{1,0:T(8,128)(2,1)S(1)}, u32[]{:S(2)}, u32[]{:S(2)}) collective-permute-start(bf16[64,1152]{1,0:T(8,128)(2,1)S(1)} %get-tuple-element.51.refs_0_), channel_id=1, source_target_pairs={{0,3},{1,2},{2,1},{3,0},{4,7},{5,6},{6,5},{7,4},{8,11},{9,10},{10,... | collective-permute-start | bytes 442376 | tf_op jit(solution)/shard_map/ppermute | solution.py:672
  17.1 0.9 %collective-permute-done.6.refs_1_ = bf16[64,1152]{1,0:T(8,128)(2,1)S(1)} collective-permute-done((bf16[64,1152]{1,0:T(8,128)(2,1)S(1)}, bf16[64,1152]{1,0:T(8,128)(2,1)S(1)}, u32[]{:S(2)}, u32[]{:S(2)}) %collective-permute-start.6) | collective-permute-done | bytes 147488 | tf_op jit(solution)/shard_map/ppermute | solution.py:672
  18.0 0.1 collective-permute-start.7
  18.1 0.0 collective-permute-done.4.refs_2_
  18.1 3.7 %projections_near.1 = (f32[128,1536]{1,0:T(8,128)S(1)}, f32[128,128]{1,0:T(8,128)S(1)}, bf16[3,1024,512]{2,1,0:T(8,128)(2,1)S(1)}, bf16[3,1024,512]{2,1,0:T(8,128)(2,1)S(1)}) custom-call(bf16[64,1152]{1,0:T(8,128)(2,1)S(1)} %get-tuple-element.51.refs_0_, bf16[64,1152]{1,0:T(8,128)(2,1)S(1)} %get-tuple-element.48.refs_1_, ...), custom_call_target="tpu_custom_call" | custom-call | bytes 1024 | tf_op jit(solution)/shard_map/projections_near/pallas_call | solution.py:440
  21.8 0.0 collective-permute-done.3.refs_0_
  21.8 0.5 collective-permute-start.5
  22.3 0.6 %projections_far.1 = (f32[128,1536]{1,0:T(8,128)S(1)}, f32[128,128]{1,0:T(8,128)S(1)}) custom-call(bf16[64,1152]{1,0:T(8,128)(2,1)S(1)} %collective-permute-done.3.refs_0_, bf16[64,1152]{1,0:T(8,128)(2,1)S(1)} %collective-permute-done.6.refs_1_, bf16[3,1024,512]{2,1,0:T(8,128)(2,1)S(1)} %get-tuple-element.58.refs_2_, ...), custom_call_target="tpu_custom_call" | custom-call | bytes 1024 | tf_op jit(solution)/shard_map/projections_far/pallas_call | solution.py:475
  22.8 0.0 collective-permute-done.7.refs_1_
  22.9 0.4 collective-permute-done.5.refs_0_
  23.3 0.7 %projections_last.1 = (bf16[384,128]{1,0:T(8,128)(2,1)S(1)}, bf16[384,128]{1,0:T(8,128)(2,1)S(1)}, bf16[384,128]{1,0:T(8,128)(2,1)S(1)}, bf16[384,128]{1,0:T(8,128)(2,1)S(1)}) custom-call(bf16[64,1152]{1,0:T(8,128)(2,1)S(1)} %collective-permute-done.5.refs_0_, bf16[64,1152]{1,0:T(8,128)(2,1)S(1)} %collective-permute-done.7.refs_1_, ...), custom_call_target="tpu_custom_call" | custom-call | bytes 1024 | tf_op jit(solution)/shard_map/projections_last/pallas_call | solution.py:512
  24.0 0.4 collective-permute-start.10
  24.4 1.7 %collective-permute-start.11 = (bf16[384,128]{1,0:T(8,128)(2,1)S(1)}, bf16[384,128]{1,0:T(8,128)(2,1)S(1)}, u32[]{:S(2)}, u32[]{:S(2)}) collective-permute-start(bf16[384,128]{1,0:T(8,128)(2,1)S(1)} %get-tuple-element.65), channel_id=1, source_target_pairs={{0,9},{1,8},{2,11},{3,10},{4,13},{5,12},{6,15},{7,14},{8,1},{9,0},... | collective-permute-start | bytes 294920 | tf_op jit(solution)/shard_map/ppermute | solution.py:717
  26.1 2.4 %collective-permute-start.12 = (bf16[384,128]{1,0:T(8,128)(2,1)S(1)}, bf16[384,128]{1,0:T(8,128)(2,1)S(1)}, u32[]{:S(2)}, u32[]{:S(2)}) collective-permute-start(bf16[384,128]{1,0:T(8,128)(2,1)S(1)} %get-tuple-element.66), channel_id=1, source_target_pairs={{0,17},{1,16},{2,19},{3,18},{4,21},{5,20},{6,23},{7,22},{8,25},{9,... | collective-permute-start | bytes 294920 | tf_op jit(solution)/shard_map/ppermute | solution.py:717
  28.4 0.0 collective-permute-start.8
  28.4 0.0 collective-permute-done.10.refs_0_
  28.5 1.1 %collective-permute-start.13 = (bf16[256,128]{1,0:T(8,128)(2,1)S(1)}, bf16[256,128]{1,0:T(8,128)(2,1)S(1)}, u32[]{:S(2)}, u32[]{:S(2)}) collective-permute-start(bf16[256,128]{1,0:T(8,128)(2,1)S(1)} %slice.17), channel_id=1, source_target_pairs={{0,4},{4,0},{8,12},{12,8},{16,20},{20,16},{24,28},{28,24},{1,5},{5... | collective-permute-start | bytes 196616 | tf_op jit(solution)/shard_map/ppermute | solution.py:720
  29.6 0.0 collective-permute-done.11.refs_1_
  29.6 0.6 %collective-permute-start.14 = (bf16[256,128]{1,0:T(8,128)(2,1)S(1)}, bf16[256,128]{1,0:T(8,128)(2,1)S(1)}, u32[]{:S(2)}, u32[]{:S(2)}) collective-permute-start(bf16[256,128]{1,0:T(8,128)(2,1)S(1)} %slice.18), channel_id=1, source_target_pairs={{0,4},{4,0},{8,12},{12,8},{16,20},{20,16},{24,28},{28,24},{1,5},{5... | collective-permute-start | bytes 196616 | tf_op jit(solution)/shard_map/ppermute | solution.py:720
  30.2 6.0 %collective-permute-done.12.refs_2_ = bf16[384,128]{1,0:T(8,128)(2,1)S(1)} collective-permute-done((bf16[384,128]{1,0:T(8,128)(2,1)S(1)}, bf16[384,128]{1,0:T(8,128)(2,1)S(1)}, u32[]{:S(2)}, u32[]{:S(2)}) %collective-permute-start.12) | collective-permute-done | bytes 98336 | tf_op jit(solution)/shard_map/ppermute | solution.py:717
  36.2 0.9 %collective-permute-start.15 = (bf16[256,128]{1,0:T(8,128)(2,1)S(1)}, bf16[256,128]{1,0:T(8,128)(2,1)S(1)}, u32[]{:S(2)}, u32[]{:S(2)}) collective-permute-start(bf16[256,128]{1,0:T(8,128)(2,1)S(1)} %slice.19), channel_id=1, source_target_pairs={{0,4},{4,0},{8,12},{12,8},{16,20},{20,16},{24,28},{28,24},{1,5},{5... | collective-permute-start | bytes 196616 | tf_op jit(solution)/shard_map/ppermute | solution.py:720
  37.2 0.0 collective-permute-done.8.refs_3_
  37.2 0.6 %collective-permute-start.9 = (bf16[256,128]{1,0:T(8,128)(2,1)S(1)}, bf16[256,128]{1,0:T(8,128)(2,1)S(1)}, u32[]{:S(2)}, u32[]{:S(2)}) collective-permute-start(bf16[256,128]{1,0:T(8,128)(2,1)S(1)} %slice.16), channel_id=1, source_target_pairs={{0,4},{4,0},{8,12},{12,8},{16,20},{20,16},{24,28},{28,24},{1,5},{5... | collective-permute-start | bytes 196616 | tf_op jit(solution)/shard_map/ppermute | solution.py:720
  37.8 0.0 collective-permute-done.13.refs_4_
  37.8 0.0 collective-permute-done.14.refs_5_
  37.8 2.3 %collective-permute-done.15.refs_6_ = bf16[256,128]{1,0:T(8,128)(2,1)S(1)} collective-permute-done((bf16[256,128]{1,0:T(8,128)(2,1)S(1)}, bf16[256,128]{1,0:T(8,128)(2,1)S(1)}, u32[]{:S(2)}, u32[]{:S(2)}) %collective-permute-start.15) | collective-permute-done | bytes 65568 | tf_op jit(solution)/shard_map/ppermute | solution.py:720
  40.1 1.3 %attention_most.1 = (bf16[512,128]{1,0:T(8,128)(2,1)S(1)}, f32[512,128]{1,0:T(8,128)S(1)}, f32[512,128]{1,0:T(8,128)S(1)}, f32[512,128]{1,0:T(8,128)S(1)}) custom-call(bf16[384,128]{1,0:T(8,128)(2,1)S(1)} %collective-permute-done.10.refs_0_, bf16[384,128]{1,0:T(8,128)(2,1)S(1)} %collective-permute-done.11.refs_1_, ...), custom_call_target="tpu_custom_call" | custom-call | bytes 1024 | tf_op jit(solution)/shard_map/attention_most/pallas_call | solution.py:573
  41.4 0.0 collective-permute-done.9.other_ref
  41.4 0.5 %attention_rest.1 = (bf16[128,128]{1,0:T(8,128)(2,1)S(1)}, bf16[128,128]{1,0:T(8,128)(2,1)S(1)}, bf16[128,128]{1,0:T(8,128)(2,1)S(1)}, bf16[128,128]{1,0:T(8,128)(2,1)S(1)}) custom-call(bf16[256,128]{1,0:T(8,128)(2,1)S(1)} %collective-permute-done.9.other_ref, bf16[512,128]{1,0:T(8,128)(2,1)S(1)} %get-tuple-element.67.query_ref, ...), custom_call_target="tpu_custom_call" | custom-call | bytes 1024 | tf_op jit(solution)/shard_map/attention_rest/pallas_call | solution.py:606
  42.0 3.1 %collective-permute-start.16 = (bf16[128,128]{1,0:T(8,128)(2,1)S(1)}, bf16[128,128]{1,0:T(8,128)(2,1)S(1)}, u32[]{:S(2)}, u32[]{:S(2)}) collective-permute-start(bf16[128,128]{1,0:T(8,128)(2,1)S(1)} %get-tuple-element.71), channel_id=1, source_target_pairs={{0,25},{1,24},{2,27},{3,26},{4,29},{5,28},{6,31},{7,30},{8,17},{9,... | collective-permute-start | bytes 98312 | tf_op jit(solution)/shard_map/ppermute | solution.py:717
  45.0 0.0 collective-permute-start.17
  45.0 0.3 collective-permute-start.18
  45.3 1.0 %collective-permute-start.19 = (bf16[128,128]{1,0:T(8,128)(2,1)S(1)}, bf16[128,128]{1,0:T(8,128)(2,1)S(1)}, u32[]{:S(2)}, u32[]{:S(2)}) collective-permute-start(bf16[128,128]{1,0:T(8,128)(2,1)S(1)} %get-tuple-element.74), channel_id=1, source_target_pairs={{0,1},{1,0},{2,3},{3,2},{4,5},{5,4},{6,7},{7,6},{8,9},{9,8},{10,11... | collective-permute-start | bytes 98312 | tf_op jit(solution)/shard_map/ppermute | solution.py:717
  46.3 0.9 %collective-permute-done.16.refs_0_ = bf16[128,128]{1,0:T(8,128)(2,1)S(1)} collective-permute-done((bf16[128,128]{1,0:T(8,128)(2,1)S(1)}, bf16[128,128]{1,0:T(8,128)(2,1)S(1)}, u32[]{:S(2)}, u32[]{:S(2)}) %collective-permute-start.16) | collective-permute-done | bytes 32800 | tf_op jit(solution)/shard_map/ppermute | solution.py:717
  47.2 2.1 %collective-permute-done.17.refs_1_ = bf16[128,128]{1,0:T(8,128)(2,1)S(1)} collective-permute-done((bf16[128,128]{1,0:T(8,128)(2,1)S(1)}, bf16[128,128]{1,0:T(8,128)(2,1)S(1)}, u32[]{:S(2)}, u32[]{:S(2)}) %collective-permute-start.17) | collective-permute-done | bytes 32800 | tf_op jit(solution)/shard_map/ppermute | solution.py:717
  49.3 0.0 collective-permute-done.18.refs_2_
  49.3 0.0 collective-permute-done.19.refs_3_
  49.3 0.7 %join_heads.1 = bf16[128,512]{1,0:T(8,128)(2,1)} custom-call(bf16[128,128]{1,0:T(8,128)(2,1)S(1)} %collective-permute-done.16.refs_0_, bf16[128,128]{1,0:T(8,128)(2,1)S(1)} %collective-permute-done.17.refs_1_, bf16[128,128]{1,0:T(8,128)(2,1)S(1)} %collective-permute-done.18.refs_2_, bf16[128,128]{1,0:T(8,128)(2,1)S(1)} %collective-permute-done.19.refs_3_), custom_call_target="tpu_custom_call" | custom-call | bytes 1024 | tf_op jit(solution)/shard_map/join_heads/pallas_call | solution.py:626
  (4 shorter events, 0.0 us)
Async XLA Ops:
  1.3 9.1 %collective-permute-start.1 = (bf16[64,1024]{1,0:T(8,128)(2,1)S(1)}, bf16[64,1024]{1,0:T(8,128)(2,1)S(1)}, u32[]{:S(2)}, u32[]{:S(2)}) collective-permute-start(bf16[64,1024]{1,0:T(8,128)(2,1)S(1)} %get-tuple-element.41.high_ref), channel_id=1, source_target_pairs={{0,4},{4,8},{8,12},{12,16},{16,20},{20,24},{24,28},{1,5},{5,9},{9,... | collective-permute-start | bytes 393224 | tf_op jit(solution)/shard_map/ppermute | solution.py:678
  5.3 8.3 %collective-permute-start = (bf16[80,1024]{1,0:T(8,128)(2,1)S(1)}, bf16[80,1024]{1,0:T(8,128)(2,1)S(1)}, u32[]{:S(2)}, u32[]{:S(2)}) collective-permute-start(bf16[80,1024]{1,0:T(8,128)(2,1)S(1)} %get-tuple-element.40.low_ref), channel_id=1, source_target_pairs={{0,4},{4,8},{8,12},{12,16},{16,20},{20,24},{24,28},{1,5},{5,9},{9,... | collective-permute-start | bytes 491528 | tf_op jit(solution)/shard_map/ppermute | solution.py:678
  8.5 2.0 %copy-start = (f32[1024]{0:T(1024)S(1)}, f32[1024]{0:T(1024)}, u32[]{:S(2)}) copy-start(f32[1024]{0:T(1024)} %param.10) | copy-start | bytes 12292
  11.1 2.5 %collective-permute-start.2 = (bf16[64,1152]{1,0:T(8,128)(2,1)S(1)}, bf16[64,1152]{1,0:T(8,128)(2,1)S(1)}, u32[]{:S(2)}, u32[]{:S(2)}) collective-permute-start(bf16[64,1152]{1,0:T(8,128)(2,1)S(1)} %get-tuple-element.48.refs_1_), channel_id=1, source_target_pairs={{0,1},{1,0},{2,3},{3,2},{4,5},{5,4},{6,7},{7,6},{8,9},{9,8},{10,11... | collective-permute-start | bytes 442376 | tf_op jit(solution)/shard_map/ppermute | solution.py:672
  12.4 5.5 %collective-permute-start.6 = (bf16[64,1152]{1,0:T(8,128)(2,1)S(1)}, bf16[64,1152]{1,0:T(8,128)(2,1)S(1)}, u32[]{:S(2)}, u32[]{:S(2)}) collective-permute-start(bf16[64,1152]{1,0:T(8,128)(2,1)S(1)} %get-tuple-element.48.refs_1_), channel_id=1, source_target_pairs={{0,3},{1,2},{2,1},{3,0},{4,7},{5,6},{6,5},{7,4},{8,11},{9,10},{10,... | collective-permute-start | bytes 442376 | tf_op jit(solution)/shard_map/ppermute | solution.py:672
  15.6 2.5 %collective-permute-start.4 = (bf16[64,1152]{1,0:T(8,128)(2,1)S(1)}, bf16[64,1152]{1,0:T(8,128)(2,1)S(1)}, u32[]{:S(2)}, u32[]{:S(2)}) collective-permute-start(bf16[64,1152]{1,0:T(8,128)(2,1)S(1)} %get-tuple-element.51.refs_0_), channel_id=1, source_target_pairs={{0,1},{1,0},{2,3},{3,2},{4,5},{5,4},{6,7},{7,6},{8,9},{9,8},{10,11... | collective-permute-start | bytes 442376 | tf_op jit(solution)/shard_map/ppermute | solution.py:672
  16.1 5.7 %collective-permute-start.3 = (bf16[64,1152]{1,0:T(8,128)(2,1)S(1)}, bf16[64,1152]{1,0:T(8,128)(2,1)S(1)}, u32[]{:S(2)}, u32[]{:S(2)}) collective-permute-start(bf16[64,1152]{1,0:T(8,128)(2,1)S(1)} %get-tuple-element.51.refs_0_), channel_id=1, source_target_pairs={{0,3},{1,2},{2,1},{3,0},{4,7},{5,6},{6,5},{7,4},{8,11},{9,10},{10,... | collective-permute-start | bytes 442376 | tf_op jit(solution)/shard_map/ppermute | solution.py:672
  18.0 4.9 %collective-permute-start.7 = (bf16[64,1152]{1,0:T(8,128)(2,1)S(1)}, bf16[64,1152]{1,0:T(8,128)(2,1)S(1)}, u32[]{:S(2)}, u32[]{:S(2)}) collective-permute-start(bf16[64,1152]{1,0:T(8,128)(2,1)S(1)} %collective-permute-done.6.refs_1_), channel_id=1, source_target_pairs={{0,1},{1,0},{2,3},{3,2},{4,5},{5,4},{6,7},{7,6},{8,9},{9,8},{10,11... | collective-permute-start | bytes 442376 | tf_op jit(solution)/shard_map/ppermute | solution.py:672
  21.8 1.5 %collective-permute-start.5 = (bf16[64,1152]{1,0:T(8,128)(2,1)S(1)}, bf16[64,1152]{1,0:T(8,128)(2,1)S(1)}, u32[]{:S(2)}, u32[]{:S(2)}) collective-permute-start(bf16[64,1152]{1,0:T(8,128)(2,1)S(1)} %collective-permute-done.3.refs_0_), channel_id=1, source_target_pairs={{0,1},{1,0},{2,3},{3,2},{4,5},{5,4},{6,7},{7,6},{8,9},{9,8},{10,11... | collective-permute-start | bytes 442376 | tf_op jit(solution)/shard_map/ppermute | solution.py:672
  24.0 4.5 %collective-permute-start.10 = (bf16[384,128]{1,0:T(8,128)(2,1)S(1)}, bf16[384,128]{1,0:T(8,128)(2,1)S(1)}, u32[]{:S(2)}, u32[]{:S(2)}) collective-permute-start(bf16[384,128]{1,0:T(8,128)(2,1)S(1)} %get-tuple-element.64), channel_id=1, source_target_pairs={{0,1},{1,0},{2,3},{3,2},{4,5},{5,4},{6,7},{7,6},{8,9},{9,8},{10,11... | collective-permute-start | bytes 294920 | tf_op jit(solution)/shard_map/ppermute | solution.py:717
  24.4 5.2 %collective-permute-start.11 = (bf16[384,128]{1,0:T(8,128)(2,1)S(1)}, bf16[384,128]{1,0:T(8,128)(2,1)S(1)}, u32[]{:S(2)}, u32[]{:S(2)}) collective-permute-start(bf16[384,128]{1,0:T(8,128)(2,1)S(1)} %get-tuple-element.65), channel_id=1, source_target_pairs={{0,9},{1,8},{2,11},{3,10},{4,13},{5,12},{6,15},{7,14},{8,1},{9,0},... | collective-permute-start | bytes 294920 | tf_op jit(solution)/shard_map/ppermute | solution.py:717
  26.1 10.1 %collective-permute-start.12 = (bf16[384,128]{1,0:T(8,128)(2,1)S(1)}, bf16[384,128]{1,0:T(8,128)(2,1)S(1)}, u32[]{:S(2)}, u32[]{:S(2)}) collective-permute-start(bf16[384,128]{1,0:T(8,128)(2,1)S(1)} %get-tuple-element.66), channel_id=1, source_target_pairs={{0,17},{1,16},{2,19},{3,18},{4,21},{5,20},{6,23},{7,22},{8,25},{9,... | collective-permute-start | bytes 294920 | tf_op jit(solution)/shard_map/ppermute | solution.py:717
  28.4 8.7 %collective-permute-start.8 = (bf16[384,128]{1,0:T(8,128)(2,1)S(1)}, bf16[384,128]{1,0:T(8,128)(2,1)S(1)}, u32[]{:S(2)}, u32[]{:S(2)}) collective-permute-start(bf16[384,128]{1,0:T(8,128)(2,1)S(1)} %get-tuple-element.63), channel_id=1, source_target_pairs={{0,25},{1,24},{2,27},{3,26},{4,29},{5,28},{6,31},{7,30},{8,17},{9,... | collective-permute-start | bytes 294920 | tf_op jit(solution)/shard_map/ppermute | solution.py:717
  28.5 9.3 %collective-permute-start.13 = (bf16[256,128]{1,0:T(8,128)(2,1)S(1)}, bf16[256,128]{1,0:T(8,128)(2,1)S(1)}, u32[]{:S(2)}, u32[]{:S(2)}) collective-permute-start(bf16[256,128]{1,0:T(8,128)(2,1)S(1)} %slice.17), channel_id=1, source_target_pairs={{0,4},{4,0},{8,12},{12,8},{16,20},{20,16},{24,28},{28,24},{1,5},{5... | collective-permute-start | bytes 196616 | tf_op jit(solution)/shard_map/ppermute | solution.py:720
  29.6 8.2 %collective-permute-start.14 = (bf16[256,128]{1,0:T(8,128)(2,1)S(1)}, bf16[256,128]{1,0:T(8,128)(2,1)S(1)}, u32[]{:S(2)}, u32[]{:S(2)}) collective-permute-start(bf16[256,128]{1,0:T(8,128)(2,1)S(1)} %slice.18), channel_id=1, source_target_pairs={{0,4},{4,0},{8,12},{12,8},{16,20},{20,16},{24,28},{28,24},{1,5},{5... | collective-permute-start | bytes 196616 | tf_op jit(solution)/shard_map/ppermute | solution.py:720
  36.2 3.9 %collective-permute-start.15 = (bf16[256,128]{1,0:T(8,128)(2,1)S(1)}, bf16[256,128]{1,0:T(8,128)(2,1)S(1)}, u32[]{:S(2)}, u32[]{:S(2)}) collective-permute-start(bf16[256,128]{1,0:T(8,128)(2,1)S(1)} %slice.19), channel_id=1, source_target_pairs={{0,4},{4,0},{8,12},{12,8},{16,20},{20,16},{24,28},{28,24},{1,5},{5... | collective-permute-start | bytes 196616 | tf_op jit(solution)/shard_map/ppermute | solution.py:720
  37.2 4.2 %collective-permute-start.9 = (bf16[256,128]{1,0:T(8,128)(2,1)S(1)}, bf16[256,128]{1,0:T(8,128)(2,1)S(1)}, u32[]{:S(2)}, u32[]{:S(2)}) collective-permute-start(bf16[256,128]{1,0:T(8,128)(2,1)S(1)} %slice.16), channel_id=1, source_target_pairs={{0,4},{4,0},{8,12},{12,8},{16,20},{20,16},{24,28},{28,24},{1,5},{5... | collective-permute-start | bytes 196616 | tf_op jit(solution)/shard_map/ppermute | solution.py:720
  42.0 5.2 %collective-permute-start.16 = (bf16[128,128]{1,0:T(8,128)(2,1)S(1)}, bf16[128,128]{1,0:T(8,128)(2,1)S(1)}, u32[]{:S(2)}, u32[]{:S(2)}) collective-permute-start(bf16[128,128]{1,0:T(8,128)(2,1)S(1)} %get-tuple-element.71), channel_id=1, source_target_pairs={{0,25},{1,24},{2,27},{3,26},{4,29},{5,28},{6,31},{7,30},{8,17},{9,... | collective-permute-start | bytes 98312 | tf_op jit(solution)/shard_map/ppermute | solution.py:717
  45.0 4.2 %collective-permute-start.17 = (bf16[128,128]{1,0:T(8,128)(2,1)S(1)}, bf16[128,128]{1,0:T(8,128)(2,1)S(1)}, u32[]{:S(2)}, u32[]{:S(2)}) collective-permute-start(bf16[128,128]{1,0:T(8,128)(2,1)S(1)} %get-tuple-element.72), channel_id=1, source_target_pairs={{0,17},{1,16},{2,19},{3,18},{4,21},{5,20},{6,23},{7,22},{8,25},{9,... | collective-permute-start | bytes 98312 | tf_op jit(solution)/shard_map/ppermute | solution.py:717
  45.0 4.2 %collective-permute-start.18 = (bf16[128,128]{1,0:T(8,128)(2,1)S(1)}, bf16[128,128]{1,0:T(8,128)(2,1)S(1)}, u32[]{:S(2)}, u32[]{:S(2)}) collective-permute-start(bf16[128,128]{1,0:T(8,128)(2,1)S(1)} %get-tuple-element.73), channel_id=1, source_target_pairs={{0,9},{1,8},{2,11},{3,10},{4,13},{5,12},{6,15},{7,14},{8,1},{9,0},... | collective-permute-start | bytes 98312 | tf_op jit(solution)/shard_map/ppermute | solution.py:717
  45.3 4.0 %collective-permute-start.19 = (bf16[128,128]{1,0:T(8,128)(2,1)S(1)}, bf16[128,128]{1,0:T(8,128)(2,1)S(1)}, u32[]{:S(2)}, u32[]{:S(2)}) collective-permute-start(bf16[128,128]{1,0:T(8,128)(2,1)S(1)} %get-tuple-element.74), channel_id=1, source_target_pairs={{0,1},{1,0},{2,3},{3,2},{4,5},{5,4},{6,7},{7,6},{8,9},{9,8},{10,11... | collective-permute-start | bytes 98312 | tf_op jit(solution)/shard_map/ppermute | solution.py:717

commit v9 on v8

--- a/solution.py
+++ b/solution.py
@@ -14,7 +14,6 @@
 PHASES = 4
 SUBS = 9
 HELD = 8
-PAD = 16
 EPS = 1e-06
 BF16 = jnp.bfloat16
 F32 = jnp.float32
@@ -97,7 +96,7 @@
         before = now
 
 
-def emit(full_ref, gate_ref, first, gain_ref, sent_ref):
+def emit(full_ref, gate_ref, first, gain_ref, sent_ref, first_half, second_half):
     rows = sent_ref.shape[0]
     squares = jnp.zeros((rows, LANES), F32)
     for group in range(SLAB):
@@ -122,6 +121,8 @@
     for place, piece in enumerate(pieces):
         row = jnp.where(lane == place, piece, row)
     sent_ref[:, SLAB * LANES :] = row.astype(BF16)
+    first_half[...] = sent_ref[: rows // 2, :]
+    second_half[...] = sent_ref[rows // 2 :, :]
 
 
 def mixed_kernel(
@@ -167,7 +168,7 @@
         mixed_kernel,
         out_shape=(
             jax.ShapeDtypeStruct((half, channels), BF16),
-            jax.ShapeDtypeStruct((half + PAD, channels), BF16),
+            jax.ShapeDtypeStruct((half, channels), BF16),
             jax.ShapeDtypeStruct(taps.shape, F32),
             jax.ShapeDtypeStruct(gate.shape, BF16),
         ),
@@ -275,7 +276,18 @@
 
 
 def high_kernel(
-    rim_ref, sums_ref, tap_subs, gate_ref, gain_ref, sent_ref, x_subs, last_ref, slab_ref, z_ref
+    rim_ref,
+    sums_ref,
+    tap_subs,
+    gate_ref,
+    gain_ref,
+    sent_ref,
+    first_ref,
+    second_ref,
+    x_subs,
+    last_ref,
+    slab_ref,
+    z_ref,
 ):
     rows = sent_ref.shape[0]
     eighth = rows // PHASES
@@ -297,7 +309,14 @@
 
     lax.fori_loop(0, SUBS, sub, 0)
     finish(z_ref, eighth, slab_ref)
-    emit(slab_ref, gate_ref, rows, gain_ref, sent_ref)
+    emit(slab_ref, gate_ref, rows, gain_ref, sent_ref, first_ref, second_ref)
+
+
+def sent_shapes(rows):
+    return tuple(
+        jax.ShapeDtypeStruct((length, (SLAB + 1) * LANES), BF16)
+        for length in (rows, rows // 2, rows // 2)
+    )
 
 
 def high_part(rim, sums, taps, gate, gain):
@@ -305,13 +324,9 @@
     eighth = rows // PHASES
     return pl.pallas_call(
         high_kernel,
-        out_shape=(
-            jax.ShapeDtypeStruct((rows, (SLAB + 1) * LANES), BF16),
-            slabs(SUBS * eighth),
-            slabs(SUBS),
-        ),
+        out_shape=sent_shapes(rows) + (slabs(SUBS * eighth), slabs(SUBS)),
         in_specs=[VMEM] * 5,
-        out_specs=(VMEM,) * 3,
+        out_specs=(VMEM,) * 5,
         scratch_shapes=[slab_scratch(rows), slab_scratch(SUBS * (eighth + 1))],
         compiler_params=params(16),
         cost_estimate=cost(),
@@ -330,6 +345,8 @@
     gain_ref,
     weight_hbm,
     sent_ref,
+    first_ref,
+    second_ref,
     weight_ref,
     slab_ref,
     x_subs,
@@ -358,7 +375,7 @@
 
     lax.fori_loop(0, SUBS, sub, 0)
     finish(z_ref, eighth, slab_ref)
-    emit(slab_ref, gate_ref, 0, gain_ref, sent_ref)
+    emit(slab_ref, gate_ref, 0, gain_ref, sent_ref, first_ref, second_ref)
     for copy in copies:
         copy.wait()
 
@@ -368,12 +385,9 @@
     eighth = rows // PHASES
     return pl.pallas_call(
         functools.partial(low_kernel, offsets),
-        out_shape=(
-            jax.ShapeDtypeStruct((rows, (SLAB + 1) * LANES), BF16),
-            weight_rows(weight, len(offsets), channels),
-        ),
+        out_shape=sent_shapes(rows) + (weight_rows(weight, len(offsets), channels),),
         in_specs=[VMEM] * 7 + [HBM],
-        out_specs=(VMEM, VMEM),
+        out_specs=(VMEM,) * 4,
         scratch_shapes=[
             slab_scratch(rows),
             slab_scratch(SUBS * eighth),
@@ -397,7 +411,7 @@
 
 def project(blocks, weight_refs, acc_ref, ssq_ref):
     width = weight_refs[0].shape[2]
-    whole = [jnp.concatenate([low[...], high[...]], axis=0) for low, high in blocks]
+    whole = [jnp.concatenate([piece[...] for piece in pieces], axis=0) for pieces in blocks]
     channels = whole[0].shape[1] - LANES
     for block in whole:
         ssq_ref[...] += block[:, channels:].astype(F32)
@@ -418,23 +432,20 @@
     return [weight_ref.at[:, pl.ds(n * channels, channels), :] for n in range(count)]
 
 
-def near_kernel(far, last, *refs):
-    blocks = [(refs[0], refs[1]), (refs[2], refs[3])]
-    own_ref, beside_ref, weight_hbm, acc_ref, ssq_ref, far_ref, last_ref, far_sems, last_sems = (
-        refs[4:]
-    )
+def near_kernel(far, last, low_ref, high_ref, own_ref, weight_hbm, *refs):
+    acc_ref, ssq_ref, far_ref, last_ref, far_sems, last_sems = refs
     copies = weight_copies(weight_hbm, far_ref, far, far_sems)
     copies += weight_copies(weight_hbm, last_ref, last, last_sems)
     for copy in copies:
         copy.start()
     acc_ref[...] = jnp.zeros_like(acc_ref)
     ssq_ref[...] = jnp.zeros_like(ssq_ref)
-    project(blocks, [own_ref, beside_ref], acc_ref, ssq_ref)
+    project([(low_ref, high_ref)], [own_ref], acc_ref, ssq_ref)
     for copy in copies:
         copy.wait()
 
 
-def near_projection(mine, beside, own_weight, beside_weight, weight, far, last):
+def near_projection(mine, own_weight, weight, far, last):
     rows = 2 * mine[0].shape[0]
     channels, width = own_weight.shape[1:]
     return pl.pallas_call(
@@ -445,7 +456,7 @@
             weight_rows(weight, len(far), channels),
             weight_rows(weight, len(last), channels),
         ),
-        in_specs=[VMEM] * 6 + [HBM],
+        in_specs=[VMEM] * 3 + [HBM],
         out_specs=(VMEM,) * 4,
         scratch_shapes=[
             pltpu.SemaphoreType.DMA((len(far),)),
@@ -454,36 +465,34 @@
         compiler_params=params(16),
         cost_estimate=cost(),
         name="projections_near",
-    )(
-        *mine,
-        *beside,
-        own_weight,
-        beside_weight,
-        pltpu.with_memory_space_constraint(weight, pltpu.HBM),
-    )
-
-
-def partial_kernel(count, *refs):
-    blocks = [(refs[2 * n], refs[2 * n + 1]) for n in range(count)]
-    weight_ref, acc_in, ssq_in, acc_ref, ssq_ref = refs[2 * count :]
+    )(*mine, own_weight, pltpu.with_memory_space_constraint(weight, pltpu.HBM))
+
+
+def partial_kernel(sizes, *refs):
+    blocks, rest = [], list(refs)
+    for size in sizes:
+        blocks.append(rest[:size])
+        del rest[:size]
+    weight_ref, acc_in, ssq_in, acc_ref, ssq_ref = rest
     acc_ref[...] = acc_in[...]
     ssq_ref[...] = ssq_in[...]
-    project(blocks, split_rows(weight_ref, count), acc_ref, ssq_ref)
+    project(blocks, split_rows(weight_ref, len(blocks)), acc_ref, ssq_ref)
 
 
 def part_projection(blocks, weight, acc, ssq):
-    return pl.pallas_call(
-        functools.partial(partial_kernel, len(blocks)),
+    sizes = tuple(len(pieces) for pieces in blocks)
+    return pl.pallas_call(
+        functools.partial(partial_kernel, sizes),
         out_shape=(
             jax.ShapeDtypeStruct(acc.shape, F32),
             jax.ShapeDtypeStruct(ssq.shape, F32),
         ),
-        in_specs=[VMEM] * (2 * len(blocks) + 3),
+        in_specs=[VMEM] * (sum(sizes) + 3),
         out_specs=(VMEM,) * 2,
         compiler_params=params(24),
         cost_estimate=cost(),
-        name="projections_far",
-    )(*[half for pair in blocks for half in pair], weight, acc, ssq)
+        name="projections_part",
+    )(*[piece for pieces in blocks for piece in pieces], weight, acc, ssq)
 
 
 def last_kernel(count, model, spread, *refs):
@@ -679,31 +688,27 @@
     )
     gain = widened(norm_gain[None])
     sums_low, sums_high, taps, own_weight = own_part(low, high, taps, weight, channels)
-    sent_high, x_high, last = high_part(rim_high, sums_high, taps, gate, gain)
+    *high, x_high, last = high_part(rim_high, sums_high, taps, gate, gain)
     steps = [(tp >> n) ^ 1 for n in range(1, tp.bit_length() - 1)]
     offsets = []
     for by in steps:
         offsets += [o ^ by for o in [0] + offsets]
-    sent_high = narrowed(sent_high)
-    near_high = swapped(sent_high, 1)
-    x_high, near_high = lax.optimization_barrier((x_high, near_high))
-    sent_low, beside_weight = low_part(
+    sent_high, *halves = map(narrowed, high)
+    near_high = [swapped(half, 1) for half in halves]
+    x_high, near_high[0] = lax.optimization_barrier((x_high, near_high[0]))
+    *low, beside_weight = low_part(
         rim_low, sums_low, x_high, last, taps, gate, gain, weight, (1,), channels
     )
-    sent_low = narrowed(sent_low)
+    sent_low, *halves = map(narrowed, low)
+    near_low = [swapped(half, 1) for half in halves]
     sent = (sent_low, sent_high)
     far = []
     for by in steps:
         far += [tuple(swapped(part, by) for part in pair) for pair in [sent] + far]
     acc, ssq, far_weight, last_weight = near_projection(
-        sent,
-        (swapped(sent_low, 1), near_high),
-        own_weight,
-        beside_weight,
-        weight,
-        tuple(offsets),
-        tuple(o ^ 1 for o in offsets),
-    )
+        sent, own_weight, weight, tuple(offsets), tuple(o ^ 1 for o in offsets)
+    )
+    acc, ssq = part_projection([near_low + near_high], beside_weight, acc, ssq)
     last_low, acc = lax.optimization_barrier((far[-1][0], acc))
     far[-1] = (last_low, far[-1][1])
     swaps = [tuple(swapped(part, 1) for part in pair) for pair in far]

time: 50.2 us -> 49.8 us (level)
  waiting for transfers between devices: 12.7 us -> 11.8 us
  starting transfers between devices: 23.7 us -> 24.4 us
    pallas_call x1, Pallas kernels: 3.69 us -> 2.88 us  [near_projection(): pl.pallas_call(functools.partial(near_kernel, far, last), out_shape=(jax....]
    ppermute x6 -> x8, waiting for transfers between devices: 1.3 us -> 0.6 us  [swapped(): return lax.ppermute(value, 'tp', [(i, i ^ by) for i in range(tp)])]
    ppermute x6 -> x8, starting transfers between devices: 4.57 us -> 5.2 us  [swapped(): return lax.ppermute(value, 'tp', [(i, i ^ by) for i in range(tp)])]
    pallas_call x3 -> x4, Pallas kernels: 3.21 us -> 3.82 us  [the longest x1 1.95 us: low_part(): pl.pallas_call(functools.partial(low_kernel, offsets), out_shape=sent_sha...]
  transfers between devices with their start and end apart: 20 -> 22, of which waited for: 6 -> 6; matrix products, arithmetic and copies ran while one was open for 0% -> 0% of each run, Pallas kernels for 20% -> 20%
where the time goes in v9:
time: 49.8 us; the launch traced here: 49.6 us
  starting transfers between devices  24.4 us (49%)
  Pallas kernels  13.2 us (27%)
  waiting for transfers between devices  11.8 us (24%)
    ppermute x8, waiting for transfers between devices, over_z(): return lax.ppermute(value, ('ctx', 'tp'), pairs)  8.96 us
    ppermute x8, starting transfers between devices, over_z(): return lax.ppermute(value, ('ctx', 'tp'), pairs)  8.74 us
    ppermute x2, starting transfers between devices, body(): lax.ppermute(part, 'ctx', [(i, i + 1) for i in range(ctx - 1)])  7.13 us
    ppermute x8, starting transfers between devices, swapped(): return lax.ppermute(value, 'tp', [(i, i ^ by) for i in range(tp)])  5.2 us
    ppermute x4, starting transfers between devices, over_y(): return lax.ppermute(value, 'ctx', [(i, i ^ 1) for i in range(ctx)])  3.29 us
    pallas_call x1, Pallas kernels, near_projection(): pl.pallas_call(functools.partial(near_kernel, far, last), out_shape=(jax....  2.88 us
    ppermute x4, waiting for transfers between devices, over_y(): return lax.ppermute(value, 'ctx', [(i, i ^ 1) for i in range(ctx)])  2.29 us
    pallas_call x1, Pallas kernels, low_part(): pl.pallas_call(functools.partial(low_kernel, offsets), out_shape=sent_sha...  1.95 us
  transfers between devices with their start and end apart: 22, of which 6 were waited for; matrix products, arithmetic and copies ran while one was open for 0% of the time, Pallas kernels for 20%

profile of v9, /device:TPU:1, one launch (start us, length us, event | category | flops | bytes accessed | tf_op | source)
XLA Modules:
  0.0 49.6 jit_solution(15202487268767643447)
XLA Ops:
  0.0 1.3 %conv_times_value.1 = (bf16[64,1024]{1,0:T(8,128)(2,1)S(1)}, bf16[64,1024]{1,0:T(8,128)(2,1)S(1)}, f32[128,1024]{1,0:T(8,128)S(1)}, bf16[128,1024]{1,0:T(8,128)(2,1)S(1)}) custom-call(bf16[128,1024]{1,0:T(8,128)(2,1)} %conv_hbm.1, bf16[128,1024]{1,0:T(8,128)(2,1)} %value_hbm.1, f32[128,1024]{1,0:T(8,128)} %taps_hbm.1, bf16[128,1024]{1,0:T(8,128)(2,1)} %gate_hbm.1), custom_call_target="tpu_custom_call" | custom-call | bytes 1024 | tf_op jit(solution)/shard_map/conv_times_value/pallas_call | solution.py:167
  1.3 4.0 %collective-permute-start.1 = (bf16[64,1024]{1,0:T(8,128)(2,1)S(1)}, bf16[64,1024]{1,0:T(8,128)(2,1)S(1)}, u32[]{:S(2)}, u32[]{:S(2)}) collective-permute-start(bf16[64,1024]{1,0:T(8,128)(2,1)S(1)} %get-tuple-element.47.high_ref), channel_id=1, source_target_pairs={{0,4},{4,8},{8,12},{12,16},{16,20},{20,24},{24,28},{1,5},{5,9},{9,... | collective-permute-start | bytes 393224 | tf_op jit(solution)/shard_map/ppermute | solution.py:687
  5.3 3.1 %collective-permute-start = (bf16[64,1024]{1,0:T(8,128)(2,1)S(1)}, bf16[64,1024]{1,0:T(8,128)(2,1)S(1)}, u32[]{:S(2)}, u32[]{:S(2)}) collective-permute-start(bf16[64,1024]{1,0:T(8,128)(2,1)S(1)} %get-tuple-element.46.low_ref), channel_id=1, source_target_pairs={{0,4},{4,8},{8,12},{12,16},{16,20},{20,24},{24,28},{1,5},{5,9},{9,... | collective-permute-start | bytes 393224 | tf_op jit(solution)/shard_map/ppermute | solution.py:687
  8.5 0.0 copy-start
  8.5 2.0 %fir_own_rows.1 = (f32[1152,128]{1,0:T(8,128)S(1)}, f32[1224,128]{1,0:T(8,128)S(1)}, f32[2304,128]{1,0:T(8,128)S(1)}, bf16[3,1024,512]{2,1,0:T(8,128)(2,1)S(1)}) custom-call(bf16[64,1024]{1,0:T(8,128)(2,1)S(1)} %get-tuple-element.46.low_ref, bf16[64,1024]{1,0:T(8,128)(2,1)S(1)} %get-tuple-element.47.high_ref, f32[128,1024]{1,0:T(8,128)S(1)} %get-tuple-element.48.taps_ref, ...), custom_call_target="tpu_custom_call" | custom-call | bytes 1024 | tf_op jit(solution)/shard_map/fir_own_rows/pallas_call | solution.py:257
  10.4 0.0 collective-permute-done.1.rim_ref
  10.4 0.0 copy-done
  10.4 0.7 %fir_later_rows.1 = (bf16[64,1152]{1,0:T(8,128)(2,1)S(1)}, bf16[32,1152]{1,0:T(8,128)(2,1)S(1)}, bf16[32,1152]{1,0:T(8,128)(2,1)S(1)}, f32[1152,128]{1,0:T(8,128)S(1)}, f32[72,128]{1,0:T(8,128)S(1)}) custom-call(bf16[64,1024]{1,0:T(8,128)(2,1)S(1)} %collective-permute-done.1.rim_ref, f32[1224,128]{1,0:T(8,128)S(1)} %get-tuple-element.50.sums_ref, ...), custom_call_target="tpu_custom_call" | custom-call | bytes 1024 | tf_op jit(solution)/shard_map/fir_later_rows/pallas_call | solution.py:325
  11.1 1.3 %collective-permute-start.2 = (bf16[32,1152]{1,0:T(8,128)(2,1)S(1)}, bf16[32,1152]{1,0:T(8,128)(2,1)S(1)}, u32[]{:S(2)}, u32[]{:S(2)}) collective-permute-start(bf16[32,1152]{1,0:T(8,128)(2,1)S(1)} %get-tuple-element.54), channel_id=1, source_target_pairs={{0,1},{1,0},{2,3},{3,2},{4,5},{5,4},{6,7},{7,6},{8,9},{9,8},{10,11... | collective-permute-start | bytes 221192 | tf_op jit(solution)/shard_map/ppermute | solution.py:681
  12.4 1.2 %collective-permute-start.8 = (bf16[64,1152]{1,0:T(8,128)(2,1)S(1)}, bf16[64,1152]{1,0:T(8,128)(2,1)S(1)}, u32[]{:S(2)}, u32[]{:S(2)}) collective-permute-start(bf16[64,1152]{1,0:T(8,128)(2,1)S(1)} %get-tuple-element.63.high_ref), channel_id=1, source_target_pairs={{0,3},{1,2},{2,1},{3,0},{4,7},{5,6},{6,5},{7,4},{8,11},{9,10},{10,... | collective-permute-start | bytes 442376 | tf_op jit(solution)/shard_map/ppermute | solution.py:681
  13.6 0.0 collective-permute-done.2.refs_2_
  13.6 0.0 collective-permute-done.rim_ref
  13.6 2.0 %fir_earlier_rows.1 = (bf16[64,1152]{1,0:T(8,128)(2,1)S(1)}, bf16[32,1152]{1,0:T(8,128)(2,1)S(1)}, bf16[32,1152]{1,0:T(8,128)(2,1)S(1)}, bf16[3,1024,512]{2,1,0:T(8,128)(2,1)S(1)}) custom-call(bf16[64,1024]{1,0:T(8,128)(2,1)S(1)} %collective-permute-done.rim_ref, f32[1152,128]{1,0:T(8,128)S(1)} %get-tuple-element.49.sums_ref, ...), custom_call_target="tpu_custom_call" | custom-call | bytes 1024 | tf_op jit(solution)/shard_map/fir_earlier_rows/pallas_call | solution.py:386
  15.6 1.2 %collective-permute-start.3 = (bf16[64,1152]{1,0:T(8,128)(2,1)S(1)}, bf16[64,1152]{1,0:T(8,128)(2,1)S(1)}, u32[]{:S(2)}, u32[]{:S(2)}) collective-permute-start(bf16[64,1152]{1,0:T(8,128)(2,1)S(1)} %get-tuple-element.57.low_ref), channel_id=1, source_target_pairs={{0,3},{1,2},{2,1},{3,0},{4,7},{5,6},{6,5},{7,4},{8,11},{9,10},{10,... | collective-permute-start | bytes 442376 | tf_op jit(solution)/shard_map/ppermute | solution.py:681
  16.8 0.2 collective-permute-start.6
  17.0 0.4 collective-permute-start.4
  17.3 0.2 collective-permute-start.5
  17.5 2.9 %projections_near.1 = (f32[128,1536]{1,0:T(8,128)S(1)}, f32[128,128]{1,0:T(8,128)S(1)}, bf16[3,1024,512]{2,1,0:T(8,128)(2,1)S(1)}, bf16[3,1024,512]{2,1,0:T(8,128)(2,1)S(1)}) custom-call(bf16[64,1152]{1,0:T(8,128)(2,1)S(1)} %get-tuple-element.57.low_ref, bf16[64,1152]{1,0:T(8,128)(2,1)S(1)} %get-tuple-element.63.high_ref, ...), custom_call_target="tpu_custom_call" | custom-call | bytes 1024 | tf_op jit(solution)/shard_map/projections_near/pallas_call | solution.py:451
  20.4 0.0 collective-permute-done.8.refs_1_
  20.4 0.4 collective-permute-start.9
  20.8 0.0 collective-permute-done.6.refs_3_
  20.8 0.0 collective-permute-done.4.refs_0_
  20.8 0.0 collective-permute-done.5.refs_1_
  20.8 0.6 %projections_part.2 = (f32[128,1536]{1,0:T(8,128)S(1)}, f32[128,128]{1,0:T(8,128)S(1)}) custom-call(bf16[32,1152]{1,0:T(8,128)(2,1)S(1)} %collective-permute-done.4.refs_0_, bf16[32,1152]{1,0:T(8,128)(2,1)S(1)} %collective-permute-done.5.refs_1_, bf16[32,1152]{1,0:T(8,128)(2,1)S(1)} %collective-permute-done.2.refs_2_, ...), custom_call_target="tpu_custom_call" | custom-call | bytes 1024 | tf_op jit(solution)/shard_map/projections_part/pallas_call | solution.py:484
  21.4 0.2 collective-permute-done.3.refs_0_
  21.6 0.4 collective-permute-start.7
  22.0 0.6 %projections_part.3 = (f32[128,1536]{1,0:T(8,128)S(1)}, f32[128,128]{1,0:T(8,128)S(1)}) custom-call(bf16[64,1152]{1,0:T(8,128)(2,1)S(1)} %collective-permute-done.3.refs_0_, bf16[64,1152]{1,0:T(8,128)(2,1)S(1)} %collective-permute-done.8.refs_1_, bf16[3,1024,512]{2,1,0:T(8,128)(2,1)S(1)} %get-tuple-element.70.refs_2_, ...), custom_call_target="tpu_custom_call" | custom-call | bytes 1024 | tf_op jit(solution)/shard_map/projections_part/pallas_call | solution.py:484
  22.6 0.0 collective-permute-done.9.refs_1_
  22.6 0.4 collective-permute-done.7.refs_0_
  23.0 0.7 %projections_last.1 = (bf16[384,128]{1,0:T(8,128)(2,1)S(1)}, bf16[384,128]{1,0:T(8,128)(2,1)S(1)}, bf16[384,128]{1,0:T(8,128)(2,1)S(1)}, bf16[384,128]{1,0:T(8,128)(2,1)S(1)}) custom-call(bf16[64,1152]{1,0:T(8,128)(2,1)S(1)} %collective-permute-done.7.refs_0_, bf16[64,1152]{1,0:T(8,128)(2,1)S(1)} %collective-permute-done.9.refs_1_, ...), custom_call_target="tpu_custom_call" | custom-call | bytes 1024 | tf_op jit(solution)/shard_map/projections_last/pallas_call | solution.py:521
  23.7 0.4 collective-permute-start.12
  24.1 1.5 %collective-permute-start.13 = (bf16[384,128]{1,0:T(8,128)(2,1)S(1)}, bf16[384,128]{1,0:T(8,128)(2,1)S(1)}, u32[]{:S(2)}, u32[]{:S(2)}) collective-permute-start(bf16[384,128]{1,0:T(8,128)(2,1)S(1)} %get-tuple-element.77), channel_id=1, source_target_pairs={{0,9},{1,8},{2,11},{3,10},{4,13},{5,12},{6,15},{7,14},{8,1},{9,0},... | collective-permute-start | bytes 294920 | tf_op jit(solution)/shard_map/ppermute | solution.py:722
  25.6 2.5 %collective-permute-start.14 = (bf16[384,128]{1,0:T(8,128)(2,1)S(1)}, bf16[384,128]{1,0:T(8,128)(2,1)S(1)}, u32[]{:S(2)}, u32[]{:S(2)}) collective-permute-start(bf16[384,128]{1,0:T(8,128)(2,1)S(1)} %get-tuple-element.78), channel_id=1, source_target_pairs={{0,17},{1,16},{2,19},{3,18},{4,21},{5,20},{6,23},{7,22},{8,25},{9,... | collective-permute-start | bytes 294920 | tf_op jit(solution)/shard_map/ppermute | solution.py:722
  28.2 0.0 collective-permute-start.10
  28.2 0.0 collective-permute-done.12.refs_0_
  28.2 1.2 %collective-permute-start.15 = (bf16[256,128]{1,0:T(8,128)(2,1)S(1)}, bf16[256,128]{1,0:T(8,128)(2,1)S(1)}, u32[]{:S(2)}, u32[]{:S(2)}) collective-permute-start(bf16[256,128]{1,0:T(8,128)(2,1)S(1)} %slice.17), channel_id=1, source_target_pairs={{0,4},{4,0},{8,12},{12,8},{16,20},{20,16},{24,28},{28,24},{1,5},{5... | collective-permute-start | bytes 196616 | tf_op jit(solution)/shard_map/ppermute | solution.py:725
  29.3 0.0 collective-permute-done.13.refs_1_
  29.3 0.6 %collective-permute-start.16 = (bf16[256,128]{1,0:T(8,128)(2,1)S(1)}, bf16[256,128]{1,0:T(8,128)(2,1)S(1)}, u32[]{:S(2)}, u32[]{:S(2)}) collective-permute-start(bf16[256,128]{1,0:T(8,128)(2,1)S(1)} %slice.18), channel_id=1, source_target_pairs={{0,4},{4,0},{8,12},{12,8},{16,20},{20,16},{24,28},{28,24},{1,5},{5... | collective-permute-start | bytes 196616 | tf_op jit(solution)/shard_map/ppermute | solution.py:725
  29.9 5.8 %collective-permute-done.14.refs_2_ = bf16[384,128]{1,0:T(8,128)(2,1)S(1)} collective-permute-done((bf16[384,128]{1,0:T(8,128)(2,1)S(1)}, bf16[384,128]{1,0:T(8,128)(2,1)S(1)}, u32[]{:S(2)}, u32[]{:S(2)}) %collective-permute-start.14) | collective-permute-done | bytes 98336 | tf_op jit(solution)/shard_map/ppermute | solution.py:722
  35.8 1.2 %collective-permute-start.17 = (bf16[256,128]{1,0:T(8,128)(2,1)S(1)}, bf16[256,128]{1,0:T(8,128)(2,1)S(1)}, u32[]{:S(2)}, u32[]{:S(2)}) collective-permute-start(bf16[256,128]{1,0:T(8,128)(2,1)S(1)} %slice.19), channel_id=1, source_target_pairs={{0,4},{4,0},{8,12},{12,8},{16,20},{20,16},{24,28},{28,24},{1,5},{5... | collective-permute-start | bytes 196616 | tf_op jit(solution)/shard_map/ppermute | solution.py:725
  36.9 0.0 collective-permute-done.10.refs_3_
  36.9 0.4 collective-permute-start.11
  37.3 0.0 collective-permute-done.15.refs_4_
  37.3 0.0 collective-permute-done.16.refs_5_
  37.3 2.3 %collective-permute-done.17.refs_6_ = bf16[256,128]{1,0:T(8,128)(2,1)S(1)} collective-permute-done((bf16[256,128]{1,0:T(8,128)(2,1)S(1)}, bf16[256,128]{1,0:T(8,128)(2,1)S(1)}, u32[]{:S(2)}, u32[]{:S(2)}) %collective-permute-start.17) | collective-permute-done | bytes 65568 | tf_op jit(solution)/shard_map/ppermute | solution.py:725
  39.6 1.3 %attention_most.1 = (bf16[512,128]{1,0:T(8,128)(2,1)S(1)}, f32[512,128]{1,0:T(8,128)S(1)}, f32[512,128]{1,0:T(8,128)S(1)}, f32[512,128]{1,0:T(8,128)S(1)}) custom-call(bf16[384,128]{1,0:T(8,128)(2,1)S(1)} %collective-permute-done.12.refs_0_, bf16[384,128]{1,0:T(8,128)(2,1)S(1)} %collective-permute-done.13.refs_1_, ...), custom_call_target="tpu_custom_call" | custom-call | bytes 1024 | tf_op jit(solution)/shard_map/attention_most/pallas_call | solution.py:582
  40.9 0.0 collective-permute-done.11.other_ref
  40.9 0.5 %attention_rest.1 = (bf16[128,128]{1,0:T(8,128)(2,1)S(1)}, bf16[128,128]{1,0:T(8,128)(2,1)S(1)}, bf16[128,128]{1,0:T(8,128)(2,1)S(1)}, bf16[128,128]{1,0:T(8,128)(2,1)S(1)}) custom-call(bf16[256,128]{1,0:T(8,128)(2,1)S(1)} %collective-permute-done.11.other_ref, bf16[512,128]{1,0:T(8,128)(2,1)S(1)} %get-tuple-element.79.query_ref, ...), custom_call_target="tpu_custom_call" | custom-call | bytes 1024 | tf_op jit(solution)/shard_map/attention_rest/pallas_call | solution.py:615
  41.5 3.2 %collective-permute-start.18 = (bf16[128,128]{1,0:T(8,128)(2,1)S(1)}, bf16[128,128]{1,0:T(8,128)(2,1)S(1)}, u32[]{:S(2)}, u32[]{:S(2)}) collective-permute-start(bf16[128,128]{1,0:T(8,128)(2,1)S(1)} %get-tuple-element.83), channel_id=1, source_target_pairs={{0,25},{1,24},{2,27},{3,26},{4,29},{5,28},{6,31},{7,30},{8,17},{9,... | collective-permute-start | bytes 98312 | tf_op jit(solution)/shard_map/ppermute | solution.py:722
  44.6 0.0 collective-permute-start.19
  44.6 0.1 collective-permute-start.20
  44.8 1.0 %collective-permute-start.21 = (bf16[128,128]{1,0:T(8,128)(2,1)S(1)}, bf16[128,128]{1,0:T(8,128)(2,1)S(1)}, u32[]{:S(2)}, u32[]{:S(2)}) collective-permute-start(bf16[128,128]{1,0:T(8,128)(2,1)S(1)} %get-tuple-element.86), channel_id=1, source_target_pairs={{0,1},{1,0},{2,3},{3,2},{4,5},{5,4},{6,7},{7,6},{8,9},{9,8},{10,11... | collective-permute-start | bytes 98312 | tf_op jit(solution)/shard_map/ppermute | solution.py:722
  45.8 0.9 %collective-permute-done.18.refs_0_ = bf16[128,128]{1,0:T(8,128)(2,1)S(1)} collective-permute-done((bf16[128,128]{1,0:T(8,128)(2,1)S(1)}, bf16[128,128]{1,0:T(8,128)(2,1)S(1)}, u32[]{:S(2)}, u32[]{:S(2)}) %collective-permute-start.18) | collective-permute-done | bytes 32800 | tf_op jit(solution)/shard_map/ppermute | solution.py:722
  46.7 2.2 %collective-permute-done.19.refs_1_ = bf16[128,128]{1,0:T(8,128)(2,1)S(1)} collective-permute-done((bf16[128,128]{1,0:T(8,128)(2,1)S(1)}, bf16[128,128]{1,0:T(8,128)(2,1)S(1)}, u32[]{:S(2)}, u32[]{:S(2)}) %collective-permute-start.19) | collective-permute-done | bytes 32800 | tf_op jit(solution)/shard_map/ppermute | solution.py:722
  48.9 0.0 collective-permute-done.20.refs_2_
  48.9 0.0 collective-permute-done.21.refs_3_
  48.9 0.7 %join_heads.1 = bf16[128,512]{1,0:T(8,128)(2,1)} custom-call(bf16[128,128]{1,0:T(8,128)(2,1)S(1)} %collective-permute-done.18.refs_0_, bf16[128,128]{1,0:T(8,128)(2,1)S(1)} %collective-permute-done.19.refs_1_, bf16[128,128]{1,0:T(8,128)(2,1)S(1)} %collective-permute-done.20.refs_2_, bf16[128,128]{1,0:T(8,128)(2,1)S(1)} %collective-permute-done.21.refs_3_), custom_call_target="tpu_custom_call" | custom-call | bytes 1024 | tf_op jit(solution)/shard_map/join_heads/pallas_call | solution.py:635
  (4 shorter events, 0.0 us)
Async XLA Ops:
  1.3 9.1 %collective-permute-start.1 = (bf16[64,1024]{1,0:T(8,128)(2,1)S(1)}, bf16[64,1024]{1,0:T(8,128)(2,1)S(1)}, u32[]{:S(2)}, u32[]{:S(2)}) collective-permute-start(bf16[64,1024]{1,0:T(8,128)(2,1)S(1)} %get-tuple-element.47.high_ref), channel_id=1, source_target_pairs={{0,4},{4,8},{8,12},{12,16},{16,20},{20,24},{24,28},{1,5},{5,9},{9,... | collective-permute-start | bytes 393224 | tf_op jit(solution)/shard_map/ppermute | solution.py:687
  5.3 8.3 %collective-permute-start = (bf16[64,1024]{1,0:T(8,128)(2,1)S(1)}, bf16[64,1024]{1,0:T(8,128)(2,1)S(1)}, u32[]{:S(2)}, u32[]{:S(2)}) collective-permute-start(bf16[64,1024]{1,0:T(8,128)(2,1)S(1)} %get-tuple-element.46.low_ref), channel_id=1, source_target_pairs={{0,4},{4,8},{8,12},{12,16},{16,20},{20,24},{24,28},{1,5},{5,9},{9,... | collective-permute-start | bytes 393224 | tf_op jit(solution)/shard_map/ppermute | solution.py:687
  8.5 2.0 %copy-start = (f32[1024]{0:T(1024)S(1)}, f32[1024]{0:T(1024)}, u32[]{:S(2)}) copy-start(f32[1024]{0:T(1024)} %param.10) | copy-start | bytes 12292
  11.1 2.5 %collective-permute-start.2 = (bf16[32,1152]{1,0:T(8,128)(2,1)S(1)}, bf16[32,1152]{1,0:T(8,128)(2,1)S(1)}, u32[]{:S(2)}, u32[]{:S(2)}) collective-permute-start(bf16[32,1152]{1,0:T(8,128)(2,1)S(1)} %get-tuple-element.54), channel_id=1, source_target_pairs={{0,1},{1,0},{2,3},{3,2},{4,5},{5,4},{6,7},{7,6},{8,9},{9,8},{10,11... | collective-permute-start | bytes 221192 | tf_op jit(solution)/shard_map/ppermute | solution.py:681
  12.4 8.0 %collective-permute-start.8 = (bf16[64,1152]{1,0:T(8,128)(2,1)S(1)}, bf16[64,1152]{1,0:T(8,128)(2,1)S(1)}, u32[]{:S(2)}, u32[]{:S(2)}) collective-permute-start(bf16[64,1152]{1,0:T(8,128)(2,1)S(1)} %get-tuple-element.63.high_ref), channel_id=1, source_target_pairs={{0,3},{1,2},{2,1},{3,0},{4,7},{5,6},{6,5},{7,4},{8,11},{9,10},{10,... | collective-permute-start | bytes 442376 | tf_op jit(solution)/shard_map/ppermute | solution.py:681
  15.6 6.0 %collective-permute-start.3 = (bf16[64,1152]{1,0:T(8,128)(2,1)S(1)}, bf16[64,1152]{1,0:T(8,128)(2,1)S(1)}, u32[]{:S(2)}, u32[]{:S(2)}) collective-permute-start(bf16[64,1152]{1,0:T(8,128)(2,1)S(1)} %get-tuple-element.57.low_ref), channel_id=1, source_target_pairs={{0,3},{1,2},{2,1},{3,0},{4,7},{5,6},{6,5},{7,4},{8,11},{9,10},{10,... | collective-permute-start | bytes 442376 | tf_op jit(solution)/shard_map/ppermute | solution.py:681
  16.8 4.0 %collective-permute-start.6 = (bf16[32,1152]{1,0:T(8,128)(2,1)S(1)}, bf16[32,1152]{1,0:T(8,128)(2,1)S(1)}, u32[]{:S(2)}, u32[]{:S(2)}) collective-permute-start(bf16[32,1152]{1,0:T(8,128)(2,1)S(1)} %get-tuple-element.61), channel_id=1, source_target_pairs={{0,1},{1,0},{2,3},{3,2},{4,5},{5,4},{6,7},{7,6},{8,9},{9,8},{10,11... | collective-permute-start | bytes 221192 | tf_op jit(solution)/shard_map/ppermute | solution.py:681
  17.0 3.8 %collective-permute-start.4 = (bf16[32,1152]{1,0:T(8,128)(2,1)S(1)}, bf16[32,1152]{1,0:T(8,128)(2,1)S(1)}, u32[]{:S(2)}, u32[]{:S(2)}) collective-permute-start(bf16[32,1152]{1,0:T(8,128)(2,1)S(1)} %get-tuple-element.58), channel_id=1, source_target_pairs={{0,1},{1,0},{2,3},{3,2},{4,5},{5,4},{6,7},{7,6},{8,9},{9,8},{10,11... | collective-permute-start | bytes 221192 | tf_op jit(solution)/shard_map/ppermute | solution.py:681
  17.3 3.5 %collective-permute-start.5 = (bf16[32,1152]{1,0:T(8,128)(2,1)S(1)}, bf16[32,1152]{1,0:T(8,128)(2,1)S(1)}, u32[]{:S(2)}, u32[]{:S(2)}) collective-permute-start(bf16[32,1152]{1,0:T(8,128)(2,1)S(1)} %get-tuple-element.59), channel_id=1, source_target_pairs={{0,1},{1,0},{2,3},{3,2},{4,5},{5,4},{6,7},{7,6},{8,9},{9,8},{10,11... | collective-permute-start | bytes 221192 | tf_op jit(solution)/shard_map/ppermute | solution.py:681
  20.4 2.2 %collective-permute-start.9 = (bf16[64,1152]{1,0:T(8,128)(2,1)S(1)}, bf16[64,1152]{1,0:T(8,128)(2,1)S(1)}, u32[]{:S(2)}, u32[]{:S(2)}) collective-permute-start(bf16[64,1152]{1,0:T(8,128)(2,1)S(1)} %collective-permute-done.8.refs_1_), channel_id=1, source_target_pairs={{0,1},{1,0},{2,3},{3,2},{4,5},{5,4},{6,7},{7,6},{8,9},{9,8},{10,11... | collective-permute-start | bytes 442376 | tf_op jit(solution)/shard_map/ppermute | solution.py:681
  21.6 1.4 %collective-permute-start.7 = (bf16[64,1152]{1,0:T(8,128)(2,1)S(1)}, bf16[64,1152]{1,0:T(8,128)(2,1)S(1)}, u32[]{:S(2)}, u32[]{:S(2)}) collective-permute-start(bf16[64,1152]{1,0:T(8,128)(2,1)S(1)} %collective-permute-done.3.refs_0_), channel_id=1, source_target_pairs={{0,1},{1,0},{2,3},{3,2},{4,5},{5,4},{6,7},{7,6},{8,9},{9,8},{10,11... | collective-permute-start | bytes 442376 | tf_op jit(solution)/shard_map/ppermute | solution.py:681
  23.7 4.5 %collective-permute-start.12 = (bf16[384,128]{1,0:T(8,128)(2,1)S(1)}, bf16[384,128]{1,0:T(8,128)(2,1)S(1)}, u32[]{:S(2)}, u32[]{:S(2)}) collective-permute-start(bf16[384,128]{1,0:T(8,128)(2,1)S(1)} %get-tuple-element.76), channel_id=1, source_target_pairs={{0,1},{1,0},{2,3},{3,2},{4,5},{5,4},{6,7},{7,6},{8,9},{9,8},{10,11... | collective-permute-start | bytes 294920 | tf_op jit(solution)/shard_map/ppermute | solution.py:722
  24.1 5.2 %collective-permute-start.13 = (bf16[384,128]{1,0:T(8,128)(2,1)S(1)}, bf16[384,128]{1,0:T(8,128)(2,1)S(1)}, u32[]{:S(2)}, u32[]{:S(2)}) collective-permute-start(bf16[384,128]{1,0:T(8,128)(2,1)S(1)} %get-tuple-element.77), channel_id=1, source_target_pairs={{0,9},{1,8},{2,11},{3,10},{4,13},{5,12},{6,15},{7,14},{8,1},{9,0},... | collective-permute-start | bytes 294920 | tf_op jit(solution)/shard_map/ppermute | solution.py:722
  25.6 10.1 %collective-permute-start.14 = (bf16[384,128]{1,0:T(8,128)(2,1)S(1)}, bf16[384,128]{1,0:T(8,128)(2,1)S(1)}, u32[]{:S(2)}, u32[]{:S(2)}) collective-permute-start(bf16[384,128]{1,0:T(8,128)(2,1)S(1)} %get-tuple-element.78), channel_id=1, source_target_pairs={{0,17},{1,16},{2,19},{3,18},{4,21},{5,20},{6,23},{7,22},{8,25},{9,... | collective-permute-start | bytes 294920 | tf_op jit(solution)/shard_map/ppermute | solution.py:722
  28.2 8.8 %collective-permute-start.10 = (bf16[384,128]{1,0:T(8,128)(2,1)S(1)}, bf16[384,128]{1,0:T(8,128)(2,1)S(1)}, u32[]{:S(2)}, u32[]{:S(2)}) collective-permute-start(bf16[384,128]{1,0:T(8,128)(2,1)S(1)} %get-tuple-element.75), channel_id=1, source_target_pairs={{0,25},{1,24},{2,27},{3,26},{4,29},{5,28},{6,31},{7,30},{8,17},{9,... | collective-permute-start | bytes 294920 | tf_op jit(solution)/shard_map/ppermute | solution.py:722
  28.2 9.1 %collective-permute-start.15 = (bf16[256,128]{1,0:T(8,128)(2,1)S(1)}, bf16[256,128]{1,0:T(8,128)(2,1)S(1)}, u32[]{:S(2)}, u32[]{:S(2)}) collective-permute-start(bf16[256,128]{1,0:T(8,128)(2,1)S(1)} %slice.17), channel_id=1, source_target_pairs={{0,4},{4,0},{8,12},{12,8},{16,20},{20,16},{24,28},{28,24},{1,5},{5... | collective-permute-start | bytes 196616 | tf_op jit(solution)/shard_map/ppermute | solution.py:725
  29.3 8.0 %collective-permute-start.16 = (bf16[256,128]{1,0:T(8,128)(2,1)S(1)}, bf16[256,128]{1,0:T(8,128)(2,1)S(1)}, u32[]{:S(2)}, u32[]{:S(2)}) collective-permute-start(bf16[256,128]{1,0:T(8,128)(2,1)S(1)} %slice.18), channel_id=1, source_target_pairs={{0,4},{4,0},{8,12},{12,8},{16,20},{20,16},{24,28},{28,24},{1,5},{5... | collective-permute-start | bytes 196616 | tf_op jit(solution)/shard_map/ppermute | solution.py:725
  35.8 3.8 %collective-permute-start.17 = (bf16[256,128]{1,0:T(8,128)(2,1)S(1)}, bf16[256,128]{1,0:T(8,128)(2,1)S(1)}, u32[]{:S(2)}, u32[]{:S(2)}) collective-permute-start(bf16[256,128]{1,0:T(8,128)(2,1)S(1)} %slice.19), channel_id=1, source_target_pairs={{0,4},{4,0},{8,12},{12,8},{16,20},{20,16},{24,28},{28,24},{1,5},{5... | collective-permute-start | bytes 196616 | tf_op jit(solution)/shard_map/ppermute | solution.py:725
  36.9 4.0 %collective-permute-start.11 = (bf16[256,128]{1,0:T(8,128)(2,1)S(1)}, bf16[256,128]{1,0:T(8,128)(2,1)S(1)}, u32[]{:S(2)}, u32[]{:S(2)}) collective-permute-start(bf16[256,128]{1,0:T(8,128)(2,1)S(1)} %slice.16), channel_id=1, source_target_pairs={{0,4},{4,0},{8,12},{12,8},{16,20},{20,16},{24,28},{28,24},{1,5},{5... | collective-permute-start | bytes 196616 | tf_op jit(solution)/shard_map/ppermute | solution.py:725
  41.5 5.2 %collective-permute-start.18 = (bf16[128,128]{1,0:T(8,128)(2,1)S(1)}, bf16[128,128]{1,0:T(8,128)(2,1)S(1)}, u32[]{:S(2)}, u32[]{:S(2)}) collective-permute-start(bf16[128,128]{1,0:T(8,128)(2,1)S(1)} %get-tuple-element.83), channel_id=1, source_target_pairs={{0,25},{1,24},{2,27},{3,26},{4,29},{5,28},{6,31},{7,30},{8,17},{9,... | collective-permute-start | bytes 98312 | tf_op jit(solution)/shard_map/ppermute | solution.py:722
  44.6 4.2 %collective-permute-start.19 = (bf16[128,128]{1,0:T(8,128)(2,1)S(1)}, bf16[128,128]{1,0:T(8,128)(2,1)S(1)}, u32[]{:S(2)}, u32[]{:S(2)}) collective-permute-start(bf16[128,128]{1,0:T(8,128)(2,1)S(1)} %get-tuple-element.84), channel_id=1, source_target_pairs={{0,17},{1,16},{2,19},{3,18},{4,21},{5,20},{6,23},{7,22},{8,25},{9,... | collective-permute-start | bytes 98312 | tf_op jit(solution)/shard_map/ppermute | solution.py:722
  44.6 4.2 %collective-permute-start.20 = (bf16[128,128]{1,0:T(8,128)(2,1)S(1)}, bf16[128,128]{1,0:T(8,128)(2,1)S(1)}, u32[]{:S(2)}, u32[]{:S(2)}) collective-permute-start(bf16[128,128]{1,0:T(8,128)(2,1)S(1)} %get-tuple-element.85), channel_id=1, source_target_pairs={{0,9},{1,8},{2,11},{3,10},{4,13},{5,12},{6,15},{7,14},{8,1},{9,0},... | collective-permute-start | bytes 98312 | tf_op jit(solution)/shard_map/ppermute | solution.py:722
  44.8 4.1 %collective-permute-start.21 = (bf16[128,128]{1,0:T(8,128)(2,1)S(1)}, bf16[128,128]{1,0:T(8,128)(2,1)S(1)}, u32[]{:S(2)}, u32[]{:S(2)}) collective-permute-start(bf16[128,128]{1,0:T(8,128)(2,1)S(1)} %get-tuple-element.86), channel_id=1, source_target_pairs={{0,1},{1,0},{2,3},{3,2},{4,5},{5,4},{6,7},{7,6},{8,9},{9,8},{10,11... | collective-permute-start | bytes 98312 | tf_op jit(solution)/shard_map/ppermute | solution.py:722

commit v10 on v9

--- a/solution.py
+++ b/solution.py
@@ -11,6 +11,8 @@
 HEAD_DIM = 128
 LANES = 128
 SLAB = 8
+TAKEN = {4: (0, 3, 1, 2)}
+GIVEN = {4: (2, 3, 1, 0)}
 PHASES = 4
 SUBS = 9
 HELD = 8
@@ -546,7 +548,7 @@
     return jnp.where(query_base >= key_base, product, -1e30)
 
 
-def most_kernel(count, *refs):
+def most_kernel(count, taken, *refs):
     blocks, others = refs[:count], refs[count : 2 * count - 1]
     query_ref, top_ref, total_ref, summed_ref, key_ref, value_ref = refs[2 * count - 1 :]
     rows = blocks[0].shape[0] // 3
@@ -562,7 +564,7 @@
     key_base = jnp.concatenate(
         [
             base_of((1, count * rows), 1, rows, y),
-            base_of((1, (count - 1) * rows), 1, rows, 1 - y),
+            *(base_of((1, count * rows), 1, rows, 1 - y)[:, k * rows : (k + 1) * rows] for k in taken),
         ],
         axis=1,
     )
@@ -574,13 +576,13 @@
     summed_ref[...] = jnp.dot(expo.astype(BF16), value_ref[...], preferred_element_type=F32)
 
 
-def attend_most(blocks, others):
+def attend_most(blocks, others, taken):
     count = len(blocks)
     rows = blocks[0].shape[0] // 3
     keys = pltpu.VMEM(((2 * count - 1) * rows, HEAD_DIM), BF16)
     shape = jax.ShapeDtypeStruct((count * rows, LANES), F32)
     return pl.pallas_call(
-        functools.partial(most_kernel, count),
+        functools.partial(most_kernel, count, taken),
         out_shape=(jax.ShapeDtypeStruct((count * rows, HEAD_DIM), BF16), shape, shape, shape),
         in_specs=[VMEM] * (2 * count - 1),
         out_specs=(VMEM,) * 4,
@@ -591,11 +593,11 @@
     )(*blocks, *others)
 
 
-def rest_kernel(other_ref, query_ref, top_ref, total_ref, summed_ref, *outs):
+def rest_kernel(last, other_ref, query_ref, top_ref, total_ref, summed_ref, *outs):
     count = len(outs)
     rows = outs[0].shape[0]
     y = lax.axis_index("ctx") % 2
-    key_base = base_of((1, count * rows), 1, rows, 1 - y)[:, (count - 1) * rows :]
+    key_base = base_of((1, count * rows), 1, rows, 1 - y)[:, last * rows : (last + 1) * rows]
     scores = scores_of(query_ref[...], other_ref[:rows, :], rows, key_base)
     before = top_ref[...]
     top = jnp.maximum(before[:, :1], jnp.max(scores, axis=1, keepdims=True))
@@ -610,10 +612,10 @@
         out[...] = attended[n * rows : (n + 1) * rows, :]
 
 
-def attend_rest(other, state, count):
+def attend_rest(other, state, count, last):
     rows = other.shape[0] // 2
     return pl.pallas_call(
-        rest_kernel,
+        functools.partial(rest_kernel, last),
         out_shape=tuple(jax.ShapeDtypeStruct((rows, HEAD_DIM), BF16) for _ in range(count)),
         in_specs=[VMEM] * 5,
         out_specs=(VMEM,) * count,
@@ -623,17 +625,17 @@
     )(other, *state)
 
 
-def join_kernel(*refs):
+def join_kernel(given, *refs):
     blocks, out = refs[:-1], refs[-1]
     for n, block in enumerate(blocks):
-        head = jnp.bitwise_xor(lax.axis_index("ctx") // 2, len(blocks) - 1 - n)
+        head = jnp.bitwise_xor(lax.axis_index("ctx") // 2, given[n])
         out[:, pl.ds(pl.multiple_of(head * HEAD_DIM, LANES), HEAD_DIM)] = block[...]
 
 
-def join(blocks):
+def join(blocks, given):
     rows = blocks[0].shape[0]
     return pl.pallas_call(
-        join_kernel,
+        functools.partial(join_kernel, given),
         out_shape=jax.ShapeDtypeStruct((rows, len(blocks) * HEAD_DIM), BF16),
         in_specs=[VMEM] * len(blocks),
         out_specs=VMEM,
@@ -727,9 +729,12 @@
     order = range(heads - 1, -1, -1)
     held = [over_z(value, k) for value, k in zip(messages, order)]
     others = [over_y(value[rows:]) for value in held]
-    held, others = held[::-1], others[::-1]
-    done = attend_rest(others[-1], attend_most(held, others[:-1]), heads)
-    return join([over_z(value, k) for value, k in zip(done, order)])
+    taken = TAKEN.get(heads, tuple(range(heads)))
+    given = GIVEN.get(heads, tuple(order))
+    held, others = held[::-1], [others[heads - 1 - k] for k in taken]
+    state = attend_most(held, others[:-1], taken[:-1])
+    done = attend_rest(others[-1], state, heads, taken[-1])
+    return join([over_z(done[heads - 1 - k], k) for k in given], given)
 
 
 def solution(mesh):

time: 49.8 us -> 48.5 us (0.974)
  waiting for transfers between devices: 11.8 us -> 8.94 us
  starting transfers between devices: 24.4 us -> 26 us
    ppermute x4, waiting for transfers between devices: 2.29 us -> 0.72 us  [over_y(): return lax.ppermute(value, 'ctx', [(i, i ^ 1) for i in range(ctx)])]
    ppermute x8, waiting for transfers between devices: 8.96 us -> 7.61 us  [over_z(): return lax.ppermute(value, ('ctx', 'tp'), pairs)]
    ppermute x4, starting transfers between devices: 3.29 us -> 4.57 us  [over_y(): return lax.ppermute(value, 'ctx', [(i, i ^ 1) for i in range(ctx)])]
  transfers between devices with their start and end apart: 22 -> 22, of which waited for: 6 -> 7; matrix products, arithmetic and copies ran while one was open for 0% -> 0% of each run, Pallas kernels for 20% -> 21%
where the time goes in v10:
time: 48.5 us; the launch traced here: 48.3 us
  starting transfers between devices  26 us (54%)
  Pallas kernels  13.2 us (27%)
  waiting for transfers between devices  8.94 us (18%)
    ppermute x8, starting transfers between devices, over_z(): return lax.ppermute(value, ('ctx', 'tp'), pairs)  9.07 us
    ppermute x8, waiting for transfers between devices, over_z(): return lax.ppermute(value, ('ctx', 'tp'), pairs)  7.61 us
    ppermute x2, starting transfers between devices, body(): lax.ppermute(part, 'ctx', [(i, i + 1) for i in range(ctx - 1)])  7.13 us
    ppermute x8, starting transfers between devices, swapped(): return lax.ppermute(value, 'tp', [(i, i ^ by) for i in range(tp)])  5.2 us
    ppermute x4, starting transfers between devices, over_y(): return lax.ppermute(value, 'ctx', [(i, i ^ 1) for i in range(ctx)])  4.57 us
    pallas_call x1, Pallas kernels, near_projection(): pl.pallas_call(functools.partial(near_kernel, far, last), out_shape=(jax....  2.88 us
    pallas_call x1, Pallas kernels, own_part(): pl.pallas_call(own_kernel, out_shape=(slabs(SUBS * eighth), slabs(SUBS *...  1.95 us
    pallas_call x1, Pallas kernels, low_part(): pl.pallas_call(functools.partial(low_kernel, offsets), out_shape=sent_sha...  1.95 us
  transfers between devices with their start and end apart: 22, of which 7 were waited for; matrix products, arithmetic and copies ran while one was open for 0% of the time, Pallas kernels for 21%

profile of v10, /device:TPU:1, one launch (start us, length us, event | category | flops | bytes accessed | tf_op | source)
XLA Modules:
  0.0 48.3 jit_solution(3932318445152643020)
XLA Ops:
  0.0 1.3 %conv_times_value.1 = (bf16[64,1024]{1,0:T(8,128)(2,1)S(1)}, bf16[64,1024]{1,0:T(8,128)(2,1)S(1)}, f32[128,1024]{1,0:T(8,128)S(1)}, bf16[128,1024]{1,0:T(8,128)(2,1)S(1)}) custom-call(bf16[128,1024]{1,0:T(8,128)(2,1)} %conv_hbm.1, bf16[128,1024]{1,0:T(8,128)(2,1)} %value_hbm.1, f32[128,1024]{1,0:T(8,128)} %taps_hbm.1, bf16[128,1024]{1,0:T(8,128)(2,1)} %gate_hbm.1), custom_call_target="tpu_custom_call" | custom-call | bytes 1024 | tf_op jit(solution)/shard_map/conv_times_value/pallas_call | solution.py:169
  1.3 4.0 %collective-permute-start.1 = (bf16[64,1024]{1,0:T(8,128)(2,1)S(1)}, bf16[64,1024]{1,0:T(8,128)(2,1)S(1)}, u32[]{:S(2)}, u32[]{:S(2)}) collective-permute-start(bf16[64,1024]{1,0:T(8,128)(2,1)S(1)} %get-tuple-element.47.high_ref), channel_id=1, source_target_pairs={{0,4},{4,8},{8,12},{12,16},{16,20},{20,24},{24,28},{1,5},{5,9},{9,... | collective-permute-start | bytes 393224 | tf_op jit(solution)/shard_map/ppermute | solution.py:689
  5.3 3.1 %collective-permute-start = (bf16[64,1024]{1,0:T(8,128)(2,1)S(1)}, bf16[64,1024]{1,0:T(8,128)(2,1)S(1)}, u32[]{:S(2)}, u32[]{:S(2)}) collective-permute-start(bf16[64,1024]{1,0:T(8,128)(2,1)S(1)} %get-tuple-element.46.low_ref), channel_id=1, source_target_pairs={{0,4},{4,8},{8,12},{12,16},{16,20},{20,24},{24,28},{1,5},{5,9},{9,... | collective-permute-start | bytes 393224 | tf_op jit(solution)/shard_map/ppermute | solution.py:689
  8.5 0.0 copy-start
  8.5 2.0 %fir_own_rows.1 = (f32[1152,128]{1,0:T(8,128)S(1)}, f32[1224,128]{1,0:T(8,128)S(1)}, f32[2304,128]{1,0:T(8,128)S(1)}, bf16[3,1024,512]{2,1,0:T(8,128)(2,1)S(1)}) custom-call(bf16[64,1024]{1,0:T(8,128)(2,1)S(1)} %get-tuple-element.46.low_ref, bf16[64,1024]{1,0:T(8,128)(2,1)S(1)} %get-tuple-element.47.high_ref, f32[128,1024]{1,0:T(8,128)S(1)} %get-tuple-element.48.taps_ref, ...), custom_call_target="tpu_custom_call" | custom-call | bytes 1024 | tf_op jit(solution)/shard_map/fir_own_rows/pallas_call | solution.py:259
  10.4 0.0 collective-permute-done.1.rim_ref
  10.4 0.0 copy-done
  10.4 0.7 %fir_later_rows.1 = (bf16[64,1152]{1,0:T(8,128)(2,1)S(1)}, bf16[32,1152]{1,0:T(8,128)(2,1)S(1)}, bf16[32,1152]{1,0:T(8,128)(2,1)S(1)}, f32[1152,128]{1,0:T(8,128)S(1)}, f32[72,128]{1,0:T(8,128)S(1)}) custom-call(bf16[64,1024]{1,0:T(8,128)(2,1)S(1)} %collective-permute-done.1.rim_ref, f32[1224,128]{1,0:T(8,128)S(1)} %get-tuple-element.50.sums_ref, ...), custom_call_target="tpu_custom_call" | custom-call | bytes 1024 | tf_op jit(solution)/shard_map/fir_later_rows/pallas_call | solution.py:327
  11.1 1.3 %collective-permute-start.2 = (bf16[32,1152]{1,0:T(8,128)(2,1)S(1)}, bf16[32,1152]{1,0:T(8,128)(2,1)S(1)}, u32[]{:S(2)}, u32[]{:S(2)}) collective-permute-start(bf16[32,1152]{1,0:T(8,128)(2,1)S(1)} %get-tuple-element.54), channel_id=1, source_target_pairs={{0,1},{1,0},{2,3},{3,2},{4,5},{5,4},{6,7},{7,6},{8,9},{9,8},{10,11... | collective-permute-start | bytes 221192 | tf_op jit(solution)/shard_map/ppermute | solution.py:683
  12.4 1.2 %collective-permute-start.8 = (bf16[64,1152]{1,0:T(8,128)(2,1)S(1)}, bf16[64,1152]{1,0:T(8,128)(2,1)S(1)}, u32[]{:S(2)}, u32[]{:S(2)}) collective-permute-start(bf16[64,1152]{1,0:T(8,128)(2,1)S(1)} %get-tuple-element.63.high_ref), channel_id=1, source_target_pairs={{0,3},{1,2},{2,1},{3,0},{4,7},{5,6},{6,5},{7,4},{8,11},{9,10},{10,... | collective-permute-start | bytes 442376 | tf_op jit(solution)/shard_map/ppermute | solution.py:683
  13.6 0.0 collective-permute-done.2.refs_2_
  13.6 0.0 collective-permute-done.rim_ref
  13.6 2.0 %fir_earlier_rows.1 = (bf16[64,1152]{1,0:T(8,128)(2,1)S(1)}, bf16[32,1152]{1,0:T(8,128)(2,1)S(1)}, bf16[32,1152]{1,0:T(8,128)(2,1)S(1)}, bf16[3,1024,512]{2,1,0:T(8,128)(2,1)S(1)}) custom-call(bf16[64,1024]{1,0:T(8,128)(2,1)S(1)} %collective-permute-done.rim_ref, f32[1152,128]{1,0:T(8,128)S(1)} %get-tuple-element.49.sums_ref, ...), custom_call_target="tpu_custom_call" | custom-call | bytes 1024 | tf_op jit(solution)/shard_map/fir_earlier_rows/pallas_call | solution.py:388
  15.6 1.2 %collective-permute-start.3 = (bf16[64,1152]{1,0:T(8,128)(2,1)S(1)}, bf16[64,1152]{1,0:T(8,128)(2,1)S(1)}, u32[]{:S(2)}, u32[]{:S(2)}) collective-permute-start(bf16[64,1152]{1,0:T(8,128)(2,1)S(1)} %get-tuple-element.57.low_ref), channel_id=1, source_target_pairs={{0,3},{1,2},{2,1},{3,0},{4,7},{5,6},{6,5},{7,4},{8,11},{9,10},{10,... | collective-permute-start | bytes 442376 | tf_op jit(solution)/shard_map/ppermute | solution.py:683
  16.8 0.2 collective-permute-start.6
  17.0 0.4 collective-permute-start.4
  17.3 0.2 collective-permute-start.5
  17.5 2.9 %projections_near.1 = (f32[128,1536]{1,0:T(8,128)S(1)}, f32[128,128]{1,0:T(8,128)S(1)}, bf16[3,1024,512]{2,1,0:T(8,128)(2,1)S(1)}, bf16[3,1024,512]{2,1,0:T(8,128)(2,1)S(1)}) custom-call(bf16[64,1152]{1,0:T(8,128)(2,1)S(1)} %get-tuple-element.57.low_ref, bf16[64,1152]{1,0:T(8,128)(2,1)S(1)} %get-tuple-element.63.high_ref, ...), custom_call_target="tpu_custom_call" | custom-call | bytes 1024 | tf_op jit(solution)/shard_map/projections_near/pallas_call | solution.py:453
  20.4 0.0 collective-permute-done.8.refs_1_
  20.4 0.4 collective-permute-start.9
  20.8 0.0 collective-permute-done.6.refs_3_
  20.8 0.0 collective-permute-done.4.refs_0_
  20.8 0.0 collective-permute-done.5.refs_1_
  20.8 0.6 %projections_part.2 = (f32[128,1536]{1,0:T(8,128)S(1)}, f32[128,128]{1,0:T(8,128)S(1)}) custom-call(bf16[32,1152]{1,0:T(8,128)(2,1)S(1)} %collective-permute-done.4.refs_0_, bf16[32,1152]{1,0:T(8,128)(2,1)S(1)} %collective-permute-done.5.refs_1_, bf16[32,1152]{1,0:T(8,128)(2,1)S(1)} %collective-permute-done.2.refs_2_, ...), custom_call_target="tpu_custom_call" | custom-call | bytes 1024 | tf_op jit(solution)/shard_map/projections_part/pallas_call | solution.py:486
  21.4 0.2 collective-permute-done.3.refs_0_
  21.6 0.4 collective-permute-start.7
  22.0 0.6 %projections_part.3 = (f32[128,1536]{1,0:T(8,128)S(1)}, f32[128,128]{1,0:T(8,128)S(1)}) custom-call(bf16[64,1152]{1,0:T(8,128)(2,1)S(1)} %collective-permute-done.3.refs_0_, bf16[64,1152]{1,0:T(8,128)(2,1)S(1)} %collective-permute-done.8.refs_1_, bf16[3,1024,512]{2,1,0:T(8,128)(2,1)S(1)} %get-tuple-element.70.refs_2_, ...), custom_call_target="tpu_custom_call" | custom-call | bytes 1024 | tf_op jit(solution)/shard_map/projections_part/pallas_call | solution.py:486
  22.6 0.0 collective-permute-done.9.refs_1_
  22.6 0.4 collective-permute-done.7.refs_0_
  23.0 0.7 %projections_last.1 = (bf16[384,128]{1,0:T(8,128)(2,1)S(1)}, bf16[384,128]{1,0:T(8,128)(2,1)S(1)}, bf16[384,128]{1,0:T(8,128)(2,1)S(1)}, bf16[384,128]{1,0:T(8,128)(2,1)S(1)}) custom-call(bf16[64,1152]{1,0:T(8,128)(2,1)S(1)} %collective-permute-done.7.refs_0_, bf16[64,1152]{1,0:T(8,128)(2,1)S(1)} %collective-permute-done.9.refs_1_, ...), custom_call_target="tpu_custom_call" | custom-call | bytes 1024 | tf_op jit(solution)/shard_map/projections_last/pallas_call | solution.py:523
  23.7 0.4 collective-permute-start.12
  24.1 3.5 %collective-permute-start.14 = (bf16[384,128]{1,0:T(8,128)(2,1)S(1)}, bf16[384,128]{1,0:T(8,128)(2,1)S(1)}, u32[]{:S(2)}, u32[]{:S(2)}) collective-permute-start(bf16[384,128]{1,0:T(8,128)(2,1)S(1)} %get-tuple-element.78), channel_id=1, source_target_pairs={{0,25},{1,24},{2,27},{3,26},{4,29},{5,28},{6,31},{7,30},{8,17},{9,... | collective-permute-start | bytes 294920 | tf_op jit(solution)/shard_map/ppermute | solution.py:724
  27.6 0.0 collective-permute-start.13
  27.6 0.5 %collective-permute-start.10 = (bf16[384,128]{1,0:T(8,128)(2,1)S(1)}, bf16[384,128]{1,0:T(8,128)(2,1)S(1)}, u32[]{:S(2)}, u32[]{:S(2)}) collective-permute-start(bf16[384,128]{1,0:T(8,128)(2,1)S(1)} %get-tuple-element.75), channel_id=1, source_target_pairs={{0,17},{1,16},{2,19},{3,18},{4,21},{5,20},{6,23},{7,22},{8,25},{9,... | collective-permute-start | bytes 294920 | tf_op jit(solution)/shard_map/ppermute | solution.py:724
  28.2 0.0 collective-permute-done.12.refs_0_
  28.2 1.2 %collective-permute-start.15 = (bf16[256,128]{1,0:T(8,128)(2,1)S(1)}, bf16[256,128]{1,0:T(8,128)(2,1)S(1)}, u32[]{:S(2)}, u32[]{:S(2)}) collective-permute-start(bf16[256,128]{1,0:T(8,128)(2,1)S(1)} %slice.17), channel_id=1, source_target_pairs={{0,4},{4,0},{8,12},{12,8},{16,20},{20,16},{24,28},{28,24},{1,5},{5... | collective-permute-start | bytes 196616 | tf_op jit(solution)/shard_map/ppermute | solution.py:727
  29.3 1.7 %collective-permute-done.14.refs_3_ = bf16[384,128]{1,0:T(8,128)(2,1)S(1)} collective-permute-done((bf16[384,128]{1,0:T(8,128)(2,1)S(1)}, bf16[384,128]{1,0:T(8,128)(2,1)S(1)}, u32[]{:S(2)}, u32[]{:S(2)}) %collective-permute-start.14) | collective-permute-done | bytes 98336 | tf_op jit(solution)/shard_map/ppermute | solution.py:724
  31.0 1.2 %collective-permute-start.16 = (bf16[256,128]{1,0:T(8,128)(2,1)S(1)}, bf16[256,128]{1,0:T(8,128)(2,1)S(1)}, u32[]{:S(2)}, u32[]{:S(2)}) collective-permute-start(bf16[256,128]{1,0:T(8,128)(2,1)S(1)} %slice.18), channel_id=1, source_target_pairs={{0,4},{4,0},{8,12},{12,8},{16,20},{20,16},{24,28},{28,24},{1,5},{5... | collective-permute-start | bytes 196616 | tf_op jit(solution)/shard_map/ppermute | solution.py:727
  32.2 1.8 %collective-permute-done.13.refs_1_ = bf16[384,128]{1,0:T(8,128)(2,1)S(1)} collective-permute-done((bf16[384,128]{1,0:T(8,128)(2,1)S(1)}, bf16[384,128]{1,0:T(8,128)(2,1)S(1)}, u32[]{:S(2)}, u32[]{:S(2)}) %collective-permute-start.13) | collective-permute-done | bytes 98336 | tf_op jit(solution)/shard_map/ppermute | solution.py:724
  34.1 1.1 %collective-permute-start.17 = (bf16[256,128]{1,0:T(8,128)(2,1)S(1)}, bf16[256,128]{1,0:T(8,128)(2,1)S(1)}, u32[]{:S(2)}, u32[]{:S(2)}) collective-permute-start(bf16[256,128]{1,0:T(8,128)(2,1)S(1)} %slice.19), channel_id=1, source_target_pairs={{0,4},{4,0},{8,12},{12,8},{16,20},{20,16},{24,28},{28,24},{1,5},{5... | collective-permute-start | bytes 196616 | tf_op jit(solution)/shard_map/ppermute | solution.py:727
  35.2 1.0 %collective-permute-done.10.refs_2_ = bf16[384,128]{1,0:T(8,128)(2,1)S(1)} collective-permute-done((bf16[384,128]{1,0:T(8,128)(2,1)S(1)}, bf16[384,128]{1,0:T(8,128)(2,1)S(1)}, u32[]{:S(2)}, u32[]{:S(2)}) %collective-permute-start.10) | collective-permute-done | bytes 98336 | tf_op jit(solution)/shard_map/ppermute | solution.py:724
  36.2 1.1 %collective-permute-start.11 = (bf16[256,128]{1,0:T(8,128)(2,1)S(1)}, bf16[256,128]{1,0:T(8,128)(2,1)S(1)}, u32[]{:S(2)}, u32[]{:S(2)}) collective-permute-start(bf16[256,128]{1,0:T(8,128)(2,1)S(1)} %slice.16), channel_id=1, source_target_pairs={{0,4},{4,0},{8,12},{12,8},{16,20},{20,16},{24,28},{28,24},{1,5},{5... | collective-permute-start | bytes 196616 | tf_op jit(solution)/shard_map/ppermute | solution.py:727
  37.3 0.0 collective-permute-done.15.refs_4_
  37.3 0.0 collective-permute-done.16.refs_5_
  37.3 0.0 collective-permute-done.17.refs_6_
  37.3 1.3 %attention_most.1 = (bf16[512,128]{1,0:T(8,128)(2,1)S(1)}, f32[512,128]{1,0:T(8,128)S(1)}, f32[512,128]{1,0:T(8,128)S(1)}, f32[512,128]{1,0:T(8,128)S(1)}) custom-call(bf16[384,128]{1,0:T(8,128)(2,1)S(1)} %collective-permute-done.12.refs_0_, bf16[384,128]{1,0:T(8,128)(2,1)S(1)} %collective-permute-done.13.refs_1_, ...), custom_call_target="tpu_custom_call" | custom-call | bytes 1024 | tf_op jit(solution)/shard_map/attention_most/pallas_call | solution.py:584
  38.6 0.7 %collective-permute-done.11.other_ref = bf16[256,128]{1,0:T(8,128)(2,1)S(1)} collective-permute-done((bf16[256,128]{1,0:T(8,128)(2,1)S(1)}, bf16[256,128]{1,0:T(8,128)(2,1)S(1)}, u32[]{:S(2)}, u32[]{:S(2)}) %collective-permute-start.11) | collective-permute-done | bytes 65568 | tf_op jit(solution)/shard_map/ppermute | solution.py:727
  39.3 0.5 %attention_rest.1 = (bf16[128,128]{1,0:T(8,128)(2,1)S(1)}, bf16[128,128]{1,0:T(8,128)(2,1)S(1)}, bf16[128,128]{1,0:T(8,128)(2,1)S(1)}, bf16[128,128]{1,0:T(8,128)(2,1)S(1)}) custom-call(bf16[256,128]{1,0:T(8,128)(2,1)S(1)} %collective-permute-done.11.other_ref, bf16[512,128]{1,0:T(8,128)(2,1)S(1)} %get-tuple-element.79.query_ref, ...), custom_call_target="tpu_custom_call" | custom-call | bytes 1024 | tf_op jit(solution)/shard_map/attention_rest/pallas_call | solution.py:617
  39.9 2.6 %collective-permute-start.18 = (bf16[128,128]{1,0:T(8,128)(2,1)S(1)}, bf16[128,128]{1,0:T(8,128)(2,1)S(1)}, u32[]{:S(2)}, u32[]{:S(2)}) collective-permute-start(bf16[128,128]{1,0:T(8,128)(2,1)S(1)} %get-tuple-element.83), channel_id=1, source_target_pairs={{0,17},{1,16},{2,19},{3,18},{4,21},{5,20},{6,23},{7,22},{8,25},{9,... | collective-permute-start | bytes 98312 | tf_op jit(solution)/shard_map/ppermute | solution.py:724
  42.4 1.4 %collective-permute-start.19 = (bf16[128,128]{1,0:T(8,128)(2,1)S(1)}, bf16[128,128]{1,0:T(8,128)(2,1)S(1)}, u32[]{:S(2)}, u32[]{:S(2)}) collective-permute-start(bf16[128,128]{1,0:T(8,128)(2,1)S(1)} %get-tuple-element.84), channel_id=1, source_target_pairs={{0,25},{1,24},{2,27},{3,26},{4,29},{5,28},{6,31},{7,30},{8,17},{9,... | collective-permute-start | bytes 98312 | tf_op jit(solution)/shard_map/ppermute | solution.py:724
  43.9 0.4 collective-permute-start.20
  44.3 0.2 collective-permute-start.21
  44.5 0.0 collective-permute-done.18.refs_0_
  44.5 3.1 %collective-permute-done.19.refs_1_ = bf16[128,128]{1,0:T(8,128)(2,1)S(1)} collective-permute-done((bf16[128,128]{1,0:T(8,128)(2,1)S(1)}, bf16[128,128]{1,0:T(8,128)(2,1)S(1)}, u32[]{:S(2)}, u32[]{:S(2)}) %collective-permute-start.19) | collective-permute-done | bytes 32800 | tf_op jit(solution)/shard_map/ppermute | solution.py:724
  47.6 0.0 collective-permute-done.20.refs_2_
  47.6 0.0 collective-permute-done.21.refs_3_
  47.6 0.7 %join_heads.1 = bf16[128,512]{1,0:T(8,128)(2,1)} custom-call(bf16[128,128]{1,0:T(8,128)(2,1)S(1)} %collective-permute-done.18.refs_0_, bf16[128,128]{1,0:T(8,128)(2,1)S(1)} %collective-permute-done.19.refs_1_, bf16[128,128]{1,0:T(8,128)(2,1)S(1)} %collective-permute-done.20.refs_2_, bf16[128,128]{1,0:T(8,128)(2,1)S(1)} %collective-permute-done.21.refs_3_), custom_call_target="tpu_custom_call" | custom-call | bytes 1024 | tf_op jit(solution)/shard_map/join_heads/pallas_call | solution.py:637
  (4 shorter events, 0.0 us)
Async XLA Ops:
  1.3 9.1 %collective-permute-start.1 = (bf16[64,1024]{1,0:T(8,128)(2,1)S(1)}, bf16[64,1024]{1,0:T(8,128)(2,1)S(1)}, u32[]{:S(2)}, u32[]{:S(2)}) collective-permute-start(bf16[64,1024]{1,0:T(8,128)(2,1)S(1)} %get-tuple-element.47.high_ref), channel_id=1, source_target_pairs={{0,4},{4,8},{8,12},{12,16},{16,20},{20,24},{24,28},{1,5},{5,9},{9,... | collective-permute-start | bytes 393224 | tf_op jit(solution)/shard_map/ppermute | solution.py:689
  5.3 8.3 %collective-permute-start = (bf16[64,1024]{1,0:T(8,128)(2,1)S(1)}, bf16[64,1024]{1,0:T(8,128)(2,1)S(1)}, u32[]{:S(2)}, u32[]{:S(2)}) collective-permute-start(bf16[64,1024]{1,0:T(8,128)(2,1)S(1)} %get-tuple-element.46.low_ref), channel_id=1, source_target_pairs={{0,4},{4,8},{8,12},{12,16},{16,20},{20,24},{24,28},{1,5},{5,9},{9,... | collective-permute-start | bytes 393224 | tf_op jit(solution)/shard_map/ppermute | solution.py:689
  8.5 2.0 %copy-start = (f32[1024]{0:T(1024)S(1)}, f32[1024]{0:T(1024)}, u32[]{:S(2)}) copy-start(f32[1024]{0:T(1024)} %param.10) | copy-start | bytes 12292
  11.1 2.5 %collective-permute-start.2 = (bf16[32,1152]{1,0:T(8,128)(2,1)S(1)}, bf16[32,1152]{1,0:T(8,128)(2,1)S(1)}, u32[]{:S(2)}, u32[]{:S(2)}) collective-permute-start(bf16[32,1152]{1,0:T(8,128)(2,1)S(1)} %get-tuple-element.54), channel_id=1, source_target_pairs={{0,1},{1,0},{2,3},{3,2},{4,5},{5,4},{6,7},{7,6},{8,9},{9,8},{10,11... | collective-permute-start | bytes 221192 | tf_op jit(solution)/shard_map/ppermute | solution.py:683
  12.4 8.0 %collective-permute-start.8 = (bf16[64,1152]{1,0:T(8,128)(2,1)S(1)}, bf16[64,1152]{1,0:T(8,128)(2,1)S(1)}, u32[]{:S(2)}, u32[]{:S(2)}) collective-permute-start(bf16[64,1152]{1,0:T(8,128)(2,1)S(1)} %get-tuple-element.63.high_ref), channel_id=1, source_target_pairs={{0,3},{1,2},{2,1},{3,0},{4,7},{5,6},{6,5},{7,4},{8,11},{9,10},{10,... | collective-permute-start | bytes 442376 | tf_op jit(solution)/shard_map/ppermute | solution.py:683
  15.6 6.0 %collective-permute-start.3 = (bf16[64,1152]{1,0:T(8,128)(2,1)S(1)}, bf16[64,1152]{1,0:T(8,128)(2,1)S(1)}, u32[]{:S(2)}, u32[]{:S(2)}) collective-permute-start(bf16[64,1152]{1,0:T(8,128)(2,1)S(1)} %get-tuple-element.57.low_ref), channel_id=1, source_target_pairs={{0,3},{1,2},{2,1},{3,0},{4,7},{5,6},{6,5},{7,4},{8,11},{9,10},{10,... | collective-permute-start | bytes 442376 | tf_op jit(solution)/shard_map/ppermute | solution.py:683
  16.8 4.0 %collective-permute-start.6 = (bf16[32,1152]{1,0:T(8,128)(2,1)S(1)}, bf16[32,1152]{1,0:T(8,128)(2,1)S(1)}, u32[]{:S(2)}, u32[]{:S(2)}) collective-permute-start(bf16[32,1152]{1,0:T(8,128)(2,1)S(1)} %get-tuple-element.61), channel_id=1, source_target_pairs={{0,1},{1,0},{2,3},{3,2},{4,5},{5,4},{6,7},{7,6},{8,9},{9,8},{10,11... | collective-permute-start | bytes 221192 | tf_op jit(solution)/shard_map/ppermute | solution.py:683
  17.0 3.8 %collective-permute-start.4 = (bf16[32,1152]{1,0:T(8,128)(2,1)S(1)}, bf16[32,1152]{1,0:T(8,128)(2,1)S(1)}, u32[]{:S(2)}, u32[]{:S(2)}) collective-permute-start(bf16[32,1152]{1,0:T(8,128)(2,1)S(1)} %get-tuple-element.58), channel_id=1, source_target_pairs={{0,1},{1,0},{2,3},{3,2},{4,5},{5,4},{6,7},{7,6},{8,9},{9,8},{10,11... | collective-permute-start | bytes 221192 | tf_op jit(solution)/shard_map/ppermute | solution.py:683
  17.3 3.5 %collective-permute-start.5 = (bf16[32,1152]{1,0:T(8,128)(2,1)S(1)}, bf16[32,1152]{1,0:T(8,128)(2,1)S(1)}, u32[]{:S(2)}, u32[]{:S(2)}) collective-permute-start(bf16[32,1152]{1,0:T(8,128)(2,1)S(1)} %get-tuple-element.59), channel_id=1, source_target_pairs={{0,1},{1,0},{2,3},{3,2},{4,5},{5,4},{6,7},{7,6},{8,9},{9,8},{10,11... | collective-permute-start | bytes 221192 | tf_op jit(solution)/shard_map/ppermute | solution.py:683
  20.4 2.2 %collective-permute-start.9 = (bf16[64,1152]{1,0:T(8,128)(2,1)S(1)}, bf16[64,1152]{1,0:T(8,128)(2,1)S(1)}, u32[]{:S(2)}, u32[]{:S(2)}) collective-permute-start(bf16[64,1152]{1,0:T(8,128)(2,1)S(1)} %collective-permute-done.8.refs_1_), channel_id=1, source_target_pairs={{0,1},{1,0},{2,3},{3,2},{4,5},{5,4},{6,7},{7,6},{8,9},{9,8},{10,11... | collective-permute-start | bytes 442376 | tf_op jit(solution)/shard_map/ppermute | solution.py:683
  21.6 1.4 %collective-permute-start.7 = (bf16[64,1152]{1,0:T(8,128)(2,1)S(1)}, bf16[64,1152]{1,0:T(8,128)(2,1)S(1)}, u32[]{:S(2)}, u32[]{:S(2)}) collective-permute-start(bf16[64,1152]{1,0:T(8,128)(2,1)S(1)} %collective-permute-done.3.refs_0_), channel_id=1, source_target_pairs={{0,1},{1,0},{2,3},{3,2},{4,5},{5,4},{6,7},{7,6},{8,9},{9,8},{10,11... | collective-permute-start | bytes 442376 | tf_op jit(solution)/shard_map/ppermute | solution.py:683
  23.7 4.5 %collective-permute-start.12 = (bf16[384,128]{1,0:T(8,128)(2,1)S(1)}, bf16[384,128]{1,0:T(8,128)(2,1)S(1)}, u32[]{:S(2)}, u32[]{:S(2)}) collective-permute-start(bf16[384,128]{1,0:T(8,128)(2,1)S(1)} %get-tuple-element.76), channel_id=1, source_target_pairs={{0,1},{1,0},{2,3},{3,2},{4,5},{5,4},{6,7},{7,6},{8,9},{9,8},{10,11... | collective-permute-start | bytes 294920 | tf_op jit(solution)/shard_map/ppermute | solution.py:724
  24.1 6.9 %collective-permute-start.14 = (bf16[384,128]{1,0:T(8,128)(2,1)S(1)}, bf16[384,128]{1,0:T(8,128)(2,1)S(1)}, u32[]{:S(2)}, u32[]{:S(2)}) collective-permute-start(bf16[384,128]{1,0:T(8,128)(2,1)S(1)} %get-tuple-element.78), channel_id=1, source_target_pairs={{0,25},{1,24},{2,27},{3,26},{4,29},{5,28},{6,31},{7,30},{8,17},{9,... | collective-permute-start | bytes 294920 | tf_op jit(solution)/shard_map/ppermute | solution.py:724
  27.6 6.4 %collective-permute-start.13 = (bf16[384,128]{1,0:T(8,128)(2,1)S(1)}, bf16[384,128]{1,0:T(8,128)(2,1)S(1)}, u32[]{:S(2)}, u32[]{:S(2)}) collective-permute-start(bf16[384,128]{1,0:T(8,128)(2,1)S(1)} %get-tuple-element.77), channel_id=1, source_target_pairs={{0,9},{1,8},{2,11},{3,10},{4,13},{5,12},{6,15},{7,14},{8,1},{9,0},... | collective-permute-start | bytes 294920 | tf_op jit(solution)/shard_map/ppermute | solution.py:724
  27.6 8.5 %collective-permute-start.10 = (bf16[384,128]{1,0:T(8,128)(2,1)S(1)}, bf16[384,128]{1,0:T(8,128)(2,1)S(1)}, u32[]{:S(2)}, u32[]{:S(2)}) collective-permute-start(bf16[384,128]{1,0:T(8,128)(2,1)S(1)} %get-tuple-element.75), channel_id=1, source_target_pairs={{0,17},{1,16},{2,19},{3,18},{4,21},{5,20},{6,23},{7,22},{8,25},{9,... | collective-permute-start | bytes 294920 | tf_op jit(solution)/shard_map/ppermute | solution.py:724
  28.2 9.1 %collective-permute-start.15 = (bf16[256,128]{1,0:T(8,128)(2,1)S(1)}, bf16[256,128]{1,0:T(8,128)(2,1)S(1)}, u32[]{:S(2)}, u32[]{:S(2)}) collective-permute-start(bf16[256,128]{1,0:T(8,128)(2,1)S(1)} %slice.17), channel_id=1, source_target_pairs={{0,4},{4,0},{8,12},{12,8},{16,20},{20,16},{24,28},{28,24},{1,5},{5... | collective-permute-start | bytes 196616 | tf_op jit(solution)/shard_map/ppermute | solution.py:727
  31.0 6.3 %collective-permute-start.16 = (bf16[256,128]{1,0:T(8,128)(2,1)S(1)}, bf16[256,128]{1,0:T(8,128)(2,1)S(1)}, u32[]{:S(2)}, u32[]{:S(2)}) collective-permute-start(bf16[256,128]{1,0:T(8,128)(2,1)S(1)} %slice.18), channel_id=1, source_target_pairs={{0,4},{4,0},{8,12},{12,8},{16,20},{20,16},{24,28},{28,24},{1,5},{5... | collective-permute-start | bytes 196616 | tf_op jit(solution)/shard_map/ppermute | solution.py:727
  34.1 3.2 %collective-permute-start.17 = (bf16[256,128]{1,0:T(8,128)(2,1)S(1)}, bf16[256,128]{1,0:T(8,128)(2,1)S(1)}, u32[]{:S(2)}, u32[]{:S(2)}) collective-permute-start(bf16[256,128]{1,0:T(8,128)(2,1)S(1)} %slice.19), channel_id=1, source_target_pairs={{0,4},{4,0},{8,12},{12,8},{16,20},{20,16},{24,28},{28,24},{1,5},{5... | collective-permute-start | bytes 196616 | tf_op jit(solution)/shard_map/ppermute | solution.py:727
  36.2 3.1 %collective-permute-start.11 = (bf16[256,128]{1,0:T(8,128)(2,1)S(1)}, bf16[256,128]{1,0:T(8,128)(2,1)S(1)}, u32[]{:S(2)}, u32[]{:S(2)}) collective-permute-start(bf16[256,128]{1,0:T(8,128)(2,1)S(1)} %slice.16), channel_id=1, source_target_pairs={{0,4},{4,0},{8,12},{12,8},{16,20},{20,16},{24,28},{28,24},{1,5},{5... | collective-permute-start | bytes 196616 | tf_op jit(solution)/shard_map/ppermute | solution.py:727
  39.9 4.6 %collective-permute-start.18 = (bf16[128,128]{1,0:T(8,128)(2,1)S(1)}, bf16[128,128]{1,0:T(8,128)(2,1)S(1)}, u32[]{:S(2)}, u32[]{:S(2)}) collective-permute-start(bf16[128,128]{1,0:T(8,128)(2,1)S(1)} %get-tuple-element.83), channel_id=1, source_target_pairs={{0,17},{1,16},{2,19},{3,18},{4,21},{5,20},{6,23},{7,22},{8,25},{9,... | collective-permute-start | bytes 98312 | tf_op jit(solution)/shard_map/ppermute | solution.py:724
  42.4 5.1 %collective-permute-start.19 = (bf16[128,128]{1,0:T(8,128)(2,1)S(1)}, bf16[128,128]{1,0:T(8,128)(2,1)S(1)}, u32[]{:S(2)}, u32[]{:S(2)}) collective-permute-start(bf16[128,128]{1,0:T(8,128)(2,1)S(1)} %get-tuple-element.84), channel_id=1, source_target_pairs={{0,25},{1,24},{2,27},{3,26},{4,29},{5,28},{6,31},{7,30},{8,17},{9,... | collective-permute-start | bytes 98312 | tf_op jit(solution)/shard_map/ppermute | solution.py:724
  43.9 3.7 %collective-permute-start.20 = (bf16[128,128]{1,0:T(8,128)(2,1)S(1)}, bf16[128,128]{1,0:T(8,128)(2,1)S(1)}, u32[]{:S(2)}, u32[]{:S(2)}) collective-permute-start(bf16[128,128]{1,0:T(8,128)(2,1)S(1)} %get-tuple-element.85), channel_id=1, source_target_pairs={{0,9},{1,8},{2,11},{3,10},{4,13},{5,12},{6,15},{7,14},{8,1},{9,0},... | collective-permute-start | bytes 98312 | tf_op jit(solution)/shard_map/ppermute | solution.py:724
  44.3 3.3 %collective-permute-start.21 = (bf16[128,128]{1,0:T(8,128)(2,1)S(1)}, bf16[128,128]{1,0:T(8,128)(2,1)S(1)}, u32[]{:S(2)}, u32[]{:S(2)}) collective-permute-start(bf16[128,128]{1,0:T(8,128)(2,1)S(1)} %get-tuple-element.86), channel_id=1, source_target_pairs={{0,1},{1,0},{2,3},{3,2},{4,5},{5,4},{6,7},{7,6},{8,9},{9,8},{10,11... | collective-permute-start | bytes 98312 | tf_op jit(solution)/shard_map/ppermute | solution.py:724

commit v11 on v10

--- a/solution.py
+++ b/solution.py
@@ -233,14 +233,18 @@
         copy.wait()
 
 
-def weight_copies(weight_hbm, weight_ref, offsets, sems):
+def weight_copies(weight_hbm, weight_ref, offsets, sems, first=0):
     copies = []
     channels = weight_ref.shape[1] // len(offsets)
     for n, offset in enumerate(offsets):
         owner = jnp.bitwise_xor(lax.axis_index("tp"), offset)
         copies.append(
             pltpu.make_async_copy(
-                weight_hbm.at[:, pl.ds(pl.multiple_of(owner * channels, channels), channels), :],
+                weight_hbm.at[
+                    pl.ds(first, weight_ref.shape[0]),
+                    pl.ds(pl.multiple_of(owner * channels, channels), channels),
+                    :,
+                ],
                 weight_ref.at[:, pl.ds(n * channels, channels), :],
                 sems.at[n],
             )
@@ -248,8 +252,8 @@
     return copies
 
 
-def weight_rows(weight, count, channels):
-    return jax.ShapeDtypeStruct((3, count * channels, weight.shape[2]), BF16)
+def weight_rows(weight, count, channels, kinds=3):
+    return jax.ShapeDtypeStruct((kinds, count * channels, weight.shape[2]), BF16)
 
 
 def own_part(low, high, taps, weight, channels):
@@ -387,7 +391,7 @@
     eighth = rows // PHASES
     return pl.pallas_call(
         functools.partial(low_kernel, offsets),
-        out_shape=sent_shapes(rows) + (weight_rows(weight, len(offsets), channels),),
+        out_shape=sent_shapes(rows) + (weight_rows(weight, len(offsets), channels, 2),),
         in_specs=[VMEM] * 7 + [HBM],
         out_specs=(VMEM,) * 4,
         scratch_shapes=[
@@ -412,7 +416,7 @@
 
 
 def project(blocks, weight_refs, acc_ref, ssq_ref):
-    width = weight_refs[0].shape[2]
+    width = weight_refs[0][0].shape[1]
     whole = [jnp.concatenate([piece[...] for piece in pieces], axis=0) for pieces in blocks]
     channels = whole[0].shape[1] - LANES
     for block in whole:
@@ -423,7 +427,7 @@
         for ref, block in zip(weight_refs, whole):
             total = total + jnp.dot(
                 block[:, :channels],
-                ref[which],
+                ref[which][...],
                 preferred_element_type=F32,
             )
         acc_ref[:, lanes] = total
@@ -435,8 +439,9 @@
 
 
 def near_kernel(far, last, low_ref, high_ref, own_ref, weight_hbm, *refs):
-    acc_ref, ssq_ref, far_ref, last_ref, far_sems, last_sems = refs
-    copies = weight_copies(weight_hbm, far_ref, far, far_sems)
+    acc_ref, ssq_ref, beside_ref, far_ref, last_ref, beside_sems, far_sems, last_sems = refs
+    copies = weight_copies(weight_hbm, beside_ref, (1,), beside_sems, 2)
+    copies += weight_copies(weight_hbm, far_ref, far, far_sems)
     copies += weight_copies(weight_hbm, last_ref, last, last_sems)
     for copy in copies:
         copy.start()
@@ -455,12 +460,14 @@
         out_shape=(
             jax.ShapeDtypeStruct((rows, 3 * width), F32),
             jax.ShapeDtypeStruct((rows, LANES), F32),
+            weight_rows(weight, 1, channels, 1),
             weight_rows(weight, len(far), channels),
             weight_rows(weight, len(last), channels),
         ),
         in_specs=[VMEM] * 3 + [HBM],
-        out_specs=(VMEM,) * 4,
+        out_specs=(VMEM,) * 5,
         scratch_shapes=[
+            pltpu.SemaphoreType.DMA((1,)),
             pltpu.SemaphoreType.DMA((len(far),)),
             pltpu.SemaphoreType.DMA((len(last),)),
         ],
@@ -475,13 +482,18 @@
     for size in sizes:
         blocks.append(rest[:size])
         del rest[:size]
-    weight_ref, acc_in, ssq_in, acc_ref, ssq_ref = rest
+    *weight_refs, acc_in, ssq_in, acc_ref, ssq_ref = rest
     acc_ref[...] = acc_in[...]
     ssq_ref[...] = ssq_in[...]
-    project(blocks, split_rows(weight_ref, len(blocks)), acc_ref, ssq_ref)
-
-
-def part_projection(blocks, weight, acc, ssq):
+    parts = [split_rows(ref, len(blocks)) for ref in weight_refs]
+    kinds = [
+        [part[n].at[i] for part in parts for i in range(part[n].shape[0])]
+        for n in range(len(blocks))
+    ]
+    project(blocks, kinds, acc_ref, ssq_ref)
+
+
+def part_projection(blocks, weights, acc, ssq):
     sizes = tuple(len(pieces) for pieces in blocks)
     return pl.pallas_call(
         functools.partial(partial_kernel, sizes),
@@ -489,12 +501,12 @@
             jax.ShapeDtypeStruct(acc.shape, F32),
             jax.ShapeDtypeStruct(ssq.shape, F32),
         ),
-        in_specs=[VMEM] * (sum(sizes) + 3),
+        in_specs=[VMEM] * (sum(sizes) + len(weights) + 2),
         out_specs=(VMEM,) * 2,
         compiler_params=params(24),
         cost_estimate=cost(),
         name="projections_part",
-    )(*[piece for pieces in blocks for piece in pieces], weight, acc, ssq)
+    )(*[piece for pieces in blocks for piece in pieces], *weights, acc, ssq)
 
 
 def last_kernel(count, model, spread, *refs):
@@ -707,14 +719,14 @@
     far = []
     for by in steps:
         far += [tuple(swapped(part, by) for part in pair) for pair in [sent] + far]
-    acc, ssq, far_weight, last_weight = near_projection(
+    acc, ssq, beside_value, far_weight, last_weight = near_projection(
         sent, own_weight, weight, tuple(offsets), tuple(o ^ 1 for o in offsets)
     )
-    acc, ssq = part_projection([near_low + near_high], beside_weight, acc, ssq)
+    acc, ssq = part_projection([near_low + near_high], (beside_weight, beside_value), acc, ssq)
     last_low, acc = lax.optimization_barrier((far[-1][0], acc))
     far[-1] = (last_low, far[-1][1])
     swaps = [tuple(swapped(part, 1) for part in pair) for pair in far]
-    acc, ssq = part_projection(far, far_weight, acc, ssq)
+    acc, ssq = part_projection(far, (far_weight,), acc, ssq)
     messages = last_projection(swaps, last_weight, acc, ssq, model, chip_per_head)
     if not chip_per_head:
         return gathered_attention(messages[::-1], heads, rows)

time: 48.5 us -> 49.1 us (1.012)
    pallas_call x1, Pallas kernels: 2.88 us -> 3.63 us  [near_projection(): pl.pallas_call(functools.partial(near_kernel, far, last), out_shape=(jax....]
where the time goes in v11:
time: 49.1 us; the launch traced here: 48.9 us
  starting transfers between devices  25.7 us (52%)
  Pallas kernels  13.6 us (28%)
  waiting for transfers between devices  9.34 us (19%)
    ppermute x8, starting transfers between devices, over_z(): return lax.ppermute(value, ('ctx', 'tp'), pairs)  9.06 us
    ppermute x8, waiting for transfers between devices, over_z(): return lax.ppermute(value, ('ctx', 'tp'), pairs)  7.9 us
    ppermute x2, starting transfers between devices, body(): lax.ppermute(part, 'ctx', [(i, i + 1) for i in range(ctx - 1)])  7.13 us
    ppermute x8, starting transfers between devices, swapped(): return lax.ppermute(value, 'tp', [(i, i ^ by) for i in range(tp)])  5.04 us
    ppermute x4, starting transfers between devices, over_y(): return lax.ppermute(value, 'ctx', [(i, i ^ 1) for i in range(ctx)])  4.49 us
    pallas_call x1, Pallas kernels, near_projection(): pl.pallas_call(functools.partial(near_kernel, far, last), out_shape=(jax....  3.63 us
    pallas_call x1, Pallas kernels, own_part(): pl.pallas_call(own_kernel, out_shape=(slabs(SUBS * eighth), slabs(SUBS *...  1.95 us
    pallas_call x1, Pallas kernels, low_part(): pl.pallas_call(functools.partial(low_kernel, offsets), out_shape=sent_sha...  1.65 us
  transfers between devices with their start and end apart: 22, of which 7 were waited for; matrix products, arithmetic and copies ran while one was open for 0% of the time, Pallas kernels for 21%

profile of v11, /device:TPU:1, one launch (start us, length us, event | category | flops | bytes accessed | tf_op | source)
XLA Modules:
  0.0 48.9 jit_solution(16083102588860238421)
XLA Ops:
  0.0 1.3 %conv_times_value.1 = (bf16[64,1024]{1,0:T(8,128)(2,1)S(1)}, bf16[64,1024]{1,0:T(8,128)(2,1)S(1)}, f32[128,1024]{1,0:T(8,128)S(1)}, bf16[128,1024]{1,0:T(8,128)(2,1)S(1)}) custom-call(bf16[128,1024]{1,0:T(8,128)(2,1)} %conv_hbm.1, bf16[128,1024]{1,0:T(8,128)(2,1)} %value_hbm.1, f32[128,1024]{1,0:T(8,128)} %taps_hbm.1, bf16[128,1024]{1,0:T(8,128)(2,1)} %gate_hbm.1), custom_call_target="tpu_custom_call" | custom-call | bytes 1024 | tf_op jit(solution)/shard_map/conv_times_value/pallas_call | solution.py:169
  1.3 4.0 %collective-permute-start.1 = (bf16[64,1024]{1,0:T(8,128)(2,1)S(1)}, bf16[64,1024]{1,0:T(8,128)(2,1)S(1)}, u32[]{:S(2)}, u32[]{:S(2)}) collective-permute-start(bf16[64,1024]{1,0:T(8,128)(2,1)S(1)} %get-tuple-element.48.high_ref), channel_id=1, source_target_pairs={{0,4},{4,8},{8,12},{12,16},{16,20},{20,24},{24,28},{1,5},{5,9},{9,... | collective-permute-start | bytes 393224 | tf_op jit(solution)/shard_map/ppermute | solution.py:701
  5.3 3.1 %collective-permute-start = (bf16[64,1024]{1,0:T(8,128)(2,1)S(1)}, bf16[64,1024]{1,0:T(8,128)(2,1)S(1)}, u32[]{:S(2)}, u32[]{:S(2)}) collective-permute-start(bf16[64,1024]{1,0:T(8,128)(2,1)S(1)} %get-tuple-element.47.low_ref), channel_id=1, source_target_pairs={{0,4},{4,8},{8,12},{12,16},{16,20},{20,24},{24,28},{1,5},{5,9},{9,... | collective-permute-start | bytes 393224 | tf_op jit(solution)/shard_map/ppermute | solution.py:701
  8.5 0.0 copy-start
  8.5 2.0 %fir_own_rows.1 = (f32[1152,128]{1,0:T(8,128)S(1)}, f32[1224,128]{1,0:T(8,128)S(1)}, f32[2304,128]{1,0:T(8,128)S(1)}, bf16[3,1024,512]{2,1,0:T(8,128)(2,1)S(1)}) custom-call(bf16[64,1024]{1,0:T(8,128)(2,1)S(1)} %get-tuple-element.47.low_ref, bf16[64,1024]{1,0:T(8,128)(2,1)S(1)} %get-tuple-element.48.high_ref, f32[128,1024]{1,0:T(8,128)S(1)} %get-tuple-element.49.taps_ref, ...), custom_call_target="tpu_custom_call" | custom-call | bytes 1024 | tf_op jit(solution)/shard_map/fir_own_rows/pallas_call | solution.py:263
  10.4 0.0 collective-permute-done.1.rim_ref
  10.4 0.0 copy-done
  10.4 0.7 %fir_later_rows.1 = (bf16[64,1152]{1,0:T(8,128)(2,1)S(1)}, bf16[32,1152]{1,0:T(8,128)(2,1)S(1)}, bf16[32,1152]{1,0:T(8,128)(2,1)S(1)}, f32[1152,128]{1,0:T(8,128)S(1)}, f32[72,128]{1,0:T(8,128)S(1)}) custom-call(bf16[64,1024]{1,0:T(8,128)(2,1)S(1)} %collective-permute-done.1.rim_ref, f32[1224,128]{1,0:T(8,128)S(1)} %get-tuple-element.51.sums_ref, ...), custom_call_target="tpu_custom_call" | custom-call | bytes 1024 | tf_op jit(solution)/shard_map/fir_later_rows/pallas_call | solution.py:331
  11.1 1.3 %collective-permute-start.2 = (bf16[32,1152]{1,0:T(8,128)(2,1)S(1)}, bf16[32,1152]{1,0:T(8,128)(2,1)S(1)}, u32[]{:S(2)}, u32[]{:S(2)}) collective-permute-start(bf16[32,1152]{1,0:T(8,128)(2,1)S(1)} %get-tuple-element.55), channel_id=1, source_target_pairs={{0,1},{1,0},{2,3},{3,2},{4,5},{5,4},{6,7},{7,6},{8,9},{9,8},{10,11... | collective-permute-start | bytes 221192 | tf_op jit(solution)/shard_map/ppermute | solution.py:695
  12.4 1.2 %collective-permute-start.8 = (bf16[64,1152]{1,0:T(8,128)(2,1)S(1)}, bf16[64,1152]{1,0:T(8,128)(2,1)S(1)}, u32[]{:S(2)}, u32[]{:S(2)}) collective-permute-start(bf16[64,1152]{1,0:T(8,128)(2,1)S(1)} %get-tuple-element.64.high_ref), channel_id=1, source_target_pairs={{0,3},{1,2},{2,1},{3,0},{4,7},{5,6},{6,5},{7,4},{8,11},{9,10},{10,... | collective-permute-start | bytes 442376 | tf_op jit(solution)/shard_map/ppermute | solution.py:695
  13.6 0.0 collective-permute-done.2.refs_2_
  13.6 0.0 collective-permute-done.rim_ref
  13.6 1.7 %fir_earlier_rows.1 = (bf16[64,1152]{1,0:T(8,128)(2,1)S(1)}, bf16[32,1152]{1,0:T(8,128)(2,1)S(1)}, bf16[32,1152]{1,0:T(8,128)(2,1)S(1)}, bf16[2,1024,512]{2,1,0:T(8,128)(2,1)S(1)}) custom-call(bf16[64,1024]{1,0:T(8,128)(2,1)S(1)} %collective-permute-done.rim_ref, f32[1152,128]{1,0:T(8,128)S(1)} %get-tuple-element.50.sums_ref, ...), custom_call_target="tpu_custom_call" | custom-call | bytes 1024 | tf_op jit(solution)/shard_map/fir_earlier_rows/pallas_call | solution.py:392
  15.3 1.2 %collective-permute-start.3 = (bf16[64,1152]{1,0:T(8,128)(2,1)S(1)}, bf16[64,1152]{1,0:T(8,128)(2,1)S(1)}, u32[]{:S(2)}, u32[]{:S(2)}) collective-permute-start(bf16[64,1152]{1,0:T(8,128)(2,1)S(1)} %get-tuple-element.58.low_ref), channel_id=1, source_target_pairs={{0,3},{1,2},{2,1},{3,0},{4,7},{5,6},{6,5},{7,4},{8,11},{9,10},{10,... | collective-permute-start | bytes 442376 | tf_op jit(solution)/shard_map/ppermute | solution.py:695
  16.5 0.2 collective-permute-start.6
  16.7 0.4 collective-permute-start.4
  17.1 0.2 collective-permute-start.5
  17.2 3.6 %projections_near.1 = (f32[128,1536]{1,0:T(8,128)S(1)}, f32[128,128]{1,0:T(8,128)S(1)}, bf16[1,1024,512]{2,1,0:T(8,128)(2,1)S(1)}, bf16[3,1024,512]{2,1,0:T(8,128)(2,1)S(1)}, bf16[3,1024,512]{2,1,0:T(8,128)(2,1)S(1)}) custom-call(bf16[64,1152]{1,0:T(8,128)(2,1)S(1)} %get-tuple-element.58.low_ref, bf16[64,1152]{1,0:T(8,128)(2,1)S(1)} %get-tuple-element.64.high_ref, ...), custom_call_target="tpu_custom_call" | custom-call | bytes 1024 | tf_op jit(solution)/shard_map/projections_near/pallas_call | solution.py:458
  20.9 0.0 collective-permute-done.8.refs_1_
  20.9 0.4 collective-permute-start.9
  21.3 0.0 collective-permute-done.6.refs_3_
  21.3 0.0 collective-permute-done.4.refs_0_
  21.3 0.0 collective-permute-done.5.refs_1_
  21.3 0.6 %projections_part.2 = (f32[128,1536]{1,0:T(8,128)S(1)}, f32[128,128]{1,0:T(8,128)S(1)}) custom-call(bf16[32,1152]{1,0:T(8,128)(2,1)S(1)} %collective-permute-done.4.refs_0_, bf16[32,1152]{1,0:T(8,128)(2,1)S(1)} %collective-permute-done.5.refs_1_, bf16[32,1152]{1,0:T(8,128)(2,1)S(1)} %collective-permute-done.2.refs_2_, ...), custom_call_target="tpu_custom_call" | custom-call | bytes 1024 | tf_op jit(solution)/shard_map/projections_part/pallas_call | solution.py:498
  21.9 0.0 collective-permute-done.3.refs_0_
  21.9 0.2 collective-permute-start.7
  22.1 0.6 %projections_part.3 = (f32[128,1536]{1,0:T(8,128)S(1)}, f32[128,128]{1,0:T(8,128)S(1)}) custom-call(bf16[64,1152]{1,0:T(8,128)(2,1)S(1)} %collective-permute-done.3.refs_0_, bf16[64,1152]{1,0:T(8,128)(2,1)S(1)} %collective-permute-done.8.refs_1_, bf16[3,1024,512]{2,1,0:T(8,128)(2,1)S(1)} %get-tuple-element.72.refs_2_, ...), custom_call_target="tpu_custom_call" | custom-call | bytes 1024 | tf_op jit(solution)/shard_map/projections_part/pallas_call | solution.py:498
  22.7 0.0 collective-permute-done.9.refs_1_
  22.7 0.6 %collective-permute-done.7.refs_0_ = bf16[64,1152]{1,0:T(8,128)(2,1)S(1)} collective-permute-done((bf16[64,1152]{1,0:T(8,128)(2,1)S(1)}, bf16[64,1152]{1,0:T(8,128)(2,1)S(1)}, u32[]{:S(2)}, u32[]{:S(2)}) %collective-permute-start.7) | collective-permute-done | bytes 147488 | tf_op jit(solution)/shard_map/ppermute | solution.py:695
  23.3 0.7 %projections_last.1 = (bf16[384,128]{1,0:T(8,128)(2,1)S(1)}, bf16[384,128]{1,0:T(8,128)(2,1)S(1)}, bf16[384,128]{1,0:T(8,128)(2,1)S(1)}, bf16[384,128]{1,0:T(8,128)(2,1)S(1)}) custom-call(bf16[64,1152]{1,0:T(8,128)(2,1)S(1)} %collective-permute-done.7.refs_0_, bf16[64,1152]{1,0:T(8,128)(2,1)S(1)} %collective-permute-done.9.refs_1_, ...), custom_call_target="tpu_custom_call" | custom-call | bytes 1024 | tf_op jit(solution)/shard_map/projections_last/pallas_call | solution.py:535
  24.0 0.2 collective-permute-start.12
  24.3 3.9 %collective-permute-start.14 = (bf16[384,128]{1,0:T(8,128)(2,1)S(1)}, bf16[384,128]{1,0:T(8,128)(2,1)S(1)}, u32[]{:S(2)}, u32[]{:S(2)}) collective-permute-start(bf16[384,128]{1,0:T(8,128)(2,1)S(1)} %get-tuple-element.80), channel_id=1, source_target_pairs={{0,25},{1,24},{2,27},{3,26},{4,29},{5,28},{6,31},{7,30},{8,17},{9,... | collective-permute-start | bytes 294920 | tf_op jit(solution)/shard_map/ppermute | solution.py:736
  28.1 0.0 collective-permute-start.13
  28.1 0.3 collective-permute-start.10
  28.5 0.0 collective-permute-done.12.refs_0_
  28.5 1.2 %collective-permute-start.15 = (bf16[256,128]{1,0:T(8,128)(2,1)S(1)}, bf16[256,128]{1,0:T(8,128)(2,1)S(1)}, u32[]{:S(2)}, u32[]{:S(2)}) collective-permute-start(bf16[256,128]{1,0:T(8,128)(2,1)S(1)} %slice.17), channel_id=1, source_target_pairs={{0,4},{4,0},{8,12},{12,8},{16,20},{20,16},{24,28},{28,24},{1,5},{5... | collective-permute-start | bytes 196616 | tf_op jit(solution)/shard_map/ppermute | solution.py:739
  29.7 1.8 %collective-permute-done.14.refs_3_ = bf16[384,128]{1,0:T(8,128)(2,1)S(1)} collective-permute-done((bf16[384,128]{1,0:T(8,128)(2,1)S(1)}, bf16[384,128]{1,0:T(8,128)(2,1)S(1)}, u32[]{:S(2)}, u32[]{:S(2)}) %collective-permute-start.14) | collective-permute-done | bytes 98336 | tf_op jit(solution)/shard_map/ppermute | solution.py:736
  31.5 1.0 %collective-permute-start.16 = (bf16[256,128]{1,0:T(8,128)(2,1)S(1)}, bf16[256,128]{1,0:T(8,128)(2,1)S(1)}, u32[]{:S(2)}, u32[]{:S(2)}) collective-permute-start(bf16[256,128]{1,0:T(8,128)(2,1)S(1)} %slice.18), channel_id=1, source_target_pairs={{0,4},{4,0},{8,12},{12,8},{16,20},{20,16},{24,28},{28,24},{1,5},{5... | collective-permute-start | bytes 196616 | tf_op jit(solution)/shard_map/ppermute | solution.py:739
  32.4 1.7 %collective-permute-done.13.refs_1_ = bf16[384,128]{1,0:T(8,128)(2,1)S(1)} collective-permute-done((bf16[384,128]{1,0:T(8,128)(2,1)S(1)}, bf16[384,128]{1,0:T(8,128)(2,1)S(1)}, u32[]{:S(2)}, u32[]{:S(2)}) %collective-permute-start.13) | collective-permute-done | bytes 98336 | tf_op jit(solution)/shard_map/ppermute | solution.py:736
  34.2 1.3 %collective-permute-start.17 = (bf16[256,128]{1,0:T(8,128)(2,1)S(1)}, bf16[256,128]{1,0:T(8,128)(2,1)S(1)}, u32[]{:S(2)}, u32[]{:S(2)}) collective-permute-start(bf16[256,128]{1,0:T(8,128)(2,1)S(1)} %slice.19), channel_id=1, source_target_pairs={{0,4},{4,0},{8,12},{12,8},{16,20},{20,16},{24,28},{28,24},{1,5},{5... | collective-permute-start | bytes 196616 | tf_op jit(solution)/shard_map/ppermute | solution.py:739
  35.5 1.1 %collective-permute-done.10.refs_2_ = bf16[384,128]{1,0:T(8,128)(2,1)S(1)} collective-permute-done((bf16[384,128]{1,0:T(8,128)(2,1)S(1)}, bf16[384,128]{1,0:T(8,128)(2,1)S(1)}, u32[]{:S(2)}, u32[]{:S(2)}) %collective-permute-start.10) | collective-permute-done | bytes 98336 | tf_op jit(solution)/shard_map/ppermute | solution.py:736
  36.7 1.0 %collective-permute-start.11 = (bf16[256,128]{1,0:T(8,128)(2,1)S(1)}, bf16[256,128]{1,0:T(8,128)(2,1)S(1)}, u32[]{:S(2)}, u32[]{:S(2)}) collective-permute-start(bf16[256,128]{1,0:T(8,128)(2,1)S(1)} %slice.16), channel_id=1, source_target_pairs={{0,4},{4,0},{8,12},{12,8},{16,20},{20,16},{24,28},{28,24},{1,5},{5... | collective-permute-start | bytes 196616 | tf_op jit(solution)/shard_map/ppermute | solution.py:739
  37.6 0.0 collective-permute-done.15.refs_4_
  37.6 0.0 collective-permute-done.16.refs_5_
  37.6 0.1 collective-permute-done.17.refs_6_
  37.7 1.3 %attention_most.1 = (bf16[512,128]{1,0:T(8,128)(2,1)S(1)}, f32[512,128]{1,0:T(8,128)S(1)}, f32[512,128]{1,0:T(8,128)S(1)}, f32[512,128]{1,0:T(8,128)S(1)}) custom-call(bf16[384,128]{1,0:T(8,128)(2,1)S(1)} %collective-permute-done.12.refs_0_, bf16[384,128]{1,0:T(8,128)(2,1)S(1)} %collective-permute-done.13.refs_1_, ...), custom_call_target="tpu_custom_call" | custom-call | bytes 1024 | tf_op jit(solution)/shard_map/attention_most/pallas_call | solution.py:596
  39.0 0.7 %collective-permute-done.11.other_ref = bf16[256,128]{1,0:T(8,128)(2,1)S(1)} collective-permute-done((bf16[256,128]{1,0:T(8,128)(2,1)S(1)}, bf16[256,128]{1,0:T(8,128)(2,1)S(1)}, u32[]{:S(2)}, u32[]{:S(2)}) %collective-permute-start.11) | collective-permute-done | bytes 65568 | tf_op jit(solution)/shard_map/ppermute | solution.py:739
  39.8 0.5 %attention_rest.1 = (bf16[128,128]{1,0:T(8,128)(2,1)S(1)}, bf16[128,128]{1,0:T(8,128)(2,1)S(1)}, bf16[128,128]{1,0:T(8,128)(2,1)S(1)}, bf16[128,128]{1,0:T(8,128)(2,1)S(1)}) custom-call(bf16[256,128]{1,0:T(8,128)(2,1)S(1)} %collective-permute-done.11.other_ref, bf16[512,128]{1,0:T(8,128)(2,1)S(1)} %get-tuple-element.81.query_ref, ...), custom_call_target="tpu_custom_call" | custom-call | bytes 1024 | tf_op jit(solution)/shard_map/attention_rest/pallas_call | solution.py:629
  40.3 2.7 %collective-permute-start.18 = (bf16[128,128]{1,0:T(8,128)(2,1)S(1)}, bf16[128,128]{1,0:T(8,128)(2,1)S(1)}, u32[]{:S(2)}, u32[]{:S(2)}) collective-permute-start(bf16[128,128]{1,0:T(8,128)(2,1)S(1)} %get-tuple-element.85), channel_id=1, source_target_pairs={{0,17},{1,16},{2,19},{3,18},{4,21},{5,20},{6,23},{7,22},{8,25},{9,... | collective-permute-start | bytes 98312 | tf_op jit(solution)/shard_map/ppermute | solution.py:736
  43.0 1.3 %collective-permute-start.19 = (bf16[128,128]{1,0:T(8,128)(2,1)S(1)}, bf16[128,128]{1,0:T(8,128)(2,1)S(1)}, u32[]{:S(2)}, u32[]{:S(2)}) collective-permute-start(bf16[128,128]{1,0:T(8,128)(2,1)S(1)} %get-tuple-element.86), channel_id=1, source_target_pairs={{0,25},{1,24},{2,27},{3,26},{4,29},{5,28},{6,31},{7,30},{8,17},{9,... | collective-permute-start | bytes 98312 | tf_op jit(solution)/shard_map/ppermute | solution.py:736
  44.3 0.4 collective-permute-start.20
  44.7 0.3 collective-permute-start.21
  44.9 0.0 collective-permute-done.18.refs_0_
  45.0 3.2 %collective-permute-done.19.refs_1_ = bf16[128,128]{1,0:T(8,128)(2,1)S(1)} collective-permute-done((bf16[128,128]{1,0:T(8,128)(2,1)S(1)}, bf16[128,128]{1,0:T(8,128)(2,1)S(1)}, u32[]{:S(2)}, u32[]{:S(2)}) %collective-permute-start.19) | collective-permute-done | bytes 32800 | tf_op jit(solution)/shard_map/ppermute | solution.py:736
  48.2 0.0 collective-permute-done.20.refs_2_
  48.2 0.0 collective-permute-done.21.refs_3_
  48.2 0.7 %join_heads.1 = bf16[128,512]{1,0:T(8,128)(2,1)} custom-call(bf16[128,128]{1,0:T(8,128)(2,1)S(1)} %collective-permute-done.18.refs_0_, bf16[128,128]{1,0:T(8,128)(2,1)S(1)} %collective-permute-done.19.refs_1_, bf16[128,128]{1,0:T(8,128)(2,1)S(1)} %collective-permute-done.20.refs_2_, bf16[128,128]{1,0:T(8,128)(2,1)S(1)} %collective-permute-done.21.refs_3_), custom_call_target="tpu_custom_call" | custom-call | bytes 1024 | tf_op jit(solution)/shard_map/join_heads/pallas_call | solution.py:649
  (4 shorter events, 0.0 us)
Async XLA Ops:
  1.3 9.1 %collective-permute-start.1 = (bf16[64,1024]{1,0:T(8,128)(2,1)S(1)}, bf16[64,1024]{1,0:T(8,128)(2,1)S(1)}, u32[]{:S(2)}, u32[]{:S(2)}) collective-permute-start(bf16[64,1024]{1,0:T(8,128)(2,1)S(1)} %get-tuple-element.48.high_ref), channel_id=1, source_target_pairs={{0,4},{4,8},{8,12},{12,16},{16,20},{20,24},{24,28},{1,5},{5,9},{9,... | collective-permute-start | bytes 393224 | tf_op jit(solution)/shard_map/ppermute | solution.py:701
  5.3 8.3 %collective-permute-start = (bf16[64,1024]{1,0:T(8,128)(2,1)S(1)}, bf16[64,1024]{1,0:T(8,128)(2,1)S(1)}, u32[]{:S(2)}, u32[]{:S(2)}) collective-permute-start(bf16[64,1024]{1,0:T(8,128)(2,1)S(1)} %get-tuple-element.47.low_ref), channel_id=1, source_target_pairs={{0,4},{4,8},{8,12},{12,16},{16,20},{20,24},{24,28},{1,5},{5,9},{9,... | collective-permute-start | bytes 393224 | tf_op jit(solution)/shard_map/ppermute | solution.py:701
  8.5 2.0 %copy-start = (f32[1024]{0:T(1024)S(1)}, f32[1024]{0:T(1024)}, u32[]{:S(2)}) copy-start(f32[1024]{0:T(1024)} %param.10) | copy-start | bytes 12292
  11.1 2.5 %collective-permute-start.2 = (bf16[32,1152]{1,0:T(8,128)(2,1)S(1)}, bf16[32,1152]{1,0:T(8,128)(2,1)S(1)}, u32[]{:S(2)}, u32[]{:S(2)}) collective-permute-start(bf16[32,1152]{1,0:T(8,128)(2,1)S(1)} %get-tuple-element.55), channel_id=1, source_target_pairs={{0,1},{1,0},{2,3},{3,2},{4,5},{5,4},{6,7},{7,6},{8,9},{9,8},{10,11... | collective-permute-start | bytes 221192 | tf_op jit(solution)/shard_map/ppermute | solution.py:695
  12.4 8.4 %collective-permute-start.8 = (bf16[64,1152]{1,0:T(8,128)(2,1)S(1)}, bf16[64,1152]{1,0:T(8,128)(2,1)S(1)}, u32[]{:S(2)}, u32[]{:S(2)}) collective-permute-start(bf16[64,1152]{1,0:T(8,128)(2,1)S(1)} %get-tuple-element.64.high_ref), channel_id=1, source_target_pairs={{0,3},{1,2},{2,1},{3,0},{4,7},{5,6},{6,5},{7,4},{8,11},{9,10},{10,... | collective-permute-start | bytes 442376 | tf_op jit(solution)/shard_map/ppermute | solution.py:695
  15.3 6.6 %collective-permute-start.3 = (bf16[64,1152]{1,0:T(8,128)(2,1)S(1)}, bf16[64,1152]{1,0:T(8,128)(2,1)S(1)}, u32[]{:S(2)}, u32[]{:S(2)}) collective-permute-start(bf16[64,1152]{1,0:T(8,128)(2,1)S(1)} %get-tuple-element.58.low_ref), channel_id=1, source_target_pairs={{0,3},{1,2},{2,1},{3,0},{4,7},{5,6},{6,5},{7,4},{8,11},{9,10},{10,... | collective-permute-start | bytes 442376 | tf_op jit(solution)/shard_map/ppermute | solution.py:695
  16.5 4.7 %collective-permute-start.6 = (bf16[32,1152]{1,0:T(8,128)(2,1)S(1)}, bf16[32,1152]{1,0:T(8,128)(2,1)S(1)}, u32[]{:S(2)}, u32[]{:S(2)}) collective-permute-start(bf16[32,1152]{1,0:T(8,128)(2,1)S(1)} %get-tuple-element.62), channel_id=1, source_target_pairs={{0,1},{1,0},{2,3},{3,2},{4,5},{5,4},{6,7},{7,6},{8,9},{9,8},{10,11... | collective-permute-start | bytes 221192 | tf_op jit(solution)/shard_map/ppermute | solution.py:695
  16.7 4.6 %collective-permute-start.4 = (bf16[32,1152]{1,0:T(8,128)(2,1)S(1)}, bf16[32,1152]{1,0:T(8,128)(2,1)S(1)}, u32[]{:S(2)}, u32[]{:S(2)}) collective-permute-start(bf16[32,1152]{1,0:T(8,128)(2,1)S(1)} %get-tuple-element.59), channel_id=1, source_target_pairs={{0,1},{1,0},{2,3},{3,2},{4,5},{5,4},{6,7},{7,6},{8,9},{9,8},{10,11... | collective-permute-start | bytes 221192 | tf_op jit(solution)/shard_map/ppermute | solution.py:695
  17.1 4.2 %collective-permute-start.5 = (bf16[32,1152]{1,0:T(8,128)(2,1)S(1)}, bf16[32,1152]{1,0:T(8,128)(2,1)S(1)}, u32[]{:S(2)}, u32[]{:S(2)}) collective-permute-start(bf16[32,1152]{1,0:T(8,128)(2,1)S(1)} %get-tuple-element.60), channel_id=1, source_target_pairs={{0,1},{1,0},{2,3},{3,2},{4,5},{5,4},{6,7},{7,6},{8,9},{9,8},{10,11... | collective-permute-start | bytes 221192 | tf_op jit(solution)/shard_map/ppermute | solution.py:695
  20.9 1.9 %collective-permute-start.9 = (bf16[64,1152]{1,0:T(8,128)(2,1)S(1)}, bf16[64,1152]{1,0:T(8,128)(2,1)S(1)}, u32[]{:S(2)}, u32[]{:S(2)}) collective-permute-start(bf16[64,1152]{1,0:T(8,128)(2,1)S(1)} %collective-permute-done.8.refs_1_), channel_id=1, source_target_pairs={{0,1},{1,0},{2,3},{3,2},{4,5},{5,4},{6,7},{7,6},{8,9},{9,8},{10,11... | collective-permute-start | bytes 442376 | tf_op jit(solution)/shard_map/ppermute | solution.py:695
  21.9 1.4 %collective-permute-start.7 = (bf16[64,1152]{1,0:T(8,128)(2,1)S(1)}, bf16[64,1152]{1,0:T(8,128)(2,1)S(1)}, u32[]{:S(2)}, u32[]{:S(2)}) collective-permute-start(bf16[64,1152]{1,0:T(8,128)(2,1)S(1)} %collective-permute-done.3.refs_0_), channel_id=1, source_target_pairs={{0,1},{1,0},{2,3},{3,2},{4,5},{5,4},{6,7},{7,6},{8,9},{9,8},{10,11... | collective-permute-start | bytes 442376 | tf_op jit(solution)/shard_map/ppermute | solution.py:695
  24.0 4.4 %collective-permute-start.12 = (bf16[384,128]{1,0:T(8,128)(2,1)S(1)}, bf16[384,128]{1,0:T(8,128)(2,1)S(1)}, u32[]{:S(2)}, u32[]{:S(2)}) collective-permute-start(bf16[384,128]{1,0:T(8,128)(2,1)S(1)} %get-tuple-element.78), channel_id=1, source_target_pairs={{0,1},{1,0},{2,3},{3,2},{4,5},{5,4},{6,7},{7,6},{8,9},{9,8},{10,11... | collective-permute-start | bytes 294920 | tf_op jit(solution)/shard_map/ppermute | solution.py:736
  24.3 7.2 %collective-permute-start.14 = (bf16[384,128]{1,0:T(8,128)(2,1)S(1)}, bf16[384,128]{1,0:T(8,128)(2,1)S(1)}, u32[]{:S(2)}, u32[]{:S(2)}) collective-permute-start(bf16[384,128]{1,0:T(8,128)(2,1)S(1)} %get-tuple-element.80), channel_id=1, source_target_pairs={{0,25},{1,24},{2,27},{3,26},{4,29},{5,28},{6,31},{7,30},{8,17},{9,... | collective-permute-start | bytes 294920 | tf_op jit(solution)/shard_map/ppermute | solution.py:736
  28.1 6.0 %collective-permute-start.13 = (bf16[384,128]{1,0:T(8,128)(2,1)S(1)}, bf16[384,128]{1,0:T(8,128)(2,1)S(1)}, u32[]{:S(2)}, u32[]{:S(2)}) collective-permute-start(bf16[384,128]{1,0:T(8,128)(2,1)S(1)} %get-tuple-element.79), channel_id=1, source_target_pairs={{0,9},{1,8},{2,11},{3,10},{4,13},{5,12},{6,15},{7,14},{8,1},{9,0},... | collective-permute-start | bytes 294920 | tf_op jit(solution)/shard_map/ppermute | solution.py:736
  28.1 8.5 %collective-permute-start.10 = (bf16[384,128]{1,0:T(8,128)(2,1)S(1)}, bf16[384,128]{1,0:T(8,128)(2,1)S(1)}, u32[]{:S(2)}, u32[]{:S(2)}) collective-permute-start(bf16[384,128]{1,0:T(8,128)(2,1)S(1)} %get-tuple-element.77), channel_id=1, source_target_pairs={{0,17},{1,16},{2,19},{3,18},{4,21},{5,20},{6,23},{7,22},{8,25},{9,... | collective-permute-start | bytes 294920 | tf_op jit(solution)/shard_map/ppermute | solution.py:736
  28.5 9.2 %collective-permute-start.15 = (bf16[256,128]{1,0:T(8,128)(2,1)S(1)}, bf16[256,128]{1,0:T(8,128)(2,1)S(1)}, u32[]{:S(2)}, u32[]{:S(2)}) collective-permute-start(bf16[256,128]{1,0:T(8,128)(2,1)S(1)} %slice.17), channel_id=1, source_target_pairs={{0,4},{4,0},{8,12},{12,8},{16,20},{20,16},{24,28},{28,24},{1,5},{5... | collective-permute-start | bytes 196616 | tf_op jit(solution)/shard_map/ppermute | solution.py:739
  31.5 6.2 %collective-permute-start.16 = (bf16[256,128]{1,0:T(8,128)(2,1)S(1)}, bf16[256,128]{1,0:T(8,128)(2,1)S(1)}, u32[]{:S(2)}, u32[]{:S(2)}) collective-permute-start(bf16[256,128]{1,0:T(8,128)(2,1)S(1)} %slice.18), channel_id=1, source_target_pairs={{0,4},{4,0},{8,12},{12,8},{16,20},{20,16},{24,28},{28,24},{1,5},{5... | collective-permute-start | bytes 196616 | tf_op jit(solution)/shard_map/ppermute | solution.py:739
  34.2 3.6 %collective-permute-start.17 = (bf16[256,128]{1,0:T(8,128)(2,1)S(1)}, bf16[256,128]{1,0:T(8,128)(2,1)S(1)}, u32[]{:S(2)}, u32[]{:S(2)}) collective-permute-start(bf16[256,128]{1,0:T(8,128)(2,1)S(1)} %slice.19), channel_id=1, source_target_pairs={{0,4},{4,0},{8,12},{12,8},{16,20},{20,16},{24,28},{28,24},{1,5},{5... | collective-permute-start | bytes 196616 | tf_op jit(solution)/shard_map/ppermute | solution.py:739
  36.7 3.1 %collective-permute-start.11 = (bf16[256,128]{1,0:T(8,128)(2,1)S(1)}, bf16[256,128]{1,0:T(8,128)(2,1)S(1)}, u32[]{:S(2)}, u32[]{:S(2)}) collective-permute-start(bf16[256,128]{1,0:T(8,128)(2,1)S(1)} %slice.16), channel_id=1, source_target_pairs={{0,4},{4,0},{8,12},{12,8},{16,20},{20,16},{24,28},{28,24},{1,5},{5... | collective-permute-start | bytes 196616 | tf_op jit(solution)/shard_map/ppermute | solution.py:739
  40.3 4.6 %collective-permute-start.18 = (bf16[128,128]{1,0:T(8,128)(2,1)S(1)}, bf16[128,128]{1,0:T(8,128)(2,1)S(1)}, u32[]{:S(2)}, u32[]{:S(2)}) collective-permute-start(bf16[128,128]{1,0:T(8,128)(2,1)S(1)} %get-tuple-element.85), channel_id=1, source_target_pairs={{0,17},{1,16},{2,19},{3,18},{4,21},{5,20},{6,23},{7,22},{8,25},{9,... | collective-permute-start | bytes 98312 | tf_op jit(solution)/shard_map/ppermute | solution.py:736
  43.0 5.2 %collective-permute-start.19 = (bf16[128,128]{1,0:T(8,128)(2,1)S(1)}, bf16[128,128]{1,0:T(8,128)(2,1)S(1)}, u32[]{:S(2)}, u32[]{:S(2)}) collective-permute-start(bf16[128,128]{1,0:T(8,128)(2,1)S(1)} %get-tuple-element.86), channel_id=1, source_target_pairs={{0,25},{1,24},{2,27},{3,26},{4,29},{5,28},{6,31},{7,30},{8,17},{9,... | collective-permute-start | bytes 98312 | tf_op jit(solution)/shard_map/ppermute | solution.py:736
  44.3 3.8 %collective-permute-start.20 = (bf16[128,128]{1,0:T(8,128)(2,1)S(1)}, bf16[128,128]{1,0:T(8,128)(2,1)S(1)}, u32[]{:S(2)}, u32[]{:S(2)}) collective-permute-start(bf16[128,128]{1,0:T(8,128)(2,1)S(1)} %get-tuple-element.87), channel_id=1, source_target_pairs={{0,9},{1,8},{2,11},{3,10},{4,13},{5,12},{6,15},{7,14},{8,1},{9,0},... | collective-permute-start | bytes 98312 | tf_op jit(solution)/shard_map/ppermute | solution.py:736
  44.7 3.5 %collective-permute-start.21 = (bf16[128,128]{1,0:T(8,128)(2,1)S(1)}, bf16[128,128]{1,0:T(8,128)(2,1)S(1)}, u32[]{:S(2)}, u32[]{:S(2)}) collective-permute-start(bf16[128,128]{1,0:T(8,128)(2,1)S(1)} %get-tuple-element.88), channel_id=1, source_target_pairs={{0,1},{1,0},{2,3},{3,2},{4,5},{5,4},{6,7},{7,6},{8,9},{9,8},{10,11... | collective-permute-start | bytes 98312 | tf_op jit(solution)/shard_map/ppermute | solution.py:736
